TPU v7x, 256 devices: a whole 4x4x8 slice. The times are simulated.
256 devices in a mesh: gx: 16 (over z_hi, x), gy: 16 (over z_lo, y, core).
Axes of the slice: x: 4, y: 4, z: 8 (z_hi: 4, z_lo: 2; z = z_hi * 2 + z_lo), core: 2. Of those that a mesh axis runs over, the one named last changes fastest.
Arguments:
- skip_feat: bfloat16 [64, 32, 128, 128], P(None, 'gx', 'gy'), may hold values from -6 to 6
- cotangent: bfloat16 [64, 32, 128, 128], P(None, 'gx', 'gy'), may hold values from -6 to 6
- w_coarse: bfloat16 [27, 64, 128], replicated, may hold values from -0.15625 to 0.15625
- w_dec: bfloat16 [27, 192, 64], replicated, may hold values from -0.078125 to 0.078125
Outputs:
- skip_grad: bfloat16 [64, 32, 128, 128], P(None, 'gx', 'gy')
- dec_total: float32 [27, 192, 64], replicated
- coarse_total: float32 [27, 64, 128], replicated
All inputs are finite; a program needn't handle non-finite values.
Results may differ from a plain program's by a relative error of at most 0.01.
Values may be sent and summed in bfloat16 or wider, within the bound.
No kernel may reach another device: no remote copies, remote signals or barrier semaphores. Data moves between devices by JAX's collectives and lax.ppermute only.
A program may use at most 128 MiB of HBM per device.

v0:
```python
import math

import jax
import jax.numpy as jnp
from jax import lax
from jax.sharding import PartitionSpec as P


def extended(block, sides, width):
    for axis, dim in sides:
        count = lax.axis_size(axis)
        forward = [(i, i + 1) for i in range(count - 1)]
        backward = [(target, source) for source, target in forward]
        low = lax.ppermute(
            lax.slice_in_dim(block, block.shape[dim] - width, None, axis=dim), axis, forward
        )
        high = lax.ppermute(lax.slice_in_dim(block, 0, width, axis=dim), axis, backward)
        block = jnp.concatenate([low, block, high], axis=dim)
    return block


def offsets_list():
    return [
        (first, second, third) for first in range(3) for second in range(3) for third in range(3)
    ]


def upsample(field):
    chans, size_x, size_y, size_z = field.shape
    grown = jnp.broadcast_to(
        field[:, :, None, :, None, :, None], (chans, size_x, 2, size_y, 2, size_z, 2)
    )
    return grown.reshape(chans, 2 * size_x, 2 * size_y, 2 * size_z)


def block_pool(field):
    chans, size_x, size_y, size_z = field.shape
    return field.reshape(chans, size_x // 2, 2, size_y // 2, 2, size_z // 2, 2)


def pad_depth(field):
    return jnp.pad(field, ((0, 0), (0, 0), (0, 0), (1, 1)))


def forward_slice(padded, shape, first, second, third):
    return padded[:, first : first + shape[1], second : second + shape[2], third : third + shape[3]]


def backward_slice(padded, shape, first, second, third):
    return forward_slice(padded, shape, 2 - first, 2 - second, 2 - third)


def conv_forward(padded, weights, shape):
    total = jnp.zeros((weights.shape[2],) + tuple(shape[1:]), jnp.float32)
    for index, (first, second, third) in enumerate(offsets_list()):
        total = total + jnp.einsum(
            "cxyz,co->oxyz",
            forward_slice(padded, shape, first, second, third),
            weights[index],
            preferred_element_type=jnp.float32,
        )
    return total


def conv_backward(padded, weights, shape):
    total = jnp.zeros((weights.shape[1],) + tuple(shape[1:]), jnp.float32)
    for index, (first, second, third) in enumerate(offsets_list()):
        total = total + jnp.einsum(
            "kxyz,ck->cxyz",
            backward_slice(padded, shape, first, second, third),
            weights[index],
            preferred_element_type=jnp.float32,
        )
    return total


def body(skip_feat, cotangent, w_coarse, w_dec):
    shape_fine = skip_feat.shape
    cells_total = (
        shape_fine[1] * shape_fine[2] * shape_fine[3] * lax.axis_size("gx") * lax.axis_size("gy")
    )
    factor = 1.0 / math.sqrt(cells_total)
    n_coarse = w_coarse.shape[2]
    pooled = block_pool(skip_feat.astype(jnp.float32)).mean(axis=(2, 4, 6)).astype(jnp.bfloat16)
    shape_coarse = pooled.shape
    pooled_rim = pad_depth(extended(pooled, (("gx", 1), ("gy", 2)), 1))
    pre_b = conv_forward(pooled_rim, w_coarse, shape_coarse)
    coarse_out = jax.nn.silu(pre_b).astype(jnp.bfloat16)
    joined = jnp.concatenate([upsample(coarse_out), skip_feat], axis=0)
    cot_rim = pad_depth(extended(cotangent, (("gx", 1), ("gy", 2)), 1))
    joined_grad = conv_backward(cot_rim, w_dec, shape_fine)
    joined_rim = pad_depth(extended(joined, (("gx", 1), ("gy", 2)), 1))
    dec_grad = jnp.stack(
        [
            jnp.einsum(
                "cxyz,kxyz->ck",
                forward_slice(joined_rim, shape_fine, a, b, c),
                cotangent,
                preferred_element_type=jnp.float32,
            )
            for a, b, c in offsets_list()
        ]
    )
    dec_grad = dec_grad * factor
    coarse_grad = block_pool(joined_grad[:n_coarse]).sum(axis=(2, 4, 6))
    sigmoid_pre = jax.nn.sigmoid(pre_b)
    pre_grad = (coarse_grad * sigmoid_pre * (1.0 + pre_b * (1.0 - sigmoid_pre))).astype(
        jnp.bfloat16
    )
    coarse_grad_w = (
        jnp.stack(
            [
                jnp.einsum(
                    "cxyz,oxyz->co",
                    forward_slice(pooled_rim, shape_coarse, a, b, c),
                    pre_grad,
                    preferred_element_type=jnp.float32,
                )
                for a, b, c in offsets_list()
            ]
        )
        * factor
    )
    pre_rim = pad_depth(extended(pre_grad, (("gx", 1), ("gy", 2)), 1))
    pooled_grad = conv_backward(pre_rim, w_coarse, pre_grad.shape)
    skip_grad = (joined_grad[n_coarse:] + upsample(pooled_grad) * 0.125).astype(jnp.bfloat16)
    dec_total, coarse_total = lax.psum((dec_grad, coarse_grad_w), ("gx", "gy"))
    return (skip_grad, dec_total, coarse_total)


def solution(mesh):
    placed = (P(None, "gx", "gy", None), P(None, "gx", "gy", None), P(), P())
    return jax.shard_map(
        body,
        mesh=mesh,
        in_specs=placed,
        out_specs=(P(None, "gx", "gy", None), P(), P()),
        check_vma=False,
    )
```

profile of v0, /device:TPU:1, one launch (start us, length us, event | category | flops | bytes accessed | tf_op | source)
XLA Modules:
  0.0 451.8 jit_solution(5305478483482216543)
XLA Ops:
  10.4 4.6 %collective-permute-start.4 = (bf16[64,1,4,64]{0,3,2,1:T(8,128)(2,1)S(1)}, bf16[64,1,4,64]{0,3,2,1:T(8,128)(2,1)S(1)}, u32[]{:S(2)}, u32[]{:S(2)}) collective-permute-start(bf16[64,1,4,64]{0,3,2,1:T(8,128)(2,1)S(1)} %fusion.427), channel_id=1, source_target_pairs={{0,16},{16,32},{32,48},{48,64},{64,80},{80,96},{96,112},{112,128},... | collective-permute-start | bytes 98312 | tf_op jit(solution)/shard_map/ppermute | solution.py:14
  15.1 3.4 collective-permute-start
  21.8 3.7 collective-permute-start.7
  25.5 2.8 collective-permute-start.6
  38.7 4.2 collective-permute-start.2
  43.0 2.1 collective-permute-start.3
  45.1 2.3 fusion.146
  47.4 2.3 fusion.142
  57.4 1.6 fusion.173
  62.2 1.6 fusion.179
  63.8 1.6 fusion.181
  67.0 1.6 fusion.185
  70.2 1.7 fusion.189
  83.0 1.6 fusion.200
  84.6 11.5 %bitcast_add_fusion = f32[192,2,8,128]{3,0,2,1:T(8,128)S(1)} fusion(f32[2,8,128,192]{2,3,1,0:T(8,128)} %fusion.195, f32[2,8,128,192]{2,3,1,0:T(8,128)S(1)} %fusion.161, f32[2,8,128,192]{2,3,1,0:T(8,128)S(1)} %fusion.163, f32[2,8,128,192]{2,3,1,0:T(8,128)} %fusion.146, f32[2,8,128,192]{2,3,1,0:T(8,128)S(1)} %fusion.165, f32[2,8,128,192]{2,3,1,0:T(8,128)S(1)} %fusion.167, ...), kind=kOutput, calls=%fused_computation.17 | convolution fusion | flops 60555264 | bytes 42762240 | tf_op jit(solution)/shard_map/kxyz,ck->cxyz/dot_general | solution.py:68
  100.1 4.9 %collective-permute-start.8 = (bf16[128,1,4,64]{0,3,2,1:T(8,128)(2,1)S(1)}, bf16[128,1,4,64]{0,3,2,1:T(8,128)(2,1)S(1)}, u32[]{:S(2)}, u32[]{:S(2)}) collective-permute-start(bf16[128,1,4,64]{0,3,2,1:T(8,128)(2,1)S(1)} %bitcast.1064), channel_id=1, source_target_pairs={{0,16},{16,32},{32,48},{48,64},{64,80},{80,96},{96,112},{112,128},... | collective-permute-start | bytes 196616 | tf_op jit(solution)/shard_map/ppermute | solution.py:14
  107.8 6.2 %collective-permute-start.12 = (bf16[192,1,8,128]{3,0,2,1:T(8,128)(2,1)S(1)}, bf16[192,1,8,128]{3,0,2,1:T(8,128)(2,1)S(1)}, u32[]{:S(2)}, u32[]{:S(2)}) collective-permute-start(bf16[192,1,8,128]{3,0,2,1:T(8,128)(2,1)S(1)} %get-tuple-element.16), channel_id=1, source_target_pairs={{0,16},{16,32},{32,48},{48,64},{64,80},{80,96},{96,112},{112,128},... | collective-permute-start | bytes 1179656 | tf_op jit(solution)/shard_map/ppermute | solution.py:14
  119.8 1.9 collective-permute-start.11
  121.7 4.2 collective-permute-start.10
  134.3 1.9 collective-permute-start.15
  136.3 4.2 collective-permute-start.14
  143.1 4.4 select_maximum_fusion
  163.7 277.4 %all-reduce.7.cloned.1.call-done = (f32[27,192,64]{1,2,0:T(8,128)}, f32[27,64,128]{2,1,0:T(8,128)}) async-done(((f32[27,192,64]{1,2,0:T(8,128)}, f32[27,64,128]{2,1,0:T(8,128)}), (f32[27,192,64]{1,2,0:T(8,128)}, f32[27,64,128]{2,1,0:T(8,128)})) %all-reduce.7.cloned.1.call-update) | async-done | bytes 2211856 | tf_op jit(solution)/shard_map/psum | solution.py:127
  441.1 3.0 copy.395
  (241 shorter events, 81.9 us)
Async XLA Ops:
  7.2 433.9 %all-reduce.7.cloned.1.call-start = ((), (), s32[]{:S(2)}) async-start(), calls=%async_computation | async-start | bytes 5308416 | tf_op jit(solution)/shard_map/psum | solution.py:127
  8.5 12.4 %copy-start.11 = (bf16[64,2,8,128]{3,2,1,0:T(8,128)(2,1)S(1)}, bf16[64,2,8,128]{3,2,1,0:T(8,128)(2,1)}, u32[]{:S(2)}) copy-start(bf16[64,2,8,128]{3,2,1,0:T(8,128)(2,1)} %param.4) | copy-start | bytes 786436
  8.9 27.5 %copy-start.7 = (f32[64,4,64]{0,2,1:T(8,128)}, f32[64,4,64]{0,2,1:T(8,128)S(1)}, u32[]{:S(2)}) copy-start(f32[64,4,64]{0,2,1:T(8,128)S(1)} %reduce_sum.37) | copy-start | bytes 196612
  9.0 19.3 %copy-start.9 = (bf16[27,64,128]{2,1,0:T(8,128)(2,1)S(1)}, bf16[27,64,128]{2,1,0:T(8,128)(2,1)}, u32[]{:S(2)}) copy-start(bf16[27,64,128]{2,1,0:T(8,128)(2,1)} %param.6) | copy-start | bytes 1327108
  9.0 12.7 %collective-permute-start.5 = (bf16[64,1,4,64]{0,3,2,1:T(8,128)(2,1)S(1)}, bf16[64,1,4,64]{0,3,2,1:T(8,128)(2,1)S(1)}, u32[]{:S(2)}, u32[]{:S(2)}) collective-permute-start(bf16[64,1,4,64]{0,3,2,1:T(8,128)(2,1)S(1)} %fusion.427), channel_id=1, source_target_pairs={{16,0},{32,16},{48,32},{64,48},{80,64},{96,80},{112,96},{128,112},... | collective-permute-start | bytes 98312 | tf_op jit(solution)/shard_map/ppermute | solution.py:17
  10.4 11.3 %collective-permute-start.4 = (bf16[64,1,4,64]{0,3,2,1:T(8,128)(2,1)S(1)}, bf16[64,1,4,64]{0,3,2,1:T(8,128)(2,1)S(1)}, u32[]{:S(2)}, u32[]{:S(2)}) collective-permute-start(bf16[64,1,4,64]{0,3,2,1:T(8,128)(2,1)S(1)} %fusion.427), channel_id=1, source_target_pairs={{0,16},{16,32},{32,48},{48,64},{64,80},{80,96},{96,112},{112,128},... | collective-permute-start | bytes 98312 | tf_op jit(solution)/shard_map/ppermute | solution.py:14
  15.1 23.5 %collective-permute-start = (bf16[64,1,8,128]{3,0,2,1:T(8,128)(2,1)S(1)}, bf16[64,1,8,128]{3,0,2,1:T(8,128)(2,1)S(1)}, u32[]{:S(2)}, u32[]{:S(2)}) collective-permute-start(bf16[64,1,8,128]{3,0,2,1:T(8,128)(2,1)S(1)} %get-tuple-element.21), channel_id=1, source_target_pairs={{0,16},{16,32},{32,48},{48,64},{64,80},{80,96},{96,112},{112,128},... | collective-permute-start | bytes 393224 | tf_op jit(solution)/shard_map/ppermute | solution.py:14
  18.5 20.2 %collective-permute-start.1 = (bf16[64,1,8,128]{3,0,2,1:T(8,128)(2,1)S(1)}, bf16[64,1,8,128]{3,0,2,1:T(8,128)(2,1)S(1)}, u32[]{:S(2)}, u32[]{:S(2)}) collective-permute-start(bf16[64,1,8,128]{3,0,2,1:T(8,128)(2,1)S(1)} %get-tuple-element.20), channel_id=1, source_target_pairs={{16,0},{32,16},{48,32},{64,48},{80,64},{96,80},{112,96},{128,112},... | collective-permute-start | bytes 393224 | tf_op jit(solution)/shard_map/ppermute | solution.py:17
  21.7 14.0 %copy-start.3 = (bf16[64,1,4,64]{0,3,2,1:T(8,128)(2,1)}, bf16[64,1,4,64]{0,3,2,1:T(8,128)(2,1)S(1)}, u32[]{:S(2)}) copy-start(bf16[64,1,4,64]{0,3,2,1:T(8,128)(2,1)S(1)} %collective-permute-done.5) | copy-start | bytes 98308
  21.7 14.0 %copy-start.5 = (bf16[64,1,4,64]{0,3,2,1:T(8,128)(2,1)}, bf16[64,1,4,64]{0,3,2,1:T(8,128)(2,1)S(1)}, u32[]{:S(2)}) copy-start(bf16[64,1,4,64]{0,3,2,1:T(8,128)(2,1)S(1)} %collective-permute-done.4) | copy-start | bytes 98308
  21.8 7.3 %collective-permute-start.7 = (bf16[64,3,1,64]{0,3,2,1:T(8,128)(2,1)S(1)}, bf16[64,3,1,64]{0,3,2,1:T(8,128)(2,1)S(1)}, u32[]{:S(2)}, u32[]{:S(2)}) collective-permute-start(bf16[64,3,1,64]{0,3,2,1:T(8,128)(2,1)S(1)} %get-tuple-element.31), channel_id=1, source_target_pairs={{1,0},{2,1},{3,2},{4,3},{5,4},{6,5},{7,6},{8,7},{9,8},{10,9},{11,1... | collective-permute-start | bytes 73736 | tf_op jit(solution)/shard_map/ppermute | solution.py:17
  25.5 4.0 collective-permute-start.6
  38.7 11.0 %collective-permute-start.2 = (bf16[64,4,1,128]{3,0,2,1:T(8,128)(2,1)S(1)}, bf16[64,4,1,128]{3,0,2,1:T(8,128)(2,1)S(1)}, u32[]{:S(2)}, u32[]{:S(2)}) collective-permute-start(bf16[64,4,1,128]{3,0,2,1:T(8,128)(2,1)S(1)} %get-tuple-element.19), channel_id=1, source_target_pairs={{0,1},{1,2},{2,3},{3,4},{4,5},{5,6},{6,7},{7,8},{8,9},{9,10},{10,1... | collective-permute-start | bytes 196616 | tf_op jit(solution)/shard_map/ppermute | solution.py:14
  43.0 6.8 %collective-permute-start.3 = (bf16[64,4,1,128]{3,0,2,1:T(8,128)(2,1)S(1)}, bf16[64,4,1,128]{3,0,2,1:T(8,128)(2,1)S(1)}, u32[]{:S(2)}, u32[]{:S(2)}) collective-permute-start(bf16[64,4,1,128]{3,0,2,1:T(8,128)(2,1)S(1)} %get-tuple-element.18), channel_id=1, source_target_pairs={{1,0},{2,1},{3,2},{4,3},{5,4},{6,5},{7,6},{8,7},{9,8},{10,9},{11,1... | collective-permute-start | bytes 196616 | tf_op jit(solution)/shard_map/ppermute | solution.py:17
  98.6 15.4 %copy-start.21 = (bf16[64,4,64]{0,2,1:T(8,128)(2,1)S(1)}, bf16[64,4,64]{0,2,1:T(8,128)(2,1)}, u32[]{:S(2)}) copy-start(bf16[64,4,64]{0,2,1:T(8,128)(2,1)} %copy-done.20) | copy-start | bytes 98308
  98.6 21.2 %collective-permute-start.9 = (bf16[128,1,4,64]{0,3,2,1:T(8,128)(2,1)S(1)}, bf16[128,1,4,64]{0,3,2,1:T(8,128)(2,1)S(1)}, u32[]{:S(2)}, u32[]{:S(2)}) collective-permute-start(bf16[128,1,4,64]{0,3,2,1:T(8,128)(2,1)S(1)} %bitcast.1063), channel_id=1, source_target_pairs={{16,0},{32,16},{48,32},{64,48},{80,64},{96,80},{112,96},{128,112},... | collective-permute-start | bytes 196616 | tf_op jit(solution)/shard_map/ppermute | solution.py:17
  100.1 19.7 %collective-permute-start.8 = (bf16[128,1,4,64]{0,3,2,1:T(8,128)(2,1)S(1)}, bf16[128,1,4,64]{0,3,2,1:T(8,128)(2,1)S(1)}, u32[]{:S(2)}, u32[]{:S(2)}) collective-permute-start(bf16[128,1,4,64]{0,3,2,1:T(8,128)(2,1)S(1)} %bitcast.1064), channel_id=1, source_target_pairs={{0,16},{16,32},{32,48},{48,64},{64,80},{80,96},{96,112},{112,128},... | collective-permute-start | bytes 196616 | tf_op jit(solution)/shard_map/ppermute | solution.py:14
  106.3 10.5 %copy-start.19 = (bf16[64,4,64]{0,2,1:T(8,128)(2,1)S(1)}, bf16[64,4,64]{0,2,1:T(8,128)(2,1)}, u32[]{:S(2)}) copy-start(bf16[64,4,64]{0,2,1:T(8,128)(2,1)} %copy-done.18) | copy-start | bytes 98308
  106.4 27.9 %collective-permute-start.13 = (bf16[192,1,8,128]{3,0,2,1:T(8,128)(2,1)S(1)}, bf16[192,1,8,128]{3,0,2,1:T(8,128)(2,1)S(1)}, u32[]{:S(2)}, u32[]{:S(2)}) collective-permute-start(bf16[192,1,8,128]{3,0,2,1:T(8,128)(2,1)S(1)} %get-tuple-element.17), channel_id=1, source_target_pairs={{16,0},{32,16},{48,32},{64,48},{80,64},{96,80},{112,96},{128,112},... | collective-permute-start | bytes 1179656 | tf_op jit(solution)/shard_map/ppermute | solution.py:17
  107.8 26.5 %collective-permute-start.12 = (bf16[192,1,8,128]{3,0,2,1:T(8,128)(2,1)S(1)}, bf16[192,1,8,128]{3,0,2,1:T(8,128)(2,1)S(1)}, u32[]{:S(2)}, u32[]{:S(2)}) collective-permute-start(bf16[192,1,8,128]{3,0,2,1:T(8,128)(2,1)S(1)} %get-tuple-element.16), channel_id=1, source_target_pairs={{0,16},{16,32},{32,48},{48,64},{64,80},{80,96},{96,112},{112,128},... | collective-permute-start | bytes 1179656 | tf_op jit(solution)/shard_map/ppermute | solution.py:14
  119.8 6.9 %collective-permute-start.11 = (bf16[128,3,1,64]{0,3,2,1:T(8,128)(2,1)S(1)}, bf16[128,3,1,64]{0,3,2,1:T(8,128)(2,1)S(1)}, u32[]{:S(2)}, u32[]{:S(2)}) collective-permute-start(bf16[128,3,1,64]{0,3,2,1:T(8,128)(2,1)S(1)} %get-tuple-element.29), channel_id=1, source_target_pairs={{1,0},{2,1},{3,2},{4,3},{5,4},{6,5},{7,6},{8,7},{9,8},{10,9},{11,1... | collective-permute-start | bytes 147464 | tf_op jit(solution)/shard_map/ppermute | solution.py:17
  121.7 5.4 %collective-permute-start.10 = (bf16[128,3,1,64]{0,3,2,1:T(8,128)(2,1)S(1)}, bf16[128,3,1,64]{0,3,2,1:T(8,128)(2,1)S(1)}, u32[]{:S(2)}, u32[]{:S(2)}) collective-permute-start(bf16[128,3,1,64]{0,3,2,1:T(8,128)(2,1)S(1)} %get-tuple-element.28), channel_id=1, source_target_pairs={{0,1},{1,2},{2,3},{3,4},{4,5},{5,6},{6,7},{7,8},{8,9},{9,10},{10,1... | collective-permute-start | bytes 147464 | tf_op jit(solution)/shard_map/ppermute | solution.py:14
  134.3 7.6 %collective-permute-start.15 = (bf16[192,4,1,128]{3,0,2,1:T(8,128)(2,1)S(1)}, bf16[192,4,1,128]{3,0,2,1:T(8,128)(2,1)S(1)}, u32[]{:S(2)}, u32[]{:S(2)}) collective-permute-start(bf16[192,4,1,128]{3,0,2,1:T(8,128)(2,1)S(1)} %get-tuple-element.15), channel_id=1, source_target_pairs={{1,0},{2,1},{3,2},{4,3},{5,4},{6,5},{7,6},{8,7},{9,8},{10,9},{11,1... | collective-permute-start | bytes 589832 | tf_op jit(solution)/shard_map/ppermute | solution.py:17
  136.3 6.8 %collective-permute-start.14 = (bf16[192,4,1,128]{3,0,2,1:T(8,128)(2,1)S(1)}, bf16[192,4,1,128]{3,0,2,1:T(8,128)(2,1)S(1)}, u32[]{:S(2)}, u32[]{:S(2)}) collective-permute-start(bf16[192,4,1,128]{3,0,2,1:T(8,128)(2,1)S(1)} %get-tuple-element.14), channel_id=1, source_target_pairs={{0,1},{1,2},{2,3},{3,4},{4,5},{5,6},{6,7},{7,8},{8,9},{9,10},{10,1... | collective-permute-start | bytes 589832 | tf_op jit(solution)/shard_map/ppermute | solution.py:14
  (23 other events, 95.7 us)
Sparse Core Ops, SparseCore 0:
  160.1 280.9 all-reduce.6
where the time goes:
time: 455 us; the launch traced here: 452 us
  waiting for transfers between devices  280 us (62%)
  matrix products  88.4 us (19%)
  starting transfers between devices  49.8 us (11%)
  between operations  15.1 us (3%)
  other arithmetic  10.5 us (2%)
  local copies, waits for them, and re-layouts  8.14 us (2%)
    psum x1, waiting for transfers between devices, body(): dec_total, coarse_total = lax.psum((dec_grad, coarse_grad_w), ('gx', 'gy'))  277 us
    dot_general x54, matrix products, conv_backward(): jnp.einsum('kxyz,ck->cxyz', backward_slice(padded, shape, first, second,...  61.7 us
    ppermute x8, starting transfers between devices, extended(): lax.ppermute(lax.slice_in_dim(block, block.shape[dim] - width, None, axis...  34.5 us
    ppermute x8, starting transfers between devices, extended(): lax.ppermute(lax.slice_in_dim(block, 0, width, axis=dim), axis, backward)  15.2 us
    dot_general x27, matrix products, body(): jnp.einsum('cxyz,kxyz->ck', forward_slice(joined_rim, shape_fine, a, b, c...  11 us
    dot_general x27, matrix products, conv_forward(): jnp.einsum('cxyz,co->oxyz', forward_slice(padded, shape, first, second, t...  10.3 us
  transfers between devices with their start and end apart: 17, of which 5 were waited for; matrix products, arithmetic and copies ran while one was open for 8% of the time, Pallas kernels for 0%

commit v1 on v0

v1 whole, which is shorter than its diff:
```python
import functools
import math

import jax
import jax.numpy as jnp
from jax import lax
from jax.experimental import pallas as pl
from jax.experimental.pallas import tpu as pltpu
from jax.sharding import PartitionSpec as P

LANES = 128
SKIP, COARSE, JOINED = 64, 128, 192
SIZE_X, SIZE_Y = 2, 8
BLOCKS, BLOCKS_C = SIZE_X * SIZE_Y, SIZE_Y // 2
TAPS = 27
DEC = TAPS * SKIP
PACKED = DEC + DEC // 2 + DEC
ROWS = 136
CHUNKS = 32
SENT = CHUNKS // 2 * ROWS
FACE, FACE_Y = SIZE_Y + BLOCKS_C // 2, SIZE_X + 1
BF16, F32 = jnp.bfloat16, jnp.float32


def params(mib):
    return pltpu.CompilerParams(vmem_limit_bytes=mib << 20)


def lane_of(shape):
    return lax.broadcasted_iota(jnp.int32, shape, len(shape) - 1)


def is_even(value):
    return (lane_of(value.shape) & 1) == 0


def paired(value):
    return value + jnp.where(is_even(value), pltpu.roll(value, LANES - 1, 1), pltpu.roll(value, 1, 1))


def pack(first, second):
    return jnp.where(is_even(first), first, second)


def unpack_pair(value):
    even = is_even(value)
    return (
        jnp.where(even, value, pltpu.roll(value, 1, 1)),
        jnp.where(even, pltpu.roll(value, LANES - 1, 1), value),
    )


def shifted(value, step):
    if step == 0:
        return value
    lane = lane_of(value.shape)
    inside = lane < LANES - step if step > 0 else lane >= -step
    return jnp.where(inside, pltpu.roll(value, (-step) % LANES, 1), 0.0)


def places():
    return lax.axis_index("gx"), lax.axis_index("gy")


def sides(place):
    odd = (place & 1).astype(F32)
    inner = jnp.where((place == 0) | (place == 15), 0.0, 1.0).astype(F32)
    return (odd, (1.0 - odd) * inner), (1.0 - odd, odd * inner)


def mixed(weights, first, second):
    return weights[0] * first.astype(F32) + weights[1] * second.astype(F32)


def split_kernel(
    skip_hbm, cot_hbm, skip_out, cot_out, pool_out, *refs,
):
    faces, (skip_ref, cot_ref, rows_ref, arrived) = refs[:8], refs[8:]
    ups = [(1 - (place & 1), place & 1) for place in places()]
    copies = [
        pltpu.make_async_copy(source, target, arrived.at[index])
        for index, (source, target) in enumerate(((cot_hbm, cot_ref), (skip_hbm, skip_ref)))
    ]
    for copy in copies:
        copy.start()

    def block_of(index):
        return rows_ref[pl.ds(index, SKIP, stride=BLOCKS), :]

    copies[0].wait()
    rows_ref[...] = cot_ref[...].astype(F32).reshape(SKIP * BLOCKS, LANES)
    for index in range(BLOCKS):
        cot_out[index] = block_of(index).astype(BF16)
    copies[1].wait()
    rows_ref[...] = skip_ref[...].astype(F32).reshape(SKIP * BLOCKS, LANES)
    pools = []
    for coarse in range(BLOCKS_C):
        total = None
        for index in (2 * coarse, 2 * coarse + 1, SIZE_Y + 2 * coarse, SIZE_Y + 2 * coarse + 1):
            block = block_of(index)
            skip_out[index] = block.astype(BF16)
            total = block if total is None else total + block
        pools.append(paired(total) * 0.125)
        pool_out[coarse] = pools[-1].astype(BF16)
    packed = [pack(pools[2 * index], pools[2 * index + 1]).astype(BF16) for index in range(BLOCKS_C // 2)]
    for which in range(2):
        up_x, up_y = ups[0][which], ups[1][which]
        for row in range(SIZE_Y):
            faces[which][row] = cot_out[up_x * SIZE_Y + row]
        for index, value in enumerate(packed):
            faces[which][SIZE_Y + index] = value
        row, row_c = up_y * (SIZE_Y - 1), up_y * (BLOCKS_C - 1)
        for plane in range(SIZE_X):
            faces[2 + which][plane] = cot_out[plane * SIZE_Y + row]
        faces[2 + which][SIZE_X] = pool_out[row_c]
        for other in range(2):
            corner = faces[4 + 2 * other + which]
            corner[0] = cot_out[ups[0][other] * SIZE_Y + row]
            corner[1] = pool_out[row_c]


def vmem():
    return pl.BlockSpec(memory_space=pltpu.VMEM)


def call(kernel, name, outs, scratch, mib, cost, *operands, held=pltpu.VMEM):
    return pl.pallas_call(
        kernel,
        out_shape=tuple(jax.ShapeDtypeStruct(shape, dtype) for shape, dtype in outs),
        in_specs=[pl.BlockSpec(memory_space=held)] * len(operands),
        out_specs=tuple(vmem() for _ in outs),
        scratch_shapes=[pltpu.VMEM(*form) if isinstance(form, tuple) else form for form in scratch],
        compiler_params=params(mib),
        cost_estimate=pl.CostEstimate(flops=cost[0], bytes_accessed=cost[1], transcendentals=0),
        name=name,
    )(*operands)


def grads_kernel(
    skip_ref, cot_ref, pool_ref, xone_ref, xtwo_ref, yone_ref, ytwo_ref, *refs,
):
    corner_refs, (wdec_ref, wpre_ref, wback_ref) = refs[:4], refs[4:7]
    send_out, keep_out, jskip_out, rim_out, two_out = refs[7:12]
    cells_ref, pooled_ref, joined_ref, jgrad_ref, full_ref, pre_ref = refs[12:]
    factor = 1.0 / math.sqrt(524288)
    place = places()
    xlow, xhigh = sides(place[0])
    ylow, yhigh = sides(place[1])

    def corner(xside, yside, index):
        first = mixed(yside, corner_refs[0][index], corner_refs[1][index])
        second = mixed(yside, corner_refs[2][index], corner_refs[3][index])
        return mixed(xside, first, second)

    def fine(plane, row):
        yside = {0: ylow, SIZE_Y + 1: yhigh}.get(row)
        xside = {0: xlow, SIZE_X + 1: xhigh}.get(plane)
        if xside and yside:
            return corner(xside, yside, 0)
        if yside:
            return mixed(yside, yone_ref[plane - 1], ytwo_ref[plane - 1])
        if xside:
            return mixed(xside, xone_ref[row - 1], xtwo_ref[row - 1])
        return cot_ref[(plane - 1) * SIZE_Y + row - 1].astype(F32)

    wide_pool = {}
    for row, yside in ((0, ylow), (BLOCKS_C + 1, yhigh)):
        wide_pool[0, row] = corner(xlow, yside, 1)
        wide_pool[1, row] = mixed(yside, yone_ref[SIZE_X], ytwo_ref[SIZE_X])
        wide_pool[2, row] = corner(xhigh, yside, 1)
    for plane, weights in ((0, xlow), (2, xhigh)):
        for index in range(BLOCKS_C // 2):
            at = SIZE_Y + index
            first, second = unpack_pair(mixed(weights, xone_ref[at], xtwo_ref[at]))
            wide_pool[plane, 2 * index + 1], wide_pool[plane, 2 * index + 2] = first, second
    for row in range(BLOCKS_C):
        wide_pool[1, row + 1] = pool_ref[row].astype(F32)

    for plane in range(3):
        for row in range(BLOCKS_C + 2):
            for k in range(3):
                value = shifted(wide_pool[plane, row], 2 * (k - 1)).astype(BF16)
                for j in range(3):
                    if 0 <= row - j < BLOCKS_C:
                        tap = 9 * plane + 3 * j + k
                        pooled_ref[tap * SKIP : (tap + 1) * SKIP, (row - j) * LANES : (row - j + 1) * LANES] = value
    pre_b = jnp.dot(wpre_ref[...], pooled_ref[...], preferred_element_type=F32)
    sig = 1.0 / (1.0 + jnp.exp(-pre_b))
    coarse_out = (pre_b * sig).astype(BF16)
    slope = sig * (1.0 + pre_b * (1.0 - sig))
    for index in range(BLOCKS):
        at = (index % SIZE_Y) // 2
        joined_ref[:COARSE, index * LANES : (index + 1) * LANES] = coarse_out[:, at * LANES : (at + 1) * LANES]
        joined_ref[COARSE:, index * LANES : (index + 1) * LANES] = skip_ref[index]
    for plane in range(SIZE_X + 2):
        for row in range(SIZE_Y + 2):
            wide = fine(plane, row)
            for k in range(3):
                value = shifted(wide, 1 - k).astype(BF16)
                for i in range(3):
                    for j in range(3):
                        x, y = plane - 2 + i, row - 2 + j
                        if 0 <= x < SIZE_X and 0 <= y < SIZE_Y:
                            tap, at = 9 * i + 3 * j + k, x * SIZE_Y + y
                            cells_ref[tap * SKIP : (tap + 1) * SKIP, at * LANES : (at + 1) * LANES] = value
    jgrad_ref[...] = jnp.dot(wdec_ref[...], cells_ref[...], preferred_element_type=F32)
    for index in range(BLOCKS):
        jskip_out[index] = jgrad_ref[COARSE:, index * LANES : (index + 1) * LANES]
    pre_parts = []
    for at in range(BLOCKS_C):
        total = None
        for index in (2 * at, 2 * at + 1, SIZE_Y + 2 * at, SIZE_Y + 2 * at + 1):
            part = jgrad_ref[:COARSE, index * LANES : (index + 1) * LANES]
            total = part if total is None else total + part
        pre_part = (paired(total) * slope[:, at * LANES : (at + 1) * LANES]).astype(BF16)
        pre_parts.append(pre_part)
        wide = pre_part.astype(F32)
        for k in range(3):
            pre_ref[k * COARSE : (k + 1) * COARSE, at * LANES : (at + 1) * LANES] = shifted(wide, 2 * (1 - k)).astype(BF16)
    pre_grad = jnp.concatenate(pre_parts, axis=1)

    terms = jnp.dot(wback_ref[...], pre_ref[...], preferred_element_type=F32) * 0.125

    def rim_row(i, row):
        total = None
        for j in range(3):
            if 0 <= row - j < BLOCKS_C:
                first = (3 * i + j) * SKIP
                part = terms[first : first + SKIP, (row - j) * LANES : (row - j + 1) * LANES]
                total = part if total is None else total + part
        return total

    for i in range(3):
        for row in range(BLOCKS_C):
            rim_out[BLOCKS_C * i + row] = rim_row(i, row + 1)
    odd = (place[1] & 1).astype(F32)
    for index in range(2):
        down, up = (
            pack(rim_row(0, row), rim_row(1, row)) if index == 0 else rim_row(2, row) for row in (0, BLOCKS_C + 1)
        )
        send_out[SENT + index * SKIP : SENT + (index + 1) * SKIP] = ((1.0 - odd) * up + odd * down).astype(BF16)
        two_out[index] = ((1.0 - odd) * down + odd * up).astype(BF16)

    across = (((1,), (1,)), ((), ()))
    dec = lax.dot_general(cells_ref[...], joined_ref[...], across, preferred_element_type=F32) * factor
    full_ref[:DEC] = dec[:, :LANES]
    full_ref[DEC : DEC + DEC // 2] = jnp.concatenate([dec[: DEC // 2, LANES:], dec[DEC // 2 :, LANES:]], axis=1)
    full_ref[DEC + DEC // 2 : PACKED] = lax.dot_general(
        pooled_ref[...], pre_grad, across, preferred_element_type=F32
    ) * (0.5 * factor)
    full_ref[PACKED:] = jnp.zeros((CHUNKS * ROWS - PACKED, LANES), F32)
    core, y, x = place[1] & 1, (place[1] >> 1) & 3, place[0] & 3
    for yr in range(4):
        leave = []
        for xr in range(4):
            at = (y ^ yr) * 4 + (x ^ xr)
            row = pl.multiple_of((at + 16 * core) * ROWS, ROWS)
            keep_out[yr, xr] = full_ref[pl.ds(row, ROWS), :]
            row = pl.multiple_of((at + 16 * (1 - core)) * ROWS, ROWS)
            leave.append(full_ref[pl.ds(row, ROWS), :])
        send_out[4 * yr * ROWS : 4 * (yr + 1) * ROWS] = jnp.concatenate(leave).astype(BF16)


def fold_kernel(rim_ref, yone_ref, ytwo_ref, rows_out, one_out, two_out):
    place = places()
    planes = [[rim_ref[BLOCKS_C * i + row] for row in range(BLOCKS_C)] for i in range(3)]
    for weights, row in zip(sides(place[1]), (0, BLOCKS_C - 1)):
        first, second = unpack_pair(mixed(weights, yone_ref[0], ytwo_ref[0]))
        third = mixed(weights, yone_ref[1], ytwo_ref[1])
        for i, terms in enumerate((first, second, third)):
            planes[i][row] = planes[i][row] + terms
    for row in range(BLOCKS_C):
        rows_out[row] = planes[1][row]
    odd = (place[0] & 1).astype(F32)
    for index in range(BLOCKS_C // 2):
        down, up = (pack(planes[i][2 * index], planes[i][2 * index + 1]) for i in (0, 2))
        one_out[index] = ((1.0 - odd) * up + odd * down).astype(BF16)
        two_out[index] = ((1.0 - odd) * down + odd * up).astype(BF16)


def skip_kernel(rows_ref, xone_ref, xtwo_ref, jskip_ref, out_ref, cells_ref):
    low, high = sides(places()[0])
    weights = (low[0] + high[0], low[1] + high[1])
    for pair in range(BLOCKS_C // 2):
        for at, terms in zip((2 * pair, 2 * pair + 1), unpack_pair(mixed(weights, xone_ref[pair], xtwo_ref[pair]))):
            total = rows_ref[at] + terms
            for index in (2 * at, 2 * at + 1, SIZE_Y + 2 * at, SIZE_Y + 2 * at + 1):
                cells_ref[pl.ds(index, SKIP, stride=BLOCKS), :] = jskip_ref[index] + total
    out_ref[...] = cells_ref[...].reshape(SKIP, SIZE_X, SIZE_Y, LANES).astype(BF16)


def unpack_kernel(a0_ref, a1_ref, b0_ref, b1_ref, core_ref, dec_out, coarse_out, full_ref):
    place = places()
    core, y, x = place[1] & 1, (place[1] >> 1) & 3, place[0] & 3
    for half, (refs, order) in enumerate((((a0_ref, a1_ref), ORDER_A), ((b0_ref, b1_ref), ORDER_B))):
        for index, yr in enumerate(order):
            for xr in range(2):
                at = (y ^ yr) * 4 + (x ^ (2 * half + xr))
                row = pl.multiple_of((at + 16 * core) * ROWS, ROWS)
                full_ref[pl.ds(row, ROWS), :] = refs[index // 2][index % 2, xr].astype(F32)
                row = pl.multiple_of((at + 16 * (1 - core)) * ROWS, ROWS)
                full_ref[pl.ds(row, ROWS), :] = core_ref[4 * half + index, xr].astype(F32)
    half = LANES // 2
    dec_out[:, :LANES] = full_ref[:DEC]
    dec_out[: DEC // 2, LANES:] = full_ref[DEC : DEC + DEC // 2, :half]
    dec_out[DEC // 2 :, LANES:] = full_ref[DEC : DEC + DEC // 2, half:]
    coarse_out[...] = full_ref[DEC + DEC // 2 : PACKED]


def swap(value, axis, flip):
    return lax.ppermute(value, axis, [(i, i ^ flip) for i in range(lax.axis_size(axis))])


def partner(index, which, count):
    return index ^ 1 if which == 0 else (index + 2 * (index % 2) - 1) % count


def swap_side(value, axis, which):
    count = lax.axis_size(axis)
    return lax.ppermute(value, axis, [(i, partner(i, which, count)) for i in range(count)])


def swap_corner(value, which_x, which_y):
    size_x, size_y = lax.axis_size("gx"), lax.axis_size("gy")
    pairs = [
        (i * size_y + j, partner(i, which_x, size_x) * size_y + partner(j, which_y, size_y))
        for i in range(size_x)
        for j in range(size_y)
    ]
    return lax.ppermute(value, ("gx", "gy"), pairs)


together = lax.optimization_barrier
A_FIRST, A_SECOND = 1, 3
B_FIRST, B_SECOND = 3, 1
ORDER_A = (0, A_SECOND, A_FIRST, 2)
ORDER_B = (0, B_SECOND, B_FIRST, 2)


def swap_y(value, flip):
    return swap(value, "gy", 2 * flip)


def wide(value):
    return value.astype(F32)


def body(skip_feat, cotangent, w_coarse, w_dec):
    w_join = w_dec.transpose(1, 0, 2).reshape(JOINED, DEC)
    w_pre = w_coarse.transpose(2, 0, 1).reshape(COARSE, DEC)
    w_back = w_coarse.reshape(9, 3, SKIP, COARSE).transpose(0, 2, 1, 3).reshape(9 * SKIP, 3 * COARSE)

    block = (SKIP, LANES)
    face, face_y, corner = (FACE,) + block, (FACE_Y,) + block, (2,) + block
    fine = (BLOCKS,) + block
    skip, cot, pooled, *faces = call(
        split_kernel, "split_blocks",
        (
            (fine, BF16), (fine, BF16), ((BLOCKS_C,) + block, BF16),
            (face, BF16), (face, BF16), (face_y, BF16), (face_y, BF16),
            (corner, BF16), (corner, BF16), (corner, BF16), (corner, BF16),
        ),
        (
            (skip_feat.shape, BF16), (skip_feat.shape, BF16), ((SKIP * BLOCKS, LANES), F32),
            pltpu.SemaphoreType.DMA((2,)),
        ),
        8, (1_000_000, 1_500_000), *(pltpu.with_memory_space_constraint(x, pltpu.HBM) for x in (skip_feat, cotangent)),
        held=pltpu.HBM,
    )
    xtwo = swap_side(faces[1], "gx", 1)
    corners = [swap_corner(faces[4 + 2 * i + j], i, j) for i, j in ((0, 0), (0, 1), (1, 0), (1, 1))]
    xone = swap_side(faces[0], "gx", 0)
    yone, ytwo = (swap_side(faces[2 + which], "gy", which) for which in range(2))
    chunks = (4, 4, ROWS, LANES)
    send, keep, jskip, own, rtwo = call(
        grads_kernel, "local_grads",
        (
            ((SENT + 2 * SKIP, LANES), BF16), (chunks, F32), (fine, F32),
            ((3 * BLOCKS_C,) + block, F32), (corner, BF16),
        ),
        (
            ((DEC, BLOCKS * LANES), BF16),
            ((DEC, BLOCKS_C * LANES), BF16),
            ((JOINED, BLOCKS * LANES), BF16),
            ((JOINED, BLOCKS * LANES), F32),
            ((CHUNKS * ROWS, LANES), F32),
            ((3 * COARSE, BLOCKS_C * LANES), BF16),
        ),
        36, (3_000_000_000, 8_000_000), skip, cot, pooled, xone, xtwo, yone, ytwo, *corners,
        w_join, w_pre, w_back,
    )

    send, rtwo = swap(send, "gy", 1), swap_side(rtwo, "gy", 1)
    part = keep + wide(send[:SENT].reshape(chunks))
    rone = send[SENT:].reshape(corner)
    a, b = part[:, :2], part[:, 2:]
    a_got = swap_y(jnp.stack([a[A_FIRST], a[2]]).astype(BF16), A_FIRST)
    b_got = swap_y(jnp.stack([b[B_FIRST], b[2]]).astype(BF16), B_FIRST)
    a_got, b_got, rone, rtwo = together((a_got, b_got, rone, rtwo))
    rows, qone, qtwo = call(
        fold_kernel, "fold_rim", (((BLOCKS_C,) + block, F32), (corner, BF16), (corner, BF16)), (), 8, (100_000, 600_000),
        own, rone, rtwo,
    )
    a_own, a_leave = a[0] + wide(a_got[0]), a[A_SECOND] + wide(a_got[1])
    b_own, b_leave = b[0] + wide(b_got[0]), b[B_SECOND] + wide(b_got[1])
    a_got, b_got = swap_y(a_leave.astype(BF16), A_SECOND), swap_y(b_leave.astype(BF16), B_SECOND)
    a_got, b_got, rows, qone, qtwo = together((a_got, b_got, rows, qone, qtwo))
    part = jnp.concatenate([a_own + wide(a_got), b_own + wide(b_got)])
    leave = part.astype(BF16)
    qtwo = swap_side(qtwo, "gx", 1)
    got = swap(jnp.concatenate([leave[1], qone.reshape(2 * SKIP, LANES)]), "gx", 1)
    got = [got[:ROWS], swap(leave[2], "gx", 2), swap(leave[3], "gx", 3), got[ROWS:].reshape(corner)]
    *got, qone, qtwo = together((*got, qtwo))
    (skip_grad,) = call(
        skip_kernel, "skip_gradient", (((SKIP, SIZE_X, SIZE_Y, LANES), BF16),), (((SKIP * BLOCKS, LANES), F32),),
        8, (1_000_000, 1_000_000), rows, qone, qtwo, jskip,
    )
    part = (part[0] + wide(got[0])) + (wide(got[1]) + wide(got[2]))
    mine = part.astype(BF16)
    got = [swap(mine, "gx", 4 * flip) for flip in (1, 2, 3)]
    *got, skip_grad = together((*got, skip_grad))
    part = (wide(mine) + wide(got[0])) + (wide(got[1]) + wide(got[2]))
    part = (part + swap(part, "gy", 8)).astype(BF16)
    part = jnp.stack(together([part] + [swap(part, "gx", flip) for flip in (1, 2, 3)]))
    a, b = part[:2], part[2:]
    a_got, b_got = together((swap_y(a, A_SECOND), swap_y(b, B_SECOND)))
    a_near, b_near = jnp.stack([a, a_got]), jnp.stack([b, b_got])
    a_far, b_far = together((swap_y(a_near, A_FIRST), swap_y(b_near, B_FIRST)))
    other = swap(jnp.concatenate([a_near, a_far, b_near, b_far]), "gy", 1)
    dec, coarse = call(
        unpack_kernel, "unpack", (((DEC, JOINED), F32), ((DEC, COARSE), F32)), (((CHUNKS * ROWS, LANES), F32),),
        16, (1_000_000, 5_000_000), a_near, a_far, b_near, b_far, other,
    )
    return (
        skip_grad,
        dec.reshape(TAPS, SKIP, JOINED).transpose(0, 2, 1),
        coarse.reshape(TAPS, SKIP, COARSE),
    )


def solution(mesh):
    placed = (P(None, "gx", "gy", None), P(None, "gx", "gy", None), P(), P())
    return jax.shard_map(
        body,
        mesh=mesh,
        in_specs=placed,
        out_specs=(P(None, "gx", "gy", None), P(), P()),
        check_vma=False,
    )
```

time: 455 us -> 109 us (0.24)
  waiting for transfers between devices: 280 us -> 35.4 us
  matrix products: 88.4 us -> 0 us
  between operations: 15.1 us -> 0.9 us
  Pallas kernels: 0 us -> 10.2 us
  other arithmetic: 10.5 us -> 0.39 us
  starting transfers between devices: 49.8 us -> 58.3 us
  local copies, waits for them, and re-layouts: 8.14 us -> 3.29 us
    psum x1 -> x0, waiting for transfers between devices: 277 us -> none  [body(): dec_total, coarse_total = lax.psum((dec_grad, coarse_grad_w), ('gx', 'gy'))]
    dot_general x135 -> x0, matrix products: 88.4 us -> none  [the longest x54 61.7 us: conv_backward(): jnp.einsum('kxyz,ck->cxyz', backward_slice(padded, shape, first, second,...]
    ppermute x16 -> x30, waiting for transfers between devices: 2.53 us -> 35.4 us  [the longest x20 22.4 us: swap(): lax.ppermute(value, axis, [(i, i ^ flip) for i in range(lax.axis_size(axi...]
    pallas_call x0 -> x5, Pallas kernels: none -> 10.2 us  [call(): pl.pallas_call(kernel, out_shape=tuple((jax.ShapeDtypeStruct(shape, dtype...]
    ppermute x16 -> x30, starting transfers between devices: 49.7 us -> 58.3 us  [the longest x20 32.3 us: swap(): lax.ppermute(value, axis, [(i, i ^ flip) for i in range(lax.axis_size(axi...]
    unnamed x67 -> x6, local copies, waits for them, and re-layouts: 6.92 us -> 0.12 us
    concatenate x5 -> x1, other arithmetic: 5.36 us -> 0.01 us  [body(): jnp.concatenate([leave[1], qone.reshape(2 * SKIP, LANES)])]
  transfers between devices with their start and end apart: 17 -> 30, of which waited for: 5 -> 15; matrix products, arithmetic and copies ran while one was open for 8% -> 3% of each run, Pallas kernels for 0% -> 1%
where the time goes in v1:
time: 109 us; the launch traced here: 108 us
  starting transfers between devices  58.3 us (53%)
  waiting for transfers between devices  35.4 us (32%)
  Pallas kernels  10.2 us (9%)
  local copies, waits for them, and re-layouts  3.29 us (3%)
    ppermute x20, starting transfers between devices, swap(): lax.ppermute(value, axis, [(i, i ^ flip) for i in range(lax.axis_size(axi...  32.3 us
    ppermute x20, waiting for transfers between devices, swap(): lax.ppermute(value, axis, [(i, i ^ flip) for i in range(lax.axis_size(axi...  22.4 us
    ppermute x6, starting transfers between devices, swap_side(): lax.ppermute(value, axis, [(i, partner(i, which, count)) for i in range(c...  18.2 us
    pallas_call x5, Pallas kernels, call(): pl.pallas_call(kernel, out_shape=tuple((jax.ShapeDtypeStruct(shape, dtype...  10.2 us
    ppermute x4, starting transfers between devices, swap_corner(): return lax.ppermute(value, ('gx', 'gy'), pairs)  7.74 us
    ppermute x4, waiting for transfers between devices, swap_corner(): return lax.ppermute(value, ('gx', 'gy'), pairs)  7.32 us
    ppermute x6, waiting for transfers between devices, swap_side(): lax.ppermute(value, axis, [(i, partner(i, which, count)) for i in range(c...  5.6 us
  transfers between devices with their start and end apart: 30, of which 15 were waited for; matrix products, arithmetic and copies ran while one was open for 3% of the time, Pallas kernels for 1%

profile of v1, /device:TPU:1, one launch (start us, length us, event | category | flops | bytes accessed | tf_op | source)
XLA Modules:
  0.0 108.4 jit_solution(5048651294814383646)
XLA Ops:
  2.1 2.1 %collective-permute-start = (bf16[10,64,128]{2,1,0:T(8,128)(2,1)S(1)}, bf16[10,64,128]{2,1,0:T(8,128)(2,1)S(1)}, u32[]{:S(2)}, u32[]{:S(2)}) collective-permute-start(bf16[10,64,128]{2,1,0:T(8,128)(2,1)S(1)} %get-tuple-element.53), channel_id=1, source_target_pairs={{0,16},{16,0},{32,48},{48,32},{64,80},{80,64},{96,112},{112,96},{1... | collective-permute-start | bytes 491528 | tf_op jit(solution)/shard_map/ppermute | solution.py:320
  4.3 7.6 %collective-permute-start.1 = (bf16[10,64,128]{2,1,0:T(8,128)(2,1)S(1)}, bf16[10,64,128]{2,1,0:T(8,128)(2,1)S(1)}, u32[]{:S(2)}, u32[]{:S(2)}) collective-permute-start(bf16[10,64,128]{2,1,0:T(8,128)(2,1)S(1)} %get-tuple-element.54), channel_id=1, source_target_pairs={{0,240},{16,32},{32,16},{48,64},{64,48},{80,96},{96,80},{112,128},... | collective-permute-start | bytes 491528 | tf_op jit(solution)/shard_map/ppermute | solution.py:320
  11.8 2.8 %collective-permute-start.5 = (bf16[2,64,128]{2,1,0:T(8,128)(2,1)S(1)}, bf16[2,64,128]{2,1,0:T(8,128)(2,1)S(1)}, u32[]{:S(2)}, u32[]{:S(2)}) collective-permute-start(bf16[2,64,128]{2,1,0:T(8,128)(2,1)S(1)} %get-tuple-element.58), channel_id=1, source_target_pairs={{0,31},{1,18},{2,17},{3,20},{4,19},{5,22},{6,21},{7,24},{8,23},{9,... | collective-permute-start | bytes 98312 | tf_op jit(solution)/shard_map/ppermute | solution.py:330
  14.6 2.7 %collective-permute-start.6 = (bf16[2,64,128]{2,1,0:T(8,128)(2,1)S(1)}, bf16[2,64,128]{2,1,0:T(8,128)(2,1)S(1)}, u32[]{:S(2)}, u32[]{:S(2)}) collective-permute-start(bf16[2,64,128]{2,1,0:T(8,128)(2,1)S(1)} %get-tuple-element.59), channel_id=1, source_target_pairs={{0,241},{1,240},{2,243},{3,242},{4,245},{5,244},{6,247},{7,246},{8... | collective-permute-start | bytes 98312 | tf_op jit(solution)/shard_map/ppermute | solution.py:330
  18.5 4.1 %collective-permute-done.6.refs_2_ = bf16[2,64,128]{2,1,0:T(8,128)(2,1)S(1)} collective-permute-done((bf16[2,64,128]{2,1,0:T(8,128)(2,1)S(1)}, bf16[2,64,128]{2,1,0:T(8,128)(2,1)S(1)}, u32[]{:S(2)}, u32[]{:S(2)}) %collective-permute-start.6) | collective-permute-done | bytes 32800 | tf_op jit(solution)/shard_map/ppermute | solution.py:330
  22.6 2.2 %collective-permute-start.7 = (bf16[2,64,128]{2,1,0:T(8,128)(2,1)S(1)}, bf16[2,64,128]{2,1,0:T(8,128)(2,1)S(1)}, u32[]{:S(2)}, u32[]{:S(2)}) collective-permute-start(bf16[2,64,128]{2,1,0:T(8,128)(2,1)S(1)} %get-tuple-element.60), channel_id=1, source_target_pairs={{0,255},{1,242},{2,241},{3,244},{4,243},{5,246},{6,245},{7,248},{8... | collective-permute-start | bytes 98312 | tf_op jit(solution)/shard_map/ppermute | solution.py:330
  28.0 3.2 %collective-permute-done.7.refs_3_ = bf16[2,64,128]{2,1,0:T(8,128)(2,1)S(1)} collective-permute-done((bf16[2,64,128]{2,1,0:T(8,128)(2,1)S(1)}, bf16[2,64,128]{2,1,0:T(8,128)(2,1)S(1)}, u32[]{:S(2)}, u32[]{:S(2)}) %collective-permute-start.7) | collective-permute-done | bytes 32800 | tf_op jit(solution)/shard_map/ppermute | solution.py:330
  31.2 5.7 %local_grads.1 = (bf16[2304,128]{1,0:T(8,128)(2,1)S(1)}, f32[4,4,136,128]{3,2,1,0:T(8,128)S(1)}, f32[16,64,128]{2,1,0:T(8,128)S(1)}, f32[12,64,128]{2,1,0:T(8,128)S(1)}, bf16[2,64,128]{2,1,0:T(8,128)(2,1)S(1)}) custom-call(bf16[16,64,128]{2,1,0:T(8,128)(2,1)S(1)} %get-tuple-element.50.skip_ref, bf16[16,64,128]{2,1,0:T(8,128)(2,1)S(1)} %get-tuple-element.51.cot_ref, ...), custom_call_target="tpu_custom_call" | custom-call | flops 3000000000 | bytes 8000000 | tf_op jit(solution)/shard_map/local_grads/pallas_call | solution.py:127
  37.0 3.1 %collective-permute-start.8 = (bf16[2304,128]{1,0:T(8,128)(2,1)S(1)}, bf16[2304,128]{1,0:T(8,128)(2,1)S(1)}, u32[]{:S(2)}, u32[]{:S(2)}) collective-permute-start(bf16[2304,128]{1,0:T(8,128)(2,1)S(1)} %get-tuple-element.62), channel_id=1, source_target_pairs={{0,1},{1,0},{2,3},{3,2},{4,5},{5,4},{6,7},{7,6},{8,9},{9,8},{10,11... | collective-permute-start | bytes 1769480 | tf_op jit(solution)/shard_map/ppermute | solution.py:311
  43.2 2.3 %collective-permute-start.11 = (bf16[2,64,128]{2,1,0:T(8,128)(2,1)S(1)}, bf16[2,64,128]{2,1,0:T(8,128)(2,1)S(1)}, u32[]{:S(2)}, u32[]{:S(2)}) collective-permute-start(bf16[2,64,128]{2,1,0:T(8,128)(2,1)S(1)} %get-tuple-element.63), channel_id=1, source_target_pairs={{0,15},{1,2},{2,1},{3,4},{4,3},{5,6},{6,5},{7,8},{8,7},{9,10},{10,... | collective-permute-start | bytes 98312 | tf_op jit(solution)/shard_map/ppermute | solution.py:320
  45.4 3.8 %collective-permute-done.11.ytwo_ref = bf16[2,64,128]{2,1,0:T(8,128)(2,1)S(1)} collective-permute-done((bf16[2,64,128]{2,1,0:T(8,128)(2,1)S(1)}, bf16[2,64,128]{2,1,0:T(8,128)(2,1)S(1)}, u32[]{:S(2)}, u32[]{:S(2)}) %collective-permute-start.11) | collective-permute-done | bytes 32800 | tf_op jit(solution)/shard_map/ppermute | solution.py:320
  54.1 3.1 %collective-permute-start.15 = (bf16[136,128]{1,0:T(8,128)(2,1)S(1)}, bf16[136,128]{1,0:T(8,128)(2,1)S(1)}, u32[]{:S(2)}, u32[]{:S(2)}) collective-permute-start(bf16[136,128]{1,0:T(8,128)(2,1)S(1)} %get-tuple-element.110), channel_id=1, source_target_pairs={{0,32},{16,48},{32,0},{48,16},{64,96},{80,112},{96,64},{112,80},{1... | collective-permute-start | bytes 104456 | tf_op jit(solution)/shard_map/ppermute | solution.py:311
  57.2 5.1 %collective-permute-start.17 = (bf16[2,64,128]{2,1,0:T(8,128)(2,1)S(1)}, bf16[2,64,128]{2,1,0:T(8,128)(2,1)S(1)}, u32[]{:S(2)}, u32[]{:S(2)}) collective-permute-start(bf16[2,64,128]{2,1,0:T(8,128)(2,1)S(1)} %get-tuple-element.75), channel_id=1, source_target_pairs={{0,240},{16,32},{32,16},{48,64},{64,48},{80,96},{96,80},{112,128},... | collective-permute-start | bytes 98312 | tf_op jit(solution)/shard_map/ppermute | solution.py:320
  64.3 2.6 %collective-permute-start.20 = (bf16[136,128]{1,0:T(8,128)(2,1)S(1)}, bf16[136,128]{1,0:T(8,128)(2,1)S(1)}, u32[]{:S(2)}, u32[]{:S(2)}) collective-permute-start(bf16[136,128]{1,0:T(8,128)(2,1)S(1)} %fusion.11), channel_id=1, source_target_pairs={{0,192},{16,208},{32,224},{48,240},{64,128},{80,144},{96,160},{112... | collective-permute-start | bytes 104456 | tf_op jit(solution)/shard_map/ppermute | solution.py:311
  67.8 2.2 %collective-permute-start.18 = (bf16[136,128]{1,0:T(8,128)(2,1)S(1)}, bf16[136,128]{1,0:T(8,128)(2,1)S(1)}, u32[]{:S(2)}, u32[]{:S(2)}) collective-permute-start(bf16[136,128]{1,0:T(8,128)(2,1)S(1)} %fusion.11), channel_id=1, source_target_pairs={{0,64},{16,80},{32,96},{48,112},{64,0},{80,16},{96,32},{112,48},{1... | collective-permute-start | bytes 104456 | tf_op jit(solution)/shard_map/ppermute | solution.py:311
  71.0 2.7 %collective-permute-done.19 = bf16[136,128]{1,0:T(8,128)(2,1)S(1)} collective-permute-done((bf16[136,128]{1,0:T(8,128)(2,1)S(1)}, bf16[136,128]{1,0:T(8,128)(2,1)S(1)}, u32[]{:S(2)}, u32[]{:S(2)}) %collective-permute-start.19) | collective-permute-done | bytes 34848 | tf_op jit(solution)/shard_map/ppermute | solution.py:311
  74.2 3.2 %collective-permute-done.21 = f32[136,128]{1,0:T(8,128)S(1)} collective-permute-done((f32[136,128]{1,0:T(8,128)S(1)}, f32[136,128]{1,0:T(8,128)S(1)}, u32[]{:S(2)}, u32[]{:S(2)}) %collective-permute-start.21) | collective-permute-done | bytes 69664 | tf_op jit(solution)/shard_map/ppermute | solution.py:311
  77.4 3.6 %collective-permute-start.24 = (bf16[136,128]{1,0:T(8,128)(2,1)S(1)}, bf16[136,128]{1,0:T(8,128)(2,1)S(1)}, u32[]{:S(2)}, u32[]{:S(2)}) collective-permute-start(bf16[136,128]{1,0:T(8,128)(2,1)S(1)} %add_convert_fusion), channel_id=1, source_target_pairs={{0,48},{16,32},{32,16},{48,0},{64,112},{80,96},{96,80},{112,64},{1... | collective-permute-start | bytes 104456 | tf_op jit(solution)/shard_map/ppermute | solution.py:311
  82.3 3.0 %collective-permute-done.23 = bf16[136,128]{1,0:T(8,128)(2,1)S(1)} collective-permute-done((bf16[136,128]{1,0:T(8,128)(2,1)S(1)}, bf16[136,128]{1,0:T(8,128)(2,1)S(1)}, u32[]{:S(2)}, u32[]{:S(2)}) %collective-permute-start.23) | collective-permute-done | bytes 34848 | tf_op jit(solution)/shard_map/ppermute | solution.py:311
  86.3 3.4 %collective-permute-done.25 = bf16[2,136,128]{2,1,0:T(8,128)(2,1)S(1)} collective-permute-done((bf16[2,136,128]{2,1,0:T(8,128)(2,1)S(1)}, bf16[2,136,128]{2,1,0:T(8,128)(2,1)S(1)}, u32[]{:S(2)}, u32[]{:S(2)}) %collective-permute-start.25) | collective-permute-done | bytes 69664 | tf_op jit(solution)/shard_map/ppermute | solution.py:311
  89.9 1.9 %collective-permute-start.28 = (bf16[2,2,136,128]{3,2,1,0:T(8,128)(2,1)S(1)}, bf16[2,2,136,128]{3,2,1,0:T(8,128)(2,1)S(1)}, u32[]{:S(2)}, u32[]{:S(2)}) collective-permute-start(bf16[2,2,136,128]{3,2,1,0:T(8,128)(2,1)S(1)} %pad_maximum_fusion.2.b0_ref), channel_id=1, source_target_pairs={{0,6},{1,7},{2,4},{3,5},{4,2},{5,3},{6,0},{7,1},{8,14},{9,15},{10,... | collective-permute-start | bytes 417800 | tf_op jit(solution)/shard_map/ppermute | solution.py:311
  91.8 1.9 %collective-permute-done.27.a1_ref = bf16[2,2,136,128]{3,2,1,0:T(8,128)(2,1)S(1)} collective-permute-done((bf16[2,2,136,128]{3,2,1,0:T(8,128)(2,1)S(1)}, bf16[2,2,136,128]{3,2,1,0:T(8,128)(2,1)S(1)}, u32[]{:S(2)}, u32[]{:S(2)}) %collective-permute-start.27) | collective-permute-done | bytes 139296 | tf_op jit(solution)/shard_map/ppermute | solution.py:311
  95.2 9.7 %collective-permute-start.29 = (bf16[8,2,136,128]{3,2,1,0:T(8,128)(2,1)S(1)}, bf16[8,2,136,128]{3,2,1,0:T(8,128)(2,1)S(1)}, u32[]{:S(2)}, u32[]{:S(2)}) collective-permute-start(bf16[8,2,136,128]{3,2,1,0:T(8,128)(2,1)S(1)} %constant_dynamic-update-slice_fusion), channel_id=1, source_target_pairs={{0,1},{1,0},{2,3},{3,2},{4,5},{5,4},{6,7},{7,6},{8,9},{9,8},{10,11... | collective-permute-start | bytes 1671176 | tf_op jit(solution)/shard_map/ppermute | solution.py:311
  106.5 1.9 %unpack.1 = (f32[1728,192]{1,0:T(8,128)}, f32[1728,128]{1,0:T(8,128)}) custom-call(bf16[2,2,136,128]{3,2,1,0:T(8,128)(2,1)S(1)} %pad_maximum_fusion.1.a0_ref, bf16[2,2,136,128]{3,2,1,0:T(8,128)(2,1)S(1)} %collective-permute-done.27.a1_ref, bf16[2,2,136,128]{3,2,1,0:T(8,128)(2,1)S(1)} %pad_maximum_fusion.2.b0_ref, ...), custom_call_target="tpu_custom_call" | custom-call | flops 1000000 | bytes 5000000 | tf_op jit(solution)/shard_map/unpack/pallas_call | solution.py:127
  (73 shorter events, 23.6 us)
Async XLA Ops:
  2.1 29.1 %collective-permute-start = (bf16[10,64,128]{2,1,0:T(8,128)(2,1)S(1)}, bf16[10,64,128]{2,1,0:T(8,128)(2,1)S(1)}, u32[]{:S(2)}, u32[]{:S(2)}) collective-permute-start(bf16[10,64,128]{2,1,0:T(8,128)(2,1)S(1)} %get-tuple-element.53), channel_id=1, source_target_pairs={{0,16},{16,0},{32,48},{48,32},{64,80},{80,64},{96,112},{112,96},{1... | collective-permute-start | bytes 491528 | tf_op jit(solution)/shard_map/ppermute | solution.py:320
  4.3 27.0 %collective-permute-start.1 = (bf16[10,64,128]{2,1,0:T(8,128)(2,1)S(1)}, bf16[10,64,128]{2,1,0:T(8,128)(2,1)S(1)}, u32[]{:S(2)}, u32[]{:S(2)}) collective-permute-start(bf16[10,64,128]{2,1,0:T(8,128)(2,1)S(1)} %get-tuple-element.54), channel_id=1, source_target_pairs={{0,240},{16,32},{32,16},{48,64},{64,48},{80,96},{96,80},{112,128},... | collective-permute-start | bytes 491528 | tf_op jit(solution)/shard_map/ppermute | solution.py:320
  11.8 5.5 %collective-permute-start.4 = (bf16[2,64,128]{2,1,0:T(8,128)(2,1)S(1)}, bf16[2,64,128]{2,1,0:T(8,128)(2,1)S(1)}, u32[]{:S(2)}, u32[]{:S(2)}) collective-permute-start(bf16[2,64,128]{2,1,0:T(8,128)(2,1)S(1)} %get-tuple-element.57), channel_id=1, source_target_pairs={{0,17},{1,16},{2,19},{3,18},{4,21},{5,20},{6,23},{7,22},{8,25},{9,... | collective-permute-start | bytes 98312 | tf_op jit(solution)/shard_map/ppermute | solution.py:330
  11.8 5.9 %collective-permute-start.5 = (bf16[2,64,128]{2,1,0:T(8,128)(2,1)S(1)}, bf16[2,64,128]{2,1,0:T(8,128)(2,1)S(1)}, u32[]{:S(2)}, u32[]{:S(2)}) collective-permute-start(bf16[2,64,128]{2,1,0:T(8,128)(2,1)S(1)} %get-tuple-element.58), channel_id=1, source_target_pairs={{0,31},{1,18},{2,17},{3,20},{4,19},{5,22},{6,21},{7,24},{8,23},{9,... | collective-permute-start | bytes 98312 | tf_op jit(solution)/shard_map/ppermute | solution.py:330
  14.6 8.0 %collective-permute-start.6 = (bf16[2,64,128]{2,1,0:T(8,128)(2,1)S(1)}, bf16[2,64,128]{2,1,0:T(8,128)(2,1)S(1)}, u32[]{:S(2)}, u32[]{:S(2)}) collective-permute-start(bf16[2,64,128]{2,1,0:T(8,128)(2,1)S(1)} %get-tuple-element.59), channel_id=1, source_target_pairs={{0,241},{1,240},{2,243},{3,242},{4,245},{5,244},{6,247},{7,246},{8... | collective-permute-start | bytes 98312 | tf_op jit(solution)/shard_map/ppermute | solution.py:330
  17.3 13.9 %collective-permute-start.2 = (bf16[3,64,128]{2,1,0:T(8,128)(2,1)S(1)}, bf16[3,64,128]{2,1,0:T(8,128)(2,1)S(1)}, u32[]{:S(2)}, u32[]{:S(2)}) collective-permute-start(bf16[3,64,128]{2,1,0:T(8,128)(2,1)S(1)} %get-tuple-element.55), channel_id=1, source_target_pairs={{0,1},{1,0},{2,3},{3,2},{4,5},{5,4},{6,7},{7,6},{8,9},{9,8},{10,11... | collective-permute-start | bytes 147464 | tf_op jit(solution)/shard_map/ppermute | solution.py:320
  17.7 13.5 %collective-permute-start.3 = (bf16[3,64,128]{2,1,0:T(8,128)(2,1)S(1)}, bf16[3,64,128]{2,1,0:T(8,128)(2,1)S(1)}, u32[]{:S(2)}, u32[]{:S(2)}) collective-permute-start(bf16[3,64,128]{2,1,0:T(8,128)(2,1)S(1)} %get-tuple-element.56), channel_id=1, source_target_pairs={{0,15},{1,2},{2,1},{3,4},{4,3},{5,6},{6,5},{7,8},{8,7},{9,10},{10,... | collective-permute-start | bytes 147464 | tf_op jit(solution)/shard_map/ppermute | solution.py:320
  22.6 8.6 %collective-permute-start.7 = (bf16[2,64,128]{2,1,0:T(8,128)(2,1)S(1)}, bf16[2,64,128]{2,1,0:T(8,128)(2,1)S(1)}, u32[]{:S(2)}, u32[]{:S(2)}) collective-permute-start(bf16[2,64,128]{2,1,0:T(8,128)(2,1)S(1)} %get-tuple-element.60), channel_id=1, source_target_pairs={{0,255},{1,242},{2,241},{3,244},{4,243},{5,246},{6,245},{7,248},{8... | collective-permute-start | bytes 98312 | tf_op jit(solution)/shard_map/ppermute | solution.py:330
  37.0 4.7 %collective-permute-start.8 = (bf16[2304,128]{1,0:T(8,128)(2,1)S(1)}, bf16[2304,128]{1,0:T(8,128)(2,1)S(1)}, u32[]{:S(2)}, u32[]{:S(2)}) collective-permute-start(bf16[2304,128]{1,0:T(8,128)(2,1)S(1)} %get-tuple-element.62), channel_id=1, source_target_pairs={{0,1},{1,0},{2,3},{3,2},{4,5},{5,4},{6,7},{7,6},{8,9},{9,8},{10,11... | collective-permute-start | bytes 1769480 | tf_op jit(solution)/shard_map/ppermute | solution.py:311
  42.0 7.2 %collective-permute-start.10 = (bf16[2,2,136,128]{3,2,1,0:T(8,128)(2,1)S(1)}, bf16[2,2,136,128]{3,2,1,0:T(8,128)(2,1)S(1)}, u32[]{:S(2)}, u32[]{:S(2)}) collective-permute-start(bf16[2,2,136,128]{3,2,1,0:T(8,128)(2,1)S(1)} %pad_maximum_fusion), channel_id=1, source_target_pairs={{0,6},{1,7},{2,4},{3,5},{4,2},{5,3},{6,0},{7,1},{8,14},{9,15},{10,... | collective-permute-start | bytes 417800 | tf_op jit(solution)/shard_map/ppermute | solution.py:311
  43.2 6.1 %collective-permute-start.9 = (bf16[2,2,136,128]{3,2,1,0:T(8,128)(2,1)S(1)}, bf16[2,2,136,128]{3,2,1,0:T(8,128)(2,1)S(1)}, u32[]{:S(2)}, u32[]{:S(2)}) collective-permute-start(bf16[2,2,136,128]{3,2,1,0:T(8,128)(2,1)S(1)} %stack.56), channel_id=1, source_target_pairs={{0,2},{1,3},{2,0},{3,1},{4,6},{5,7},{6,4},{7,5},{8,10},{9,11},{10,... | collective-permute-start | bytes 417800 | tf_op jit(solution)/shard_map/ppermute | solution.py:311
  43.2 6.0 %collective-permute-start.11 = (bf16[2,64,128]{2,1,0:T(8,128)(2,1)S(1)}, bf16[2,64,128]{2,1,0:T(8,128)(2,1)S(1)}, u32[]{:S(2)}, u32[]{:S(2)}) collective-permute-start(bf16[2,64,128]{2,1,0:T(8,128)(2,1)S(1)} %get-tuple-element.63), channel_id=1, source_target_pairs={{0,15},{1,2},{2,1},{3,4},{4,3},{5,6},{6,5},{7,8},{8,7},{9,10},{10,... | collective-permute-start | bytes 98312 | tf_op jit(solution)/shard_map/ppermute | solution.py:320
  49.4 4.5 %collective-permute-start.12 = (bf16[2,136,128]{2,1,0:T(8,128)(2,1)S(1)}, bf16[2,136,128]{2,1,0:T(8,128)(2,1)S(1)}, u32[]{:S(2)}, u32[]{:S(2)}) collective-permute-start(bf16[2,136,128]{2,1,0:T(8,128)(2,1)S(1)} %get-tuple-element.102), channel_id=1, source_target_pairs={{0,6},{1,7},{2,4},{3,5},{4,2},{5,3},{6,0},{7,1},{8,14},{9,15},{10,... | collective-permute-start | bytes 208904 | tf_op jit(solution)/shard_map/ppermute | solution.py:311
  53.9 8.5 %collective-permute-start.14 = (bf16[264,128]{1,0:T(8,128)(2,1)S(1)}, bf16[264,128]{1,0:T(8,128)(2,1)S(1)}, u32[]{:S(2)}, u32[]{:S(2)}) collective-permute-start(bf16[264,128]{1,0:T(8,128)(2,1)S(1)} %pad_maximum_fusion.5), channel_id=1, source_target_pairs={{0,16},{16,0},{32,48},{48,32},{64,80},{80,64},{96,112},{112,96},{1... | collective-permute-start | bytes 202760 | tf_op jit(solution)/shard_map/ppermute | solution.py:311
  54.0 10.2 %collective-permute-start.16 = (bf16[136,128]{1,0:T(8,128)(2,1)S(1)}, bf16[136,128]{1,0:T(8,128)(2,1)S(1)}, u32[]{:S(2)}, u32[]{:S(2)}) collective-permute-start(bf16[136,128]{1,0:T(8,128)(2,1)S(1)} %get-tuple-element.109), channel_id=1, source_target_pairs={{0,48},{16,32},{32,16},{48,0},{64,112},{80,96},{96,80},{112,64},{1... | collective-permute-start | bytes 104456 | tf_op jit(solution)/shard_map/ppermute | solution.py:311
  54.1 10.1 %collective-permute-start.15 = (bf16[136,128]{1,0:T(8,128)(2,1)S(1)}, bf16[136,128]{1,0:T(8,128)(2,1)S(1)}, u32[]{:S(2)}, u32[]{:S(2)}) collective-permute-start(bf16[136,128]{1,0:T(8,128)(2,1)S(1)} %get-tuple-element.110), channel_id=1, source_target_pairs={{0,32},{16,48},{32,0},{48,16},{64,96},{80,112},{96,64},{112,80},{1... | collective-permute-start | bytes 104456 | tf_op jit(solution)/shard_map/ppermute | solution.py:311
  57.2 7.0 %collective-permute-start.17 = (bf16[2,64,128]{2,1,0:T(8,128)(2,1)S(1)}, bf16[2,64,128]{2,1,0:T(8,128)(2,1)S(1)}, u32[]{:S(2)}, u32[]{:S(2)}) collective-permute-start(bf16[2,64,128]{2,1,0:T(8,128)(2,1)S(1)} %get-tuple-element.75), channel_id=1, source_target_pairs={{0,240},{16,32},{32,16},{48,64},{64,48},{80,96},{96,80},{112,128},... | collective-permute-start | bytes 98312 | tf_op jit(solution)/shard_map/ppermute | solution.py:320
  64.3 6.7 %collective-permute-start.20 = (bf16[136,128]{1,0:T(8,128)(2,1)S(1)}, bf16[136,128]{1,0:T(8,128)(2,1)S(1)}, u32[]{:S(2)}, u32[]{:S(2)}) collective-permute-start(bf16[136,128]{1,0:T(8,128)(2,1)S(1)} %fusion.11), channel_id=1, source_target_pairs={{0,192},{16,208},{32,224},{48,240},{64,128},{80,144},{96,160},{112... | collective-permute-start | bytes 104456 | tf_op jit(solution)/shard_map/ppermute | solution.py:311
  66.8 6.8 %collective-permute-start.19 = (bf16[136,128]{1,0:T(8,128)(2,1)S(1)}, bf16[136,128]{1,0:T(8,128)(2,1)S(1)}, u32[]{:S(2)}, u32[]{:S(2)}) collective-permute-start(bf16[136,128]{1,0:T(8,128)(2,1)S(1)} %fusion.11), channel_id=1, source_target_pairs={{0,128},{16,144},{32,160},{48,176},{64,192},{80,208},{96,224},{112... | collective-permute-start | bytes 104456 | tf_op jit(solution)/shard_map/ppermute | solution.py:311
  67.8 5.8 %collective-permute-start.18 = (bf16[136,128]{1,0:T(8,128)(2,1)S(1)}, bf16[136,128]{1,0:T(8,128)(2,1)S(1)}, u32[]{:S(2)}, u32[]{:S(2)}) collective-permute-start(bf16[136,128]{1,0:T(8,128)(2,1)S(1)} %fusion.11), channel_id=1, source_target_pairs={{0,64},{16,80},{32,96},{48,112},{64,0},{80,16},{96,32},{112,48},{1... | collective-permute-start | bytes 104456 | tf_op jit(solution)/shard_map/ppermute | solution.py:311
  77.4 4.9 %collective-permute-start.24 = (bf16[136,128]{1,0:T(8,128)(2,1)S(1)}, bf16[136,128]{1,0:T(8,128)(2,1)S(1)}, u32[]{:S(2)}, u32[]{:S(2)}) collective-permute-start(bf16[136,128]{1,0:T(8,128)(2,1)S(1)} %add_convert_fusion), channel_id=1, source_target_pairs={{0,48},{16,32},{32,16},{48,0},{64,112},{80,96},{96,80},{112,64},{1... | collective-permute-start | bytes 104456 | tf_op jit(solution)/shard_map/ppermute | solution.py:311
  85.3 4.5 %collective-permute-start.25 = (bf16[2,136,128]{2,1,0:T(8,128)(2,1)S(1)}, bf16[2,136,128]{2,1,0:T(8,128)(2,1)S(1)}, u32[]{:S(2)}, u32[]{:S(2)}) collective-permute-start(bf16[2,136,128]{2,1,0:T(8,128)(2,1)S(1)} %get-tuple-element.108), channel_id=1, source_target_pairs={{0,6},{1,7},{2,4},{3,5},{4,2},{5,3},{6,0},{7,1},{8,14},{9,15},{10,... | collective-permute-start | bytes 208904 | tf_op jit(solution)/shard_map/ppermute | solution.py:311
  89.9 5.2 %collective-permute-start.28 = (bf16[2,2,136,128]{3,2,1,0:T(8,128)(2,1)S(1)}, bf16[2,2,136,128]{3,2,1,0:T(8,128)(2,1)S(1)}, u32[]{:S(2)}, u32[]{:S(2)}) collective-permute-start(bf16[2,2,136,128]{3,2,1,0:T(8,128)(2,1)S(1)} %pad_maximum_fusion.2.b0_ref), channel_id=1, source_target_pairs={{0,6},{1,7},{2,4},{3,5},{4,2},{5,3},{6,0},{7,1},{8,14},{9,15},{10,... | collective-permute-start | bytes 417800 | tf_op jit(solution)/shard_map/ppermute | solution.py:311
  95.2 11.3 %collective-permute-start.29 = (bf16[8,2,136,128]{3,2,1,0:T(8,128)(2,1)S(1)}, bf16[8,2,136,128]{3,2,1,0:T(8,128)(2,1)S(1)}, u32[]{:S(2)}, u32[]{:S(2)}) collective-permute-start(bf16[8,2,136,128]{3,2,1,0:T(8,128)(2,1)S(1)} %constant_dynamic-update-slice_fusion), channel_id=1, source_target_pairs={{0,1},{1,0},{2,3},{3,2},{4,5},{5,4},{6,7},{7,6},{8,9},{9,8},{10,11... | collective-permute-start | bytes 1671176 | tf_op jit(solution)/shard_map/ppermute | solution.py:311
  (7 other events, 48.5 us)

commit v2 on v1

--- a/solution.py
+++ b/solution.py
@@ -18,7 +18,7 @@
 ROWS = 136
 CHUNKS = 32
 SENT = CHUNKS // 2 * ROWS
-FACE, FACE_Y = SIZE_Y + BLOCKS_C // 2, SIZE_X + 1
+FACE, FACE_Y = SIZE_Y + BLOCKS_C // 2, SIZE_X + 2 + 2
 BF16, F32 = jnp.bfloat16, jnp.float32
 
 
@@ -72,11 +72,8 @@
     return weights[0] * first.astype(F32) + weights[1] * second.astype(F32)
 
 
-def split_kernel(
-    skip_hbm, cot_hbm, skip_out, cot_out, pool_out, *refs,
-):
-    faces, (skip_ref, cot_ref, rows_ref, arrived) = refs[:8], refs[8:]
-    ups = [(1 - (place & 1), place & 1) for place in places()]
+def split_kernel(skip_hbm, cot_hbm, skip_out, cot_out, pool_out, two_out, one_out, skip_ref, cot_ref, rows_ref, arrived):
+    odd = places()[0] & 1
     copies = [
         pltpu.make_async_copy(source, target, arrived.at[index])
         for index, (source, target) in enumerate(((cot_hbm, cot_ref), (skip_hbm, skip_ref)))
@@ -91,6 +88,9 @@
     rows_ref[...] = cot_ref[...].astype(F32).reshape(SKIP * BLOCKS, LANES)
     for index in range(BLOCKS):
         cot_out[index] = block_of(index).astype(BF16)
+    for row in range(SIZE_Y):
+        one_out[row] = cot_out[(1 - odd) * SIZE_Y + row]
+        two_out[row] = cot_out[odd * SIZE_Y + row]
     copies[1].wait()
     rows_ref[...] = skip_ref[...].astype(F32).reshape(SKIP * BLOCKS, LANES)
     pools = []
@@ -102,32 +102,21 @@
             total = block if total is None else total + block
         pools.append(paired(total) * 0.125)
         pool_out[coarse] = pools[-1].astype(BF16)
-    packed = [pack(pools[2 * index], pools[2 * index + 1]).astype(BF16) for index in range(BLOCKS_C // 2)]
-    for which in range(2):
-        up_x, up_y = ups[0][which], ups[1][which]
-        for row in range(SIZE_Y):
-            faces[which][row] = cot_out[up_x * SIZE_Y + row]
-        for index, value in enumerate(packed):
-            faces[which][SIZE_Y + index] = value
-        row, row_c = up_y * (SIZE_Y - 1), up_y * (BLOCKS_C - 1)
-        for plane in range(SIZE_X):
-            faces[2 + which][plane] = cot_out[plane * SIZE_Y + row]
-        faces[2 + which][SIZE_X] = pool_out[row_c]
-        for other in range(2):
-            corner = faces[4 + 2 * other + which]
-            corner[0] = cot_out[ups[0][other] * SIZE_Y + row]
-            corner[1] = pool_out[row_c]
+    for index in range(BLOCKS_C // 2):
+        packed = pack(pools[2 * index], pools[2 * index + 1]).astype(BF16)
+        one_out[SIZE_Y + index] = packed
+        two_out[SIZE_Y + index] = packed
 
 
 def vmem():
     return pl.BlockSpec(memory_space=pltpu.VMEM)
 
 
-def call(kernel, name, outs, scratch, mib, cost, *operands, held=pltpu.VMEM):
+def call(kernel, name, outs, scratch, mib, cost, *operands, held=()):
     return pl.pallas_call(
         kernel,
         out_shape=tuple(jax.ShapeDtypeStruct(shape, dtype) for shape, dtype in outs),
-        in_specs=[pl.BlockSpec(memory_space=held)] * len(operands),
+        in_specs=[pl.BlockSpec(memory_space=space) for space in held or (pltpu.VMEM,) * len(operands)],
         out_specs=tuple(vmem() for _ in outs),
         scratch_shapes=[pltpu.VMEM(*form) if isinstance(form, tuple) else form for form in scratch],
         compiler_params=params(mib),
@@ -136,38 +125,62 @@
     )(*operands)
 
 
+def faces_kernel(cot_ref, pool_ref, xtwo_ref, xone_ref, *refs):
+    one_out, two_out = refs[-2:]
+    place = places()
+    low, high = sides(place[0])
+    odd = place[1] & 1
+    for out, up in ((one_out, 1 - odd), (two_out, odd)):
+        row = up * (SIZE_Y - 1)
+        out[0] = mixed(low, xone_ref[row], xtwo_ref[row]).astype(BF16)
+        out[1] = cot_ref[row]
+        out[2] = cot_ref[SIZE_Y + row]
+        out[3] = mixed(high, xone_ref[row], xtwo_ref[row]).astype(BF16)
+        pair = SIZE_Y + up * (BLOCKS_C // 2 - 1)
+        upper = up.astype(F32)
+
+        def pooled_of(weights):
+            first, second = unpack_pair(mixed(weights, xone_ref[pair], xtwo_ref[pair]))
+            return (1.0 - upper) * first + upper * second
+
+        out[4] = pack(pooled_of(low), pool_ref[up * (BLOCKS_C - 1)].astype(F32)).astype(BF16)
+        out[5] = pooled_of(high).astype(BF16)
+
+
+def row_of(place, core, yp, xp):
+    def ring(own, position):
+        return own ^ (0, 1 + 2 * core, 3 - 2 * core, 2)[position]
+
+    at = 16 * core + 4 * ring((place[1] >> 1) & 3, yp) + ring(place[0] & 3, xp)
+    return pl.multiple_of(at * ROWS, ROWS)
+
+
 def grads_kernel(
-    skip_ref, cot_ref, pool_ref, xone_ref, xtwo_ref, yone_ref, ytwo_ref, *refs,
+    skip_ref, cot_ref, pool_ref, xtwo_ref, xone_ref, ytwo_ref, yone_ref, *refs,
 ):
-    corner_refs, (wdec_ref, wpre_ref, wback_ref) = refs[:4], refs[4:7]
-    send_out, keep_out, jskip_out, rim_out, two_out = refs[7:12]
-    cells_ref, pooled_ref, joined_ref, jgrad_ref, full_ref, pre_ref = refs[12:]
+    wdec_ref, wpre_ref, wback_ref = refs[:3]
+    send_out, keep_out, jskip_out, rim_out, two_out = refs[3:8]
+    cells_ref, pooled_ref, joined_ref, jgrad_ref, full_ref, pre_ref = refs[8:]
     factor = 1.0 / math.sqrt(524288)
     place = places()
     xlow, xhigh = sides(place[0])
     ylow, yhigh = sides(place[1])
 
-    def corner(xside, yside, index):
-        first = mixed(yside, corner_refs[0][index], corner_refs[1][index])
-        second = mixed(yside, corner_refs[2][index], corner_refs[3][index])
-        return mixed(xside, first, second)
-
     def fine(plane, row):
-        yside = {0: ylow, SIZE_Y + 1: yhigh}.get(row)
-        xside = {0: xlow, SIZE_X + 1: xhigh}.get(plane)
-        if xside and yside:
-            return corner(xside, yside, 0)
-        if yside:
-            return mixed(yside, yone_ref[plane - 1], ytwo_ref[plane - 1])
-        if xside:
-            return mixed(xside, xone_ref[row - 1], xtwo_ref[row - 1])
+        if row == 0:
+            return mixed(ylow, yone_ref[plane], ytwo_ref[plane])
+        if row == SIZE_Y + 1:
+            return mixed(yhigh, yone_ref[plane], ytwo_ref[plane])
+        if plane == 0:
+            return mixed(xlow, xone_ref[row - 1], xtwo_ref[row - 1])
+        if plane == SIZE_X + 1:
+            return mixed(xhigh, xone_ref[row - 1], xtwo_ref[row - 1])
         return cot_ref[(plane - 1) * SIZE_Y + row - 1].astype(F32)
 
     wide_pool = {}
-    for row, yside in ((0, ylow), (BLOCKS_C + 1, yhigh)):
-        wide_pool[0, row] = corner(xlow, yside, 1)
-        wide_pool[1, row] = mixed(yside, yone_ref[SIZE_X], ytwo_ref[SIZE_X])
-        wide_pool[2, row] = corner(xhigh, yside, 1)
+    for row, weights in ((0, ylow), (BLOCKS_C + 1, yhigh)):
+        wide_pool[0, row], wide_pool[1, row] = unpack_pair(mixed(weights, yone_ref[4], ytwo_ref[4]))
+        wide_pool[2, row] = mixed(weights, yone_ref[5], ytwo_ref[5])
     for plane, weights in ((0, xlow), (2, xhigh)):
         for index in range(BLOCKS_C // 2):
             at = SIZE_Y + index
@@ -249,16 +262,13 @@
         pooled_ref[...], pre_grad, across, preferred_element_type=F32
     ) * (0.5 * factor)
     full_ref[PACKED:] = jnp.zeros((CHUNKS * ROWS - PACKED, LANES), F32)
-    core, y, x = place[1] & 1, (place[1] >> 1) & 3, place[0] & 3
-    for yr in range(4):
+    core = place[1] & 1
+    for yp in range(4):
         leave = []
-        for xr in range(4):
-            at = (y ^ yr) * 4 + (x ^ xr)
-            row = pl.multiple_of((at + 16 * core) * ROWS, ROWS)
-            keep_out[yr, xr] = full_ref[pl.ds(row, ROWS), :]
-            row = pl.multiple_of((at + 16 * (1 - core)) * ROWS, ROWS)
-            leave.append(full_ref[pl.ds(row, ROWS), :])
-        send_out[4 * yr * ROWS : 4 * (yr + 1) * ROWS] = jnp.concatenate(leave).astype(BF16)
+        for xp in range(4):
+            keep_out[yp, xp] = full_ref[pl.ds(row_of(place, core, yp, xp), ROWS), :]
+            leave.append(full_ref[pl.ds(row_of(place, 1 - core, yp, xp), ROWS), :])
+        send_out[4 * yp * ROWS : 4 * (yp + 1) * ROWS] = jnp.concatenate(leave).astype(BF16)
 
 
 def fold_kernel(rim_ref, yone_ref, ytwo_ref, rows_out, one_out, two_out):
@@ -278,28 +288,28 @@
         two_out[index] = ((1.0 - odd) * down + odd * up).astype(BF16)
 
 
-def skip_kernel(rows_ref, xone_ref, xtwo_ref, jskip_ref, out_ref, cells_ref):
-    low, high = sides(places()[0])
-    weights = (low[0] + high[0], low[1] + high[1])
+def skip_kernel(rows_ref, one0_ref, one1_ref, xtwo_ref, jskip_ref, out_ref, cells_ref):
+    place = places()
+    low, high = sides(place[0])
+    core = (place[1] & 1).astype(F32)
     for pair in range(BLOCKS_C // 2):
-        for at, terms in zip((2 * pair, 2 * pair + 1), unpack_pair(mixed(weights, xone_ref[pair], xtwo_ref[pair]))):
+        one = mixed((1.0 - core, core), one0_ref[pair], one1_ref[pair])
+        terms_of = unpack_pair(mixed((low[0] + high[0], low[1] + high[1]), one, xtwo_ref[pair]))
+        for at, terms in zip((2 * pair, 2 * pair + 1), terms_of):
             total = rows_ref[at] + terms
             for index in (2 * at, 2 * at + 1, SIZE_Y + 2 * at, SIZE_Y + 2 * at + 1):
                 cells_ref[pl.ds(index, SKIP, stride=BLOCKS), :] = jskip_ref[index] + total
     out_ref[...] = cells_ref[...].reshape(SKIP, SIZE_X, SIZE_Y, LANES).astype(BF16)
 
 
-def unpack_kernel(a0_ref, a1_ref, b0_ref, b1_ref, core_ref, dec_out, coarse_out, full_ref):
+def unpack_kernel(near_ref, far_ref, other_ref, dec_out, coarse_out, full_ref):
     place = places()
-    core, y, x = place[1] & 1, (place[1] >> 1) & 3, place[0] & 3
-    for half, (refs, order) in enumerate((((a0_ref, a1_ref), ORDER_A), ((b0_ref, b1_ref), ORDER_B))):
-        for index, yr in enumerate(order):
-            for xr in range(2):
-                at = (y ^ yr) * 4 + (x ^ (2 * half + xr))
-                row = pl.multiple_of((at + 16 * core) * ROWS, ROWS)
-                full_ref[pl.ds(row, ROWS), :] = refs[index // 2][index % 2, xr].astype(F32)
-                row = pl.multiple_of((at + 16 * (1 - core)) * ROWS, ROWS)
-                full_ref[pl.ds(row, ROWS), :] = core_ref[4 * half + index, xr].astype(F32)
+    core = place[1] & 1
+    for yp in range(4):
+        for xp in range(4):
+            own = near_ref[yp, xp] if yp < 2 else far_ref[yp - 2, xp]
+            full_ref[pl.ds(row_of(place, core, yp, xp), ROWS), :] = own.astype(F32)
+            full_ref[pl.ds(row_of(place, 1 - core, yp, xp), ROWS), :] = other_ref[yp, xp].astype(F32)
     half = LANES // 2
     dec_out[:, :LANES] = full_ref[:DEC]
     dec_out[: DEC // 2, LANES:] = full_ref[DEC : DEC + DEC // 2, :half]
@@ -320,25 +330,31 @@
     return lax.ppermute(value, axis, [(i, partner(i, which, count)) for i in range(count)])
 
 
-def swap_corner(value, which_x, which_y):
+together = lax.optimization_barrier
+
+
+FIRST, SECOND = (3, 1), (1, 3)
+
+
+def swap_round(value, flips):
     size_x, size_y = lax.axis_size("gx"), lax.axis_size("gy")
     pairs = [
-        (i * size_y + j, partner(i, which_x, size_x) * size_y + partner(j, which_y, size_y))
+        (i * size_y + j, (i ^ flips[j % 2][0]) * size_y + (j ^ flips[j % 2][1]))
         for i in range(size_x)
         for j in range(size_y)
     ]
     return lax.ppermute(value, ("gx", "gy"), pairs)
 
 
-together = lax.optimization_barrier
-A_FIRST, A_SECOND = 1, 3
-B_FIRST, B_SECOND = 3, 1
-ORDER_A = (0, A_SECOND, A_FIRST, 2)
-ORDER_B = (0, B_SECOND, B_FIRST, 2)
-
-
-def swap_y(value, flip):
-    return swap(value, "gy", 2 * flip)
+def along_y(value, flips):
+    return swap_round(value, [(0, 2 * flip) for flip in flips])
+
+
+def along_x(value, flips):
+    return swap_round(value, [(flip, 0) for flip in flips])
+
+
+Z_ROUNDS = [((4, 0), (0, 8)), ((12, 0), (4, 0)), ((0, 8), (12, 0))]
 
 
 def wide(value):
@@ -353,24 +369,22 @@
     block = (SKIP, LANES)
     face, face_y, corner = (FACE,) + block, (FACE_Y,) + block, (2,) + block
     fine = (BLOCKS,) + block
-    skip, cot, pooled, *faces = call(
+    skip, cot, pooled, xtwo, xone = call(
         split_kernel, "split_blocks",
-        (
-            (fine, BF16), (fine, BF16), ((BLOCKS_C,) + block, BF16),
-            (face, BF16), (face, BF16), (face_y, BF16), (face_y, BF16),
-            (corner, BF16), (corner, BF16), (corner, BF16), (corner, BF16),
-        ),
+        ((fine, BF16), (fine, BF16), ((BLOCKS_C,) + block, BF16), (face, BF16), (face, BF16)),
         (
             (skip_feat.shape, BF16), (skip_feat.shape, BF16), ((SKIP * BLOCKS, LANES), F32),
             pltpu.SemaphoreType.DMA((2,)),
         ),
         8, (1_000_000, 1_500_000), *(pltpu.with_memory_space_constraint(x, pltpu.HBM) for x in (skip_feat, cotangent)),
-        held=pltpu.HBM,
-    )
-    xtwo = swap_side(faces[1], "gx", 1)
-    corners = [swap_corner(faces[4 + 2 * i + j], i, j) for i, j in ((0, 0), (0, 1), (1, 0), (1, 1))]
-    xone = swap_side(faces[0], "gx", 0)
-    yone, ytwo = (swap_side(faces[2 + which], "gy", which) for which in range(2))
+        held=(pltpu.HBM,) * 2,
+    )
+    xtwo, xone = swap_side(xtwo, "gx", 1), swap_side(xone, "gx", 0)
+    yone, ytwo = call(
+        faces_kernel, "row_faces", ((face_y, BF16), (face_y, BF16)), (), 8, (100_000, 400_000),
+        cot, pooled, xtwo, xone, w_join, w_pre, w_back, held=(pltpu.VMEM,) * 4 + (pl.ANY,) * 3,
+    )
+    yone, ytwo = swap_side(yone, "gy", 0), swap_side(ytwo, "gy", 1)
     chunks = (4, 4, ROWS, LANES)
     send, keep, jskip, own, rtwo = call(
         grads_kernel, "local_grads",
@@ -386,50 +400,43 @@
             ((CHUNKS * ROWS, LANES), F32),
             ((3 * COARSE, BLOCKS_C * LANES), BF16),
         ),
-        36, (3_000_000_000, 8_000_000), skip, cot, pooled, xone, xtwo, yone, ytwo, *corners,
+        36, (3_000_000_000, 8_000_000), skip, cot, pooled, xtwo, xone, ytwo, yone,
         w_join, w_pre, w_back,
     )
 
     send, rtwo = swap(send, "gy", 1), swap_side(rtwo, "gy", 1)
     part = keep + wide(send[:SENT].reshape(chunks))
-    rone = send[SENT:].reshape(corner)
-    a, b = part[:, :2], part[:, 2:]
-    a_got = swap_y(jnp.stack([a[A_FIRST], a[2]]).astype(BF16), A_FIRST)
-    b_got = swap_y(jnp.stack([b[B_FIRST], b[2]]).astype(BF16), B_FIRST)
-    a_got, b_got, rone, rtwo = together((a_got, b_got, rone, rtwo))
+    part = part[:2] + wide(along_y(part[2:].astype(BF16), FIRST))
+    part = part[0] + wide(along_y(part[1].astype(BF16), SECOND))
+    part = part[:2] + wide(along_x(part[2:].astype(BF16), FIRST))
+    got, rone, rtwo = together((along_x(part[1].astype(BF16), SECOND), send[SENT:].reshape(corner), rtwo))
+    part = part[0] + wide(got)
+    part = part.astype(BF16)
+    for flips in Z_ROUNDS:
+        part = wide(part) + wide(swap_round(part, flips))
+    part = part.astype(BF16)
     rows, qone, qtwo = call(
         fold_kernel, "fold_rim", (((BLOCKS_C,) + block, F32), (corner, BF16), (corner, BF16)), (), 8, (100_000, 600_000),
         own, rone, rtwo,
     )
-    a_own, a_leave = a[0] + wide(a_got[0]), a[A_SECOND] + wide(a_got[1])
-    b_own, b_leave = b[0] + wide(b_got[0]), b[B_SECOND] + wide(b_got[1])
-    a_got, b_got = swap_y(a_leave.astype(BF16), A_SECOND), swap_y(b_leave.astype(BF16), B_SECOND)
-    a_got, b_got, rows, qone, qtwo = together((a_got, b_got, rows, qone, qtwo))
-    part = jnp.concatenate([a_own + wide(a_got), b_own + wide(b_got)])
-    leave = part.astype(BF16)
-    qtwo = swap_side(qtwo, "gx", 1)
-    got = swap(jnp.concatenate([leave[1], qone.reshape(2 * SKIP, LANES)]), "gx", 1)
-    got = [got[:ROWS], swap(leave[2], "gx", 2), swap(leave[3], "gx", 3), got[ROWS:].reshape(corner)]
-    *got, qone, qtwo = together((*got, qtwo))
+    part, rows, qone, qtwo = together((part, rows, qone, qtwo))
+    rim = qone.reshape(2 * SKIP, LANES)
+    got = along_x(jnp.concatenate([part, rim]), SECOND)
+    part = jnp.stack([part, got[:ROWS]])
+    qone1 = got[ROWS:].reshape(corner)
+    got = along_x(jnp.concatenate([part.reshape(2 * ROWS, LANES), rim]), FIRST)
+    part = jnp.concatenate([part, got[: 2 * ROWS].reshape(2, ROWS, LANES)])
+    qone2 = got[2 * ROWS :].reshape(corner)
+    near = jnp.stack([part, along_y(part, SECOND)])
+    far, qtwo = together((along_y(near, FIRST), swap_side(qtwo, "gx", 1)))
+    other = swap(jnp.concatenate([near, far]), "gy", 1)
     (skip_grad,) = call(
         skip_kernel, "skip_gradient", (((SKIP, SIZE_X, SIZE_Y, LANES), BF16),), (((SKIP * BLOCKS, LANES), F32),),
-        8, (1_000_000, 1_000_000), rows, qone, qtwo, jskip,
-    )
-    part = (part[0] + wide(got[0])) + (wide(got[1]) + wide(got[2]))
-    mine = part.astype(BF16)
-    got = [swap(mine, "gx", 4 * flip) for flip in (1, 2, 3)]
-    *got, skip_grad = together((*got, skip_grad))
-    part = (wide(mine) + wide(got[0])) + (wide(got[1]) + wide(got[2]))
-    part = (part + swap(part, "gy", 8)).astype(BF16)
-    part = jnp.stack(together([part] + [swap(part, "gx", flip) for flip in (1, 2, 3)]))
-    a, b = part[:2], part[2:]
-    a_got, b_got = together((swap_y(a, A_SECOND), swap_y(b, B_SECOND)))
-    a_near, b_near = jnp.stack([a, a_got]), jnp.stack([b, b_got])
-    a_far, b_far = together((swap_y(a_near, A_FIRST), swap_y(b_near, B_FIRST)))
-    other = swap(jnp.concatenate([a_near, a_far, b_near, b_far]), "gy", 1)
+        8, (1_000_000, 1_000_000), rows, qone1, qone2, qtwo, jskip,
+    )
     dec, coarse = call(
         unpack_kernel, "unpack", (((DEC, JOINED), F32), ((DEC, COARSE), F32)), (((CHUNKS * ROWS, LANES), F32),),
-        16, (1_000_000, 5_000_000), a_near, a_far, b_near, b_far, other,
+        16, (1_000_000, 5_000_000), near, far, other,
     )
     return (
         skip_grad,

time: 109 us -> 105 us (0.963)
  starting transfers between devices: 58.3 us -> 56.1 us
  waiting for transfers between devices: 35.4 us -> 34 us
    ppermute x20 -> x2, waiting for transfers between devices: 22.4 us -> 2.25 us  [swap(): lax.ppermute(value, axis, [(i, i ^ flip) for i in range(lax.axis_size(axi...]
    ppermute x4 -> x11, waiting for transfers between devices: 7.32 us -> 26.3 us  [swap_round(): return lax.ppermute(value, ('gx', 'gy'), pairs)]
    ppermute x20 -> x2, starting transfers between devices: 32.3 us -> 13.7 us  [swap(): lax.ppermute(value, axis, [(i, i ^ flip) for i in range(lax.axis_size(axi...]
    ppermute x4 -> x11, starting transfers between devices: 7.74 us -> 16.2 us  [swap_round(): return lax.ppermute(value, ('gx', 'gy'), pairs)]
    ppermute x6, starting transfers between devices: 18.2 us -> 26.2 us  [swap_side(): lax.ppermute(value, axis, [(i, partner(i, which, count)) for i in range(c...]
    pallas_call x5 -> x6, Pallas kernels: 10.2 us -> 10.4 us  [call(): pl.pallas_call(kernel, out_shape=tuple((jax.ShapeDtypeStruct(shape, dtype...]
  transfers between devices with their start and end apart: 30 -> 19, of which waited for: 15 -> 17; matrix products, arithmetic and copies ran while one was open for 3% -> 3% of each run, Pallas kernels for 1% -> 1%
where the time goes in v2:
time: 105 us
  starting transfers between devices  56.1 us (53%)
  waiting for transfers between devices  34 us (32%)
  Pallas kernels  10.4 us (10%)
  local copies, waits for them, and re-layouts  3.27 us (3%)
    ppermute x11, waiting for transfers between devices, swap_round(): return lax.ppermute(value, ('gx', 'gy'), pairs)  26.3 us
    ppermute x6, starting transfers between devices, swap_side(): lax.ppermute(value, axis, [(i, partner(i, which, count)) for i in range(c...  26.2 us
    ppermute x11, starting transfers between devices, swap_round(): return lax.ppermute(value, ('gx', 'gy'), pairs)  16.2 us
    ppermute x2, starting transfers between devices, swap(): lax.ppermute(value, axis, [(i, i ^ flip) for i in range(lax.axis_size(axi...  13.7 us
    pallas_call x6, Pallas kernels, call(): pl.pallas_call(kernel, out_shape=tuple((jax.ShapeDtypeStruct(shape, dtype...  10.4 us
    ppermute x6, waiting for transfers between devices, swap_side(): lax.ppermute(value, axis, [(i, partner(i, which, count)) for i in range(c...  5.44 us
    ppermute x2, waiting for transfers between devices, swap(): lax.ppermute(value, axis, [(i, i ^ flip) for i in range(lax.axis_size(axi...  2.25 us
  transfers between devices with their start and end apart: 19, of which 17 were waited for; matrix products, arithmetic and copies ran while one was open for 3% of the time, Pallas kernels for 1%

profile of v2, /device:TPU:1, one launch (start us, length us, event | category | flops | bytes accessed | tf_op | source)
XLA Modules:
  0.0 105.0 jit_solution(13279258164057972042)
XLA Ops:
  2.1 9.1 %collective-permute-start = (bf16[10,64,128]{2,1,0:T(8,128)(2,1)S(1)}, bf16[10,64,128]{2,1,0:T(8,128)(2,1)S(1)}, u32[]{:S(2)}, u32[]{:S(2)}) collective-permute-start(bf16[10,64,128]{2,1,0:T(8,128)(2,1)S(1)} %get-tuple-element.32), channel_id=1, source_target_pairs={{0,240},{16,32},{32,16},{48,64},{64,48},{80,96},{96,80},{112,128},... | collective-permute-start | bytes 491528 | tf_op jit(solution)/shard_map/ppermute | solution.py:330
  16.2 4.4 %collective-permute-start.2 = (bf16[6,64,128]{2,1,0:T(8,128)(2,1)S(1)}, bf16[6,64,128]{2,1,0:T(8,128)(2,1)S(1)}, u32[]{:S(2)}, u32[]{:S(2)}) collective-permute-start(bf16[6,64,128]{2,1,0:T(8,128)(2,1)S(1)} %get-tuple-element.34), channel_id=1, source_target_pairs={{0,15},{1,2},{2,1},{3,4},{4,3},{5,6},{6,5},{7,8},{8,7},{9,10},{10,... | collective-permute-start | bytes 294920 | tf_op jit(solution)/shard_map/ppermute | solution.py:330
  20.6 2.2 %collective-permute-start.3 = (bf16[6,64,128]{2,1,0:T(8,128)(2,1)S(1)}, bf16[6,64,128]{2,1,0:T(8,128)(2,1)S(1)}, u32[]{:S(2)}, u32[]{:S(2)}) collective-permute-start(bf16[6,64,128]{2,1,0:T(8,128)(2,1)S(1)} %get-tuple-element.35), channel_id=1, source_target_pairs={{0,1},{1,0},{2,3},{3,2},{4,5},{5,4},{6,7},{7,6},{8,9},{9,8},{10,11... | collective-permute-start | bytes 294920 | tf_op jit(solution)/shard_map/ppermute | solution.py:330
  23.8 5.8 %local_grads.1 = (bf16[2304,128]{1,0:T(8,128)(2,1)S(1)}, f32[4,4,136,128]{3,2,1,0:T(8,128)S(1)}, f32[16,64,128]{2,1,0:T(8,128)S(1)}, f32[12,64,128]{2,1,0:T(8,128)S(1)}, bf16[2,64,128]{2,1,0:T(8,128)(2,1)S(1)}) custom-call(bf16[16,64,128]{2,1,0:T(8,128)(2,1)S(1)} %get-tuple-element.29.skip_ref, bf16[16,64,128]{2,1,0:T(8,128)(2,1)S(1)} %get-tuple-element.30.cot_ref, ...), custom_call_target="tpu_custom_call" | custom-call | flops 3000000000 | bytes 8000000 | tf_op jit(solution)/shard_map/local_grads/pallas_call | solution.py:116
  29.6 1.9 %collective-permute-start.4 = (bf16[2304,128]{1,0:T(8,128)(2,1)S(1)}, bf16[2304,128]{1,0:T(8,128)(2,1)S(1)}, u32[]{:S(2)}, u32[]{:S(2)}) collective-permute-start(bf16[2304,128]{1,0:T(8,128)(2,1)S(1)} %get-tuple-element.37), channel_id=1, source_target_pairs={{0,1},{1,0},{2,3},{3,2},{4,5},{5,4},{6,7},{7,6},{8,9},{9,8},{10,11... | collective-permute-start | bytes 1769480 | tf_op jit(solution)/shard_map/ppermute | solution.py:321
  31.5 1.6 %collective-permute-done.4 = bf16[2304,128]{1,0:T(8,128)(2,1)S(1)} collective-permute-done((bf16[2304,128]{1,0:T(8,128)(2,1)S(1)}, bf16[2304,128]{1,0:T(8,128)(2,1)S(1)}, u32[]{:S(2)}, u32[]{:S(2)}) %collective-permute-start.4) | collective-permute-done | bytes 589856 | tf_op jit(solution)/shard_map/ppermute | solution.py:321
  33.4 5.7 %collective-permute-done.5 = bf16[2,4,136,128]{3,2,1,0:T(8,128)(2,1)S(1)} collective-permute-done((bf16[2,4,136,128]{3,2,1,0:T(8,128)(2,1)S(1)}, bf16[2,4,136,128]{3,2,1,0:T(8,128)(2,1)S(1)}, u32[]{:S(2)}, u32[]{:S(2)}) %collective-permute-start.5) | collective-permute-done | bytes 278560 | tf_op jit(solution)/shard_map/ppermute | solution.py:346
  39.9 4.5 %collective-permute-done.6 = bf16[4,136,128]{2,1,0:T(8,128)(2,1)S(1)} collective-permute-done((bf16[4,136,128]{2,1,0:T(8,128)(2,1)S(1)}, bf16[4,136,128]{2,1,0:T(8,128)(2,1)S(1)}, u32[]{:S(2)}, u32[]{:S(2)}) %collective-permute-start.6) | collective-permute-done | bytes 139296 | tf_op jit(solution)/shard_map/ppermute | solution.py:346
  44.5 3.1 %collective-permute-done.7 = bf16[2,136,128]{2,1,0:T(8,128)(2,1)S(1)} collective-permute-done((bf16[2,136,128]{2,1,0:T(8,128)(2,1)S(1)}, bf16[2,136,128]{2,1,0:T(8,128)(2,1)S(1)}, u32[]{:S(2)}, u32[]{:S(2)}) %collective-permute-start.7) | collective-permute-done | bytes 69664 | tf_op jit(solution)/shard_map/ppermute | solution.py:346
  48.0 4.5 %collective-permute-start.9 = (bf16[2,64,128]{2,1,0:T(8,128)(2,1)S(1)}, bf16[2,64,128]{2,1,0:T(8,128)(2,1)S(1)}, u32[]{:S(2)}, u32[]{:S(2)}) collective-permute-start(bf16[2,64,128]{2,1,0:T(8,128)(2,1)S(1)} %get-tuple-element.38), channel_id=1, source_target_pairs={{0,15},{1,2},{2,1},{3,4},{4,3},{5,6},{6,5},{7,8},{8,7},{9,10},{10,... | collective-permute-start | bytes 98312 | tf_op jit(solution)/shard_map/ppermute | solution.py:330
  52.5 1.6 %collective-permute-done.9.ytwo_ref = bf16[2,64,128]{2,1,0:T(8,128)(2,1)S(1)} collective-permute-done((bf16[2,64,128]{2,1,0:T(8,128)(2,1)S(1)}, bf16[2,64,128]{2,1,0:T(8,128)(2,1)S(1)}, u32[]{:S(2)}, u32[]{:S(2)}) %collective-permute-start.9) | collective-permute-done | bytes 32800 | tf_op jit(solution)/shard_map/ppermute | solution.py:330
  55.7 1.6 %collective-permute-done.10 = bf16[136,128]{1,0:T(8,128)(2,1)S(1)} collective-permute-done((bf16[136,128]{1,0:T(8,128)(2,1)S(1)}, bf16[136,128]{1,0:T(8,128)(2,1)S(1)}, u32[]{:S(2)}, u32[]{:S(2)}) %collective-permute-start.10) | collective-permute-done | bytes 34848 | tf_op jit(solution)/shard_map/ppermute | solution.py:346
  58.0 3.4 %collective-permute-done.11 = f32[136,128]{1,0:T(8,128)S(1)} collective-permute-done((f32[136,128]{1,0:T(8,128)S(1)}, f32[136,128]{1,0:T(8,128)S(1)}, u32[]{:S(2)}, u32[]{:S(2)}) %collective-permute-start.11) | collective-permute-done | bytes 69664 | tf_op jit(solution)/shard_map/ppermute | solution.py:346
  61.5 4.2 %collective-permute-start.12 = (f32[136,128]{1,0:T(8,128)S(1)}, f32[136,128]{1,0:T(8,128)S(1)}, u32[]{:S(2)}, u32[]{:S(2)}) collective-permute-start(f32[136,128]{1,0:T(8,128)S(1)} %fusion.5), channel_id=1, source_target_pairs={{0,8},{1,193},{2,10},{3,195},{4,12},{5,197},{6,14},{7,199},{8,0},{... | collective-permute-start | bytes 208904 | tf_op jit(solution)/shard_map/ppermute | solution.py:346
  65.8 1.7 %collective-permute-done.12 = f32[136,128]{1,0:T(8,128)S(1)} collective-permute-done((f32[136,128]{1,0:T(8,128)S(1)}, f32[136,128]{1,0:T(8,128)S(1)}, u32[]{:S(2)}, u32[]{:S(2)}) %collective-permute-start.12) | collective-permute-done | bytes 69664 | tf_op jit(solution)/shard_map/ppermute | solution.py:346
  67.5 2.7 %collective-permute-start.13 = (bf16[264,128]{1,0:T(8,128)(2,1)S(1)}, bf16[264,128]{1,0:T(8,128)(2,1)S(1)}, u32[]{:S(2)}, u32[]{:S(2)}) collective-permute-start(bf16[264,128]{1,0:T(8,128)(2,1)S(1)} %pad_maximum_fusion.5), channel_id=1, source_target_pairs={{0,16},{1,49},{2,18},{3,51},{4,20},{5,53},{6,22},{7,55},{8,24},{9,... | collective-permute-start | bytes 202760 | tf_op jit(solution)/shard_map/ppermute | solution.py:346
  70.2 1.8 %collective-permute-done.13 = bf16[264,128]{1,0:T(8,128)(2,1)S(1)} collective-permute-done((bf16[264,128]{1,0:T(8,128)(2,1)S(1)}, bf16[264,128]{1,0:T(8,128)(2,1)S(1)}, u32[]{:S(2)}, u32[]{:S(2)}) %collective-permute-start.13) | collective-permute-done | bytes 67616 | tf_op jit(solution)/shard_map/ppermute | solution.py:346
  72.0 2.2 %collective-permute-start.14 = (bf16[400,128]{1,0:T(8,128)(2,1)S(1)}, bf16[400,128]{1,0:T(8,128)(2,1)S(1)}, u32[]{:S(2)}, u32[]{:S(2)}) collective-permute-start(bf16[400,128]{1,0:T(8,128)(2,1)S(1)} %pad_maximum_fusion.3), channel_id=1, source_target_pairs={{0,48},{1,17},{2,50},{3,19},{4,52},{5,21},{6,54},{7,23},{8,56},{9,... | collective-permute-start | bytes 307208 | tf_op jit(solution)/shard_map/ppermute | solution.py:346
  74.2 2.1 %collective-permute-done.14 = bf16[400,128]{1,0:T(8,128)(2,1)S(1)} collective-permute-done((bf16[400,128]{1,0:T(8,128)(2,1)S(1)}, bf16[400,128]{1,0:T(8,128)(2,1)S(1)}, u32[]{:S(2)}, u32[]{:S(2)}) %collective-permute-start.14) | collective-permute-done | bytes 102432 | tf_op jit(solution)/shard_map/ppermute | solution.py:346
  76.3 3.6 %collective-permute-start.15 = (bf16[4,136,128]{2,1,0:T(8,128)(2,1)S(1)}, bf16[4,136,128]{2,1,0:T(8,128)(2,1)S(1)}, u32[]{:S(2)}, u32[]{:S(2)}) collective-permute-start(bf16[4,136,128]{2,1,0:T(8,128)(2,1)S(1)} %get-tuple-element.56), channel_id=1, source_target_pairs={{0,2},{1,7},{2,0},{3,5},{4,6},{5,3},{6,4},{7,1},{8,10},{9,15},{10,... | collective-permute-start | bytes 417800 | tf_op jit(solution)/shard_map/ppermute | solution.py:346
  79.9 2.4 %collective-permute-done.15 = bf16[4,136,128]{2,1,0:T(8,128)(2,1)S(1)} collective-permute-done((bf16[4,136,128]{2,1,0:T(8,128)(2,1)S(1)}, bf16[4,136,128]{2,1,0:T(8,128)(2,1)S(1)}, u32[]{:S(2)}, u32[]{:S(2)}) %collective-permute-start.15) | collective-permute-done | bytes 139296 | tf_op jit(solution)/shard_map/ppermute | solution.py:346
  82.5 5.9 %collective-permute-start.17 = (bf16[2,64,128]{2,1,0:T(8,128)(2,1)S(1)}, bf16[2,64,128]{2,1,0:T(8,128)(2,1)S(1)}, u32[]{:S(2)}, u32[]{:S(2)}) collective-permute-start(bf16[2,64,128]{2,1,0:T(8,128)(2,1)S(1)} %get-tuple-element.49), channel_id=1, source_target_pairs={{0,240},{16,32},{32,16},{48,64},{64,48},{80,96},{96,80},{112,128},... | collective-permute-start | bytes 98312 | tf_op jit(solution)/shard_map/ppermute | solution.py:330
  89.7 11.9 %collective-permute-start.18 = (bf16[4,4,136,128]{3,2,1,0:T(8,128)(2,1)S(1)}, bf16[4,4,136,128]{3,2,1,0:T(8,128)(2,1)S(1)}, u32[]{:S(2)}, u32[]{:S(2)}) collective-permute-start(bf16[4,4,136,128]{3,2,1,0:T(8,128)(2,1)S(1)} %pad_maximum_fusion), channel_id=1, source_target_pairs={{0,1},{1,0},{2,3},{3,2},{4,5},{5,4},{6,7},{7,6},{8,9},{9,8},{10,11... | collective-permute-start | bytes 1671176 | tf_op jit(solution)/shard_map/ppermute | solution.py:321
  103.1 1.9 %unpack.1 = (f32[1728,192]{1,0:T(8,128)}, f32[1728,128]{1,0:T(8,128)}) custom-call(bf16[2,4,136,128]{3,2,1,0:T(8,128)(2,1)S(1)} %pad_maximum_fusion.1.near_ref, bf16[2,4,136,128]{3,2,1,0:T(8,128)(2,1)S(1)} %collective-permute-done.16.far_ref, bf16[4,4,136,128]{3,2,1,0:T(8,128)(2,1)S(1)} %collective-permute-done.18.other_ref), custom_call_target="tpu_custom_call" | custom-call | flops 1000000 | bytes 5000000 | tf_op jit(solution)/shard_map/unpack/pallas_call | solution.py:116
  (50 shorter events, 14.4 us)
Async XLA Ops:
  0.6 11.9 %copy-start = (bf16[27,64,128]{2,1,0:T(8,128)(2,1)S(1)}, bf16[27,64,128]{2,1,0:T(8,128)(2,1)}, u32[]{:S(2)}) copy-start(bf16[27,64,128]{2,1,0:T(8,128)(2,1)} %param.6) | copy-start | bytes 1327108
  2.1 13.6 %collective-permute-start = (bf16[10,64,128]{2,1,0:T(8,128)(2,1)S(1)}, bf16[10,64,128]{2,1,0:T(8,128)(2,1)S(1)}, u32[]{:S(2)}, u32[]{:S(2)}) collective-permute-start(bf16[10,64,128]{2,1,0:T(8,128)(2,1)S(1)} %get-tuple-element.32), channel_id=1, source_target_pairs={{0,240},{16,32},{32,16},{48,64},{64,48},{80,96},{96,80},{112,128},... | collective-permute-start | bytes 491528 | tf_op jit(solution)/shard_map/ppermute | solution.py:330
  11.3 4.7 %collective-permute-start.1 = (bf16[10,64,128]{2,1,0:T(8,128)(2,1)S(1)}, bf16[10,64,128]{2,1,0:T(8,128)(2,1)S(1)}, u32[]{:S(2)}, u32[]{:S(2)}) collective-permute-start(bf16[10,64,128]{2,1,0:T(8,128)(2,1)S(1)} %get-tuple-element.33), channel_id=1, source_target_pairs={{0,16},{16,0},{32,48},{48,32},{64,80},{80,64},{96,112},{112,96},{1... | collective-permute-start | bytes 491528 | tf_op jit(solution)/shard_map/ppermute | solution.py:330
  16.2 6.7 %collective-permute-start.2 = (bf16[6,64,128]{2,1,0:T(8,128)(2,1)S(1)}, bf16[6,64,128]{2,1,0:T(8,128)(2,1)S(1)}, u32[]{:S(2)}, u32[]{:S(2)}) collective-permute-start(bf16[6,64,128]{2,1,0:T(8,128)(2,1)S(1)} %get-tuple-element.34), channel_id=1, source_target_pairs={{0,15},{1,2},{2,1},{3,4},{4,3},{5,6},{6,5},{7,8},{8,7},{9,10},{10,... | collective-permute-start | bytes 294920 | tf_op jit(solution)/shard_map/ppermute | solution.py:330
  20.6 3.2 %collective-permute-start.3 = (bf16[6,64,128]{2,1,0:T(8,128)(2,1)S(1)}, bf16[6,64,128]{2,1,0:T(8,128)(2,1)S(1)}, u32[]{:S(2)}, u32[]{:S(2)}) collective-permute-start(bf16[6,64,128]{2,1,0:T(8,128)(2,1)S(1)} %get-tuple-element.35), channel_id=1, source_target_pairs={{0,1},{1,0},{2,3},{3,2},{4,5},{5,4},{6,7},{7,6},{8,9},{9,8},{10,11... | collective-permute-start | bytes 294920 | tf_op jit(solution)/shard_map/ppermute | solution.py:330
  29.6 3.5 %collective-permute-start.4 = (bf16[2304,128]{1,0:T(8,128)(2,1)S(1)}, bf16[2304,128]{1,0:T(8,128)(2,1)S(1)}, u32[]{:S(2)}, u32[]{:S(2)}) collective-permute-start(bf16[2304,128]{1,0:T(8,128)(2,1)S(1)} %get-tuple-element.37), channel_id=1, source_target_pairs={{0,1},{1,0},{2,3},{3,2},{4,5},{5,4},{6,7},{7,6},{8,9},{9,8},{10,11... | collective-permute-start | bytes 1769480 | tf_op jit(solution)/shard_map/ppermute | solution.py:321
  33.3 5.8 %collective-permute-start.5 = (bf16[2,4,136,128]{3,2,1,0:T(8,128)(2,1)S(1)}, bf16[2,4,136,128]{3,2,1,0:T(8,128)(2,1)S(1)}, u32[]{:S(2)}, u32[]{:S(2)}) collective-permute-start(bf16[2,4,136,128]{3,2,1,0:T(8,128)(2,1)S(1)} %slice.93), channel_id=1, source_target_pairs={{0,6},{1,3},{2,4},{3,1},{4,2},{5,7},{6,0},{7,5},{8,14},{9,11},{10,... | collective-permute-start | bytes 835592 | tf_op jit(solution)/shard_map/ppermute | solution.py:346
  39.2 5.2 %collective-permute-start.6 = (bf16[4,136,128]{2,1,0:T(8,128)(2,1)S(1)}, bf16[4,136,128]{2,1,0:T(8,128)(2,1)S(1)}, u32[]{:S(2)}, u32[]{:S(2)}) collective-permute-start(bf16[4,136,128]{2,1,0:T(8,128)(2,1)S(1)} %fusion.1), channel_id=1, source_target_pairs={{0,2},{1,7},{2,0},{3,5},{4,6},{5,3},{6,4},{7,1},{8,10},{9,15},{10,... | collective-permute-start | bytes 417800 | tf_op jit(solution)/shard_map/ppermute | solution.py:346
  44.4 3.2 %collective-permute-start.7 = (bf16[2,136,128]{2,1,0:T(8,128)(2,1)S(1)}, bf16[2,136,128]{2,1,0:T(8,128)(2,1)S(1)}, u32[]{:S(2)}, u32[]{:S(2)}) collective-permute-start(bf16[2,136,128]{2,1,0:T(8,128)(2,1)S(1)} %slice.94), channel_id=1, source_target_pairs={{0,48},{1,17},{2,50},{3,19},{4,52},{5,21},{6,54},{7,23},{8,56},{9,... | collective-permute-start | bytes 208904 | tf_op jit(solution)/shard_map/ppermute | solution.py:346
  47.7 6.4 %collective-permute-start.8 = (bf16[136,128]{1,0:T(8,128)(2,1)S(1)}, bf16[136,128]{1,0:T(8,128)(2,1)S(1)}, u32[]{:S(2)}, u32[]{:S(2)}) collective-permute-start(bf16[136,128]{1,0:T(8,128)(2,1)S(1)} %fusion.4), channel_id=1, source_target_pairs={{0,16},{1,49},{2,18},{3,51},{4,20},{5,53},{6,22},{7,55},{8,24},{9,... | collective-permute-start | bytes 104456 | tf_op jit(solution)/shard_map/ppermute | solution.py:346
  48.0 6.1 %collective-permute-start.9 = (bf16[2,64,128]{2,1,0:T(8,128)(2,1)S(1)}, bf16[2,64,128]{2,1,0:T(8,128)(2,1)S(1)}, u32[]{:S(2)}, u32[]{:S(2)}) collective-permute-start(bf16[2,64,128]{2,1,0:T(8,128)(2,1)S(1)} %get-tuple-element.38), channel_id=1, source_target_pairs={{0,15},{1,2},{2,1},{3,4},{4,3},{5,6},{6,5},{7,8},{8,7},{9,10},{10,... | collective-permute-start | bytes 98312 | tf_op jit(solution)/shard_map/ppermute | solution.py:330
  54.1 3.2 %collective-permute-start.10 = (bf16[136,128]{1,0:T(8,128)(2,1)S(1)}, bf16[136,128]{1,0:T(8,128)(2,1)S(1)}, u32[]{:S(2)}, u32[]{:S(2)}) collective-permute-start(bf16[136,128]{1,0:T(8,128)(2,1)S(1)} %fusion.3), channel_id=1, source_target_pairs={{0,64},{1,9},{2,66},{3,11},{4,68},{5,13},{6,70},{7,15},{8,72},{9,1... | collective-permute-start | bytes 104456 | tf_op jit(solution)/shard_map/ppermute | solution.py:346
  57.3 4.1 %collective-permute-start.11 = (f32[136,128]{1,0:T(8,128)S(1)}, f32[136,128]{1,0:T(8,128)S(1)}, u32[]{:S(2)}, u32[]{:S(2)}) collective-permute-start(f32[136,128]{1,0:T(8,128)S(1)} %convert_add_fusion.1), channel_id=1, source_target_pairs={{0,192},{1,65},{2,194},{3,67},{4,196},{5,69},{6,198},{7,71},{8,200... | collective-permute-start | bytes 208904 | tf_op jit(solution)/shard_map/ppermute | solution.py:346
  61.5 6.0 %collective-permute-start.12 = (f32[136,128]{1,0:T(8,128)S(1)}, f32[136,128]{1,0:T(8,128)S(1)}, u32[]{:S(2)}, u32[]{:S(2)}) collective-permute-start(f32[136,128]{1,0:T(8,128)S(1)} %fusion.5), channel_id=1, source_target_pairs={{0,8},{1,193},{2,10},{3,195},{4,12},{5,197},{6,14},{7,199},{8,0},{... | collective-permute-start | bytes 208904 | tf_op jit(solution)/shard_map/ppermute | solution.py:346
  67.5 4.4 %collective-permute-start.13 = (bf16[264,128]{1,0:T(8,128)(2,1)S(1)}, bf16[264,128]{1,0:T(8,128)(2,1)S(1)}, u32[]{:S(2)}, u32[]{:S(2)}) collective-permute-start(bf16[264,128]{1,0:T(8,128)(2,1)S(1)} %pad_maximum_fusion.5), channel_id=1, source_target_pairs={{0,16},{1,49},{2,18},{3,51},{4,20},{5,53},{6,22},{7,55},{8,24},{9,... | collective-permute-start | bytes 202760 | tf_op jit(solution)/shard_map/ppermute | solution.py:346
  72.0 4.2 %collective-permute-start.14 = (bf16[400,128]{1,0:T(8,128)(2,1)S(1)}, bf16[400,128]{1,0:T(8,128)(2,1)S(1)}, u32[]{:S(2)}, u32[]{:S(2)}) collective-permute-start(bf16[400,128]{1,0:T(8,128)(2,1)S(1)} %pad_maximum_fusion.3), channel_id=1, source_target_pairs={{0,48},{1,17},{2,50},{3,19},{4,52},{5,21},{6,54},{7,23},{8,56},{9,... | collective-permute-start | bytes 307208 | tf_op jit(solution)/shard_map/ppermute | solution.py:346
  76.3 6.1 %collective-permute-start.15 = (bf16[4,136,128]{2,1,0:T(8,128)(2,1)S(1)}, bf16[4,136,128]{2,1,0:T(8,128)(2,1)S(1)}, u32[]{:S(2)}, u32[]{:S(2)}) collective-permute-start(bf16[4,136,128]{2,1,0:T(8,128)(2,1)S(1)} %get-tuple-element.56), channel_id=1, source_target_pairs={{0,2},{1,7},{2,0},{3,5},{4,6},{5,3},{6,4},{7,1},{8,10},{9,15},{10,... | collective-permute-start | bytes 417800 | tf_op jit(solution)/shard_map/ppermute | solution.py:346
  82.4 7.3 %collective-permute-start.16 = (bf16[2,4,136,128]{3,2,1,0:T(8,128)(2,1)S(1)}, bf16[2,4,136,128]{3,2,1,0:T(8,128)(2,1)S(1)}, u32[]{:S(2)}, u32[]{:S(2)}) collective-permute-start(bf16[2,4,136,128]{3,2,1,0:T(8,128)(2,1)S(1)} %pad_maximum_fusion.1.near_ref), channel_id=1, source_target_pairs={{0,6},{1,3},{2,4},{3,1},{4,2},{5,7},{6,0},{7,5},{8,14},{9,11},{10,... | collective-permute-start | bytes 835592 | tf_op jit(solution)/shard_map/ppermute | solution.py:346
  82.5 7.2 %collective-permute-start.17 = (bf16[2,64,128]{2,1,0:T(8,128)(2,1)S(1)}, bf16[2,64,128]{2,1,0:T(8,128)(2,1)S(1)}, u32[]{:S(2)}, u32[]{:S(2)}) collective-permute-start(bf16[2,64,128]{2,1,0:T(8,128)(2,1)S(1)} %get-tuple-element.49), channel_id=1, source_target_pairs={{0,240},{16,32},{32,16},{48,64},{64,48},{80,96},{96,80},{112,128},... | collective-permute-start | bytes 98312 | tf_op jit(solution)/shard_map/ppermute | solution.py:330
  89.7 13.4 %collective-permute-start.18 = (bf16[4,4,136,128]{3,2,1,0:T(8,128)(2,1)S(1)}, bf16[4,4,136,128]{3,2,1,0:T(8,128)(2,1)S(1)}, u32[]{:S(2)}, u32[]{:S(2)}) collective-permute-start(bf16[4,4,136,128]{3,2,1,0:T(8,128)(2,1)S(1)} %pad_maximum_fusion), channel_id=1, source_target_pairs={{0,1},{1,0},{2,3},{3,2},{4,5},{5,4},{6,7},{7,6},{8,9},{9,8},{10,11... | collective-permute-start | bytes 1671176 | tf_op jit(solution)/shard_map/ppermute | solution.py:321

commit v3 on v2

--- a/solution.py
+++ b/solution.py
@@ -19,6 +19,8 @@
 CHUNKS = 32
 SENT = CHUNKS // 2 * ROWS
 FACE, FACE_Y = SIZE_Y + BLOCKS_C // 2, SIZE_X + 2 + 2
+EDGE = 3
+FACE_ROWS = (0, SIZE_Y - 1, None, *range(1, SIZE_Y - 1))
 BF16, F32 = jnp.bfloat16, jnp.float32
 
 
@@ -62,6 +64,11 @@
     return lax.axis_index("gx"), lax.axis_index("gy")
 
 
+def half_of(place):
+    gx, gy = place
+    return (gy ^ (gy >> 1) ^ (gy >> 3) ^ (gx >> 2)) & 1
+
+
 def sides(place):
     odd = (place & 1).astype(F32)
     inner = jnp.where((place == 0) | (place == 15), 0.0, 1.0).astype(F32)
@@ -72,7 +79,7 @@
     return weights[0] * first.astype(F32) + weights[1] * second.astype(F32)
 
 
-def split_kernel(skip_hbm, cot_hbm, skip_out, cot_out, pool_out, two_out, one_out, skip_ref, cot_ref, rows_ref, arrived):
+def split_kernel(skip_hbm, cot_hbm, skip_out, cot_out, pool_out, edge_out, mid_out, one_out, skip_ref, cot_ref, rows_ref, arrived):
     odd = places()[0] & 1
     copies = [
         pltpu.make_async_copy(source, target, arrived.at[index])
@@ -88,9 +95,11 @@
     rows_ref[...] = cot_ref[...].astype(F32).reshape(SKIP * BLOCKS, LANES)
     for index in range(BLOCKS):
         cot_out[index] = block_of(index).astype(BF16)
-    for row in range(SIZE_Y):
-        one_out[row] = cot_out[(1 - odd) * SIZE_Y + row]
-        two_out[row] = cot_out[odd * SIZE_Y + row]
+    for at, row in enumerate(FACE_ROWS):
+        if row is not None:
+            one_out[at] = cot_out[(1 - odd) * SIZE_Y + row]
+            two, two_at = (edge_out, at) if at < EDGE else (mid_out, at - EDGE)
+            two[two_at] = cot_out[odd * SIZE_Y + row]
     copies[1].wait()
     rows_ref[...] = skip_ref[...].astype(F32).reshape(SKIP * BLOCKS, LANES)
     pools = []
@@ -102,10 +111,9 @@
             total = block if total is None else total + block
         pools.append(paired(total) * 0.125)
         pool_out[coarse] = pools[-1].astype(BF16)
-    for index in range(BLOCKS_C // 2):
-        packed = pack(pools[2 * index], pools[2 * index + 1]).astype(BF16)
-        one_out[SIZE_Y + index] = packed
-        two_out[SIZE_Y + index] = packed
+    outer, inner = (pack(pools[i], pools[j]).astype(BF16) for i, j in ((0, 3), (1, 2)))
+    one_out[EDGE - 1], edge_out[EDGE - 1] = outer, outer
+    one_out[FACE - 1], mid_out[FACE - EDGE - 1] = inner, inner
 
 
 def vmem():
@@ -125,38 +133,46 @@
     )(*operands)
 
 
-def faces_kernel(cot_ref, pool_ref, xtwo_ref, xone_ref, *refs):
+def weights_kernel(dec_hbm, coarse_hbm, join_out, pre_out, back_out, dec_ref, coarse_ref, arrived):
+    copies = [
+        pltpu.make_async_copy(source, target, arrived.at[index])
+        for index, (source, target) in enumerate(((dec_hbm, dec_ref), (coarse_hbm, coarse_ref)))
+    ]
+    for copy in copies:
+        copy.start()
+    copies[0].wait()
+    join_out[...] = dec_ref[...].T
+    copies[1].wait()
+    pre_out[...] = coarse_ref[...].T
+    for pair in range(9):
+        for k in range(3):
+            first = (3 * pair + k) * SKIP
+            back_out[pair * SKIP : (pair + 1) * SKIP, k * COARSE : (k + 1) * COARSE] = coarse_ref[first : first + SKIP]
+
+
+def faces_kernel(cot_ref, pool_ref, xedge_ref, xone_ref, *refs):
     one_out, two_out = refs[-2:]
     place = places()
     low, high = sides(place[0])
     odd = place[1] & 1
     for out, up in ((one_out, 1 - odd), (two_out, odd)):
         row = up * (SIZE_Y - 1)
-        out[0] = mixed(low, xone_ref[row], xtwo_ref[row]).astype(BF16)
+        out[0] = mixed(low, xone_ref[up], xedge_ref[up]).astype(BF16)
         out[1] = cot_ref[row]
         out[2] = cot_ref[SIZE_Y + row]
-        out[3] = mixed(high, xone_ref[row], xtwo_ref[row]).astype(BF16)
-        pair = SIZE_Y + up * (BLOCKS_C // 2 - 1)
+        out[3] = mixed(high, xone_ref[up], xedge_ref[up]).astype(BF16)
         upper = up.astype(F32)
 
         def pooled_of(weights):
-            first, second = unpack_pair(mixed(weights, xone_ref[pair], xtwo_ref[pair]))
+            first, second = unpack_pair(mixed(weights, xone_ref[EDGE - 1], xedge_ref[EDGE - 1]))
             return (1.0 - upper) * first + upper * second
 
         out[4] = pack(pooled_of(low), pool_ref[up * (BLOCKS_C - 1)].astype(F32)).astype(BF16)
         out[5] = pooled_of(high).astype(BF16)
 
 
-def row_of(place, core, yp, xp):
-    def ring(own, position):
-        return own ^ (0, 1 + 2 * core, 3 - 2 * core, 2)[position]
-
-    at = 16 * core + 4 * ring((place[1] >> 1) & 3, yp) + ring(place[0] & 3, xp)
-    return pl.multiple_of(at * ROWS, ROWS)
-
-
 def grads_kernel(
-    skip_ref, cot_ref, pool_ref, xtwo_ref, xone_ref, ytwo_ref, yone_ref, *refs,
+    skip_ref, cot_ref, pool_ref, xedge_ref, xmid_ref, xone_ref, ytwo_ref, yone_ref, *refs,
 ):
     wdec_ref, wpre_ref, wback_ref = refs[:3]
     send_out, keep_out, jskip_out, rim_out, two_out = refs[3:8]
@@ -166,15 +182,19 @@
     xlow, xhigh = sides(place[0])
     ylow, yhigh = sides(place[1])
 
+    def face(xside, at):
+        two = xedge_ref[at] if at < EDGE else xmid_ref[at - EDGE]
+        return mixed(xside, xone_ref[at], two)
+
     def fine(plane, row):
         if row == 0:
             return mixed(ylow, yone_ref[plane], ytwo_ref[plane])
         if row == SIZE_Y + 1:
             return mixed(yhigh, yone_ref[plane], ytwo_ref[plane])
         if plane == 0:
-            return mixed(xlow, xone_ref[row - 1], xtwo_ref[row - 1])
+            return face(xlow, FACE_ROWS.index(row - 1))
         if plane == SIZE_X + 1:
-            return mixed(xhigh, xone_ref[row - 1], xtwo_ref[row - 1])
+            return face(xhigh, FACE_ROWS.index(row - 1))
         return cot_ref[(plane - 1) * SIZE_Y + row - 1].astype(F32)
 
     wide_pool = {}
@@ -182,10 +202,8 @@
         wide_pool[0, row], wide_pool[1, row] = unpack_pair(mixed(weights, yone_ref[4], ytwo_ref[4]))
         wide_pool[2, row] = mixed(weights, yone_ref[5], ytwo_ref[5])
     for plane, weights in ((0, xlow), (2, xhigh)):
-        for index in range(BLOCKS_C // 2):
-            at = SIZE_Y + index
-            first, second = unpack_pair(mixed(weights, xone_ref[at], xtwo_ref[at]))
-            wide_pool[plane, 2 * index + 1], wide_pool[plane, 2 * index + 2] = first, second
+        wide_pool[plane, 1], wide_pool[plane, 4] = unpack_pair(face(weights, EDGE - 1))
+        wide_pool[plane, 2], wide_pool[plane, 3] = unpack_pair(face(weights, FACE - 1))
     for row in range(BLOCKS_C):
         wide_pool[1, row + 1] = pool_ref[row].astype(F32)
 
@@ -262,13 +280,16 @@
         pooled_ref[...], pre_grad, across, preferred_element_type=F32
     ) * (0.5 * factor)
     full_ref[PACKED:] = jnp.zeros((CHUNKS * ROWS - PACKED, LANES), F32)
-    core = place[1] & 1
-    for yp in range(4):
+    half, y, x = half_of(place), (place[1] >> 1) & 3, place[0] & 3
+    for yr in range(4):
         leave = []
-        for xp in range(4):
-            keep_out[yp, xp] = full_ref[pl.ds(row_of(place, core, yp, xp), ROWS), :]
-            leave.append(full_ref[pl.ds(row_of(place, 1 - core, yp, xp), ROWS), :])
-        send_out[4 * yp * ROWS : 4 * (yp + 1) * ROWS] = jnp.concatenate(leave).astype(BF16)
+        for xr in range(4):
+            at = (y ^ yr) * 4 + (x ^ xr)
+            row = pl.multiple_of((at + 16 * half) * ROWS, ROWS)
+            keep_out[yr, xr] = full_ref[pl.ds(row, ROWS), :]
+            row = pl.multiple_of((at + 16 * (1 - half)) * ROWS, ROWS)
+            leave.append(full_ref[pl.ds(row, ROWS), :])
+        send_out[4 * yr * ROWS : 4 * (yr + 1) * ROWS] = jnp.concatenate(leave).astype(BF16)
 
 
 def fold_kernel(rim_ref, yone_ref, ytwo_ref, rows_out, one_out, two_out):
@@ -288,37 +309,41 @@
         two_out[index] = ((1.0 - odd) * down + odd * up).astype(BF16)
 
 
-def skip_kernel(rows_ref, one0_ref, one1_ref, xtwo_ref, jskip_ref, out_ref, cells_ref):
-    place = places()
-    low, high = sides(place[0])
-    core = (place[1] & 1).astype(F32)
+def skip_kernel(rows_ref, xone_ref, xtwo_ref, jskip_ref, out_ref, cells_ref):
+    low, high = sides(places()[0])
+    weights = (low[0] + high[0], low[1] + high[1])
     for pair in range(BLOCKS_C // 2):
-        one = mixed((1.0 - core, core), one0_ref[pair], one1_ref[pair])
-        terms_of = unpack_pair(mixed((low[0] + high[0], low[1] + high[1]), one, xtwo_ref[pair]))
-        for at, terms in zip((2 * pair, 2 * pair + 1), terms_of):
+        for at, terms in zip((2 * pair, 2 * pair + 1), unpack_pair(mixed(weights, xone_ref[pair], xtwo_ref[pair]))):
             total = rows_ref[at] + terms
             for index in (2 * at, 2 * at + 1, SIZE_Y + 2 * at, SIZE_Y + 2 * at + 1):
                 cells_ref[pl.ds(index, SKIP, stride=BLOCKS), :] = jskip_ref[index] + total
     out_ref[...] = cells_ref[...].reshape(SKIP, SIZE_X, SIZE_Y, LANES).astype(BF16)
 
 
-def unpack_kernel(near_ref, far_ref, other_ref, dec_out, coarse_out, full_ref):
+def unpack_kernel(a0_ref, a1_ref, b0_ref, b1_ref, core_ref, dec_out, coarse_out, full_ref):
     place = places()
-    core = place[1] & 1
-    for yp in range(4):
-        for xp in range(4):
-            own = near_ref[yp, xp] if yp < 2 else far_ref[yp - 2, xp]
-            full_ref[pl.ds(row_of(place, core, yp, xp), ROWS), :] = own.astype(F32)
-            full_ref[pl.ds(row_of(place, 1 - core, yp, xp), ROWS), :] = other_ref[yp, xp].astype(F32)
-    half = LANES // 2
+    half, y, x = half_of(place), (place[1] >> 1) & 3, place[0] & 3
+    for side, (refs, order) in enumerate((((a0_ref, a1_ref), ORDER_A), ((b0_ref, b1_ref), ORDER_B))):
+        for index, yr in enumerate(order):
+            for xr in range(2):
+                at = (y ^ yr) * 4 + (x ^ (2 * side + xr))
+                row = pl.multiple_of((at + 16 * half) * ROWS, ROWS)
+                full_ref[pl.ds(row, ROWS), :] = refs[index // 2][index % 2, xr].astype(F32)
+                row = pl.multiple_of((at + 16 * (1 - half)) * ROWS, ROWS)
+                full_ref[pl.ds(row, ROWS), :] = core_ref[4 * side + index, xr].astype(F32)
+    middle = LANES // 2
     dec_out[:, :LANES] = full_ref[:DEC]
-    dec_out[: DEC // 2, LANES:] = full_ref[DEC : DEC + DEC // 2, :half]
-    dec_out[DEC // 2 :, LANES:] = full_ref[DEC : DEC + DEC // 2, half:]
+    dec_out[: DEC // 2, LANES:] = full_ref[DEC : DEC + DEC // 2, :middle]
+    dec_out[DEC // 2 :, LANES:] = full_ref[DEC : DEC + DEC // 2, middle:]
     coarse_out[...] = full_ref[DEC + DEC // 2 : PACKED]
 
 
 def swap(value, axis, flip):
     return lax.ppermute(value, axis, [(i, i ^ flip) for i in range(lax.axis_size(axis))])
+
+
+def in_hbm(*operands):
+    return [pltpu.with_memory_space_constraint(operand, pltpu.HBM) for operand in operands]
 
 
 def partner(index, which, count):
@@ -333,28 +358,20 @@
 together = lax.optimization_barrier
 
 
-FIRST, SECOND = (3, 1), (1, 3)
-
-
-def swap_round(value, flips):
+A_FIRST, A_SECOND = 1, 3
+B_FIRST, B_SECOND = 3, 1
+ORDER_A = (0, A_SECOND, A_FIRST, 2)
+ORDER_B = (0, B_SECOND, B_FIRST, 2)
+
+
+def swap_y(value, flip):
+    return swap(value, "gy", 2 * flip + 1)
+
+
+def swap_z(value, flip):
     size_x, size_y = lax.axis_size("gx"), lax.axis_size("gy")
-    pairs = [
-        (i * size_y + j, (i ^ flips[j % 2][0]) * size_y + (j ^ flips[j % 2][1]))
-        for i in range(size_x)
-        for j in range(size_y)
-    ]
+    pairs = [(i * size_y + j, (i ^ (4 * flip)) * size_y + (j ^ (flip & 1))) for i in range(size_x) for j in range(size_y)]
     return lax.ppermute(value, ("gx", "gy"), pairs)
-
-
-def along_y(value, flips):
-    return swap_round(value, [(0, 2 * flip) for flip in flips])
-
-
-def along_x(value, flips):
-    return swap_round(value, [(flip, 0) for flip in flips])
-
-
-Z_ROUNDS = [((4, 0), (0, 8)), ((12, 0), (4, 0)), ((0, 8), (12, 0))]
 
 
 def wide(value):
@@ -362,27 +379,33 @@
 
 
 def body(skip_feat, cotangent, w_coarse, w_dec):
-    w_join = w_dec.transpose(1, 0, 2).reshape(JOINED, DEC)
-    w_pre = w_coarse.transpose(2, 0, 1).reshape(COARSE, DEC)
-    w_back = w_coarse.reshape(9, 3, SKIP, COARSE).transpose(0, 2, 1, 3).reshape(9 * SKIP, 3 * COARSE)
+    w_join, w_pre, w_back = call(
+        weights_kernel, "lay_weights",
+        (((JOINED, DEC), BF16), ((COARSE, DEC), BF16), ((9 * SKIP, 3 * COARSE), BF16)),
+        (((DEC, JOINED), BF16), ((DEC, COARSE), BF16), pltpu.SemaphoreType.DMA((2,))), 16, (1_000_000, 2_500_000),
+        *in_hbm(w_dec.transpose(0, 2, 1).reshape(DEC, JOINED), w_coarse.reshape(DEC, COARSE)), held=(pltpu.HBM,) * 2,
+    )
 
     block = (SKIP, LANES)
     face, face_y, corner = (FACE,) + block, (FACE_Y,) + block, (2,) + block
     fine = (BLOCKS,) + block
-    skip, cot, pooled, xtwo, xone = call(
+    skip, cot, pooled, xedge, xmid, xone = call(
         split_kernel, "split_blocks",
-        ((fine, BF16), (fine, BF16), ((BLOCKS_C,) + block, BF16), (face, BF16), (face, BF16)),
+        (
+            (fine, BF16), (fine, BF16), ((BLOCKS_C,) + block, BF16),
+            ((EDGE,) + block, BF16), ((FACE - EDGE,) + block, BF16), (face, BF16),
+        ),
         (
             (skip_feat.shape, BF16), (skip_feat.shape, BF16), ((SKIP * BLOCKS, LANES), F32),
             pltpu.SemaphoreType.DMA((2,)),
         ),
-        8, (1_000_000, 1_500_000), *(pltpu.with_memory_space_constraint(x, pltpu.HBM) for x in (skip_feat, cotangent)),
+        8, (1_000_000, 1_500_000), *in_hbm(skip_feat, cotangent),
         held=(pltpu.HBM,) * 2,
     )
-    xtwo, xone = swap_side(xtwo, "gx", 1), swap_side(xone, "gx", 0)
+    xedge, xmid, xone = swap_side(xedge, "gx", 1), swap_side(xmid, "gx", 1), swap_side(xone, "gx", 0)
     yone, ytwo = call(
         faces_kernel, "row_faces", ((face_y, BF16), (face_y, BF16)), (), 8, (100_000, 400_000),
-        cot, pooled, xtwo, xone, w_join, w_pre, w_back, held=(pltpu.VMEM,) * 4 + (pl.ANY,) * 3,
+        cot, pooled, xedge, xone, w_join, w_pre, w_back, held=(pltpu.VMEM,) * 4 + (pl.ANY,) * 3,
     )
     yone, ytwo = swap_side(yone, "gy", 0), swap_side(ytwo, "gy", 1)
     chunks = (4, 4, ROWS, LANES)
@@ -400,43 +423,52 @@
             ((CHUNKS * ROWS, LANES), F32),
             ((3 * COARSE, BLOCKS_C * LANES), BF16),
         ),
-        36, (3_000_000_000, 8_000_000), skip, cot, pooled, xtwo, xone, ytwo, yone,
+        36, (3_000_000_000, 8_000_000), skip, cot, pooled, xedge, xmid, xone, ytwo, yone,
         w_join, w_pre, w_back,
     )
 
-    send, rtwo = swap(send, "gy", 1), swap_side(rtwo, "gy", 1)
+    send = swap(send, "gy", 1)
     part = keep + wide(send[:SENT].reshape(chunks))
-    part = part[:2] + wide(along_y(part[2:].astype(BF16), FIRST))
-    part = part[0] + wide(along_y(part[1].astype(BF16), SECOND))
-    part = part[:2] + wide(along_x(part[2:].astype(BF16), FIRST))
-    got, rone, rtwo = together((along_x(part[1].astype(BF16), SECOND), send[SENT:].reshape(corner), rtwo))
-    part = part[0] + wide(got)
-    part = part.astype(BF16)
-    for flips in Z_ROUNDS:
-        part = wide(part) + wide(swap_round(part, flips))
-    part = part.astype(BF16)
+    rone = send[SENT:].reshape(corner)
+    a, b = part[:, :2], part[:, 2:]
+    a_got = swap_y(jnp.stack([a[A_FIRST], a[2]]).astype(BF16), A_FIRST)
+    b_got = swap_y(jnp.stack([b[B_FIRST], b[2]]).astype(BF16), B_FIRST)
+    a_got, b_got = together((a_got, b_got))
+    a_own, a_leave = a[0] + wide(a_got[0]), a[A_SECOND] + wide(a_got[1])
+    b_own, b_leave = b[0] + wide(b_got[0]), b[B_SECOND] + wide(b_got[1])
+    a_got, b_got = swap_y(a_leave.astype(BF16), A_SECOND), swap_y(b_leave.astype(BF16), B_SECOND)
+    a_got, b_got = together((a_got, b_got))
+    part = jnp.concatenate([a_own + wide(a_got), b_own + wide(b_got)])
+    leave, rtwo = together((part.astype(BF16), rtwo))
+    got = [swap(leave[flip], "gx", flip) for flip in (1, 2, 3)]
+    *got, rone, rtwo = together((*got, rone, swap_side(rtwo, "gy", 1)))
     rows, qone, qtwo = call(
         fold_kernel, "fold_rim", (((BLOCKS_C,) + block, F32), (corner, BF16), (corner, BF16)), (), 8, (100_000, 600_000),
         own, rone, rtwo,
     )
-    part, rows, qone, qtwo = together((part, rows, qone, qtwo))
-    rim = qone.reshape(2 * SKIP, LANES)
-    got = along_x(jnp.concatenate([part, rim]), SECOND)
-    part = jnp.stack([part, got[:ROWS]])
-    qone1 = got[ROWS:].reshape(corner)
-    got = along_x(jnp.concatenate([part.reshape(2 * ROWS, LANES), rim]), FIRST)
-    part = jnp.concatenate([part, got[: 2 * ROWS].reshape(2, ROWS, LANES)])
-    qone2 = got[2 * ROWS :].reshape(corner)
-    near = jnp.stack([part, along_y(part, SECOND)])
-    far, qtwo = together((along_y(near, FIRST), swap_side(qtwo, "gx", 1)))
-    other = swap(jnp.concatenate([near, far]), "gy", 1)
+    part = (part[0] + wide(got[0])) + (wide(got[1]) + wide(got[2]))
+    mine = part.astype(BF16)
+    got = [swap_z(mine, flip) for flip in (1, 2, 3)]
+    *got, rows, qone, qtwo = together((*got, rows, qone, qtwo))
+    part = (wide(mine) + wide(got[0])) + (wide(got[1]) + wide(got[2]))
+    part = (part + swap(part, "gy", 9)).astype(BF16)
+    got = swap(jnp.concatenate([part, qone.reshape(2 * SKIP, LANES)]), "gx", 1)
+    qone = got[ROWS:].reshape(corner)
+    part = jnp.stack(together([part, got[:ROWS], swap(part, "gx", 2), swap(part, "gx", 3)]))
+    a, b = part[:2], part[2:]
+    a_got, b_got = together((swap_y(a, A_SECOND), swap_y(b, B_SECOND)))
+    a_near, b_near = jnp.stack([a, a_got]), jnp.stack([b, b_got])
+    a_near, b_near, qtwo = together((a_near, b_near, qtwo))
+    qtwo = swap_side(qtwo, "gx", 1)
+    a_far, b_far, qtwo = together((swap_y(a_near, A_FIRST), swap_y(b_near, B_FIRST), qtwo))
+    other = swap(jnp.concatenate([a_near, a_far, b_near, b_far]), "gy", 1)
     (skip_grad,) = call(
         skip_kernel, "skip_gradient", (((SKIP, SIZE_X, SIZE_Y, LANES), BF16),), (((SKIP * BLOCKS, LANES), F32),),
-        8, (1_000_000, 1_000_000), rows, qone1, qone2, qtwo, jskip,
+        8, (1_000_000, 1_000_000), rows, qone, qtwo, jskip,
     )
     dec, coarse = call(
         unpack_kernel, "unpack", (((DEC, JOINED), F32), ((DEC, COARSE), F32)), (((CHUNKS * ROWS, LANES), F32),),
-        16, (1_000_000, 5_000_000), near, far, other,
+        16, (1_000_000, 5_000_000), a_near, a_far, b_near, b_far, other,
     )
     return (
         skip_grad,

time: 105 us -> 97 us (0.924)
  starting transfers between devices: 56.1 us -> 46.3 us
  waiting for transfers between devices: 34 us -> 37.2 us
  local copies, waits for them, and re-layouts: 3.27 us -> 0.08 us
  Pallas kernels: 10.4 us -> 12 us
    ppermute x11 -> x3, waiting for transfers between devices: 26.3 us -> 4.12 us  [swap_z(): return lax.ppermute(value, ('gx', 'gy'), pairs)]
    ppermute x2 -> x17, waiting for transfers between devices: 2.25 us -> 22.5 us  [swap(): lax.ppermute(value, axis, [(i, i ^ flip) for i in range(lax.axis_size(axi...]
    ppermute x6 -> x7, starting transfers between devices: 26.2 us -> 18.1 us  [swap_side(): lax.ppermute(value, axis, [(i, partner(i, which, count)) for i in range(c...]
    ppermute x11 -> x3, starting transfers between devices: 16.2 us -> 8.28 us  [swap_z(): return lax.ppermute(value, ('gx', 'gy'), pairs)]
    ppermute x2 -> x17, starting transfers between devices: 13.7 us -> 20 us  [swap(): lax.ppermute(value, axis, [(i, i ^ flip) for i in range(lax.axis_size(axi...]
    ppermute x6 -> x7, waiting for transfers between devices: 5.44 us -> 10.6 us  [swap_side(): lax.ppermute(value, axis, [(i, partner(i, which, count)) for i in range(c...]
    reshape x3 -> x0, local copies, waits for them, and re-layouts: 3.06 us -> none  [the longest x1 1.46 us: body(): w_join = w_dec.transpose(1, 0, 2).reshape(JOINED, DEC)]
    pallas_call x6 -> x7, Pallas kernels: 10.4 us -> 12 us  [call(): pl.pallas_call(kernel, out_shape=tuple((jax.ShapeDtypeStruct(shape, dtype...]
  transfers between devices with their start and end apart: 19 -> 27, of which waited for: 17 -> 16; matrix products, arithmetic and copies ran while one was open for 3% -> 0% of each run, Pallas kernels for 1% -> 3%
where the time goes in v3:
time: 97 us; the launch traced here: 96.9 us
  starting transfers between devices  46.3 us (48%)
  waiting for transfers between devices  37.2 us (38%)
  Pallas kernels  12 us (12%)
    ppermute x17, waiting for transfers between devices, swap(): lax.ppermute(value, axis, [(i, i ^ flip) for i in range(lax.axis_size(axi...  22.5 us
    ppermute x17, starting transfers between devices, swap(): lax.ppermute(value, axis, [(i, i ^ flip) for i in range(lax.axis_size(axi...  20 us
    ppermute x7, starting transfers between devices, swap_side(): lax.ppermute(value, axis, [(i, partner(i, which, count)) for i in range(c...  18.1 us
    pallas_call x7, Pallas kernels, call(): pl.pallas_call(kernel, out_shape=tuple((jax.ShapeDtypeStruct(shape, dtype...  12 us
    ppermute x7, waiting for transfers between devices, swap_side(): lax.ppermute(value, axis, [(i, partner(i, which, count)) for i in range(c...  10.6 us
    ppermute x3, starting transfers between devices, swap_z(): return lax.ppermute(value, ('gx', 'gy'), pairs)  8.28 us
    ppermute x3, waiting for transfers between devices, swap_z(): return lax.ppermute(value, ('gx', 'gy'), pairs)  4.12 us
  transfers between devices with their start and end apart: 27, of which 16 were waited for; matrix products, arithmetic and copies ran while one was open for 0% of the time, Pallas kernels for 3%

profile of v3, /device:TPU:1, one launch (start us, length us, event | category | flops | bytes accessed | tf_op | source)
XLA Modules:
  0.0 96.9 jit_solution(1778228082115158351)
XLA Ops:
  2.1 2.1 %collective-permute-start.2 = (bf16[10,64,128]{2,1,0:T(8,128)(2,1)S(1)}, bf16[10,64,128]{2,1,0:T(8,128)(2,1)S(1)}, u32[]{:S(2)}, u32[]{:S(2)}) collective-permute-start(bf16[10,64,128]{2,1,0:T(8,128)(2,1)S(1)} %get-tuple-element.58), channel_id=1, source_target_pairs={{0,16},{16,0},{32,48},{48,32},{64,80},{80,64},{96,112},{112,96},{1... | collective-permute-start | bytes 491528 | tf_op jit(solution)/shard_map/ppermute | solution.py:355
  4.2 7.6 %collective-permute-start = (bf16[3,64,128]{2,1,0:T(8,128)(2,1)S(1)}, bf16[3,64,128]{2,1,0:T(8,128)(2,1)S(1)}, u32[]{:S(2)}, u32[]{:S(2)}) collective-permute-start(bf16[3,64,128]{2,1,0:T(8,128)(2,1)S(1)} %get-tuple-element.56), channel_id=1, source_target_pairs={{0,240},{16,32},{32,16},{48,64},{64,48},{80,96},{96,80},{112,128},... | collective-permute-start | bytes 147464 | tf_op jit(solution)/shard_map/ppermute | solution.py:355
  11.8 1.7 %lay_weights.1 = (bf16[192,1728]{1,0:T(8,128)(2,1)S(1)}, bf16[128,1728]{1,0:T(8,128)(2,1)S(1)}, bf16[576,384]{1,0:T(8,128)(2,1)S(1)}) custom-call(bf16[1728,192]{1,0:T(8,128)(2,1)} %bitcast.56, bf16[1728,128]{1,0:T(8,128)(2,1)} %bitcast.57), custom_call_target="tpu_custom_call" | custom-call | flops 1000000 | bytes 2500000 | tf_op jit(solution)/shard_map/lay_weights/pallas_call | solution.py:124
  13.7 5.0 %collective-permute-start.3 = (bf16[6,64,128]{2,1,0:T(8,128)(2,1)S(1)}, bf16[6,64,128]{2,1,0:T(8,128)(2,1)S(1)}, u32[]{:S(2)}, u32[]{:S(2)}) collective-permute-start(bf16[6,64,128]{2,1,0:T(8,128)(2,1)S(1)} %get-tuple-element.62), channel_id=1, source_target_pairs={{0,15},{1,2},{2,1},{3,4},{4,3},{5,6},{6,5},{7,8},{8,7},{9,10},{10,... | collective-permute-start | bytes 294920 | tf_op jit(solution)/shard_map/ppermute | solution.py:355
  21.3 5.8 %local_grads.1 = (bf16[2304,128]{1,0:T(8,128)(2,1)S(1)}, f32[4,4,136,128]{3,2,1,0:T(8,128)S(1)}, f32[16,64,128]{2,1,0:T(8,128)S(1)}, f32[12,64,128]{2,1,0:T(8,128)S(1)}, bf16[2,64,128]{2,1,0:T(8,128)(2,1)S(1)}) custom-call(bf16[16,64,128]{2,1,0:T(8,128)(2,1)S(1)} %get-tuple-element.53.skip_ref, bf16[16,64,128]{2,1,0:T(8,128)(2,1)S(1)} %get-tuple-element.54.cot_ref, ...), custom_call_target="tpu_custom_call" | custom-call | flops 3000000000 | bytes 8000000 | tf_op jit(solution)/shard_map/local_grads/pallas_call | solution.py:124
  27.1 2.5 %collective-permute-start.5 = (bf16[2304,128]{1,0:T(8,128)(2,1)S(1)}, bf16[2304,128]{1,0:T(8,128)(2,1)S(1)}, u32[]{:S(2)}, u32[]{:S(2)}) collective-permute-start(bf16[2304,128]{1,0:T(8,128)(2,1)S(1)} %get-tuple-element.65), channel_id=1, source_target_pairs={{0,1},{1,0},{2,3},{3,2},{4,5},{5,4},{6,7},{7,6},{8,9},{9,8},{10,11... | collective-permute-start | bytes 1769480 | tf_op jit(solution)/shard_map/ppermute | solution.py:342
  29.6 1.6 %collective-permute-done.5 = bf16[2304,128]{1,0:T(8,128)(2,1)S(1)} collective-permute-done((bf16[2304,128]{1,0:T(8,128)(2,1)S(1)}, bf16[2304,128]{1,0:T(8,128)(2,1)S(1)}, u32[]{:S(2)}, u32[]{:S(2)}) %collective-permute-start.5) | collective-permute-done | bytes 589856 | tf_op jit(solution)/shard_map/ppermute | solution.py:342
  31.5 3.1 %collective-permute-start.7 = (bf16[2,2,136,128]{3,2,1,0:T(8,128)(2,1)S(1)}, bf16[2,2,136,128]{3,2,1,0:T(8,128)(2,1)S(1)}, u32[]{:S(2)}, u32[]{:S(2)}) collective-permute-start(bf16[2,2,136,128]{3,2,1,0:T(8,128)(2,1)S(1)} %pad_maximum_fusion.1), channel_id=1, source_target_pairs={{0,7},{1,6},{2,5},{3,4},{4,3},{5,2},{6,1},{7,0},{8,15},{9,14},{10,... | collective-permute-start | bytes 417800 | tf_op jit(solution)/shard_map/ppermute | solution.py:342
  34.6 3.9 %collective-permute-done.7 = bf16[2,2,136,128]{3,2,1,0:T(8,128)(2,1)S(1)} collective-permute-done((bf16[2,2,136,128]{3,2,1,0:T(8,128)(2,1)S(1)}, bf16[2,2,136,128]{3,2,1,0:T(8,128)(2,1)S(1)}, u32[]{:S(2)}, u32[]{:S(2)}) %collective-permute-start.7) | collective-permute-done | bytes 139296 | tf_op jit(solution)/shard_map/ppermute | solution.py:342
  38.5 1.5 %collective-permute-done.6 = bf16[2,2,136,128]{3,2,1,0:T(8,128)(2,1)S(1)} collective-permute-done((bf16[2,2,136,128]{3,2,1,0:T(8,128)(2,1)S(1)}, bf16[2,2,136,128]{3,2,1,0:T(8,128)(2,1)S(1)}, u32[]{:S(2)}, u32[]{:S(2)}) %collective-permute-start.6) | collective-permute-done | bytes 139296 | tf_op jit(solution)/shard_map/ppermute | solution.py:342
  41.9 2.6 %collective-permute-done.9 = bf16[2,136,128]{2,1,0:T(8,128)(2,1)S(1)} collective-permute-done((bf16[2,136,128]{2,1,0:T(8,128)(2,1)S(1)}, bf16[2,136,128]{2,1,0:T(8,128)(2,1)S(1)}, u32[]{:S(2)}, u32[]{:S(2)}) %collective-permute-start.9) | collective-permute-done | bytes 69664 | tf_op jit(solution)/shard_map/ppermute | solution.py:342
  46.0 3.1 %collective-permute-start.10 = (bf16[136,128]{1,0:T(8,128)(2,1)S(1)}, bf16[136,128]{1,0:T(8,128)(2,1)S(1)}, u32[]{:S(2)}, u32[]{:S(2)}) collective-permute-start(bf16[136,128]{1,0:T(8,128)(2,1)S(1)} %get-tuple-element.114), channel_id=1, source_target_pairs={{0,16},{16,0},{32,48},{48,32},{64,80},{80,64},{96,112},{112,96},{1... | collective-permute-start | bytes 104456 | tf_op jit(solution)/shard_map/ppermute | solution.py:342
  50.4 2.1 %collective-permute-done.13.ytwo_ref = bf16[2,64,128]{2,1,0:T(8,128)(2,1)S(1)} collective-permute-done((bf16[2,64,128]{2,1,0:T(8,128)(2,1)S(1)}, bf16[2,64,128]{2,1,0:T(8,128)(2,1)S(1)}, u32[]{:S(2)}, u32[]{:S(2)}) %collective-permute-start.13) | collective-permute-done | bytes 32800 | tf_op jit(solution)/shard_map/ppermute | solution.py:355
  52.5 5.8 %collective-permute-start.16 = (bf16[136,128]{1,0:T(8,128)(2,1)S(1)}, bf16[136,128]{1,0:T(8,128)(2,1)S(1)}, u32[]{:S(2)}, u32[]{:S(2)}) collective-permute-start(bf16[136,128]{1,0:T(8,128)(2,1)S(1)} %fusion.11), channel_id=1, source_target_pairs={{0,193},{1,192},{2,195},{3,194},{4,197},{5,196},{6,199},{7,198},{8... | collective-permute-start | bytes 104456 | tf_op jit(solution)/shard_map/ppermute | solution.py:374
  58.4 2.3 %collective-permute-start.14 = (bf16[136,128]{1,0:T(8,128)(2,1)S(1)}, bf16[136,128]{1,0:T(8,128)(2,1)S(1)}, u32[]{:S(2)}, u32[]{:S(2)}) collective-permute-start(bf16[136,128]{1,0:T(8,128)(2,1)S(1)} %fusion.11), channel_id=1, source_target_pairs={{0,65},{1,64},{2,67},{3,66},{4,69},{5,68},{6,71},{7,70},{8,73},{9,... | collective-permute-start | bytes 104456 | tf_op jit(solution)/shard_map/ppermute | solution.py:374
  60.9 4.1 %collective-permute-done.15 = bf16[136,128]{1,0:T(8,128)(2,1)S(1)} collective-permute-done((bf16[136,128]{1,0:T(8,128)(2,1)S(1)}, bf16[136,128]{1,0:T(8,128)(2,1)S(1)}, u32[]{:S(2)}, u32[]{:S(2)}) %collective-permute-start.15) | collective-permute-done | bytes 34848 | tf_op jit(solution)/shard_map/ppermute | solution.py:374
  65.2 4.1 %collective-permute-done.17 = f32[136,128]{1,0:T(8,128)S(1)} collective-permute-done((f32[136,128]{1,0:T(8,128)S(1)}, f32[136,128]{1,0:T(8,128)S(1)}, u32[]{:S(2)}, u32[]{:S(2)}) %collective-permute-start.17) | collective-permute-done | bytes 69664 | tf_op jit(solution)/shard_map/ppermute | solution.py:342
  73.0 2.0 %collective-permute-done.20 = bf16[136,128]{1,0:T(8,128)(2,1)S(1)} collective-permute-done((bf16[136,128]{1,0:T(8,128)(2,1)S(1)}, bf16[136,128]{1,0:T(8,128)(2,1)S(1)}, u32[]{:S(2)}, u32[]{:S(2)}) %collective-permute-start.20) | collective-permute-done | bytes 34848 | tf_op jit(solution)/shard_map/ppermute | solution.py:342
  76.2 3.4 %collective-permute-start.21 = (bf16[2,136,128]{2,1,0:T(8,128)(2,1)S(1)}, bf16[2,136,128]{2,1,0:T(8,128)(2,1)S(1)}, u32[]{:S(2)}, u32[]{:S(2)}) collective-permute-start(bf16[2,136,128]{2,1,0:T(8,128)(2,1)S(1)} %get-tuple-element.118), channel_id=1, source_target_pairs={{0,7},{1,6},{2,5},{3,4},{4,3},{5,2},{6,1},{7,0},{8,15},{9,14},{10,... | collective-permute-start | bytes 208904 | tf_op jit(solution)/shard_map/ppermute | solution.py:342
  79.7 1.9 %collective-permute-done.21 = bf16[2,136,128]{2,1,0:T(8,128)(2,1)S(1)} collective-permute-done((bf16[2,136,128]{2,1,0:T(8,128)(2,1)S(1)}, bf16[2,136,128]{2,1,0:T(8,128)(2,1)S(1)}, u32[]{:S(2)}, u32[]{:S(2)}) %collective-permute-start.21) | collective-permute-done | bytes 69664 | tf_op jit(solution)/shard_map/ppermute | solution.py:342
  81.6 1.8 %collective-permute-done.22 = bf16[2,136,128]{2,1,0:T(8,128)(2,1)S(1)} collective-permute-done((bf16[2,136,128]{2,1,0:T(8,128)(2,1)S(1)}, bf16[2,136,128]{2,1,0:T(8,128)(2,1)S(1)}, u32[]{:S(2)}, u32[]{:S(2)}) %collective-permute-start.22) | collective-permute-done | bytes 69664 | tf_op jit(solution)/shard_map/ppermute | solution.py:342
  84.8 2.1 %collective-permute-start.25 = (bf16[2,64,128]{2,1,0:T(8,128)(2,1)S(1)}, bf16[2,64,128]{2,1,0:T(8,128)(2,1)S(1)}, u32[]{:S(2)}, u32[]{:S(2)}) collective-permute-start(bf16[2,64,128]{2,1,0:T(8,128)(2,1)S(1)} %get-tuple-element.96), channel_id=1, source_target_pairs={{0,240},{16,32},{32,16},{48,64},{64,48},{80,96},{96,80},{112,128},... | collective-permute-start | bytes 98312 | tf_op jit(solution)/shard_map/ppermute | solution.py:355
  86.8 5.9 %collective-permute-done.25.xtwo_ref = bf16[2,64,128]{2,1,0:T(8,128)(2,1)S(1)} collective-permute-done((bf16[2,64,128]{2,1,0:T(8,128)(2,1)S(1)}, bf16[2,64,128]{2,1,0:T(8,128)(2,1)S(1)}, u32[]{:S(2)}, u32[]{:S(2)}) %collective-permute-start.25) | collective-permute-done | bytes 32800 | tf_op jit(solution)/shard_map/ppermute | solution.py:355
  95.0 1.9 %unpack.1 = (f32[1728,192]{1,0:T(8,128)}, f32[1728,128]{1,0:T(8,128)}) custom-call(bf16[2,2,136,128]{3,2,1,0:T(8,128)(2,1)S(1)} %get-tuple-element.94.a0_ref, bf16[2,2,136,128]{3,2,1,0:T(8,128)(2,1)S(1)} %collective-permute-done.23.a1_ref, bf16[2,2,136,128]{3,2,1,0:T(8,128)(2,1)S(1)} %get-tuple-element.95.b0_ref, ...), custom_call_target="tpu_custom_call" | custom-call | flops 1000000 | bytes 5000000 | tf_op jit(solution)/shard_map/unpack/pallas_call | solution.py:124
  (57 shorter events, 18.1 us)
Async XLA Ops:
  2.1 11.4 %collective-permute-start.2 = (bf16[10,64,128]{2,1,0:T(8,128)(2,1)S(1)}, bf16[10,64,128]{2,1,0:T(8,128)(2,1)S(1)}, u32[]{:S(2)}, u32[]{:S(2)}) collective-permute-start(bf16[10,64,128]{2,1,0:T(8,128)(2,1)S(1)} %get-tuple-element.58), channel_id=1, source_target_pairs={{0,16},{16,0},{32,48},{48,32},{64,80},{80,64},{96,112},{112,96},{1... | collective-permute-start | bytes 491528 | tf_op jit(solution)/shard_map/ppermute | solution.py:355
  4.2 9.3 %collective-permute-start = (bf16[3,64,128]{2,1,0:T(8,128)(2,1)S(1)}, bf16[3,64,128]{2,1,0:T(8,128)(2,1)S(1)}, u32[]{:S(2)}, u32[]{:S(2)}) collective-permute-start(bf16[3,64,128]{2,1,0:T(8,128)(2,1)S(1)} %get-tuple-element.56), channel_id=1, source_target_pairs={{0,240},{16,32},{32,16},{48,64},{64,48},{80,96},{96,80},{112,128},... | collective-permute-start | bytes 147464 | tf_op jit(solution)/shard_map/ppermute | solution.py:355
  11.8 8.3 %collective-permute-start.1 = (bf16[7,64,128]{2,1,0:T(8,128)(2,1)S(1)}, bf16[7,64,128]{2,1,0:T(8,128)(2,1)S(1)}, u32[]{:S(2)}, u32[]{:S(2)}) collective-permute-start(bf16[7,64,128]{2,1,0:T(8,128)(2,1)S(1)} %get-tuple-element.57), channel_id=1, source_target_pairs={{0,240},{16,32},{32,16},{48,64},{64,48},{80,96},{96,80},{112,128},... | collective-permute-start | bytes 344072 | tf_op jit(solution)/shard_map/ppermute | solution.py:355
  13.7 7.6 %collective-permute-start.3 = (bf16[6,64,128]{2,1,0:T(8,128)(2,1)S(1)}, bf16[6,64,128]{2,1,0:T(8,128)(2,1)S(1)}, u32[]{:S(2)}, u32[]{:S(2)}) collective-permute-start(bf16[6,64,128]{2,1,0:T(8,128)(2,1)S(1)} %get-tuple-element.62), channel_id=1, source_target_pairs={{0,15},{1,2},{2,1},{3,4},{4,3},{5,6},{6,5},{7,8},{8,7},{9,10},{10,... | collective-permute-start | bytes 294920 | tf_op jit(solution)/shard_map/ppermute | solution.py:355
  27.1 4.2 %collective-permute-start.5 = (bf16[2304,128]{1,0:T(8,128)(2,1)S(1)}, bf16[2304,128]{1,0:T(8,128)(2,1)S(1)}, u32[]{:S(2)}, u32[]{:S(2)}) collective-permute-start(bf16[2304,128]{1,0:T(8,128)(2,1)S(1)} %get-tuple-element.65), channel_id=1, source_target_pairs={{0,1},{1,0},{2,3},{3,2},{4,5},{5,4},{6,7},{7,6},{8,9},{9,8},{10,11... | collective-permute-start | bytes 1769480 | tf_op jit(solution)/shard_map/ppermute | solution.py:342
  31.5 7.0 %collective-permute-start.7 = (bf16[2,2,136,128]{3,2,1,0:T(8,128)(2,1)S(1)}, bf16[2,2,136,128]{3,2,1,0:T(8,128)(2,1)S(1)}, u32[]{:S(2)}, u32[]{:S(2)}) collective-permute-start(bf16[2,2,136,128]{3,2,1,0:T(8,128)(2,1)S(1)} %pad_maximum_fusion.1), channel_id=1, source_target_pairs={{0,7},{1,6},{2,5},{3,4},{4,3},{5,2},{6,1},{7,0},{8,15},{9,14},{10,... | collective-permute-start | bytes 417800 | tf_op jit(solution)/shard_map/ppermute | solution.py:342
  34.6 5.4 %collective-permute-start.6 = (bf16[2,2,136,128]{3,2,1,0:T(8,128)(2,1)S(1)}, bf16[2,2,136,128]{3,2,1,0:T(8,128)(2,1)S(1)}, u32[]{:S(2)}, u32[]{:S(2)}) collective-permute-start(bf16[2,2,136,128]{3,2,1,0:T(8,128)(2,1)S(1)} %stack.56), channel_id=1, source_target_pairs={{0,3},{1,2},{2,1},{3,0},{4,7},{5,6},{6,5},{7,4},{8,11},{9,10},{10,... | collective-permute-start | bytes 417800 | tf_op jit(solution)/shard_map/ppermute | solution.py:342
  40.1 4.4 %collective-permute-start.9 = (bf16[2,136,128]{2,1,0:T(8,128)(2,1)S(1)}, bf16[2,136,128]{2,1,0:T(8,128)(2,1)S(1)}, u32[]{:S(2)}, u32[]{:S(2)}) collective-permute-start(bf16[2,136,128]{2,1,0:T(8,128)(2,1)S(1)} %get-tuple-element.108), channel_id=1, source_target_pairs={{0,3},{1,2},{2,1},{3,0},{4,7},{5,6},{6,5},{7,4},{8,11},{9,10},{10,... | collective-permute-start | bytes 208904 | tf_op jit(solution)/shard_map/ppermute | solution.py:342
  40.4 5.3 %collective-permute-start.8 = (bf16[2,136,128]{2,1,0:T(8,128)(2,1)S(1)}, bf16[2,136,128]{2,1,0:T(8,128)(2,1)S(1)}, u32[]{:S(2)}, u32[]{:S(2)}) collective-permute-start(bf16[2,136,128]{2,1,0:T(8,128)(2,1)S(1)} %get-tuple-element.109), channel_id=1, source_target_pairs={{0,7},{1,6},{2,5},{3,4},{4,3},{5,2},{6,1},{7,0},{8,15},{9,14},{10,... | collective-permute-start | bytes 208904 | tf_op jit(solution)/shard_map/ppermute | solution.py:342
  45.8 6.7 %collective-permute-start.12 = (bf16[136,128]{1,0:T(8,128)(2,1)S(1)}, bf16[136,128]{1,0:T(8,128)(2,1)S(1)}, u32[]{:S(2)}, u32[]{:S(2)}) collective-permute-start(bf16[136,128]{1,0:T(8,128)(2,1)S(1)} %get-tuple-element.112), channel_id=1, source_target_pairs={{0,48},{16,32},{32,16},{48,0},{64,112},{80,96},{96,80},{112,64},{1... | collective-permute-start | bytes 104456 | tf_op jit(solution)/shard_map/ppermute | solution.py:342
  45.9 6.6 %collective-permute-start.11 = (bf16[136,128]{1,0:T(8,128)(2,1)S(1)}, bf16[136,128]{1,0:T(8,128)(2,1)S(1)}, u32[]{:S(2)}, u32[]{:S(2)}) collective-permute-start(bf16[136,128]{1,0:T(8,128)(2,1)S(1)} %get-tuple-element.113), channel_id=1, source_target_pairs={{0,32},{16,48},{32,0},{48,16},{64,96},{80,112},{96,64},{112,80},{1... | collective-permute-start | bytes 104456 | tf_op jit(solution)/shard_map/ppermute | solution.py:342
  46.0 6.5 %collective-permute-start.10 = (bf16[136,128]{1,0:T(8,128)(2,1)S(1)}, bf16[136,128]{1,0:T(8,128)(2,1)S(1)}, u32[]{:S(2)}, u32[]{:S(2)}) collective-permute-start(bf16[136,128]{1,0:T(8,128)(2,1)S(1)} %get-tuple-element.114), channel_id=1, source_target_pairs={{0,16},{16,0},{32,48},{48,32},{64,80},{80,64},{96,112},{112,96},{1... | collective-permute-start | bytes 104456 | tf_op jit(solution)/shard_map/ppermute | solution.py:342
  52.5 8.4 %collective-permute-start.16 = (bf16[136,128]{1,0:T(8,128)(2,1)S(1)}, bf16[136,128]{1,0:T(8,128)(2,1)S(1)}, u32[]{:S(2)}, u32[]{:S(2)}) collective-permute-start(bf16[136,128]{1,0:T(8,128)(2,1)S(1)} %fusion.11), channel_id=1, source_target_pairs={{0,193},{1,192},{2,195},{3,194},{4,197},{5,196},{6,199},{7,198},{8... | collective-permute-start | bytes 104456 | tf_op jit(solution)/shard_map/ppermute | solution.py:374
  58.3 6.7 %collective-permute-start.15 = (bf16[136,128]{1,0:T(8,128)(2,1)S(1)}, bf16[136,128]{1,0:T(8,128)(2,1)S(1)}, u32[]{:S(2)}, u32[]{:S(2)}) collective-permute-start(bf16[136,128]{1,0:T(8,128)(2,1)S(1)} %fusion.11), channel_id=1, source_target_pairs={{0,128},{1,129},{2,130},{3,131},{4,132},{5,133},{6,134},{7,135},{8... | collective-permute-start | bytes 104456 | tf_op jit(solution)/shard_map/ppermute | solution.py:374
  58.4 6.6 %collective-permute-start.14 = (bf16[136,128]{1,0:T(8,128)(2,1)S(1)}, bf16[136,128]{1,0:T(8,128)(2,1)S(1)}, u32[]{:S(2)}, u32[]{:S(2)}) collective-permute-start(bf16[136,128]{1,0:T(8,128)(2,1)S(1)} %fusion.11), channel_id=1, source_target_pairs={{0,65},{1,64},{2,67},{3,66},{4,69},{5,68},{6,71},{7,70},{8,73},{9,... | collective-permute-start | bytes 104456 | tf_op jit(solution)/shard_map/ppermute | solution.py:374
  65.0 4.3 %collective-permute-start.17 = (f32[136,128]{1,0:T(8,128)S(1)}, f32[136,128]{1,0:T(8,128)S(1)}, u32[]{:S(2)}, u32[]{:S(2)}) collective-permute-start(f32[136,128]{1,0:T(8,128)S(1)} %add_add_fusion), channel_id=1, source_target_pairs={{0,9},{1,8},{2,11},{3,10},{4,13},{5,12},{6,15},{7,14},{8,1},{9,0},... | collective-permute-start | bytes 208904 | tf_op jit(solution)/shard_map/ppermute | solution.py:342
  69.3 3.7 %collective-permute-start.18 = (bf16[264,128]{1,0:T(8,128)(2,1)S(1)}, bf16[264,128]{1,0:T(8,128)(2,1)S(1)}, u32[]{:S(2)}, u32[]{:S(2)}) collective-permute-start(bf16[264,128]{1,0:T(8,128)(2,1)S(1)} %pad_maximum_fusion.7), channel_id=1, source_target_pairs={{0,16},{16,0},{32,48},{48,32},{64,80},{80,64},{96,112},{112,96},{1... | collective-permute-start | bytes 202760 | tf_op jit(solution)/shard_map/ppermute | solution.py:342
  70.4 4.6 %collective-permute-start.20 = (bf16[136,128]{1,0:T(8,128)(2,1)S(1)}, bf16[136,128]{1,0:T(8,128)(2,1)S(1)}, u32[]{:S(2)}, u32[]{:S(2)}) collective-permute-start(bf16[136,128]{1,0:T(8,128)(2,1)S(1)} %add_convert_fusion), channel_id=1, source_target_pairs={{0,48},{16,32},{32,16},{48,0},{64,112},{80,96},{96,80},{112,64},{1... | collective-permute-start | bytes 104456 | tf_op jit(solution)/shard_map/ppermute | solution.py:342
  71.9 4.3 %collective-permute-start.19 = (bf16[136,128]{1,0:T(8,128)(2,1)S(1)}, bf16[136,128]{1,0:T(8,128)(2,1)S(1)}, u32[]{:S(2)}, u32[]{:S(2)}) collective-permute-start(bf16[136,128]{1,0:T(8,128)(2,1)S(1)} %add_convert_fusion), channel_id=1, source_target_pairs={{0,32},{16,48},{32,0},{48,16},{64,96},{80,112},{96,64},{112,80},{1... | collective-permute-start | bytes 104456 | tf_op jit(solution)/shard_map/ppermute | solution.py:342
  76.2 5.4 %collective-permute-start.21 = (bf16[2,136,128]{2,1,0:T(8,128)(2,1)S(1)}, bf16[2,136,128]{2,1,0:T(8,128)(2,1)S(1)}, u32[]{:S(2)}, u32[]{:S(2)}) collective-permute-start(bf16[2,136,128]{2,1,0:T(8,128)(2,1)S(1)} %get-tuple-element.118), channel_id=1, source_target_pairs={{0,7},{1,6},{2,5},{3,4},{4,3},{5,2},{6,1},{7,0},{8,15},{9,14},{10,... | collective-permute-start | bytes 208904 | tf_op jit(solution)/shard_map/ppermute | solution.py:342
  79.6 3.8 %collective-permute-start.22 = (bf16[2,136,128]{2,1,0:T(8,128)(2,1)S(1)}, bf16[2,136,128]{2,1,0:T(8,128)(2,1)S(1)}, u32[]{:S(2)}, u32[]{:S(2)}) collective-permute-start(bf16[2,136,128]{2,1,0:T(8,128)(2,1)S(1)} %get-tuple-element.116), channel_id=1, source_target_pairs={{0,3},{1,2},{2,1},{3,0},{4,7},{5,6},{6,5},{7,4},{8,11},{9,10},{10,... | collective-permute-start | bytes 208904 | tf_op jit(solution)/shard_map/ppermute | solution.py:342
  83.5 9.3 %collective-permute-start.23 = (bf16[2,2,136,128]{3,2,1,0:T(8,128)(2,1)S(1)}, bf16[2,2,136,128]{3,2,1,0:T(8,128)(2,1)S(1)}, u32[]{:S(2)}, u32[]{:S(2)}) collective-permute-start(bf16[2,2,136,128]{3,2,1,0:T(8,128)(2,1)S(1)} %get-tuple-element.94.a0_ref), channel_id=1, source_target_pairs={{0,3},{1,2},{2,1},{3,0},{4,7},{5,6},{6,5},{7,4},{8,11},{9,10},{10,... | collective-permute-start | bytes 417800 | tf_op jit(solution)/shard_map/ppermute | solution.py:342
  84.1 8.7 %collective-permute-start.24 = (bf16[2,2,136,128]{3,2,1,0:T(8,128)(2,1)S(1)}, bf16[2,2,136,128]{3,2,1,0:T(8,128)(2,1)S(1)}, u32[]{:S(2)}, u32[]{:S(2)}) collective-permute-start(bf16[2,2,136,128]{3,2,1,0:T(8,128)(2,1)S(1)} %get-tuple-element.95.b0_ref), channel_id=1, source_target_pairs={{0,7},{1,6},{2,5},{3,4},{4,3},{5,2},{6,1},{7,0},{8,15},{9,14},{10,... | collective-permute-start | bytes 417800 | tf_op jit(solution)/shard_map/ppermute | solution.py:342
  84.8 8.0 %collective-permute-start.25 = (bf16[2,64,128]{2,1,0:T(8,128)(2,1)S(1)}, bf16[2,64,128]{2,1,0:T(8,128)(2,1)S(1)}, u32[]{:S(2)}, u32[]{:S(2)}) collective-permute-start(bf16[2,64,128]{2,1,0:T(8,128)(2,1)S(1)} %get-tuple-element.96), channel_id=1, source_target_pairs={{0,240},{16,32},{32,16},{48,64},{64,48},{80,96},{96,80},{112,128},... | collective-permute-start | bytes 98312 | tf_op jit(solution)/shard_map/ppermute | solution.py:355
  (3 other events, 8.1 us)

commit v4 on v3

--- a/solution.py
+++ b/solution.py
@@ -79,7 +79,7 @@
     return weights[0] * first.astype(F32) + weights[1] * second.astype(F32)
 
 
-def split_kernel(skip_hbm, cot_hbm, skip_out, cot_out, pool_out, edge_out, mid_out, one_out, skip_ref, cot_ref, rows_ref, arrived):
+def split_kernel(skip_hbm, cot_hbm, skip_out, cot_out, pool_out, edge_out, mid_out, near_edge_out, near_mid_out, skip_ref, cot_ref, rows_ref, arrived):
     odd = places()[0] & 1
     copies = [
         pltpu.make_async_copy(source, target, arrived.at[index])
@@ -97,9 +97,9 @@
         cot_out[index] = block_of(index).astype(BF16)
     for at, row in enumerate(FACE_ROWS):
         if row is not None:
-            one_out[at] = cot_out[(1 - odd) * SIZE_Y + row]
-            two, two_at = (edge_out, at) if at < EDGE else (mid_out, at - EDGE)
-            two[two_at] = cot_out[odd * SIZE_Y + row]
+            one, two, piece = (near_edge_out, edge_out, at) if at < EDGE else (near_mid_out, mid_out, at - EDGE)
+            one[piece] = cot_out[(1 - odd) * SIZE_Y + row]
+            two[piece] = cot_out[odd * SIZE_Y + row]
     copies[1].wait()
     rows_ref[...] = skip_ref[...].astype(F32).reshape(SKIP * BLOCKS, LANES)
     pools = []
@@ -112,8 +112,8 @@
         pools.append(paired(total) * 0.125)
         pool_out[coarse] = pools[-1].astype(BF16)
     outer, inner = (pack(pools[i], pools[j]).astype(BF16) for i, j in ((0, 3), (1, 2)))
-    one_out[EDGE - 1], edge_out[EDGE - 1] = outer, outer
-    one_out[FACE - 1], mid_out[FACE - EDGE - 1] = inner, inner
+    near_edge_out[EDGE - 1], edge_out[EDGE - 1] = outer, outer
+    near_mid_out[FACE - EDGE - 1], mid_out[FACE - EDGE - 1] = inner, inner
 
 
 def vmem():
@@ -172,7 +172,7 @@
 
 
 def grads_kernel(
-    skip_ref, cot_ref, pool_ref, xedge_ref, xmid_ref, xone_ref, ytwo_ref, yone_ref, *refs,
+    skip_ref, cot_ref, pool_ref, xedge_ref, xmid_ref, oedge_ref, omid_ref, ytwo_ref, yone_ref, *refs,
 ):
     wdec_ref, wpre_ref, wback_ref = refs[:3]
     send_out, keep_out, jskip_out, rim_out, two_out = refs[3:8]
@@ -183,8 +183,9 @@
     ylow, yhigh = sides(place[1])
 
     def face(xside, at):
-        two = xedge_ref[at] if at < EDGE else xmid_ref[at - EDGE]
-        return mixed(xside, xone_ref[at], two)
+        if at < EDGE:
+            return mixed(xside, oedge_ref[at], xedge_ref[at])
+        return mixed(xside, omid_ref[at - EDGE], xmid_ref[at - EDGE])
 
     def fine(plane, row):
         if row == 0:
@@ -387,13 +388,13 @@
     )
 
     block = (SKIP, LANES)
-    face, face_y, corner = (FACE,) + block, (FACE_Y,) + block, (2,) + block
+    face_y, corner = (FACE_Y,) + block, (2,) + block
     fine = (BLOCKS,) + block
-    skip, cot, pooled, xedge, xmid, xone = call(
+    skip, cot, pooled, xedge, xmid, oedge, omid = call(
         split_kernel, "split_blocks",
         (
             (fine, BF16), (fine, BF16), ((BLOCKS_C,) + block, BF16),
-            ((EDGE,) + block, BF16), ((FACE - EDGE,) + block, BF16), (face, BF16),
+            *(((rows,) + block, BF16) for rows in (EDGE, FACE - EDGE, EDGE, FACE - EDGE)),
         ),
         (
             (skip_feat.shape, BF16), (skip_feat.shape, BF16), ((SKIP * BLOCKS, LANES), F32),
@@ -402,10 +403,11 @@
         8, (1_000_000, 1_500_000), *in_hbm(skip_feat, cotangent),
         held=(pltpu.HBM,) * 2,
     )
-    xedge, xmid, xone = swap_side(xedge, "gx", 1), swap_side(xmid, "gx", 1), swap_side(xone, "gx", 0)
+    xedge, xmid = swap_side(xedge, "gx", 1), swap_side(xmid, "gx", 1)
+    oedge, omid = swap_side(oedge, "gx", 0), swap_side(omid, "gx", 0)
     yone, ytwo = call(
         faces_kernel, "row_faces", ((face_y, BF16), (face_y, BF16)), (), 8, (100_000, 400_000),
-        cot, pooled, xedge, xone, w_join, w_pre, w_back, held=(pltpu.VMEM,) * 4 + (pl.ANY,) * 3,
+        cot, pooled, xedge, oedge, w_join, w_pre, w_back, held=(pltpu.VMEM,) * 4 + (pl.ANY,) * 3,
     )
     yone, ytwo = swap_side(yone, "gy", 0), swap_side(ytwo, "gy", 1)
     chunks = (4, 4, ROWS, LANES)
@@ -423,42 +425,40 @@
             ((CHUNKS * ROWS, LANES), F32),
             ((3 * COARSE, BLOCKS_C * LANES), BF16),
         ),
-        36, (3_000_000_000, 8_000_000), skip, cot, pooled, xedge, xmid, xone, ytwo, yone,
+        36, (3_000_000_000, 8_000_000), skip, cot, pooled, xedge, xmid, oedge, omid, ytwo, yone,
         w_join, w_pre, w_back,
     )
 
-    send = swap(send, "gy", 1)
+    send, rtwo = swap(send, "gy", 1), swap_side(rtwo, "gy", 1)
     part = keep + wide(send[:SENT].reshape(chunks))
     rone = send[SENT:].reshape(corner)
     a, b = part[:, :2], part[:, 2:]
     a_got = swap_y(jnp.stack([a[A_FIRST], a[2]]).astype(BF16), A_FIRST)
     b_got = swap_y(jnp.stack([b[B_FIRST], b[2]]).astype(BF16), B_FIRST)
-    a_got, b_got = together((a_got, b_got))
+    a_got, b_got, rone, rtwo = together((a_got, b_got, rone, rtwo))
+    rows, qone, qtwo = call(
+        fold_kernel, "fold_rim", (((BLOCKS_C,) + block, F32), (corner, BF16), (corner, BF16)), (), 8, (100_000, 600_000),
+        own, rone, rtwo,
+    )
     a_own, a_leave = a[0] + wide(a_got[0]), a[A_SECOND] + wide(a_got[1])
     b_own, b_leave = b[0] + wide(b_got[0]), b[B_SECOND] + wide(b_got[1])
     a_got, b_got = swap_y(a_leave.astype(BF16), A_SECOND), swap_y(b_leave.astype(BF16), B_SECOND)
-    a_got, b_got = together((a_got, b_got))
+    a_got, b_got, rows, qone, qtwo = together((a_got, b_got, rows, qone, qtwo))
     part = jnp.concatenate([a_own + wide(a_got), b_own + wide(b_got)])
-    leave, rtwo = together((part.astype(BF16), rtwo))
-    got = [swap(leave[flip], "gx", flip) for flip in (1, 2, 3)]
-    *got, rone, rtwo = together((*got, rone, swap_side(rtwo, "gy", 1)))
-    rows, qone, qtwo = call(
-        fold_kernel, "fold_rim", (((BLOCKS_C,) + block, F32), (corner, BF16), (corner, BF16)), (), 8, (100_000, 600_000),
-        own, rone, rtwo,
-    )
+    leave = part.astype(BF16)
+    got = swap(jnp.concatenate([leave[1], qone.reshape(2 * SKIP, LANES)]), "gx", 1)
+    got = [got[:ROWS], swap(leave[2], "gx", 2), swap(leave[3], "gx", 3), got[ROWS:].reshape(corner)]
+    *got, qone = together(got)
     part = (part[0] + wide(got[0])) + (wide(got[1]) + wide(got[2]))
     mine = part.astype(BF16)
     got = [swap_z(mine, flip) for flip in (1, 2, 3)]
-    *got, rows, qone, qtwo = together((*got, rows, qone, qtwo))
     part = (wide(mine) + wide(got[0])) + (wide(got[1]) + wide(got[2]))
     part = (part + swap(part, "gy", 9)).astype(BF16)
-    got = swap(jnp.concatenate([part, qone.reshape(2 * SKIP, LANES)]), "gx", 1)
-    qone = got[ROWS:].reshape(corner)
-    part = jnp.stack(together([part, got[:ROWS], swap(part, "gx", 2), swap(part, "gx", 3)]))
+    got = together([swap(part, "gx", flip) for flip in (1, 3, 2)])
+    part = jnp.stack([part, got[0], got[2], got[1]])
     a, b = part[:2], part[2:]
     a_got, b_got = together((swap_y(a, A_SECOND), swap_y(b, B_SECOND)))
     a_near, b_near = jnp.stack([a, a_got]), jnp.stack([b, b_got])
-    a_near, b_near, qtwo = together((a_near, b_near, qtwo))
     qtwo = swap_side(qtwo, "gx", 1)
     a_far, b_far, qtwo = together((swap_y(a_near, A_FIRST), swap_y(b_near, B_FIRST), qtwo))
     other = swap(jnp.concatenate([a_near, a_far, b_near, b_far]), "gy", 1)

time: 97 us -> 91.6 us (0.944)
  waiting for transfers between devices: 37.2 us -> 31.5 us
    ppermute x7 -> x8, waiting for transfers between devices: 10.6 us -> 6.54 us  [swap_side(): lax.ppermute(value, axis, [(i, partner(i, which, count)) for i in range(c...]
    ppermute x17, waiting for transfers between devices: 22.5 us -> 20.6 us  [swap(): lax.ppermute(value, axis, [(i, i ^ flip) for i in range(lax.axis_size(axi...]
    ppermute x7 -> x8, starting transfers between devices: 18.1 us -> 18.6 us  [swap_side(): lax.ppermute(value, axis, [(i, partner(i, which, count)) for i in range(c...]
  transfers between devices with their start and end apart: 27 -> 28, of which waited for: 16 -> 17; matrix products, arithmetic and copies ran while one was open for 0% -> 0% of each run, Pallas kernels for 3% -> 3%
where the time goes in v4:
time: 91.6 us; the launch traced here: 91.5 us
  starting transfers between devices  46.5 us (51%)
  waiting for transfers between devices  31.5 us (34%)
  Pallas kernels  12 us (13%)
    ppermute x17, waiting for transfers between devices, swap(): lax.ppermute(value, axis, [(i, i ^ flip) for i in range(lax.axis_size(axi...  20.6 us
    ppermute x17, starting transfers between devices, swap(): lax.ppermute(value, axis, [(i, i ^ flip) for i in range(lax.axis_size(axi...  19.3 us
    ppermute x8, starting transfers between devices, swap_side(): lax.ppermute(value, axis, [(i, partner(i, which, count)) for i in range(c...  18.6 us
    pallas_call x7, Pallas kernels, call(): pl.pallas_call(kernel, out_shape=tuple((jax.ShapeDtypeStruct(shape, dtype...  12 us
    ppermute x3, starting transfers between devices, swap_z(): return lax.ppermute(value, ('gx', 'gy'), pairs)  8.62 us
    ppermute x8, waiting for transfers between devices, swap_side(): lax.ppermute(value, axis, [(i, partner(i, which, count)) for i in range(c...  6.54 us
    ppermute x3, waiting for transfers between devices, swap_z(): return lax.ppermute(value, ('gx', 'gy'), pairs)  4.4 us
  transfers between devices with their start and end apart: 28, of which 17 were waited for; matrix products, arithmetic and copies ran while one was open for 0% of the time, Pallas kernels for 3%

profile of v4, /device:TPU:1, one launch (start us, length us, event | category | flops | bytes accessed | tf_op | source)
XLA Modules:
  0.0 91.5 jit_solution(11235458552393174111)
XLA Ops:
  2.1 9.1 %collective-permute-start = (bf16[3,64,128]{2,1,0:T(8,128)(2,1)S(1)}, bf16[3,64,128]{2,1,0:T(8,128)(2,1)S(1)}, u32[]{:S(2)}, u32[]{:S(2)}) collective-permute-start(bf16[3,64,128]{2,1,0:T(8,128)(2,1)S(1)} %get-tuple-element.49), channel_id=1, source_target_pairs={{0,240},{16,32},{32,16},{48,64},{64,48},{80,96},{96,80},{112,128},... | collective-permute-start | bytes 147464 | tf_op jit(solution)/shard_map/ppermute | solution.py:356
  12.7 1.7 %lay_weights.1 = (bf16[192,1728]{1,0:T(8,128)(2,1)S(1)}, bf16[128,1728]{1,0:T(8,128)(2,1)S(1)}, bf16[576,384]{1,0:T(8,128)(2,1)S(1)}) custom-call(bf16[1728,192]{1,0:T(8,128)(2,1)} %bitcast.59, bf16[1728,128]{1,0:T(8,128)(2,1)} %bitcast.60), custom_call_target="tpu_custom_call" | custom-call | flops 1000000 | bytes 2500000 | tf_op jit(solution)/shard_map/lay_weights/pallas_call | solution.py:124
  14.5 3.6 %collective-permute-start.4 = (bf16[6,64,128]{2,1,0:T(8,128)(2,1)S(1)}, bf16[6,64,128]{2,1,0:T(8,128)(2,1)S(1)}, u32[]{:S(2)}, u32[]{:S(2)}) collective-permute-start(bf16[6,64,128]{2,1,0:T(8,128)(2,1)S(1)} %get-tuple-element.56), channel_id=1, source_target_pairs={{0,15},{1,2},{2,1},{3,4},{4,3},{5,6},{6,5},{7,8},{8,7},{9,10},{10,... | collective-permute-start | bytes 294920 | tf_op jit(solution)/shard_map/ppermute | solution.py:356
  18.3 1.7 %collective-permute-done.1.xmid_ref = bf16[7,64,128]{2,1,0:T(8,128)(2,1)S(1)} collective-permute-done((bf16[7,64,128]{2,1,0:T(8,128)(2,1)S(1)}, bf16[7,64,128]{2,1,0:T(8,128)(2,1)S(1)}, u32[]{:S(2)}, u32[]{:S(2)}) %collective-permute-start.1) | collective-permute-done | bytes 114720 | tf_op jit(solution)/shard_map/ppermute | solution.py:356
  20.8 5.8 %local_grads.1 = (bf16[2304,128]{1,0:T(8,128)(2,1)S(1)}, f32[4,4,136,128]{3,2,1,0:T(8,128)S(1)}, f32[16,64,128]{2,1,0:T(8,128)S(1)}, f32[12,64,128]{2,1,0:T(8,128)S(1)}, bf16[2,64,128]{2,1,0:T(8,128)(2,1)S(1)}) custom-call(bf16[16,64,128]{2,1,0:T(8,128)(2,1)S(1)} %get-tuple-element.46.skip_ref, bf16[16,64,128]{2,1,0:T(8,128)(2,1)S(1)} %get-tuple-element.47.cot_ref, ...), custom_call_target="tpu_custom_call" | custom-call | flops 3000000000 | bytes 8000000 | tf_op jit(solution)/shard_map/local_grads/pallas_call | solution.py:124
  26.6 2.5 %collective-permute-start.6 = (bf16[2304,128]{1,0:T(8,128)(2,1)S(1)}, bf16[2304,128]{1,0:T(8,128)(2,1)S(1)}, u32[]{:S(2)}, u32[]{:S(2)}) collective-permute-start(bf16[2304,128]{1,0:T(8,128)(2,1)S(1)} %get-tuple-element.59), channel_id=1, source_target_pairs={{0,1},{1,0},{2,3},{3,2},{4,5},{5,4},{6,7},{7,6},{8,9},{9,8},{10,11... | collective-permute-start | bytes 1769480 | tf_op jit(solution)/shard_map/ppermute | solution.py:343
  29.0 1.6 %collective-permute-done.6 = bf16[2304,128]{1,0:T(8,128)(2,1)S(1)} collective-permute-done((bf16[2304,128]{1,0:T(8,128)(2,1)S(1)}, bf16[2304,128]{1,0:T(8,128)(2,1)S(1)}, u32[]{:S(2)}, u32[]{:S(2)}) %collective-permute-start.6) | collective-permute-done | bytes 589856 | tf_op jit(solution)/shard_map/ppermute | solution.py:343
  30.9 3.0 %collective-permute-start.8 = (bf16[2,2,136,128]{3,2,1,0:T(8,128)(2,1)S(1)}, bf16[2,2,136,128]{3,2,1,0:T(8,128)(2,1)S(1)}, u32[]{:S(2)}, u32[]{:S(2)}) collective-permute-start(bf16[2,2,136,128]{3,2,1,0:T(8,128)(2,1)S(1)} %pad_maximum_fusion), channel_id=1, source_target_pairs={{0,7},{1,6},{2,5},{3,4},{4,3},{5,2},{6,1},{7,0},{8,15},{9,14},{10,... | collective-permute-start | bytes 417800 | tf_op jit(solution)/shard_map/ppermute | solution.py:343
  33.9 1.7 %collective-permute-start.9 = (bf16[2,64,128]{2,1,0:T(8,128)(2,1)S(1)}, bf16[2,64,128]{2,1,0:T(8,128)(2,1)S(1)}, u32[]{:S(2)}, u32[]{:S(2)}) collective-permute-start(bf16[2,64,128]{2,1,0:T(8,128)(2,1)S(1)} %get-tuple-element.60), channel_id=1, source_target_pairs={{0,15},{1,2},{2,1},{3,4},{4,3},{5,6},{6,5},{7,8},{8,7},{9,10},{10,... | collective-permute-start | bytes 98312 | tf_op jit(solution)/shard_map/ppermute | solution.py:356
  35.6 4.1 %collective-permute-done.9.ytwo_ref = bf16[2,64,128]{2,1,0:T(8,128)(2,1)S(1)} collective-permute-done((bf16[2,64,128]{2,1,0:T(8,128)(2,1)S(1)}, bf16[2,64,128]{2,1,0:T(8,128)(2,1)S(1)}, u32[]{:S(2)}, u32[]{:S(2)}) %collective-permute-start.9) | collective-permute-done | bytes 32800 | tf_op jit(solution)/shard_map/ppermute | solution.py:356
  41.5 2.1 %collective-permute-done.11 = bf16[2,136,128]{2,1,0:T(8,128)(2,1)S(1)} collective-permute-done((bf16[2,136,128]{2,1,0:T(8,128)(2,1)S(1)}, bf16[2,136,128]{2,1,0:T(8,128)(2,1)S(1)}, u32[]{:S(2)}, u32[]{:S(2)}) %collective-permute-start.11) | collective-permute-done | bytes 69664 | tf_op jit(solution)/shard_map/ppermute | solution.py:343
  43.6 1.9 %collective-permute-done.10 = bf16[2,136,128]{2,1,0:T(8,128)(2,1)S(1)} collective-permute-done((bf16[2,136,128]{2,1,0:T(8,128)(2,1)S(1)}, bf16[2,136,128]{2,1,0:T(8,128)(2,1)S(1)}, u32[]{:S(2)}, u32[]{:S(2)}) %collective-permute-start.10) | collective-permute-done | bytes 69664 | tf_op jit(solution)/shard_map/ppermute | solution.py:343
  45.8 3.1 %collective-permute-start.13 = (bf16[136,128]{1,0:T(8,128)(2,1)S(1)}, bf16[136,128]{1,0:T(8,128)(2,1)S(1)}, u32[]{:S(2)}, u32[]{:S(2)}) collective-permute-start(bf16[136,128]{1,0:T(8,128)(2,1)S(1)} %get-tuple-element.102), channel_id=1, source_target_pairs={{0,32},{16,48},{32,0},{48,16},{64,96},{80,112},{96,64},{112,80},{1... | collective-permute-start | bytes 104456 | tf_op jit(solution)/shard_map/ppermute | solution.py:343
  50.3 6.2 %collective-permute-start.17 = (bf16[136,128]{1,0:T(8,128)(2,1)S(1)}, bf16[136,128]{1,0:T(8,128)(2,1)S(1)}, u32[]{:S(2)}, u32[]{:S(2)}) collective-permute-start(bf16[136,128]{1,0:T(8,128)(2,1)S(1)} %fusion.11), channel_id=1, source_target_pairs={{0,193},{1,192},{2,195},{3,194},{4,197},{5,196},{6,199},{7,198},{8... | collective-permute-start | bytes 104456 | tf_op jit(solution)/shard_map/ppermute | solution.py:375
  56.8 2.1 %collective-permute-start.15 = (bf16[136,128]{1,0:T(8,128)(2,1)S(1)}, bf16[136,128]{1,0:T(8,128)(2,1)S(1)}, u32[]{:S(2)}, u32[]{:S(2)}) collective-permute-start(bf16[136,128]{1,0:T(8,128)(2,1)S(1)} %fusion.11), channel_id=1, source_target_pairs={{0,65},{1,64},{2,67},{3,66},{4,69},{5,68},{6,71},{7,70},{8,73},{9,... | collective-permute-start | bytes 104456 | tf_op jit(solution)/shard_map/ppermute | solution.py:375
  58.9 4.4 %collective-permute-done.16 = bf16[136,128]{1,0:T(8,128)(2,1)S(1)} collective-permute-done((bf16[136,128]{1,0:T(8,128)(2,1)S(1)}, bf16[136,128]{1,0:T(8,128)(2,1)S(1)}, u32[]{:S(2)}, u32[]{:S(2)}) %collective-permute-start.16) | collective-permute-done | bytes 34848 | tf_op jit(solution)/shard_map/ppermute | solution.py:375
  63.4 3.7 %collective-permute-done.18 = f32[136,128]{1,0:T(8,128)S(1)} collective-permute-done((f32[136,128]{1,0:T(8,128)S(1)}, f32[136,128]{1,0:T(8,128)S(1)}, u32[]{:S(2)}, u32[]{:S(2)}) %collective-permute-start.18) | collective-permute-done | bytes 69664 | tf_op jit(solution)/shard_map/ppermute | solution.py:343
  67.1 2.1 %collective-permute-start.21 = (bf16[136,128]{1,0:T(8,128)(2,1)S(1)}, bf16[136,128]{1,0:T(8,128)(2,1)S(1)}, u32[]{:S(2)}, u32[]{:S(2)}) collective-permute-start(bf16[136,128]{1,0:T(8,128)(2,1)S(1)} %add_convert_fusion), channel_id=1, source_target_pairs={{0,32},{16,48},{32,0},{48,16},{64,96},{80,112},{96,64},{112,80},{1... | collective-permute-start | bytes 104456 | tf_op jit(solution)/shard_map/ppermute | solution.py:343
  70.7 2.5 %collective-permute-start.26 = (bf16[2,64,128]{2,1,0:T(8,128)(2,1)S(1)}, bf16[2,64,128]{2,1,0:T(8,128)(2,1)S(1)}, u32[]{:S(2)}, u32[]{:S(2)}) collective-permute-start(bf16[2,64,128]{2,1,0:T(8,128)(2,1)S(1)} %get-tuple-element.82), channel_id=1, source_target_pairs={{0,240},{16,32},{32,16},{48,64},{64,48},{80,96},{96,80},{112,128},... | collective-permute-start | bytes 98312 | tf_op jit(solution)/shard_map/ppermute | solution.py:356
  73.5 1.9 %collective-permute-start.23 = (bf16[2,136,128]{2,1,0:T(8,128)(2,1)S(1)}, bf16[2,136,128]{2,1,0:T(8,128)(2,1)S(1)}, u32[]{:S(2)}, u32[]{:S(2)}) collective-permute-start(bf16[2,136,128]{2,1,0:T(8,128)(2,1)S(1)} %get-tuple-element.98), channel_id=1, source_target_pairs={{0,3},{1,2},{2,1},{3,0},{4,7},{5,6},{6,5},{7,4},{8,11},{9,10},{10,... | collective-permute-start | bytes 208904 | tf_op jit(solution)/shard_map/ppermute | solution.py:343
  77.7 2.8 %collective-permute-done.22 = bf16[2,136,128]{2,1,0:T(8,128)(2,1)S(1)} collective-permute-done((bf16[2,136,128]{2,1,0:T(8,128)(2,1)S(1)}, bf16[2,136,128]{2,1,0:T(8,128)(2,1)S(1)}, u32[]{:S(2)}, u32[]{:S(2)}) %collective-permute-start.22) | collective-permute-done | bytes 69664 | tf_op jit(solution)/shard_map/ppermute | solution.py:343
  80.6 1.7 %collective-permute-start.25 = (bf16[2,2,136,128]{3,2,1,0:T(8,128)(2,1)S(1)}, bf16[2,2,136,128]{3,2,1,0:T(8,128)(2,1)S(1)}, u32[]{:S(2)}, u32[]{:S(2)}) collective-permute-start(bf16[2,2,136,128]{3,2,1,0:T(8,128)(2,1)S(1)} %pad_maximum_fusion.2.b0_ref), channel_id=1, source_target_pairs={{0,7},{1,6},{2,5},{3,4},{4,3},{5,2},{6,1},{7,0},{8,15},{9,14},{10,... | collective-permute-start | bytes 417800 | tf_op jit(solution)/shard_map/ppermute | solution.py:343
  82.3 3.6 %collective-permute-done.24.a1_ref = bf16[2,2,136,128]{3,2,1,0:T(8,128)(2,1)S(1)} collective-permute-done((bf16[2,2,136,128]{3,2,1,0:T(8,128)(2,1)S(1)}, bf16[2,2,136,128]{3,2,1,0:T(8,128)(2,1)S(1)}, u32[]{:S(2)}, u32[]{:S(2)}) %collective-permute-start.24) | collective-permute-done | bytes 139296 | tf_op jit(solution)/shard_map/ppermute | solution.py:343
  89.6 1.9 %unpack.1 = (f32[1728,192]{1,0:T(8,128)}, f32[1728,128]{1,0:T(8,128)}) custom-call(bf16[2,2,136,128]{3,2,1,0:T(8,128)(2,1)S(1)} %pad_maximum_fusion.1.a0_ref, bf16[2,2,136,128]{3,2,1,0:T(8,128)(2,1)S(1)} %collective-permute-done.24.a1_ref, bf16[2,2,136,128]{3,2,1,0:T(8,128)(2,1)S(1)} %pad_maximum_fusion.2.b0_ref, ...), custom_call_target="tpu_custom_call" | custom-call | flops 1000000 | bytes 5000000 | tf_op jit(solution)/shard_map/unpack/pallas_call | solution.py:124
  (65 shorter events, 15.9 us)
Async XLA Ops:
  2.1 12.3 %collective-permute-start = (bf16[3,64,128]{2,1,0:T(8,128)(2,1)S(1)}, bf16[3,64,128]{2,1,0:T(8,128)(2,1)S(1)}, u32[]{:S(2)}, u32[]{:S(2)}) collective-permute-start(bf16[3,64,128]{2,1,0:T(8,128)(2,1)S(1)} %get-tuple-element.49), channel_id=1, source_target_pairs={{0,240},{16,32},{32,16},{48,64},{64,48},{80,96},{96,80},{112,128},... | collective-permute-start | bytes 147464 | tf_op jit(solution)/shard_map/ppermute | solution.py:356
  11.2 8.8 %collective-permute-start.1 = (bf16[7,64,128]{2,1,0:T(8,128)(2,1)S(1)}, bf16[7,64,128]{2,1,0:T(8,128)(2,1)S(1)}, u32[]{:S(2)}, u32[]{:S(2)}) collective-permute-start(bf16[7,64,128]{2,1,0:T(8,128)(2,1)S(1)} %get-tuple-element.50), channel_id=1, source_target_pairs={{0,240},{16,32},{32,16},{48,64},{64,48},{80,96},{96,80},{112,128},... | collective-permute-start | bytes 344072 | tf_op jit(solution)/shard_map/ppermute | solution.py:356
  12.0 8.0 %collective-permute-start.3 = (bf16[7,64,128]{2,1,0:T(8,128)(2,1)S(1)}, bf16[7,64,128]{2,1,0:T(8,128)(2,1)S(1)}, u32[]{:S(2)}, u32[]{:S(2)}) collective-permute-start(bf16[7,64,128]{2,1,0:T(8,128)(2,1)S(1)} %get-tuple-element.52), channel_id=1, source_target_pairs={{0,16},{16,0},{32,48},{48,32},{64,80},{80,64},{96,112},{112,96},{1... | collective-permute-start | bytes 344072 | tf_op jit(solution)/shard_map/ppermute | solution.py:356
  14.5 6.2 %collective-permute-start.4 = (bf16[6,64,128]{2,1,0:T(8,128)(2,1)S(1)}, bf16[6,64,128]{2,1,0:T(8,128)(2,1)S(1)}, u32[]{:S(2)}, u32[]{:S(2)}) collective-permute-start(bf16[6,64,128]{2,1,0:T(8,128)(2,1)S(1)} %get-tuple-element.56), channel_id=1, source_target_pairs={{0,15},{1,2},{2,1},{3,4},{4,3},{5,6},{6,5},{7,8},{8,7},{9,10},{10,... | collective-permute-start | bytes 294920 | tf_op jit(solution)/shard_map/ppermute | solution.py:356
  26.6 4.1 %collective-permute-start.6 = (bf16[2304,128]{1,0:T(8,128)(2,1)S(1)}, bf16[2304,128]{1,0:T(8,128)(2,1)S(1)}, u32[]{:S(2)}, u32[]{:S(2)}) collective-permute-start(bf16[2304,128]{1,0:T(8,128)(2,1)S(1)} %get-tuple-element.59), channel_id=1, source_target_pairs={{0,1},{1,0},{2,3},{3,2},{4,5},{5,4},{6,7},{7,6},{8,9},{9,8},{10,11... | collective-permute-start | bytes 1769480 | tf_op jit(solution)/shard_map/ppermute | solution.py:343
  30.9 8.8 %collective-permute-start.8 = (bf16[2,2,136,128]{3,2,1,0:T(8,128)(2,1)S(1)}, bf16[2,2,136,128]{3,2,1,0:T(8,128)(2,1)S(1)}, u32[]{:S(2)}, u32[]{:S(2)}) collective-permute-start(bf16[2,2,136,128]{3,2,1,0:T(8,128)(2,1)S(1)} %pad_maximum_fusion), channel_id=1, source_target_pairs={{0,7},{1,6},{2,5},{3,4},{4,3},{5,2},{6,1},{7,0},{8,15},{9,14},{10,... | collective-permute-start | bytes 417800 | tf_op jit(solution)/shard_map/ppermute | solution.py:343
  33.9 5.8 %collective-permute-start.7 = (bf16[2,2,136,128]{3,2,1,0:T(8,128)(2,1)S(1)}, bf16[2,2,136,128]{3,2,1,0:T(8,128)(2,1)S(1)}, u32[]{:S(2)}, u32[]{:S(2)}) collective-permute-start(bf16[2,2,136,128]{3,2,1,0:T(8,128)(2,1)S(1)} %stack.56), channel_id=1, source_target_pairs={{0,3},{1,2},{2,1},{3,0},{4,7},{5,6},{6,5},{7,4},{8,11},{9,10},{10,... | collective-permute-start | bytes 417800 | tf_op jit(solution)/shard_map/ppermute | solution.py:343
  33.9 5.8 %collective-permute-start.9 = (bf16[2,64,128]{2,1,0:T(8,128)(2,1)S(1)}, bf16[2,64,128]{2,1,0:T(8,128)(2,1)S(1)}, u32[]{:S(2)}, u32[]{:S(2)}) collective-permute-start(bf16[2,64,128]{2,1,0:T(8,128)(2,1)S(1)} %get-tuple-element.60), channel_id=1, source_target_pairs={{0,15},{1,2},{2,1},{3,4},{4,3},{5,6},{6,5},{7,8},{8,7},{9,10},{10,... | collective-permute-start | bytes 98312 | tf_op jit(solution)/shard_map/ppermute | solution.py:356
  39.7 3.8 %collective-permute-start.11 = (bf16[2,136,128]{2,1,0:T(8,128)(2,1)S(1)}, bf16[2,136,128]{2,1,0:T(8,128)(2,1)S(1)}, u32[]{:S(2)}, u32[]{:S(2)}) collective-permute-start(bf16[2,136,128]{2,1,0:T(8,128)(2,1)S(1)} %get-tuple-element.93), channel_id=1, source_target_pairs={{0,3},{1,2},{2,1},{3,0},{4,7},{5,6},{6,5},{7,4},{8,11},{9,10},{10,... | collective-permute-start | bytes 208904 | tf_op jit(solution)/shard_map/ppermute | solution.py:343
  40.4 5.1 %collective-permute-start.10 = (bf16[2,136,128]{2,1,0:T(8,128)(2,1)S(1)}, bf16[2,136,128]{2,1,0:T(8,128)(2,1)S(1)}, u32[]{:S(2)}, u32[]{:S(2)}) collective-permute-start(bf16[2,136,128]{2,1,0:T(8,128)(2,1)S(1)} %get-tuple-element.94), channel_id=1, source_target_pairs={{0,7},{1,6},{2,5},{3,4},{4,3},{5,2},{6,1},{7,0},{8,15},{9,14},{10,... | collective-permute-start | bytes 208904 | tf_op jit(solution)/shard_map/ppermute | solution.py:343
  45.5 3.7 %collective-permute-start.12 = (bf16[264,128]{1,0:T(8,128)(2,1)S(1)}, bf16[264,128]{1,0:T(8,128)(2,1)S(1)}, u32[]{:S(2)}, u32[]{:S(2)}) collective-permute-start(bf16[264,128]{1,0:T(8,128)(2,1)S(1)} %pad_maximum_fusion.5), channel_id=1, source_target_pairs={{0,16},{16,0},{32,48},{48,32},{64,80},{80,64},{96,112},{112,96},{1... | collective-permute-start | bytes 202760 | tf_op jit(solution)/shard_map/ppermute | solution.py:343
  45.7 4.1 %collective-permute-start.14 = (bf16[136,128]{1,0:T(8,128)(2,1)S(1)}, bf16[136,128]{1,0:T(8,128)(2,1)S(1)}, u32[]{:S(2)}, u32[]{:S(2)}) collective-permute-start(bf16[136,128]{1,0:T(8,128)(2,1)S(1)} %get-tuple-element.101), channel_id=1, source_target_pairs={{0,48},{16,32},{32,16},{48,0},{64,112},{80,96},{96,80},{112,64},{1... | collective-permute-start | bytes 104456 | tf_op jit(solution)/shard_map/ppermute | solution.py:343
  45.8 4.5 %collective-permute-start.13 = (bf16[136,128]{1,0:T(8,128)(2,1)S(1)}, bf16[136,128]{1,0:T(8,128)(2,1)S(1)}, u32[]{:S(2)}, u32[]{:S(2)}) collective-permute-start(bf16[136,128]{1,0:T(8,128)(2,1)S(1)} %get-tuple-element.102), channel_id=1, source_target_pairs={{0,32},{16,48},{32,0},{48,16},{64,96},{80,112},{96,64},{112,80},{1... | collective-permute-start | bytes 104456 | tf_op jit(solution)/shard_map/ppermute | solution.py:343
  50.3 8.6 %collective-permute-start.17 = (bf16[136,128]{1,0:T(8,128)(2,1)S(1)}, bf16[136,128]{1,0:T(8,128)(2,1)S(1)}, u32[]{:S(2)}, u32[]{:S(2)}) collective-permute-start(bf16[136,128]{1,0:T(8,128)(2,1)S(1)} %fusion.11), channel_id=1, source_target_pairs={{0,193},{1,192},{2,195},{3,194},{4,197},{5,196},{6,199},{7,198},{8... | collective-permute-start | bytes 104456 | tf_op jit(solution)/shard_map/ppermute | solution.py:375
  56.4 6.9 %collective-permute-start.16 = (bf16[136,128]{1,0:T(8,128)(2,1)S(1)}, bf16[136,128]{1,0:T(8,128)(2,1)S(1)}, u32[]{:S(2)}, u32[]{:S(2)}) collective-permute-start(bf16[136,128]{1,0:T(8,128)(2,1)S(1)} %fusion.11), channel_id=1, source_target_pairs={{0,128},{1,129},{2,130},{3,131},{4,132},{5,133},{6,134},{7,135},{8... | collective-permute-start | bytes 104456 | tf_op jit(solution)/shard_map/ppermute | solution.py:375
  56.8 6.5 %collective-permute-start.15 = (bf16[136,128]{1,0:T(8,128)(2,1)S(1)}, bf16[136,128]{1,0:T(8,128)(2,1)S(1)}, u32[]{:S(2)}, u32[]{:S(2)}) collective-permute-start(bf16[136,128]{1,0:T(8,128)(2,1)S(1)} %fusion.11), channel_id=1, source_target_pairs={{0,65},{1,64},{2,67},{3,66},{4,69},{5,68},{6,71},{7,70},{8,73},{9,... | collective-permute-start | bytes 104456 | tf_op jit(solution)/shard_map/ppermute | solution.py:375
  63.3 3.8 %collective-permute-start.18 = (f32[136,128]{1,0:T(8,128)S(1)}, f32[136,128]{1,0:T(8,128)S(1)}, u32[]{:S(2)}, u32[]{:S(2)}) collective-permute-start(f32[136,128]{1,0:T(8,128)S(1)} %add_add_fusion), channel_id=1, source_target_pairs={{0,9},{1,8},{2,11},{3,10},{4,13},{5,12},{6,15},{7,14},{8,1},{9,0},... | collective-permute-start | bytes 208904 | tf_op jit(solution)/shard_map/ppermute | solution.py:343
  67.1 6.0 %collective-permute-start.21 = (bf16[136,128]{1,0:T(8,128)(2,1)S(1)}, bf16[136,128]{1,0:T(8,128)(2,1)S(1)}, u32[]{:S(2)}, u32[]{:S(2)}) collective-permute-start(bf16[136,128]{1,0:T(8,128)(2,1)S(1)} %add_convert_fusion), channel_id=1, source_target_pairs={{0,32},{16,48},{32,0},{48,16},{64,96},{80,112},{96,64},{112,80},{1... | collective-permute-start | bytes 104456 | tf_op jit(solution)/shard_map/ppermute | solution.py:343
  69.2 4.0 %collective-permute-start.20 = (bf16[136,128]{1,0:T(8,128)(2,1)S(1)}, bf16[136,128]{1,0:T(8,128)(2,1)S(1)}, u32[]{:S(2)}, u32[]{:S(2)}) collective-permute-start(bf16[136,128]{1,0:T(8,128)(2,1)S(1)} %add_convert_fusion), channel_id=1, source_target_pairs={{0,48},{16,32},{32,16},{48,0},{64,112},{80,96},{96,80},{112,64},{1... | collective-permute-start | bytes 104456 | tf_op jit(solution)/shard_map/ppermute | solution.py:343
  70.7 11.6 %collective-permute-start.26 = (bf16[2,64,128]{2,1,0:T(8,128)(2,1)S(1)}, bf16[2,64,128]{2,1,0:T(8,128)(2,1)S(1)}, u32[]{:S(2)}, u32[]{:S(2)}) collective-permute-start(bf16[2,64,128]{2,1,0:T(8,128)(2,1)S(1)} %get-tuple-element.82), channel_id=1, source_target_pairs={{0,240},{16,32},{32,16},{48,64},{64,48},{80,96},{96,80},{112,128},... | collective-permute-start | bytes 98312 | tf_op jit(solution)/shard_map/ppermute | solution.py:356
  73.5 4.2 %collective-permute-start.23 = (bf16[2,136,128]{2,1,0:T(8,128)(2,1)S(1)}, bf16[2,136,128]{2,1,0:T(8,128)(2,1)S(1)}, u32[]{:S(2)}, u32[]{:S(2)}) collective-permute-start(bf16[2,136,128]{2,1,0:T(8,128)(2,1)S(1)} %get-tuple-element.98), channel_id=1, source_target_pairs={{0,3},{1,2},{2,1},{3,0},{4,7},{5,6},{6,5},{7,4},{8,11},{9,10},{10,... | collective-permute-start | bytes 208904 | tf_op jit(solution)/shard_map/ppermute | solution.py:343
  75.4 5.0 %collective-permute-start.22 = (bf16[2,136,128]{2,1,0:T(8,128)(2,1)S(1)}, bf16[2,136,128]{2,1,0:T(8,128)(2,1)S(1)}, u32[]{:S(2)}, u32[]{:S(2)}) collective-permute-start(bf16[2,136,128]{2,1,0:T(8,128)(2,1)S(1)} %get-tuple-element.100), channel_id=1, source_target_pairs={{0,7},{1,6},{2,5},{3,4},{4,3},{5,2},{6,1},{7,0},{8,15},{9,14},{10,... | collective-permute-start | bytes 208904 | tf_op jit(solution)/shard_map/ppermute | solution.py:343
  80.4 5.5 %collective-permute-start.24 = (bf16[2,2,136,128]{3,2,1,0:T(8,128)(2,1)S(1)}, bf16[2,2,136,128]{3,2,1,0:T(8,128)(2,1)S(1)}, u32[]{:S(2)}, u32[]{:S(2)}) collective-permute-start(bf16[2,2,136,128]{3,2,1,0:T(8,128)(2,1)S(1)} %pad_maximum_fusion.1.a0_ref), channel_id=1, source_target_pairs={{0,3},{1,2},{2,1},{3,0},{4,7},{5,6},{6,5},{7,4},{8,11},{9,10},{10,... | collective-permute-start | bytes 417800 | tf_op jit(solution)/shard_map/ppermute | solution.py:343
  80.6 6.9 %collective-permute-start.25 = (bf16[2,2,136,128]{3,2,1,0:T(8,128)(2,1)S(1)}, bf16[2,2,136,128]{3,2,1,0:T(8,128)(2,1)S(1)}, u32[]{:S(2)}, u32[]{:S(2)}) collective-permute-start(bf16[2,2,136,128]{3,2,1,0:T(8,128)(2,1)S(1)} %pad_maximum_fusion.2.b0_ref), channel_id=1, source_target_pairs={{0,7},{1,6},{2,5},{3,4},{4,3},{5,2},{6,1},{7,0},{8,15},{9,14},{10,... | collective-permute-start | bytes 417800 | tf_op jit(solution)/shard_map/ppermute | solution.py:343
  (4 other events, 10.6 us)

commit v5 on v4

--- a/solution.py
+++ b/solution.py
@@ -20,6 +20,7 @@
 SENT = CHUNKS // 2 * ROWS
 FACE, FACE_Y = SIZE_Y + BLOCKS_C // 2, SIZE_X + 2 + 2
 EDGE = 3
+RIM = BLOCKS_C // 2 + 1
 FACE_ROWS = (0, SIZE_Y - 1, None, *range(1, SIZE_Y - 1))
 BF16, F32 = jnp.bfloat16, jnp.float32
 
@@ -116,16 +117,12 @@
     near_mid_out[FACE - EDGE - 1], mid_out[FACE - EDGE - 1] = inner, inner
 
 
-def vmem():
-    return pl.BlockSpec(memory_space=pltpu.VMEM)
-
-
-def call(kernel, name, outs, scratch, mib, cost, *operands, held=()):
+def call(kernel, name, outs, scratch, mib, cost, *operands, held=(), gives=pltpu.VMEM):
     return pl.pallas_call(
         kernel,
         out_shape=tuple(jax.ShapeDtypeStruct(shape, dtype) for shape, dtype in outs),
         in_specs=[pl.BlockSpec(memory_space=space) for space in held or (pltpu.VMEM,) * len(operands)],
-        out_specs=tuple(vmem() for _ in outs),
+        out_specs=tuple(pl.BlockSpec(memory_space=gives) for _ in outs),
         scratch_shapes=[pltpu.VMEM(*form) if isinstance(form, tuple) else form for form in scratch],
         compiler_params=params(mib),
         cost_estimate=pl.CostEstimate(flops=cost[0], bytes_accessed=cost[1], transcendentals=0),
@@ -175,8 +172,8 @@
     skip_ref, cot_ref, pool_ref, xedge_ref, xmid_ref, oedge_ref, omid_ref, ytwo_ref, yone_ref, *refs,
 ):
     wdec_ref, wpre_ref, wback_ref = refs[:3]
-    send_out, keep_out, jskip_out, rim_out, two_out = refs[3:8]
-    cells_ref, pooled_ref, joined_ref, jgrad_ref, full_ref, pre_ref = refs[8:]
+    send_out, keep_out, jskip_out, rim_out, one_out, two_out = refs[3:9]
+    cells_ref, pooled_ref, joined_ref, jgrad_ref, full_ref, pre_ref = refs[9:]
     factor = 1.0 / math.sqrt(524288)
     place = places()
     xlow, xhigh = sides(place[0])
@@ -262,15 +259,12 @@
                 total = part if total is None else total + part
         return total
 
-    for i in range(3):
-        for row in range(BLOCKS_C):
-            rim_out[BLOCKS_C * i + row] = rim_row(i, row + 1)
-    odd = (place[1] & 1).astype(F32)
-    for index in range(2):
-        down, up = (
-            pack(rim_row(0, row), rim_row(1, row)) if index == 0 else rim_row(2, row) for row in (0, BLOCKS_C + 1)
-        )
-        send_out[SENT + index * SKIP : SENT + (index + 1) * SKIP] = ((1.0 - odd) * up + odd * down).astype(BF16)
+    for row in range(BLOCKS_C + 2):
+        rim_out[row] = rim_row(1, row)
+    odd = (place[0] & 1).astype(F32)
+    for index in range(RIM):
+        down, up = (pack(rim_row(i, 2 * index), rim_row(i, 2 * index + 1)) for i in (0, 2))
+        one_out[index] = ((1.0 - odd) * up + odd * down).astype(BF16)
         two_out[index] = ((1.0 - odd) * down + odd * up).astype(BF16)
 
     across = (((1,), (1,)), ((), ()))
@@ -293,35 +287,36 @@
         send_out[4 * yr * ROWS : 4 * (yr + 1) * ROWS] = jnp.concatenate(leave).astype(BF16)
 
 
-def fold_kernel(rim_ref, yone_ref, ytwo_ref, rows_out, one_out, two_out):
+def fold_kernel(rim_ref, xone_ref, xtwo_ref, rows_out, one_out, two_out):
     place = places()
-    planes = [[rim_ref[BLOCKS_C * i + row] for row in range(BLOCKS_C)] for i in range(3)]
-    for weights, row in zip(sides(place[1]), (0, BLOCKS_C - 1)):
-        first, second = unpack_pair(mixed(weights, yone_ref[0], ytwo_ref[0]))
-        third = mixed(weights, yone_ref[1], ytwo_ref[1])
-        for i, terms in enumerate((first, second, third)):
-            planes[i][row] = planes[i][row] + terms
+    low, high = sides(place[0])
+    weights = (low[0] + high[0], low[1] + high[1])
+    rows = []
+    for index in range(RIM):
+        first, second = unpack_pair(mixed(weights, xone_ref[index], xtwo_ref[index]))
+        rows += [rim_ref[2 * index] + first, rim_ref[2 * index + 1] + second]
     for row in range(BLOCKS_C):
-        rows_out[row] = planes[1][row]
-    odd = (place[0] & 1).astype(F32)
-    for index in range(BLOCKS_C // 2):
-        down, up = (pack(planes[i][2 * index], planes[i][2 * index + 1]) for i in (0, 2))
-        one_out[index] = ((1.0 - odd) * up + odd * down).astype(BF16)
-        two_out[index] = ((1.0 - odd) * down + odd * up).astype(BF16)
-
-
-def skip_kernel(rows_ref, xone_ref, xtwo_ref, jskip_ref, out_ref, cells_ref):
-    low, high = sides(places()[0])
-    weights = (low[0] + high[0], low[1] + high[1])
-    for pair in range(BLOCKS_C // 2):
-        for at, terms in zip((2 * pair, 2 * pair + 1), unpack_pair(mixed(weights, xone_ref[pair], xtwo_ref[pair]))):
-            total = rows_ref[at] + terms
-            for index in (2 * at, 2 * at + 1, SIZE_Y + 2 * at, SIZE_Y + 2 * at + 1):
-                cells_ref[pl.ds(index, SKIP, stride=BLOCKS), :] = jskip_ref[index] + total
+        rows_out[row] = rows[row + 1]
+    odd = (place[1] & 1).astype(F32)
+    down, up = rows[0], rows[-1]
+    one_out[...] = ((1.0 - odd) * up + odd * down).astype(BF16)
+    two_out[...] = ((1.0 - odd) * down + odd * up).astype(BF16)
+
+
+def skip_kernel(rows_ref, yone_ref, ytwo_ref, jskip_ref, out_ref, cells_ref):
+    low, high = sides(places()[1])
+    for at in range(BLOCKS_C):
+        total = rows_ref[at]
+        if at == 0:
+            total = total + mixed(low, yone_ref[...], ytwo_ref[...])
+        if at == BLOCKS_C - 1:
+            total = total + mixed(high, yone_ref[...], ytwo_ref[...])
+        for index in (2 * at, 2 * at + 1, SIZE_Y + 2 * at, SIZE_Y + 2 * at + 1):
+            cells_ref[pl.ds(index, SKIP, stride=BLOCKS), :] = jskip_ref[index] + total
     out_ref[...] = cells_ref[...].reshape(SKIP, SIZE_X, SIZE_Y, LANES).astype(BF16)
 
 
-def unpack_kernel(a0_ref, a1_ref, b0_ref, b1_ref, core_ref, dec_out, coarse_out, full_ref):
+def unpack_kernel(a0_ref, a1_ref, b0_ref, b1_ref, other_ref, dec_hbm, coarse_hbm, full_ref, dec_ref, sent):
     place = places()
     half, y, x = half_of(place), (place[1] >> 1) & 3, place[0] & 3
     for side, (refs, order) in enumerate((((a0_ref, a1_ref), ORDER_A), ((b0_ref, b1_ref), ORDER_B))):
@@ -331,12 +326,19 @@
                 row = pl.multiple_of((at + 16 * half) * ROWS, ROWS)
                 full_ref[pl.ds(row, ROWS), :] = refs[index // 2][index % 2, xr].astype(F32)
                 row = pl.multiple_of((at + 16 * (1 - half)) * ROWS, ROWS)
-                full_ref[pl.ds(row, ROWS), :] = core_ref[4 * side + index, xr].astype(F32)
-    middle = LANES // 2
-    dec_out[:, :LANES] = full_ref[:DEC]
-    dec_out[: DEC // 2, LANES:] = full_ref[DEC : DEC + DEC // 2, :middle]
-    dec_out[DEC // 2 :, LANES:] = full_ref[DEC : DEC + DEC // 2, middle:]
-    coarse_out[...] = full_ref[DEC + DEC // 2 : PACKED]
+                full_ref[pl.ds(row, ROWS), :] = other_ref[4 * side + index, xr].astype(F32)
+    middle, part = LANES // 2, DEC // 2
+    copies = [pltpu.make_async_copy(full_ref.at[pl.ds(DEC + part, DEC)], coarse_hbm, sent.at[0])]
+    copies[0].start()
+    for index in range(2):
+        rows = slice(index * part, (index + 1) * part)
+        dec_ref[rows, :LANES] = full_ref[rows]
+        dec_ref[rows, LANES:] = full_ref[DEC : DEC + part, index * middle : (index + 1) * middle]
+        window = pl.ds(index * part, part)
+        copies.append(pltpu.make_async_copy(dec_ref.at[window], dec_hbm.at[window], sent.at[1 + index]))
+        copies[-1].start()
+    for copy in copies:
+        copy.wait()
 
 
 def swap(value, axis, flip):
@@ -388,7 +390,7 @@
     )
 
     block = (SKIP, LANES)
-    face_y, corner = (FACE_Y,) + block, (2,) + block
+    face_y, rim = (FACE_Y,) + block, (RIM,) + block
     fine = (BLOCKS,) + block
     skip, cot, pooled, xedge, xmid, oedge, omid = call(
         split_kernel, "split_blocks",
@@ -411,11 +413,11 @@
     )
     yone, ytwo = swap_side(yone, "gy", 0), swap_side(ytwo, "gy", 1)
     chunks = (4, 4, ROWS, LANES)
-    send, keep, jskip, own, rtwo = call(
+    send, keep, jskip, own, rone, rtwo = call(
         grads_kernel, "local_grads",
         (
-            ((SENT + 2 * SKIP, LANES), BF16), (chunks, F32), (fine, F32),
-            ((3 * BLOCKS_C,) + block, F32), (corner, BF16),
+            ((SENT, LANES), BF16), (chunks, F32), (fine, F32),
+            ((BLOCKS_C + 2,) + block, F32), (rim, BF16), (rim, BF16),
         ),
         (
             ((DEC, BLOCKS * LANES), BF16),
@@ -429,46 +431,47 @@
         w_join, w_pre, w_back,
     )
 
-    send, rtwo = swap(send, "gy", 1), swap_side(rtwo, "gy", 1)
-    part = keep + wide(send[:SENT].reshape(chunks))
-    rone = send[SENT:].reshape(corner)
+    part = keep + wide(swap(send, "gy", 1).reshape(chunks))
     a, b = part[:, :2], part[:, 2:]
     a_got = swap_y(jnp.stack([a[A_FIRST], a[2]]).astype(BF16), A_FIRST)
     b_got = swap_y(jnp.stack([b[B_FIRST], b[2]]).astype(BF16), B_FIRST)
-    a_got, b_got, rone, rtwo = together((a_got, b_got, rone, rtwo))
-    rows, qone, qtwo = call(
-        fold_kernel, "fold_rim", (((BLOCKS_C,) + block, F32), (corner, BF16), (corner, BF16)), (), 8, (100_000, 600_000),
-        own, rone, rtwo,
-    )
+    a_got, b_got = together((a_got, b_got))
     a_own, a_leave = a[0] + wide(a_got[0]), a[A_SECOND] + wide(a_got[1])
     b_own, b_leave = b[0] + wide(b_got[0]), b[B_SECOND] + wide(b_got[1])
     a_got, b_got = swap_y(a_leave.astype(BF16), A_SECOND), swap_y(b_leave.astype(BF16), B_SECOND)
-    a_got, b_got, rows, qone, qtwo = together((a_got, b_got, rows, qone, qtwo))
+    a_got, b_got = together((a_got, b_got))
+    rtwo = swap_side(rtwo, "gx", 1)
     part = jnp.concatenate([a_own + wide(a_got), b_own + wide(b_got)])
     leave = part.astype(BF16)
-    got = swap(jnp.concatenate([leave[1], qone.reshape(2 * SKIP, LANES)]), "gx", 1)
-    got = [got[:ROWS], swap(leave[2], "gx", 2), swap(leave[3], "gx", 3), got[ROWS:].reshape(corner)]
-    *got, qone = together(got)
+    got = swap(jnp.concatenate([leave[1], rone.reshape(RIM * SKIP, LANES)]), "gx", 1)
+    got = [got[:ROWS], swap(leave[2], "gx", 2), swap(leave[3], "gx", 3), got[ROWS:].reshape(rim)]
+    *got, rone, rtwo = together((*got, rtwo))
+    rows, qone, qtwo = call(
+        fold_kernel, "fold_rim", (((BLOCKS_C,) + block, F32), (block, BF16), (block, BF16)), (), 8, (100_000, 600_000),
+        own, rone, rtwo,
+    )
     part = (part[0] + wide(got[0])) + (wide(got[1]) + wide(got[2]))
     mine = part.astype(BF16)
     got = [swap_z(mine, flip) for flip in (1, 2, 3)]
+    *got, rows, qone, qtwo = together((*got, rows, qone, qtwo))
     part = (wide(mine) + wide(got[0])) + (wide(got[1]) + wide(got[2]))
-    part = (part + swap(part, "gy", 9)).astype(BF16)
+    got, qone, qtwo = together((swap(part, "gy", 9), swap_side(qone, "gy", 0), swap_side(qtwo, "gy", 1)))
+    part = (part + got).astype(BF16)
     got = together([swap(part, "gx", flip) for flip in (1, 3, 2)])
     part = jnp.stack([part, got[0], got[2], got[1]])
     a, b = part[:2], part[2:]
     a_got, b_got = together((swap_y(a, A_SECOND), swap_y(b, B_SECOND)))
     a_near, b_near = jnp.stack([a, a_got]), jnp.stack([b, b_got])
-    qtwo = swap_side(qtwo, "gx", 1)
-    a_far, b_far, qtwo = together((swap_y(a_near, A_FIRST), swap_y(b_near, B_FIRST), qtwo))
+    a_far, b_far = together((swap_y(a_near, A_FIRST), swap_y(b_near, B_FIRST)))
     other = swap(jnp.concatenate([a_near, a_far, b_near, b_far]), "gy", 1)
     (skip_grad,) = call(
         skip_kernel, "skip_gradient", (((SKIP, SIZE_X, SIZE_Y, LANES), BF16),), (((SKIP * BLOCKS, LANES), F32),),
         8, (1_000_000, 1_000_000), rows, qone, qtwo, jskip,
     )
     dec, coarse = call(
-        unpack_kernel, "unpack", (((DEC, JOINED), F32), ((DEC, COARSE), F32)), (((CHUNKS * ROWS, LANES), F32),),
-        16, (1_000_000, 5_000_000), a_near, a_far, b_near, b_far, other,
+        unpack_kernel, "unpack", (((DEC, JOINED), F32), ((DEC, COARSE), F32)),
+        (((CHUNKS * ROWS, LANES), F32), ((DEC, JOINED), F32), pltpu.SemaphoreType.DMA((3,))),
+        16, (1_000_000, 5_000_000), a_near, a_far, b_near, b_far, other, gives=pltpu.HBM,
     )
     return (
         skip_grad,

time: 91.6 us -> 92.6 us (1.011)
  starting transfers between devices: 46.5 us -> 48 us
    ppermute x17, starting transfers between devices: 19.3 us -> 20.7 us  [swap(): lax.ppermute(value, axis, [(i, i ^ flip) for i in range(lax.axis_size(axi...]
    ppermute x8 -> x9, waiting for transfers between devices: 6.54 us -> 5.64 us  [swap_side(): lax.ppermute(value, axis, [(i, partner(i, which, count)) for i in range(c...]
    ppermute x8 -> x9, starting transfers between devices: 18.6 us -> 19.2 us  [swap_side(): lax.ppermute(value, axis, [(i, partner(i, which, count)) for i in range(c...]
  transfers between devices with their start and end apart: 28 -> 29, of which waited for: 17 -> 20; matrix products, arithmetic and copies ran while one was open for 0% -> 0% of each run, Pallas kernels for 3% -> 3%
where the time goes in v5:
time: 92.6 us; the launch traced here: 92.5 us
  starting transfers between devices  48 us (52%)
  waiting for transfers between devices  31.1 us (34%)
  Pallas kernels  11.9 us (13%)
  between operations  1.04 us (1%)
    ppermute x17, starting transfers between devices, swap(): lax.ppermute(value, axis, [(i, i ^ flip) for i in range(lax.axis_size(axi...  20.7 us
    ppermute x17, waiting for transfers between devices, swap(): lax.ppermute(value, axis, [(i, i ^ flip) for i in range(lax.axis_size(axi...  20.3 us
    ppermute x9, starting transfers between devices, swap_side(): lax.ppermute(value, axis, [(i, partner(i, which, count)) for i in range(c...  19.2 us
    pallas_call x7, Pallas kernels, call(): pl.pallas_call(kernel, out_shape=tuple((jax.ShapeDtypeStruct(shape, dtype...  11.9 us
    ppermute x3, starting transfers between devices, swap_z(): return lax.ppermute(value, ('gx', 'gy'), pairs)  8.04 us
    ppermute x9, waiting for transfers between devices, swap_side(): lax.ppermute(value, axis, [(i, partner(i, which, count)) for i in range(c...  5.64 us
    ppermute x3, waiting for transfers between devices, swap_z(): return lax.ppermute(value, ('gx', 'gy'), pairs)  5.11 us
  transfers between devices with their start and end apart: 29, of which 20 were waited for; matrix products, arithmetic and copies ran while one was open for 0% of the time, Pallas kernels for 3%

profile of v5, /device:TPU:1, one launch (start us, length us, event | category | flops | bytes accessed | tf_op | source)
XLA Modules:
  0.0 92.5 jit_solution(12543921510557019827)
XLA Ops:
  2.1 9.1 %collective-permute-start = (bf16[3,64,128]{2,1,0:T(8,128)(2,1)S(1)}, bf16[3,64,128]{2,1,0:T(8,128)(2,1)S(1)}, u32[]{:S(2)}, u32[]{:S(2)}) collective-permute-start(bf16[3,64,128]{2,1,0:T(8,128)(2,1)S(1)} %get-tuple-element.54), channel_id=1, source_target_pairs={{0,240},{16,32},{32,16},{48,64},{64,48},{80,96},{96,80},{112,128},... | collective-permute-start | bytes 147464 | tf_op jit(solution)/shard_map/ppermute | solution.py:358
  12.7 1.7 %lay_weights.1 = (bf16[192,1728]{1,0:T(8,128)(2,1)S(1)}, bf16[128,1728]{1,0:T(8,128)(2,1)S(1)}, bf16[576,384]{1,0:T(8,128)(2,1)S(1)}) custom-call(bf16[1728,192]{1,0:T(8,128)(2,1)} %bitcast.56, bf16[1728,128]{1,0:T(8,128)(2,1)} %bitcast.58), custom_call_target="tpu_custom_call" | custom-call | flops 1000000 | bytes 2500000 | tf_op jit(solution)/shard_map/lay_weights/pallas_call | solution.py:121
  14.5 3.6 %collective-permute-start.4 = (bf16[6,64,128]{2,1,0:T(8,128)(2,1)S(1)}, bf16[6,64,128]{2,1,0:T(8,128)(2,1)S(1)}, u32[]{:S(2)}, u32[]{:S(2)}) collective-permute-start(bf16[6,64,128]{2,1,0:T(8,128)(2,1)S(1)} %get-tuple-element.61), channel_id=1, source_target_pairs={{0,15},{1,2},{2,1},{3,4},{4,3},{5,6},{6,5},{7,8},{8,7},{9,10},{10,... | collective-permute-start | bytes 294920 | tf_op jit(solution)/shard_map/ppermute | solution.py:358
  18.3 1.7 %collective-permute-done.1.xmid_ref = bf16[7,64,128]{2,1,0:T(8,128)(2,1)S(1)} collective-permute-done((bf16[7,64,128]{2,1,0:T(8,128)(2,1)S(1)}, bf16[7,64,128]{2,1,0:T(8,128)(2,1)S(1)}, u32[]{:S(2)}, u32[]{:S(2)}) %collective-permute-start.1) | collective-permute-done | bytes 114720 | tf_op jit(solution)/shard_map/ppermute | solution.py:358
  20.8 5.8 %local_grads.1 = (bf16[2176,128]{1,0:T(8,128)(2,1)S(1)}, f32[4,4,136,128]{3,2,1,0:T(8,128)S(1)}, f32[16,64,128]{2,1,0:T(8,128)S(1)}, f32[6,64,128]{2,1,0:T(8,128...) custom-call(bf16[16,64,128]{2,1,0:T(8,128)(2,1)S(1)} %get-tuple-element.51.skip_ref, ...), custom_call_target="tpu_custom_call" | custom-call | flops 3000000000 | bytes 8000000 | tf_op jit(solution)/shard_map/local_grads/pallas_call | solution.py:121
  26.6 2.5 %collective-permute-start.6 = (bf16[2176,128]{1,0:T(8,128)(2,1)S(1)}, bf16[2176,128]{1,0:T(8,128)(2,1)S(1)}, u32[]{:S(2)}, u32[]{:S(2)}) collective-permute-start(bf16[2176,128]{1,0:T(8,128)(2,1)S(1)} %get-tuple-element.64), channel_id=1, source_target_pairs={{0,1},{1,0},{2,3},{3,2},{4,5},{5,4},{6,7},{7,6},{8,9},{9,8},{10,11... | collective-permute-start | bytes 1671176 | tf_op jit(solution)/shard_map/ppermute | solution.py:345
  29.0 1.6 %collective-permute-done.6 = bf16[2176,128]{1,0:T(8,128)(2,1)S(1)} collective-permute-done((bf16[2176,128]{1,0:T(8,128)(2,1)S(1)}, bf16[2176,128]{1,0:T(8,128)(2,1)S(1)}, u32[]{:S(2)}, u32[]{:S(2)}) %collective-permute-start.6) | collective-permute-done | bytes 557088 | tf_op jit(solution)/shard_map/ppermute | solution.py:345
  30.8 3.0 %collective-permute-start.8 = (bf16[2,2,136,128]{3,2,1,0:T(8,128)(2,1)S(1)}, bf16[2,2,136,128]{3,2,1,0:T(8,128)(2,1)S(1)}, u32[]{:S(2)}, u32[]{:S(2)}) collective-permute-start(bf16[2,2,136,128]{3,2,1,0:T(8,128)(2,1)S(1)} %pad_maximum_fusion), channel_id=1, source_target_pairs={{0,7},{1,6},{2,5},{3,4},{4,3},{5,2},{6,1},{7,0},{8,15},{9,14},{10,... | collective-permute-start | bytes 417800 | tf_op jit(solution)/shard_map/ppermute | solution.py:345
  33.8 4.0 %collective-permute-done.8 = bf16[2,2,136,128]{3,2,1,0:T(8,128)(2,1)S(1)} collective-permute-done((bf16[2,2,136,128]{3,2,1,0:T(8,128)(2,1)S(1)}, bf16[2,2,136,128]{3,2,1,0:T(8,128)(2,1)S(1)}, u32[]{:S(2)}, u32[]{:S(2)}) %collective-permute-start.8) | collective-permute-done | bytes 139296 | tf_op jit(solution)/shard_map/ppermute | solution.py:345
  37.8 1.5 %collective-permute-done.7 = bf16[2,2,136,128]{3,2,1,0:T(8,128)(2,1)S(1)} collective-permute-done((bf16[2,2,136,128]{3,2,1,0:T(8,128)(2,1)S(1)}, bf16[2,2,136,128]{3,2,1,0:T(8,128)(2,1)S(1)}, u32[]{:S(2)}, u32[]{:S(2)}) %collective-permute-start.7) | collective-permute-done | bytes 139296 | tf_op jit(solution)/shard_map/ppermute | solution.py:345
  41.1 4.7 %collective-permute-start.14 = (bf16[3,64,128]{2,1,0:T(8,128)(2,1)S(1)}, bf16[3,64,128]{2,1,0:T(8,128)(2,1)S(1)}, u32[]{:S(2)}, u32[]{:S(2)}) collective-permute-start(bf16[3,64,128]{2,1,0:T(8,128)(2,1)S(1)} %get-tuple-element.70), channel_id=1, source_target_pairs={{0,240},{16,32},{32,16},{48,64},{64,48},{80,96},{96,80},{112,128},... | collective-permute-start | bytes 147464 | tf_op jit(solution)/shard_map/ppermute | solution.py:358
  46.1 3.1 %collective-permute-start.12 = (bf16[136,128]{1,0:T(8,128)(2,1)S(1)}, bf16[136,128]{1,0:T(8,128)(2,1)S(1)}, u32[]{:S(2)}, u32[]{:S(2)}) collective-permute-start(bf16[136,128]{1,0:T(8,128)(2,1)S(1)} %get-tuple-element.112), channel_id=1, source_target_pairs={{0,32},{16,48},{32,0},{48,16},{64,96},{80,112},{96,64},{112,80},{1... | collective-permute-start | bytes 104456 | tf_op jit(solution)/shard_map/ppermute | solution.py:345
  50.6 5.6 %collective-permute-start.17 = (bf16[136,128]{1,0:T(8,128)(2,1)S(1)}, bf16[136,128]{1,0:T(8,128)(2,1)S(1)}, u32[]{:S(2)}, u32[]{:S(2)}) collective-permute-start(bf16[136,128]{1,0:T(8,128)(2,1)S(1)} %fusion.11), channel_id=1, source_target_pairs={{0,193},{1,192},{2,195},{3,194},{4,197},{5,196},{6,199},{7,198},{8... | collective-permute-start | bytes 104456 | tf_op jit(solution)/shard_map/ppermute | solution.py:377
  56.7 1.9 %collective-permute-start.15 = (bf16[136,128]{1,0:T(8,128)(2,1)S(1)}, bf16[136,128]{1,0:T(8,128)(2,1)S(1)}, u32[]{:S(2)}, u32[]{:S(2)}) collective-permute-start(bf16[136,128]{1,0:T(8,128)(2,1)S(1)} %fusion.11), channel_id=1, source_target_pairs={{0,65},{1,64},{2,67},{3,66},{4,69},{5,68},{6,71},{7,70},{8,73},{9,... | collective-permute-start | bytes 104456 | tf_op jit(solution)/shard_map/ppermute | solution.py:377
  58.8 5.1 %collective-permute-done.16 = bf16[136,128]{1,0:T(8,128)(2,1)S(1)} collective-permute-done((bf16[136,128]{1,0:T(8,128)(2,1)S(1)}, bf16[136,128]{1,0:T(8,128)(2,1)S(1)}, u32[]{:S(2)}, u32[]{:S(2)}) %collective-permute-start.16) | collective-permute-done | bytes 34848 | tf_op jit(solution)/shard_map/ppermute | solution.py:377
  65.3 2.1 %collective-permute-done.20.ytwo_ref = bf16[64,128]{1,0:T(8,128)(2,1)S(1)} collective-permute-done((bf16[64,128]{1,0:T(8,128)(2,1)S(1)}, bf16[64,128]{1,0:T(8,128)(2,1)S(1)}, u32[]{:S(2)}, u32[]{:S(2)}) %collective-permute-start.20) | collective-permute-done | bytes 16416 | tf_op jit(solution)/shard_map/ppermute | solution.py:358
  68.8 1.6 %collective-permute-start.22 = (bf16[136,128]{1,0:T(8,128)(2,1)S(1)}, bf16[136,128]{1,0:T(8,128)(2,1)S(1)}, u32[]{:S(2)}, u32[]{:S(2)}) collective-permute-start(bf16[136,128]{1,0:T(8,128)(2,1)S(1)} %add_convert_fusion), channel_id=1, source_target_pairs={{0,48},{16,32},{32,16},{48,0},{64,112},{80,96},{96,80},{112,64},{1... | collective-permute-start | bytes 104456 | tf_op jit(solution)/shard_map/ppermute | solution.py:345
  70.5 1.6 %collective-permute-done.23 = bf16[136,128]{1,0:T(8,128)(2,1)S(1)} collective-permute-done((bf16[136,128]{1,0:T(8,128)(2,1)S(1)}, bf16[136,128]{1,0:T(8,128)(2,1)S(1)}, u32[]{:S(2)}, u32[]{:S(2)}) %collective-permute-start.23) | collective-permute-done | bytes 34848 | tf_op jit(solution)/shard_map/ppermute | solution.py:345
  73.3 2.5 %collective-permute-start.25 = (bf16[2,136,128]{2,1,0:T(8,128)(2,1)S(1)}, bf16[2,136,128]{2,1,0:T(8,128)(2,1)S(1)}, u32[]{:S(2)}, u32[]{:S(2)}) collective-permute-start(bf16[2,136,128]{2,1,0:T(8,128)(2,1)S(1)} %get-tuple-element.108), channel_id=1, source_target_pairs={{0,3},{1,2},{2,1},{3,0},{4,7},{5,6},{6,5},{7,4},{8,11},{9,10},{10,... | collective-permute-start | bytes 208904 | tf_op jit(solution)/shard_map/ppermute | solution.py:345
  77.7 3.1 %collective-permute-done.24 = bf16[2,136,128]{2,1,0:T(8,128)(2,1)S(1)} collective-permute-done((bf16[2,136,128]{2,1,0:T(8,128)(2,1)S(1)}, bf16[2,136,128]{2,1,0:T(8,128)(2,1)S(1)}, u32[]{:S(2)}, u32[]{:S(2)}) %collective-permute-start.24) | collective-permute-done | bytes 69664 | tf_op jit(solution)/shard_map/ppermute | solution.py:345
  80.9 2.0 %collective-permute-start.27 = (bf16[2,2,136,128]{3,2,1,0:T(8,128)(2,1)S(1)}, bf16[2,2,136,128]{3,2,1,0:T(8,128)(2,1)S(1)}, u32[]{:S(2)}, u32[]{:S(2)}) collective-permute-start(bf16[2,2,136,128]{3,2,1,0:T(8,128)(2,1)S(1)} %pad_maximum_fusion.2.b0_ref), channel_id=1, source_target_pairs={{0,7},{1,6},{2,5},{3,4},{4,3},{5,2},{6,1},{7,0},{8,15},{9,14},{10,... | collective-permute-start | bytes 417800 | tf_op jit(solution)/shard_map/ppermute | solution.py:345
  82.9 3.5 %collective-permute-done.26.a1_ref = bf16[2,2,136,128]{3,2,1,0:T(8,128)(2,1)S(1)} collective-permute-done((bf16[2,2,136,128]{3,2,1,0:T(8,128)(2,1)S(1)}, bf16[2,2,136,128]{3,2,1,0:T(8,128)(2,1)S(1)}, u32[]{:S(2)}, u32[]{:S(2)}) %collective-permute-start.26) | collective-permute-done | bytes 139296 | tf_op jit(solution)/shard_map/ppermute | solution.py:345
  87.2 1.8 %collective-permute-start.28 = (bf16[8,2,136,128]{3,2,1,0:T(8,128)(2,1)S(1)}, bf16[8,2,136,128]{3,2,1,0:T(8,128)(2,1)S(1)}, u32[]{:S(2)}, u32[]{:S(2)}) collective-permute-start(bf16[8,2,136,128]{3,2,1,0:T(8,128)(2,1)S(1)} %constant_dynamic-update-slice_fusion), channel_id=1, source_target_pairs={{0,1},{1,0},{2,3},{3,2},{4,5},{5,4},{6,7},{7,6},{8,9},{9,8},{10,11... | collective-permute-start | bytes 1671176 | tf_op jit(solution)/shard_map/ppermute | solution.py:345
  90.6 1.7 %unpack.1 = (f32[1728,192]{1,0:T(8,128)}, f32[1728,128]{1,0:T(8,128)}) custom-call(bf16[2,2,136,128]{3,2,1,0:T(8,128)(2,1)S(1)} %pad_maximum_fusion.1.a0_ref, bf16[2,2,136,128]{3,2,1,0:T(8,128)(2,1)S(1)} %collective-permute-done.26.a1_ref, bf16[2,2,136,128]{3,2,1,0:T(8,128)(2,1)S(1)} %pad_maximum_fusion.2.b0_ref, ...), custom_call_target="tpu_custom_call" | custom-call | flops 1000000 | bytes 5000000 | tf_op jit(solution)/shard_map/unpack/pallas_call | solution.py:121
  (65 shorter events, 16.8 us)
Async XLA Ops:
  2.1 12.3 %collective-permute-start = (bf16[3,64,128]{2,1,0:T(8,128)(2,1)S(1)}, bf16[3,64,128]{2,1,0:T(8,128)(2,1)S(1)}, u32[]{:S(2)}, u32[]{:S(2)}) collective-permute-start(bf16[3,64,128]{2,1,0:T(8,128)(2,1)S(1)} %get-tuple-element.54), channel_id=1, source_target_pairs={{0,240},{16,32},{32,16},{48,64},{64,48},{80,96},{96,80},{112,128},... | collective-permute-start | bytes 147464 | tf_op jit(solution)/shard_map/ppermute | solution.py:358
  11.2 8.8 %collective-permute-start.1 = (bf16[7,64,128]{2,1,0:T(8,128)(2,1)S(1)}, bf16[7,64,128]{2,1,0:T(8,128)(2,1)S(1)}, u32[]{:S(2)}, u32[]{:S(2)}) collective-permute-start(bf16[7,64,128]{2,1,0:T(8,128)(2,1)S(1)} %get-tuple-element.55), channel_id=1, source_target_pairs={{0,240},{16,32},{32,16},{48,64},{64,48},{80,96},{96,80},{112,128},... | collective-permute-start | bytes 344072 | tf_op jit(solution)/shard_map/ppermute | solution.py:358
  12.0 8.0 %collective-permute-start.3 = (bf16[7,64,128]{2,1,0:T(8,128)(2,1)S(1)}, bf16[7,64,128]{2,1,0:T(8,128)(2,1)S(1)}, u32[]{:S(2)}, u32[]{:S(2)}) collective-permute-start(bf16[7,64,128]{2,1,0:T(8,128)(2,1)S(1)} %get-tuple-element.57), channel_id=1, source_target_pairs={{0,16},{16,0},{32,48},{48,32},{64,80},{80,64},{96,112},{112,96},{1... | collective-permute-start | bytes 344072 | tf_op jit(solution)/shard_map/ppermute | solution.py:358
  14.5 6.2 %collective-permute-start.4 = (bf16[6,64,128]{2,1,0:T(8,128)(2,1)S(1)}, bf16[6,64,128]{2,1,0:T(8,128)(2,1)S(1)}, u32[]{:S(2)}, u32[]{:S(2)}) collective-permute-start(bf16[6,64,128]{2,1,0:T(8,128)(2,1)S(1)} %get-tuple-element.61), channel_id=1, source_target_pairs={{0,15},{1,2},{2,1},{3,4},{4,3},{5,6},{6,5},{7,8},{8,7},{9,10},{10,... | collective-permute-start | bytes 294920 | tf_op jit(solution)/shard_map/ppermute | solution.py:358
  26.6 4.0 %collective-permute-start.6 = (bf16[2176,128]{1,0:T(8,128)(2,1)S(1)}, bf16[2176,128]{1,0:T(8,128)(2,1)S(1)}, u32[]{:S(2)}, u32[]{:S(2)}) collective-permute-start(bf16[2176,128]{1,0:T(8,128)(2,1)S(1)} %get-tuple-element.64), channel_id=1, source_target_pairs={{0,1},{1,0},{2,3},{3,2},{4,5},{5,4},{6,7},{7,6},{8,9},{9,8},{10,11... | collective-permute-start | bytes 1671176 | tf_op jit(solution)/shard_map/ppermute | solution.py:345
  30.8 7.0 %collective-permute-start.8 = (bf16[2,2,136,128]{3,2,1,0:T(8,128)(2,1)S(1)}, bf16[2,2,136,128]{3,2,1,0:T(8,128)(2,1)S(1)}, u32[]{:S(2)}, u32[]{:S(2)}) collective-permute-start(bf16[2,2,136,128]{3,2,1,0:T(8,128)(2,1)S(1)} %pad_maximum_fusion), channel_id=1, source_target_pairs={{0,7},{1,6},{2,5},{3,4},{4,3},{5,2},{6,1},{7,0},{8,15},{9,14},{10,... | collective-permute-start | bytes 417800 | tf_op jit(solution)/shard_map/ppermute | solution.py:345
  33.8 5.4 %collective-permute-start.7 = (bf16[2,2,136,128]{3,2,1,0:T(8,128)(2,1)S(1)}, bf16[2,2,136,128]{3,2,1,0:T(8,128)(2,1)S(1)}, u32[]{:S(2)}, u32[]{:S(2)}) collective-permute-start(bf16[2,2,136,128]{3,2,1,0:T(8,128)(2,1)S(1)} %stack.56), channel_id=1, source_target_pairs={{0,3},{1,2},{2,1},{3,0},{4,7},{5,6},{6,5},{7,4},{8,11},{9,10},{10,... | collective-permute-start | bytes 417800 | tf_op jit(solution)/shard_map/ppermute | solution.py:345
  39.3 6.5 %collective-permute-start.10 = (bf16[2,136,128]{2,1,0:T(8,128)(2,1)S(1)}, bf16[2,136,128]{2,1,0:T(8,128)(2,1)S(1)}, u32[]{:S(2)}, u32[]{:S(2)}) collective-permute-start(bf16[2,136,128]{2,1,0:T(8,128)(2,1)S(1)} %get-tuple-element.103), channel_id=1, source_target_pairs={{0,3},{1,2},{2,1},{3,0},{4,7},{5,6},{6,5},{7,4},{8,11},{9,10},{10,... | collective-permute-start | bytes 208904 | tf_op jit(solution)/shard_map/ppermute | solution.py:345
  39.7 6.1 %collective-permute-start.9 = (bf16[2,136,128]{2,1,0:T(8,128)(2,1)S(1)}, bf16[2,136,128]{2,1,0:T(8,128)(2,1)S(1)}, u32[]{:S(2)}, u32[]{:S(2)}) collective-permute-start(bf16[2,136,128]{2,1,0:T(8,128)(2,1)S(1)} %get-tuple-element.104), channel_id=1, source_target_pairs={{0,7},{1,6},{2,5},{3,4},{4,3},{5,2},{6,1},{7,0},{8,15},{9,14},{10,... | collective-permute-start | bytes 208904 | tf_op jit(solution)/shard_map/ppermute | solution.py:345
  41.1 8.2 %collective-permute-start.14 = (bf16[3,64,128]{2,1,0:T(8,128)(2,1)S(1)}, bf16[3,64,128]{2,1,0:T(8,128)(2,1)S(1)}, u32[]{:S(2)}, u32[]{:S(2)}) collective-permute-start(bf16[3,64,128]{2,1,0:T(8,128)(2,1)S(1)} %get-tuple-element.70), channel_id=1, source_target_pairs={{0,240},{16,32},{32,16},{48,64},{64,48},{80,96},{96,80},{112,128},... | collective-permute-start | bytes 147464 | tf_op jit(solution)/shard_map/ppermute | solution.py:358
  45.9 3.4 %collective-permute-start.11 = (bf16[328,128]{1,0:T(8,128)(2,1)S(1)}, bf16[328,128]{1,0:T(8,128)(2,1)S(1)}, u32[]{:S(2)}, u32[]{:S(2)}) collective-permute-start(bf16[328,128]{1,0:T(8,128)(2,1)S(1)} %pad_maximum_fusion.3), channel_id=1, source_target_pairs={{0,16},{16,0},{32,48},{48,32},{64,80},{80,64},{96,112},{112,96},{1... | collective-permute-start | bytes 251912 | tf_op jit(solution)/shard_map/ppermute | solution.py:345
  46.0 4.1 %collective-permute-start.13 = (bf16[136,128]{1,0:T(8,128)(2,1)S(1)}, bf16[136,128]{1,0:T(8,128)(2,1)S(1)}, u32[]{:S(2)}, u32[]{:S(2)}) collective-permute-start(bf16[136,128]{1,0:T(8,128)(2,1)S(1)} %get-tuple-element.111), channel_id=1, source_target_pairs={{0,48},{16,32},{32,16},{48,0},{64,112},{80,96},{96,80},{112,64},{1... | collective-permute-start | bytes 104456 | tf_op jit(solution)/shard_map/ppermute | solution.py:345
  46.1 4.5 %collective-permute-start.12 = (bf16[136,128]{1,0:T(8,128)(2,1)S(1)}, bf16[136,128]{1,0:T(8,128)(2,1)S(1)}, u32[]{:S(2)}, u32[]{:S(2)}) collective-permute-start(bf16[136,128]{1,0:T(8,128)(2,1)S(1)} %get-tuple-element.112), channel_id=1, source_target_pairs={{0,32},{16,48},{32,0},{48,16},{64,96},{80,112},{96,64},{112,80},{1... | collective-permute-start | bytes 104456 | tf_op jit(solution)/shard_map/ppermute | solution.py:345
  50.6 8.2 %collective-permute-start.17 = (bf16[136,128]{1,0:T(8,128)(2,1)S(1)}, bf16[136,128]{1,0:T(8,128)(2,1)S(1)}, u32[]{:S(2)}, u32[]{:S(2)}) collective-permute-start(bf16[136,128]{1,0:T(8,128)(2,1)S(1)} %fusion.11), channel_id=1, source_target_pairs={{0,193},{1,192},{2,195},{3,194},{4,197},{5,196},{6,199},{7,198},{8... | collective-permute-start | bytes 104456 | tf_op jit(solution)/shard_map/ppermute | solution.py:377
  56.2 7.7 %collective-permute-start.16 = (bf16[136,128]{1,0:T(8,128)(2,1)S(1)}, bf16[136,128]{1,0:T(8,128)(2,1)S(1)}, u32[]{:S(2)}, u32[]{:S(2)}) collective-permute-start(bf16[136,128]{1,0:T(8,128)(2,1)S(1)} %fusion.11), channel_id=1, source_target_pairs={{0,128},{1,129},{2,130},{3,131},{4,132},{5,133},{6,134},{7,135},{8... | collective-permute-start | bytes 104456 | tf_op jit(solution)/shard_map/ppermute | solution.py:377
  56.7 7.1 %collective-permute-start.15 = (bf16[136,128]{1,0:T(8,128)(2,1)S(1)}, bf16[136,128]{1,0:T(8,128)(2,1)S(1)}, u32[]{:S(2)}, u32[]{:S(2)}) collective-permute-start(bf16[136,128]{1,0:T(8,128)(2,1)S(1)} %fusion.11), channel_id=1, source_target_pairs={{0,65},{1,64},{2,67},{3,66},{4,69},{5,68},{6,71},{7,70},{8,73},{9,... | collective-permute-start | bytes 104456 | tf_op jit(solution)/shard_map/ppermute | solution.py:377
  63.9 3.8 %collective-permute-start.18 = (f32[136,128]{1,0:T(8,128)S(1)}, f32[136,128]{1,0:T(8,128)S(1)}, u32[]{:S(2)}, u32[]{:S(2)}) collective-permute-start(f32[136,128]{1,0:T(8,128)S(1)} %add_add_fusion), channel_id=1, source_target_pairs={{0,9},{1,8},{2,11},{3,10},{4,13},{5,12},{6,15},{7,14},{8,1},{9,0},... | collective-permute-start | bytes 208904 | tf_op jit(solution)/shard_map/ppermute | solution.py:345
  67.7 4.4 %collective-permute-start.23 = (bf16[136,128]{1,0:T(8,128)(2,1)S(1)}, bf16[136,128]{1,0:T(8,128)(2,1)S(1)}, u32[]{:S(2)}, u32[]{:S(2)}) collective-permute-start(bf16[136,128]{1,0:T(8,128)(2,1)S(1)} %add_convert_fusion), channel_id=1, source_target_pairs={{0,32},{16,48},{32,0},{48,16},{64,96},{80,112},{96,64},{112,80},{1... | collective-permute-start | bytes 104456 | tf_op jit(solution)/shard_map/ppermute | solution.py:345
  68.8 4.0 %collective-permute-start.22 = (bf16[136,128]{1,0:T(8,128)(2,1)S(1)}, bf16[136,128]{1,0:T(8,128)(2,1)S(1)}, u32[]{:S(2)}, u32[]{:S(2)}) collective-permute-start(bf16[136,128]{1,0:T(8,128)(2,1)S(1)} %add_convert_fusion), channel_id=1, source_target_pairs={{0,48},{16,32},{32,16},{48,0},{64,112},{80,96},{96,80},{112,64},{1... | collective-permute-start | bytes 104456 | tf_op jit(solution)/shard_map/ppermute | solution.py:345
  73.3 4.5 %collective-permute-start.25 = (bf16[2,136,128]{2,1,0:T(8,128)(2,1)S(1)}, bf16[2,136,128]{2,1,0:T(8,128)(2,1)S(1)}, u32[]{:S(2)}, u32[]{:S(2)}) collective-permute-start(bf16[2,136,128]{2,1,0:T(8,128)(2,1)S(1)} %get-tuple-element.108), channel_id=1, source_target_pairs={{0,3},{1,2},{2,1},{3,0},{4,7},{5,6},{6,5},{7,4},{8,11},{9,10},{10,... | collective-permute-start | bytes 208904 | tf_op jit(solution)/shard_map/ppermute | solution.py:345
  75.7 5.0 %collective-permute-start.24 = (bf16[2,136,128]{2,1,0:T(8,128)(2,1)S(1)}, bf16[2,136,128]{2,1,0:T(8,128)(2,1)S(1)}, u32[]{:S(2)}, u32[]{:S(2)}) collective-permute-start(bf16[2,136,128]{2,1,0:T(8,128)(2,1)S(1)} %get-tuple-element.110), channel_id=1, source_target_pairs={{0,7},{1,6},{2,5},{3,4},{4,3},{5,2},{6,1},{7,0},{8,15},{9,14},{10,... | collective-permute-start | bytes 208904 | tf_op jit(solution)/shard_map/ppermute | solution.py:345
  80.8 5.6 %collective-permute-start.26 = (bf16[2,2,136,128]{3,2,1,0:T(8,128)(2,1)S(1)}, bf16[2,2,136,128]{3,2,1,0:T(8,128)(2,1)S(1)}, u32[]{:S(2)}, u32[]{:S(2)}) collective-permute-start(bf16[2,2,136,128]{3,2,1,0:T(8,128)(2,1)S(1)} %pad_maximum_fusion.1.a0_ref), channel_id=1, source_target_pairs={{0,3},{1,2},{2,1},{3,0},{4,7},{5,6},{6,5},{7,4},{8,11},{9,10},{10,... | collective-permute-start | bytes 417800 | tf_op jit(solution)/shard_map/ppermute | solution.py:345
  80.9 6.2 %collective-permute-start.27 = (bf16[2,2,136,128]{3,2,1,0:T(8,128)(2,1)S(1)}, bf16[2,2,136,128]{3,2,1,0:T(8,128)(2,1)S(1)}, u32[]{:S(2)}, u32[]{:S(2)}) collective-permute-start(bf16[2,2,136,128]{3,2,1,0:T(8,128)(2,1)S(1)} %pad_maximum_fusion.2.b0_ref), channel_id=1, source_target_pairs={{0,7},{1,6},{2,5},{3,4},{4,3},{5,2},{6,1},{7,0},{8,15},{9,14},{10,... | collective-permute-start | bytes 417800 | tf_op jit(solution)/shard_map/ppermute | solution.py:345
  87.2 3.4 %collective-permute-start.28 = (bf16[8,2,136,128]{3,2,1,0:T(8,128)(2,1)S(1)}, bf16[8,2,136,128]{3,2,1,0:T(8,128)(2,1)S(1)}, u32[]{:S(2)}, u32[]{:S(2)}) collective-permute-start(bf16[8,2,136,128]{3,2,1,0:T(8,128)(2,1)S(1)} %constant_dynamic-update-slice_fusion), channel_id=1, source_target_pairs={{0,1},{1,0},{2,3},{3,2},{4,5},{5,4},{6,7},{7,6},{8,9},{9,8},{10,11... | collective-permute-start | bytes 1671176 | tf_op jit(solution)/shard_map/ppermute | solution.py:345
  (5 other events, 13.1 us)

commit v6 on v5

--- a/solution.py
+++ b/solution.py
@@ -455,14 +455,13 @@
     got = [swap_z(mine, flip) for flip in (1, 2, 3)]
     *got, rows, qone, qtwo = together((*got, rows, qone, qtwo))
     part = (wide(mine) + wide(got[0])) + (wide(got[1]) + wide(got[2]))
-    got, qone, qtwo = together((swap(part, "gy", 9), swap_side(qone, "gy", 0), swap_side(qtwo, "gy", 1)))
-    part = (part + got).astype(BF16)
+    part = (part + swap(part, "gy", 9)).astype(BF16)
     got = together([swap(part, "gx", flip) for flip in (1, 3, 2)])
     part = jnp.stack([part, got[0], got[2], got[1]])
     a, b = part[:2], part[2:]
     a_got, b_got = together((swap_y(a, A_SECOND), swap_y(b, B_SECOND)))
     a_near, b_near = jnp.stack([a, a_got]), jnp.stack([b, b_got])
-    a_far, b_far = together((swap_y(a_near, A_FIRST), swap_y(b_near, B_FIRST)))
+    a_far, b_far, qone, qtwo = together((swap_y(a_near, A_FIRST), swap_y(b_near, B_FIRST), swap_side(qone, "gy", 0), swap_side(qtwo, "gy", 1)))
     other = swap(jnp.concatenate([a_near, a_far, b_near, b_far]), "gy", 1)
     (skip_grad,) = call(
         skip_kernel, "skip_gradient", (((SKIP, SIZE_X, SIZE_Y, LANES), BF16),), (((SKIP * BLOCKS, LANES), F32),),

time: 92.6 us -> 91.3 us (0.986)
  starting transfers between devices: 48 us -> 45.8 us
    ppermute x17, waiting for transfers between devices: 20.3 us -> 24.4 us  [swap(): lax.ppermute(value, axis, [(i, i ^ flip) for i in range(lax.axis_size(axi...]
    ppermute x17, starting transfers between devices: 20.7 us -> 17.5 us  [swap(): lax.ppermute(value, axis, [(i, i ^ flip) for i in range(lax.axis_size(axi...]
    ppermute x9, waiting for transfers between devices: 5.64 us -> 2.5 us  [swap_side(): lax.ppermute(value, axis, [(i, partner(i, which, count)) for i in range(c...]
    ppermute x9, starting transfers between devices: 19.2 us -> 20.2 us  [swap_side(): lax.ppermute(value, axis, [(i, partner(i, which, count)) for i in range(c...]
  transfers between devices with their start and end apart: 29 -> 29, of which waited for: 20 -> 18; matrix products, arithmetic and copies ran while one was open for 0% -> 0% of each run, Pallas kernels for 3% -> 3%
where the time goes in v6:
time: 91.3 us; the launch traced here: 91.2 us
  starting transfers between devices  45.8 us (50%)
  waiting for transfers between devices  32 us (35%)
  Pallas kernels  11.9 us (13%)
  between operations  1.04 us (1%)
    ppermute x17, waiting for transfers between devices, swap(): lax.ppermute(value, axis, [(i, i ^ flip) for i in range(lax.axis_size(axi...  24.4 us
    ppermute x9, starting transfers between devices, swap_side(): lax.ppermute(value, axis, [(i, partner(i, which, count)) for i in range(c...  20.2 us
    ppermute x17, starting transfers between devices, swap(): lax.ppermute(value, axis, [(i, i ^ flip) for i in range(lax.axis_size(axi...  17.5 us
    pallas_call x7, Pallas kernels, call(): pl.pallas_call(kernel, out_shape=tuple((jax.ShapeDtypeStruct(shape, dtype...  11.9 us
    ppermute x3, starting transfers between devices, swap_z(): return lax.ppermute(value, ('gx', 'gy'), pairs)  8.04 us
    ppermute x3, waiting for transfers between devices, swap_z(): return lax.ppermute(value, ('gx', 'gy'), pairs)  5.11 us
    ppermute x9, waiting for transfers between devices, swap_side(): lax.ppermute(value, axis, [(i, partner(i, which, count)) for i in range(c...  2.5 us
  transfers between devices with their start and end apart: 29, of which 18 were waited for; matrix products, arithmetic and copies ran while one was open for 0% of the time, Pallas kernels for 3%

profile of v6, /device:TPU:1, one launch (start us, length us, event | category | flops | bytes accessed | tf_op | source)
XLA Modules:
  0.0 91.2 jit_solution(986131357257837197)
XLA Ops:
  0.6 1.4 %split_blocks.1 = (bf16[16,64,128]{2,1,0:T(8,128)(2,1)S(1)}, bf16[16,64,128]{2,1,0:T(8,128)(2,1)S(1)}, bf16[4,64,128]{2,1,0:T(8,128)(2,1)S(1)}, bf16[3,64,128]{2...) custom-call(bf16[64,2,8,128]{3,2,1,0:T(8,128)(2,1)} %skip_hbm.1, ...), custom_call_target="tpu_custom_call" | custom-call | flops 1000000 | bytes 1500000 | tf_op jit(solution)/shard_map/split_blocks/pallas_call | solution.py:121
  2.1 9.1 %collective-permute-start = (bf16[3,64,128]{2,1,0:T(8,128)(2,1)S(1)}, bf16[3,64,128]{2,1,0:T(8,128)(2,1)S(1)}, u32[]{:S(2)}, u32[]{:S(2)}) collective-permute-start(bf16[3,64,128]{2,1,0:T(8,128)(2,1)S(1)} %get-tuple-element.53), channel_id=1, source_target_pairs={{0,240},{16,32},{32,16},{48,64},{64,48},{80,96},{96,80},{112,128},... | collective-permute-start | bytes 147464 | tf_op jit(solution)/shard_map/ppermute | solution.py:358
  12.7 1.7 %lay_weights.1 = (bf16[192,1728]{1,0:T(8,128)(2,1)S(1)}, bf16[128,1728]{1,0:T(8,128)(2,1)S(1)}, bf16[576,384]{1,0:T(8,128)(2,1)S(1)}) custom-call(bf16[1728,192]{1,0:T(8,128)(2,1)} %bitcast.56, bf16[1728,128]{1,0:T(8,128)(2,1)} %bitcast.58), custom_call_target="tpu_custom_call" | custom-call | flops 1000000 | bytes 2500000 | tf_op jit(solution)/shard_map/lay_weights/pallas_call | solution.py:121
  14.5 3.6 %collective-permute-start.4 = (bf16[6,64,128]{2,1,0:T(8,128)(2,1)S(1)}, bf16[6,64,128]{2,1,0:T(8,128)(2,1)S(1)}, u32[]{:S(2)}, u32[]{:S(2)}) collective-permute-start(bf16[6,64,128]{2,1,0:T(8,128)(2,1)S(1)} %get-tuple-element.60), channel_id=1, source_target_pairs={{0,15},{1,2},{2,1},{3,4},{4,3},{5,6},{6,5},{7,8},{8,7},{9,10},{10,... | collective-permute-start | bytes 294920 | tf_op jit(solution)/shard_map/ppermute | solution.py:358
  18.3 1.7 %collective-permute-done.1.xmid_ref = bf16[7,64,128]{2,1,0:T(8,128)(2,1)S(1)} collective-permute-done((bf16[7,64,128]{2,1,0:T(8,128)(2,1)S(1)}, bf16[7,64,128]{2,1,0:T(8,128)(2,1)S(1)}, u32[]{:S(2)}, u32[]{:S(2)}) %collective-permute-start.1) | collective-permute-done | bytes 114720 | tf_op jit(solution)/shard_map/ppermute | solution.py:358
  20.8 5.8 %local_grads.1 = (bf16[2176,128]{1,0:T(8,128)(2,1)S(1)}, f32[4,4,136,128]{3,2,1,0:T(8,128)S(1)}, f32[16,64,128]{2,1,0:T(8,128)S(1)}, f32[6,64,128]{2,1,0:T(8,128...) custom-call(bf16[16,64,128]{2,1,0:T(8,128)(2,1)S(1)} %get-tuple-element.50.skip_ref, ...), custom_call_target="tpu_custom_call" | custom-call | flops 3000000000 | bytes 8000000 | tf_op jit(solution)/shard_map/local_grads/pallas_call | solution.py:121
  26.6 2.5 %collective-permute-start.6 = (bf16[2176,128]{1,0:T(8,128)(2,1)S(1)}, bf16[2176,128]{1,0:T(8,128)(2,1)S(1)}, u32[]{:S(2)}, u32[]{:S(2)}) collective-permute-start(bf16[2176,128]{1,0:T(8,128)(2,1)S(1)} %get-tuple-element.63), channel_id=1, source_target_pairs={{0,1},{1,0},{2,3},{3,2},{4,5},{5,4},{6,7},{7,6},{8,9},{9,8},{10,11... | collective-permute-start | bytes 1671176 | tf_op jit(solution)/shard_map/ppermute | solution.py:345
  29.0 1.6 %collective-permute-done.6 = bf16[2176,128]{1,0:T(8,128)(2,1)S(1)} collective-permute-done((bf16[2176,128]{1,0:T(8,128)(2,1)S(1)}, bf16[2176,128]{1,0:T(8,128)(2,1)S(1)}, u32[]{:S(2)}, u32[]{:S(2)}) %collective-permute-start.6) | collective-permute-done | bytes 557088 | tf_op jit(solution)/shard_map/ppermute | solution.py:345
  30.8 3.0 %collective-permute-start.8 = (bf16[2,2,136,128]{3,2,1,0:T(8,128)(2,1)S(1)}, bf16[2,2,136,128]{3,2,1,0:T(8,128)(2,1)S(1)}, u32[]{:S(2)}, u32[]{:S(2)}) collective-permute-start(bf16[2,2,136,128]{3,2,1,0:T(8,128)(2,1)S(1)} %pad_maximum_fusion), channel_id=1, source_target_pairs={{0,7},{1,6},{2,5},{3,4},{4,3},{5,2},{6,1},{7,0},{8,15},{9,14},{10,... | collective-permute-start | bytes 417800 | tf_op jit(solution)/shard_map/ppermute | solution.py:345
  33.8 4.0 %collective-permute-done.8 = bf16[2,2,136,128]{3,2,1,0:T(8,128)(2,1)S(1)} collective-permute-done((bf16[2,2,136,128]{3,2,1,0:T(8,128)(2,1)S(1)}, bf16[2,2,136,128]{3,2,1,0:T(8,128)(2,1)S(1)}, u32[]{:S(2)}, u32[]{:S(2)}) %collective-permute-start.8) | collective-permute-done | bytes 139296 | tf_op jit(solution)/shard_map/ppermute | solution.py:345
  37.8 1.5 %collective-permute-done.7 = bf16[2,2,136,128]{3,2,1,0:T(8,128)(2,1)S(1)} collective-permute-done((bf16[2,2,136,128]{3,2,1,0:T(8,128)(2,1)S(1)}, bf16[2,2,136,128]{3,2,1,0:T(8,128)(2,1)S(1)}, u32[]{:S(2)}, u32[]{:S(2)}) %collective-permute-start.7) | collective-permute-done | bytes 139296 | tf_op jit(solution)/shard_map/ppermute | solution.py:345
  41.1 4.7 %collective-permute-start.14 = (bf16[3,64,128]{2,1,0:T(8,128)(2,1)S(1)}, bf16[3,64,128]{2,1,0:T(8,128)(2,1)S(1)}, u32[]{:S(2)}, u32[]{:S(2)}) collective-permute-start(bf16[3,64,128]{2,1,0:T(8,128)(2,1)S(1)} %get-tuple-element.69), channel_id=1, source_target_pairs={{0,240},{16,32},{32,16},{48,64},{64,48},{80,96},{96,80},{112,128},... | collective-permute-start | bytes 147464 | tf_op jit(solution)/shard_map/ppermute | solution.py:358
  46.1 3.1 %collective-permute-start.12 = (bf16[136,128]{1,0:T(8,128)(2,1)S(1)}, bf16[136,128]{1,0:T(8,128)(2,1)S(1)}, u32[]{:S(2)}, u32[]{:S(2)}) collective-permute-start(bf16[136,128]{1,0:T(8,128)(2,1)S(1)} %get-tuple-element.110), channel_id=1, source_target_pairs={{0,32},{16,48},{32,0},{48,16},{64,96},{80,112},{96,64},{112,80},{1... | collective-permute-start | bytes 104456 | tf_op jit(solution)/shard_map/ppermute | solution.py:345
  50.6 5.6 %collective-permute-start.17 = (bf16[136,128]{1,0:T(8,128)(2,1)S(1)}, bf16[136,128]{1,0:T(8,128)(2,1)S(1)}, u32[]{:S(2)}, u32[]{:S(2)}) collective-permute-start(bf16[136,128]{1,0:T(8,128)(2,1)S(1)} %fusion.11), channel_id=1, source_target_pairs={{0,193},{1,192},{2,195},{3,194},{4,197},{5,196},{6,199},{7,198},{8... | collective-permute-start | bytes 104456 | tf_op jit(solution)/shard_map/ppermute | solution.py:377
  56.7 1.9 %collective-permute-start.15 = (bf16[136,128]{1,0:T(8,128)(2,1)S(1)}, bf16[136,128]{1,0:T(8,128)(2,1)S(1)}, u32[]{:S(2)}, u32[]{:S(2)}) collective-permute-start(bf16[136,128]{1,0:T(8,128)(2,1)S(1)} %fusion.11), channel_id=1, source_target_pairs={{0,65},{1,64},{2,67},{3,66},{4,69},{5,68},{6,71},{7,70},{8,73},{9,... | collective-permute-start | bytes 104456 | tf_op jit(solution)/shard_map/ppermute | solution.py:377
  58.8 5.1 %collective-permute-done.16 = bf16[136,128]{1,0:T(8,128)(2,1)S(1)} collective-permute-done((bf16[136,128]{1,0:T(8,128)(2,1)S(1)}, bf16[136,128]{1,0:T(8,128)(2,1)S(1)}, u32[]{:S(2)}, u32[]{:S(2)}) %collective-permute-start.16) | collective-permute-done | bytes 34848 | tf_op jit(solution)/shard_map/ppermute | solution.py:377
  64.0 3.7 %collective-permute-done.18 = f32[136,128]{1,0:T(8,128)S(1)} collective-permute-done((f32[136,128]{1,0:T(8,128)S(1)}, f32[136,128]{1,0:T(8,128)S(1)}, u32[]{:S(2)}, u32[]{:S(2)}) %collective-permute-start.18) | collective-permute-done | bytes 69664 | tf_op jit(solution)/shard_map/ppermute | solution.py:345
  68.7 1.8 %collective-permute-start.20 = (bf16[136,128]{1,0:T(8,128)(2,1)S(1)}, bf16[136,128]{1,0:T(8,128)(2,1)S(1)}, u32[]{:S(2)}, u32[]{:S(2)}) collective-permute-start(bf16[136,128]{1,0:T(8,128)(2,1)S(1)} %add_convert_fusion), channel_id=1, source_target_pairs={{0,48},{16,32},{32,16},{48,0},{64,112},{80,96},{96,80},{112,64},{1... | collective-permute-start | bytes 104456 | tf_op jit(solution)/shard_map/ppermute | solution.py:345
  73.3 2.5 %collective-permute-start.23 = (bf16[2,136,128]{2,1,0:T(8,128)(2,1)S(1)}, bf16[2,136,128]{2,1,0:T(8,128)(2,1)S(1)}, u32[]{:S(2)}, u32[]{:S(2)}) collective-permute-start(bf16[2,136,128]{2,1,0:T(8,128)(2,1)S(1)} %get-tuple-element.106), channel_id=1, source_target_pairs={{0,3},{1,2},{2,1},{3,0},{4,7},{5,6},{6,5},{7,4},{8,11},{9,10},{10,... | collective-permute-start | bytes 208904 | tf_op jit(solution)/shard_map/ppermute | solution.py:345
  76.2 2.2 %collective-permute-done.23 = bf16[2,136,128]{2,1,0:T(8,128)(2,1)S(1)} collective-permute-done((bf16[2,136,128]{2,1,0:T(8,128)(2,1)S(1)}, bf16[2,136,128]{2,1,0:T(8,128)(2,1)S(1)}, u32[]{:S(2)}, u32[]{:S(2)}) %collective-permute-start.23) | collective-permute-done | bytes 69664 | tf_op jit(solution)/shard_map/ppermute | solution.py:345
  78.5 2.3 %collective-permute-done.22 = bf16[2,136,128]{2,1,0:T(8,128)(2,1)S(1)} collective-permute-done((bf16[2,136,128]{2,1,0:T(8,128)(2,1)S(1)}, bf16[2,136,128]{2,1,0:T(8,128)(2,1)S(1)}, u32[]{:S(2)}, u32[]{:S(2)}) %collective-permute-start.22) | collective-permute-done | bytes 69664 | tf_op jit(solution)/shard_map/ppermute | solution.py:345
  81.9 3.8 %collective-permute-done.24.a1_ref = bf16[2,2,136,128]{3,2,1,0:T(8,128)(2,1)S(1)} collective-permute-done((bf16[2,2,136,128]{3,2,1,0:T(8,128)(2,1)S(1)}, bf16[2,2,136,128]{3,2,1,0:T(8,128)(2,1)S(1)}, u32[]{:S(2)}, u32[]{:S(2)}) %collective-permute-start.24) | collective-permute-done | bytes 139296 | tf_op jit(solution)/shard_map/ppermute | solution.py:345
  85.7 1.5 %collective-permute-done.25.b1_ref = bf16[2,2,136,128]{3,2,1,0:T(8,128)(2,1)S(1)} collective-permute-done((bf16[2,2,136,128]{3,2,1,0:T(8,128)(2,1)S(1)}, bf16[2,2,136,128]{3,2,1,0:T(8,128)(2,1)S(1)}, u32[]{:S(2)}, u32[]{:S(2)}) %collective-permute-start.25) | collective-permute-done | bytes 139296 | tf_op jit(solution)/shard_map/ppermute | solution.py:345
  89.4 1.7 %unpack.1 = (f32[1728,192]{1,0:T(8,128)}, f32[1728,128]{1,0:T(8,128)}) custom-call(bf16[2,2,136,128]{3,2,1,0:T(8,128)(2,1)S(1)} %pad_maximum_fusion.1.a0_ref, bf16[2,2,136,128]{3,2,1,0:T(8,128)(2,1)S(1)} %collective-permute-done.24.a1_ref, bf16[2,2,136,128]{3,2,1,0:T(8,128)(2,1)S(1)} %pad_maximum_fusion.2.b0_ref, ...), custom_call_target="tpu_custom_call" | custom-call | flops 1000000 | bytes 5000000 | tf_op jit(solution)/shard_map/unpack/pallas_call | solution.py:121
  (65 shorter events, 14.5 us)
Async XLA Ops:
  2.1 12.3 %collective-permute-start = (bf16[3,64,128]{2,1,0:T(8,128)(2,1)S(1)}, bf16[3,64,128]{2,1,0:T(8,128)(2,1)S(1)}, u32[]{:S(2)}, u32[]{:S(2)}) collective-permute-start(bf16[3,64,128]{2,1,0:T(8,128)(2,1)S(1)} %get-tuple-element.53), channel_id=1, source_target_pairs={{0,240},{16,32},{32,16},{48,64},{64,48},{80,96},{96,80},{112,128},... | collective-permute-start | bytes 147464 | tf_op jit(solution)/shard_map/ppermute | solution.py:358
  11.2 8.8 %collective-permute-start.1 = (bf16[7,64,128]{2,1,0:T(8,128)(2,1)S(1)}, bf16[7,64,128]{2,1,0:T(8,128)(2,1)S(1)}, u32[]{:S(2)}, u32[]{:S(2)}) collective-permute-start(bf16[7,64,128]{2,1,0:T(8,128)(2,1)S(1)} %get-tuple-element.54), channel_id=1, source_target_pairs={{0,240},{16,32},{32,16},{48,64},{64,48},{80,96},{96,80},{112,128},... | collective-permute-start | bytes 344072 | tf_op jit(solution)/shard_map/ppermute | solution.py:358
  12.0 8.0 %collective-permute-start.3 = (bf16[7,64,128]{2,1,0:T(8,128)(2,1)S(1)}, bf16[7,64,128]{2,1,0:T(8,128)(2,1)S(1)}, u32[]{:S(2)}, u32[]{:S(2)}) collective-permute-start(bf16[7,64,128]{2,1,0:T(8,128)(2,1)S(1)} %get-tuple-element.56), channel_id=1, source_target_pairs={{0,16},{16,0},{32,48},{48,32},{64,80},{80,64},{96,112},{112,96},{1... | collective-permute-start | bytes 344072 | tf_op jit(solution)/shard_map/ppermute | solution.py:358
  14.5 6.2 %collective-permute-start.4 = (bf16[6,64,128]{2,1,0:T(8,128)(2,1)S(1)}, bf16[6,64,128]{2,1,0:T(8,128)(2,1)S(1)}, u32[]{:S(2)}, u32[]{:S(2)}) collective-permute-start(bf16[6,64,128]{2,1,0:T(8,128)(2,1)S(1)} %get-tuple-element.60), channel_id=1, source_target_pairs={{0,15},{1,2},{2,1},{3,4},{4,3},{5,6},{6,5},{7,8},{8,7},{9,10},{10,... | collective-permute-start | bytes 294920 | tf_op jit(solution)/shard_map/ppermute | solution.py:358
  26.6 4.0 %collective-permute-start.6 = (bf16[2176,128]{1,0:T(8,128)(2,1)S(1)}, bf16[2176,128]{1,0:T(8,128)(2,1)S(1)}, u32[]{:S(2)}, u32[]{:S(2)}) collective-permute-start(bf16[2176,128]{1,0:T(8,128)(2,1)S(1)} %get-tuple-element.63), channel_id=1, source_target_pairs={{0,1},{1,0},{2,3},{3,2},{4,5},{5,4},{6,7},{7,6},{8,9},{9,8},{10,11... | collective-permute-start | bytes 1671176 | tf_op jit(solution)/shard_map/ppermute | solution.py:345
  30.8 7.0 %collective-permute-start.8 = (bf16[2,2,136,128]{3,2,1,0:T(8,128)(2,1)S(1)}, bf16[2,2,136,128]{3,2,1,0:T(8,128)(2,1)S(1)}, u32[]{:S(2)}, u32[]{:S(2)}) collective-permute-start(bf16[2,2,136,128]{3,2,1,0:T(8,128)(2,1)S(1)} %pad_maximum_fusion), channel_id=1, source_target_pairs={{0,7},{1,6},{2,5},{3,4},{4,3},{5,2},{6,1},{7,0},{8,15},{9,14},{10,... | collective-permute-start | bytes 417800 | tf_op jit(solution)/shard_map/ppermute | solution.py:345
  33.8 5.4 %collective-permute-start.7 = (bf16[2,2,136,128]{3,2,1,0:T(8,128)(2,1)S(1)}, bf16[2,2,136,128]{3,2,1,0:T(8,128)(2,1)S(1)}, u32[]{:S(2)}, u32[]{:S(2)}) collective-permute-start(bf16[2,2,136,128]{3,2,1,0:T(8,128)(2,1)S(1)} %stack.56), channel_id=1, source_target_pairs={{0,3},{1,2},{2,1},{3,0},{4,7},{5,6},{6,5},{7,4},{8,11},{9,10},{10,... | collective-permute-start | bytes 417800 | tf_op jit(solution)/shard_map/ppermute | solution.py:345
  39.3 6.5 %collective-permute-start.10 = (bf16[2,136,128]{2,1,0:T(8,128)(2,1)S(1)}, bf16[2,136,128]{2,1,0:T(8,128)(2,1)S(1)}, u32[]{:S(2)}, u32[]{:S(2)}) collective-permute-start(bf16[2,136,128]{2,1,0:T(8,128)(2,1)S(1)} %get-tuple-element.101), channel_id=1, source_target_pairs={{0,3},{1,2},{2,1},{3,0},{4,7},{5,6},{6,5},{7,4},{8,11},{9,10},{10,... | collective-permute-start | bytes 208904 | tf_op jit(solution)/shard_map/ppermute | solution.py:345
  39.7 6.1 %collective-permute-start.9 = (bf16[2,136,128]{2,1,0:T(8,128)(2,1)S(1)}, bf16[2,136,128]{2,1,0:T(8,128)(2,1)S(1)}, u32[]{:S(2)}, u32[]{:S(2)}) collective-permute-start(bf16[2,136,128]{2,1,0:T(8,128)(2,1)S(1)} %get-tuple-element.102), channel_id=1, source_target_pairs={{0,7},{1,6},{2,5},{3,4},{4,3},{5,2},{6,1},{7,0},{8,15},{9,14},{10,... | collective-permute-start | bytes 208904 | tf_op jit(solution)/shard_map/ppermute | solution.py:345
  41.1 8.2 %collective-permute-start.14 = (bf16[3,64,128]{2,1,0:T(8,128)(2,1)S(1)}, bf16[3,64,128]{2,1,0:T(8,128)(2,1)S(1)}, u32[]{:S(2)}, u32[]{:S(2)}) collective-permute-start(bf16[3,64,128]{2,1,0:T(8,128)(2,1)S(1)} %get-tuple-element.69), channel_id=1, source_target_pairs={{0,240},{16,32},{32,16},{48,64},{64,48},{80,96},{96,80},{112,128},... | collective-permute-start | bytes 147464 | tf_op jit(solution)/shard_map/ppermute | solution.py:358
  46.0 4.1 %collective-permute-start.13 = (bf16[136,128]{1,0:T(8,128)(2,1)S(1)}, bf16[136,128]{1,0:T(8,128)(2,1)S(1)}, u32[]{:S(2)}, u32[]{:S(2)}) collective-permute-start(bf16[136,128]{1,0:T(8,128)(2,1)S(1)} %get-tuple-element.109), channel_id=1, source_target_pairs={{0,48},{16,32},{32,16},{48,0},{64,112},{80,96},{96,80},{112,64},{1... | collective-permute-start | bytes 104456 | tf_op jit(solution)/shard_map/ppermute | solution.py:345
  46.1 4.5 %collective-permute-start.12 = (bf16[136,128]{1,0:T(8,128)(2,1)S(1)}, bf16[136,128]{1,0:T(8,128)(2,1)S(1)}, u32[]{:S(2)}, u32[]{:S(2)}) collective-permute-start(bf16[136,128]{1,0:T(8,128)(2,1)S(1)} %get-tuple-element.110), channel_id=1, source_target_pairs={{0,32},{16,48},{32,0},{48,16},{64,96},{80,112},{96,64},{112,80},{1... | collective-permute-start | bytes 104456 | tf_op jit(solution)/shard_map/ppermute | solution.py:345
  50.6 8.2 %collective-permute-start.17 = (bf16[136,128]{1,0:T(8,128)(2,1)S(1)}, bf16[136,128]{1,0:T(8,128)(2,1)S(1)}, u32[]{:S(2)}, u32[]{:S(2)}) collective-permute-start(bf16[136,128]{1,0:T(8,128)(2,1)S(1)} %fusion.11), channel_id=1, source_target_pairs={{0,193},{1,192},{2,195},{3,194},{4,197},{5,196},{6,199},{7,198},{8... | collective-permute-start | bytes 104456 | tf_op jit(solution)/shard_map/ppermute | solution.py:377
  56.2 7.7 %collective-permute-start.16 = (bf16[136,128]{1,0:T(8,128)(2,1)S(1)}, bf16[136,128]{1,0:T(8,128)(2,1)S(1)}, u32[]{:S(2)}, u32[]{:S(2)}) collective-permute-start(bf16[136,128]{1,0:T(8,128)(2,1)S(1)} %fusion.11), channel_id=1, source_target_pairs={{0,128},{1,129},{2,130},{3,131},{4,132},{5,133},{6,134},{7,135},{8... | collective-permute-start | bytes 104456 | tf_op jit(solution)/shard_map/ppermute | solution.py:377
  56.7 7.1 %collective-permute-start.15 = (bf16[136,128]{1,0:T(8,128)(2,1)S(1)}, bf16[136,128]{1,0:T(8,128)(2,1)S(1)}, u32[]{:S(2)}, u32[]{:S(2)}) collective-permute-start(bf16[136,128]{1,0:T(8,128)(2,1)S(1)} %fusion.11), channel_id=1, source_target_pairs={{0,65},{1,64},{2,67},{3,66},{4,69},{5,68},{6,71},{7,70},{8,73},{9,... | collective-permute-start | bytes 104456 | tf_op jit(solution)/shard_map/ppermute | solution.py:377
  63.9 3.8 %collective-permute-start.18 = (f32[136,128]{1,0:T(8,128)S(1)}, f32[136,128]{1,0:T(8,128)S(1)}, u32[]{:S(2)}, u32[]{:S(2)}) collective-permute-start(f32[136,128]{1,0:T(8,128)S(1)} %add_add_fusion), channel_id=1, source_target_pairs={{0,9},{1,8},{2,11},{3,10},{4,13},{5,12},{6,15},{7,14},{8,1},{9,0},... | collective-permute-start | bytes 208904 | tf_op jit(solution)/shard_map/ppermute | solution.py:345
  67.7 4.4 %collective-permute-start.21 = (bf16[136,128]{1,0:T(8,128)(2,1)S(1)}, bf16[136,128]{1,0:T(8,128)(2,1)S(1)}, u32[]{:S(2)}, u32[]{:S(2)}) collective-permute-start(bf16[136,128]{1,0:T(8,128)(2,1)S(1)} %add_convert_fusion), channel_id=1, source_target_pairs={{0,32},{16,48},{32,0},{48,16},{64,96},{80,112},{96,64},{112,80},{1... | collective-permute-start | bytes 104456 | tf_op jit(solution)/shard_map/ppermute | solution.py:345
  68.7 4.0 %collective-permute-start.20 = (bf16[136,128]{1,0:T(8,128)(2,1)S(1)}, bf16[136,128]{1,0:T(8,128)(2,1)S(1)}, u32[]{:S(2)}, u32[]{:S(2)}) collective-permute-start(bf16[136,128]{1,0:T(8,128)(2,1)S(1)} %add_convert_fusion), channel_id=1, source_target_pairs={{0,48},{16,32},{32,16},{48,0},{64,112},{80,96},{96,80},{112,64},{1... | collective-permute-start | bytes 104456 | tf_op jit(solution)/shard_map/ppermute | solution.py:345
  70.5 11.4 %collective-permute-start.26 = (bf16[64,128]{1,0:T(8,128)(2,1)S(1)}, bf16[64,128]{1,0:T(8,128)(2,1)S(1)}, u32[]{:S(2)}, u32[]{:S(2)}) collective-permute-start(bf16[64,128]{1,0:T(8,128)(2,1)S(1)} %get-tuple-element.88), channel_id=1, source_target_pairs={{0,1},{1,0},{2,3},{3,2},{4,5},{5,4},{6,7},{7,6},{8,9},{9,8},{10,11... | collective-permute-start | bytes 49160 | tf_op jit(solution)/shard_map/ppermute | solution.py:358
  70.5 11.4 %collective-permute-start.27 = (bf16[64,128]{1,0:T(8,128)(2,1)S(1)}, bf16[64,128]{1,0:T(8,128)(2,1)S(1)}, u32[]{:S(2)}, u32[]{:S(2)}) collective-permute-start(bf16[64,128]{1,0:T(8,128)(2,1)S(1)} %get-tuple-element.89), channel_id=1, source_target_pairs={{0,15},{1,2},{2,1},{3,4},{4,3},{5,6},{6,5},{7,8},{8,7},{9,10},{10,... | collective-permute-start | bytes 49160 | tf_op jit(solution)/shard_map/ppermute | solution.py:358
  73.3 5.2 %collective-permute-start.23 = (bf16[2,136,128]{2,1,0:T(8,128)(2,1)S(1)}, bf16[2,136,128]{2,1,0:T(8,128)(2,1)S(1)}, u32[]{:S(2)}, u32[]{:S(2)}) collective-permute-start(bf16[2,136,128]{2,1,0:T(8,128)(2,1)S(1)} %get-tuple-element.106), channel_id=1, source_target_pairs={{0,3},{1,2},{2,1},{3,0},{4,7},{5,6},{6,5},{7,4},{8,11},{9,10},{10,... | collective-permute-start | bytes 208904 | tf_op jit(solution)/shard_map/ppermute | solution.py:345
  75.7 5.0 %collective-permute-start.22 = (bf16[2,136,128]{2,1,0:T(8,128)(2,1)S(1)}, bf16[2,136,128]{2,1,0:T(8,128)(2,1)S(1)}, u32[]{:S(2)}, u32[]{:S(2)}) collective-permute-start(bf16[2,136,128]{2,1,0:T(8,128)(2,1)S(1)} %get-tuple-element.108), channel_id=1, source_target_pairs={{0,7},{1,6},{2,5},{3,4},{4,3},{5,2},{6,1},{7,0},{8,15},{9,14},{10,... | collective-permute-start | bytes 208904 | tf_op jit(solution)/shard_map/ppermute | solution.py:345
  80.8 4.9 %collective-permute-start.24 = (bf16[2,2,136,128]{3,2,1,0:T(8,128)(2,1)S(1)}, bf16[2,2,136,128]{3,2,1,0:T(8,128)(2,1)S(1)}, u32[]{:S(2)}, u32[]{:S(2)}) collective-permute-start(bf16[2,2,136,128]{3,2,1,0:T(8,128)(2,1)S(1)} %pad_maximum_fusion.1.a0_ref), channel_id=1, source_target_pairs={{0,3},{1,2},{2,1},{3,0},{4,7},{5,6},{6,5},{7,4},{8,11},{9,10},{10,... | collective-permute-start | bytes 417800 | tf_op jit(solution)/shard_map/ppermute | solution.py:345
  80.9 6.3 %collective-permute-start.25 = (bf16[2,2,136,128]{3,2,1,0:T(8,128)(2,1)S(1)}, bf16[2,2,136,128]{3,2,1,0:T(8,128)(2,1)S(1)}, u32[]{:S(2)}, u32[]{:S(2)}) collective-permute-start(bf16[2,2,136,128]{3,2,1,0:T(8,128)(2,1)S(1)} %pad_maximum_fusion.2.b0_ref), channel_id=1, source_target_pairs={{0,7},{1,6},{2,5},{3,4},{4,3},{5,2},{6,1},{7,0},{8,15},{9,14},{10,... | collective-permute-start | bytes 417800 | tf_op jit(solution)/shard_map/ppermute | solution.py:345
  (5 other events, 14.0 us)

commit v7 on v6

--- a/solution.py
+++ b/solution.py
@@ -67,7 +67,7 @@
 
 def half_of(place):
     gx, gy = place
-    return (gy ^ (gy >> 1) ^ (gy >> 3) ^ (gx >> 2)) & 1
+    return (gy ^ (gy >> 1) ^ (gy >> 3) ^ gx ^ (gx >> 2)) & 1
 
 
 def sides(place):
@@ -172,8 +172,8 @@
     skip_ref, cot_ref, pool_ref, xedge_ref, xmid_ref, oedge_ref, omid_ref, ytwo_ref, yone_ref, *refs,
 ):
     wdec_ref, wpre_ref, wback_ref = refs[:3]
-    send_out, keep_out, jskip_out, rim_out, one_out, two_out = refs[3:9]
-    cells_ref, pooled_ref, joined_ref, jgrad_ref, full_ref, pre_ref = refs[9:]
+    send_out, keep_out, jskip_out, rim_out, two_out = refs[3:8]
+    cells_ref, pooled_ref, joined_ref, jgrad_ref, full_ref, pre_ref = refs[8:]
     factor = 1.0 / math.sqrt(524288)
     place = places()
     xlow, xhigh = sides(place[0])
@@ -264,7 +264,8 @@
     odd = (place[0] & 1).astype(F32)
     for index in range(RIM):
         down, up = (pack(rim_row(i, 2 * index), rim_row(i, 2 * index + 1)) for i in (0, 2))
-        one_out[index] = ((1.0 - odd) * up + odd * down).astype(BF16)
+        first = SENT + index * SKIP
+        send_out[first : first + SKIP] = ((1.0 - odd) * up + odd * down).astype(BF16)
         two_out[index] = ((1.0 - odd) * down + odd * up).astype(BF16)
 
     across = (((1,), (1,)), ((), ()))
@@ -371,10 +372,18 @@
     return swap(value, "gy", 2 * flip + 1)
 
 
+def swap_far(value, flip_x, cross):
+    size_x, size_y = lax.axis_size("gx"), lax.axis_size("gy")
+    pairs = [(i * size_y + j, (i ^ flip_x) * size_y + (j ^ cross)) for i in range(size_x) for j in range(size_y)]
+    return lax.ppermute(value, ("gx", "gy"), pairs)
+
+
+def swap_x(value, flip):
+    return swap_far(value, flip, flip & 1)
+
+
 def swap_z(value, flip):
-    size_x, size_y = lax.axis_size("gx"), lax.axis_size("gy")
-    pairs = [(i * size_y + j, (i ^ (4 * flip)) * size_y + (j ^ (flip & 1))) for i in range(size_x) for j in range(size_y)]
-    return lax.ppermute(value, ("gx", "gy"), pairs)
+    return swap_far(value, 4 * flip, flip & 1)
 
 
 def wide(value):
@@ -413,11 +422,11 @@
     )
     yone, ytwo = swap_side(yone, "gy", 0), swap_side(ytwo, "gy", 1)
     chunks = (4, 4, ROWS, LANES)
-    send, keep, jskip, own, rone, rtwo = call(
+    send, keep, jskip, own, rtwo = call(
         grads_kernel, "local_grads",
         (
-            ((SENT, LANES), BF16), (chunks, F32), (fine, F32),
-            ((BLOCKS_C + 2,) + block, F32), (rim, BF16), (rim, BF16),
+            ((SENT + RIM * SKIP, LANES), BF16), (chunks, F32), (fine, F32),
+            ((BLOCKS_C + 2,) + block, F32), (rim, BF16),
         ),
         (
             ((DEC, BLOCKS * LANES), BF16),
@@ -431,7 +440,8 @@
         w_join, w_pre, w_back,
     )
 
-    part = keep + wide(swap(send, "gy", 1).reshape(chunks))
+    send = swap(send, "gy", 1)
+    part = keep + wide(send[:SENT].reshape(chunks))
     a, b = part[:, :2], part[:, 2:]
     a_got = swap_y(jnp.stack([a[A_FIRST], a[2]]).astype(BF16), A_FIRST)
     b_got = swap_y(jnp.stack([b[B_FIRST], b[2]]).astype(BF16), B_FIRST)
@@ -443,8 +453,8 @@
     rtwo = swap_side(rtwo, "gx", 1)
     part = jnp.concatenate([a_own + wide(a_got), b_own + wide(b_got)])
     leave = part.astype(BF16)
-    got = swap(jnp.concatenate([leave[1], rone.reshape(RIM * SKIP, LANES)]), "gx", 1)
-    got = [got[:ROWS], swap(leave[2], "gx", 2), swap(leave[3], "gx", 3), got[ROWS:].reshape(rim)]
+    got = swap_x(jnp.concatenate([leave[1], send[SENT:]]), 1)
+    got = [got[:ROWS], swap_x(leave[2], 2), swap_x(leave[3], 3), got[ROWS:].reshape(rim)]
     *got, rone, rtwo = together((*got, rtwo))
     rows, qone, qtwo = call(
         fold_kernel, "fold_rim", (((BLOCKS_C,) + block, F32), (block, BF16), (block, BF16)), (), 8, (100_000, 600_000),
@@ -456,7 +466,7 @@
     *got, rows, qone, qtwo = together((*got, rows, qone, qtwo))
     part = (wide(mine) + wide(got[0])) + (wide(got[1]) + wide(got[2]))
     part = (part + swap(part, "gy", 9)).astype(BF16)
-    got = together([swap(part, "gx", flip) for flip in (1, 3, 2)])
+    got = together([swap_x(part, flip) for flip in (1, 3, 2)])
     part = jnp.stack([part, got[0], got[2], got[1]])
     a, b = part[:2], part[2:]
     a_got, b_got = together((swap_y(a, A_SECOND), swap_y(b, B_SECOND)))

time: 91.3 us -> 91.5 us (level)
  waiting for transfers between devices: 32 us -> 34 us
  starting transfers between devices: 45.8 us -> 43.9 us
    ppermute x17 -> x11, starting transfers between devices: 17.5 us -> 11.3 us  [swap(): lax.ppermute(value, axis, [(i, i ^ flip) for i in range(lax.axis_size(axi...]
    ppermute x3 -> x9, waiting for transfers between devices: 5.11 us -> 10.7 us  [swap_far(): return lax.ppermute(value, ('gx', 'gy'), pairs)]
    ppermute x3 -> x9, starting transfers between devices: 8.04 us -> 13 us  [swap_far(): return lax.ppermute(value, ('gx', 'gy'), pairs)]
    ppermute x17 -> x11, waiting for transfers between devices: 24.4 us -> 20.8 us  [swap(): lax.ppermute(value, axis, [(i, i ^ flip) for i in range(lax.axis_size(axi...]
  transfers between devices with their start and end apart: 29 -> 29, of which waited for: 18 -> 16; matrix products, arithmetic and copies ran while one was open for 0% -> 0% of each run, Pallas kernels for 3% -> 3%
where the time goes in v7:
time: 91.5 us; the launch traced here: 91.4 us
  starting transfers between devices  43.9 us (48%)
  waiting for transfers between devices  34 us (37%)
  Pallas kernels  11.9 us (13%)
  between operations  1.05 us (1%)
    ppermute x11, waiting for transfers between devices, swap(): lax.ppermute(value, axis, [(i, i ^ flip) for i in range(lax.axis_size(axi...  20.8 us
    ppermute x9, starting transfers between devices, swap_side(): lax.ppermute(value, axis, [(i, partner(i, which, count)) for i in range(c...  19.7 us
    ppermute x9, starting transfers between devices, swap_far(): return lax.ppermute(value, ('gx', 'gy'), pairs)  13 us
    pallas_call x7, Pallas kernels, call(): pl.pallas_call(kernel, out_shape=tuple((jax.ShapeDtypeStruct(shape, dtype...  11.9 us
    ppermute x11, starting transfers between devices, swap(): lax.ppermute(value, axis, [(i, i ^ flip) for i in range(lax.axis_size(axi...  11.3 us
    ppermute x9, waiting for transfers between devices, swap_far(): return lax.ppermute(value, ('gx', 'gy'), pairs)  10.7 us
    ppermute x9, waiting for transfers between devices, swap_side(): lax.ppermute(value, axis, [(i, partner(i, which, count)) for i in range(c...  2.5 us
  transfers between devices with their start and end apart: 29, of which 16 were waited for; matrix products, arithmetic and copies ran while one was open for 0% of the time, Pallas kernels for 3%

profile of v7, /device:TPU:1, one launch (start us, length us, event | category | flops | bytes accessed | tf_op | source)
XLA Modules:
  0.0 91.4 jit_solution(3325067586636528494)
XLA Ops:
  2.1 9.1 %collective-permute-start = (bf16[3,64,128]{2,1,0:T(8,128)(2,1)S(1)}, bf16[3,64,128]{2,1,0:T(8,128)(2,1)S(1)}, u32[]{:S(2)}, u32[]{:S(2)}) collective-permute-start(bf16[3,64,128]{2,1,0:T(8,128)(2,1)S(1)} %get-tuple-element.52), channel_id=1, source_target_pairs={{0,240},{16,32},{32,16},{48,64},{64,48},{80,96},{96,80},{112,128},... | collective-permute-start | bytes 147464 | tf_op jit(solution)/shard_map/ppermute | solution.py:359
  12.7 1.7 %lay_weights.1 = (bf16[192,1728]{1,0:T(8,128)(2,1)S(1)}, bf16[128,1728]{1,0:T(8,128)(2,1)S(1)}, bf16[576,384]{1,0:T(8,128)(2,1)S(1)}) custom-call(bf16[1728,192]{1,0:T(8,128)(2,1)} %bitcast.55, bf16[1728,128]{1,0:T(8,128)(2,1)} %bitcast.56), custom_call_target="tpu_custom_call" | custom-call | flops 1000000 | bytes 2500000 | tf_op jit(solution)/shard_map/lay_weights/pallas_call | solution.py:121
  14.5 3.6 %collective-permute-start.4 = (bf16[6,64,128]{2,1,0:T(8,128)(2,1)S(1)}, bf16[6,64,128]{2,1,0:T(8,128)(2,1)S(1)}, u32[]{:S(2)}, u32[]{:S(2)}) collective-permute-start(bf16[6,64,128]{2,1,0:T(8,128)(2,1)S(1)} %get-tuple-element.59), channel_id=1, source_target_pairs={{0,15},{1,2},{2,1},{3,4},{4,3},{5,6},{6,5},{7,8},{8,7},{9,10},{10,... | collective-permute-start | bytes 294920 | tf_op jit(solution)/shard_map/ppermute | solution.py:359
  18.3 1.7 %collective-permute-done.1.xmid_ref = bf16[7,64,128]{2,1,0:T(8,128)(2,1)S(1)} collective-permute-done((bf16[7,64,128]{2,1,0:T(8,128)(2,1)S(1)}, bf16[7,64,128]{2,1,0:T(8,128)(2,1)S(1)}, u32[]{:S(2)}, u32[]{:S(2)}) %collective-permute-start.1) | collective-permute-done | bytes 114720 | tf_op jit(solution)/shard_map/ppermute | solution.py:359
  20.8 5.8 %local_grads.1 = (bf16[2368,128]{1,0:T(8,128)(2,1)S(1)}, f32[4,4,136,128]{3,2,1,0:T(8,128)S(1)}, f32[16,64,128]{2,1,0:T(8,128)S(1)}, f32[6,64,128]{2,1,0:T(8,128)S(1)}, bf16[3,64,128]{2,1,0:T(8,128)(2,1)S(1)}) custom-call(bf16[16,64,128]{2,1,0:T(8,128)(2,1)S(1)} %get-tuple-element.49.skip_ref, bf16[16,64,128]{2,1,0:T(8,128)(2,1)S(1)} %get-tuple-element.50.cot_ref, ...), custom_call_target="tpu_custom_call" | custom-call | flops 3000000000 | bytes 8000000 | tf_op jit(solution)/shard_map/local_grads/pallas_call | solution.py:121
  26.6 2.5 %collective-permute-start.6 = (bf16[2368,128]{1,0:T(8,128)(2,1)S(1)}, bf16[2368,128]{1,0:T(8,128)(2,1)S(1)}, u32[]{:S(2)}, u32[]{:S(2)}) collective-permute-start(bf16[2368,128]{1,0:T(8,128)(2,1)S(1)} %get-tuple-element.62), channel_id=1, source_target_pairs={{0,1},{1,0},{2,3},{3,2},{4,5},{5,4},{6,7},{7,6},{8,9},{9,8},{10,11... | collective-permute-start | bytes 1818632 | tf_op jit(solution)/shard_map/ppermute | solution.py:346
  29.0 1.7 %collective-permute-done.6 = bf16[2368,128]{1,0:T(8,128)(2,1)S(1)} collective-permute-done((bf16[2368,128]{1,0:T(8,128)(2,1)S(1)}, bf16[2368,128]{1,0:T(8,128)(2,1)S(1)}, u32[]{:S(2)}, u32[]{:S(2)}) %collective-permute-start.6) | collective-permute-done | bytes 606240 | tf_op jit(solution)/shard_map/ppermute | solution.py:346
  30.9 3.0 %collective-permute-start.8 = (bf16[2,2,136,128]{3,2,1,0:T(8,128)(2,1)S(1)}, bf16[2,2,136,128]{3,2,1,0:T(8,128)(2,1)S(1)}, u32[]{:S(2)}, u32[]{:S(2)}) collective-permute-start(bf16[2,2,136,128]{3,2,1,0:T(8,128)(2,1)S(1)} %pad_maximum_fusion), channel_id=1, source_target_pairs={{0,7},{1,6},{2,5},{3,4},{4,3},{5,2},{6,1},{7,0},{8,15},{9,14},{10,... | collective-permute-start | bytes 417800 | tf_op jit(solution)/shard_map/ppermute | solution.py:346
  33.9 4.0 %collective-permute-done.8 = bf16[2,2,136,128]{3,2,1,0:T(8,128)(2,1)S(1)} collective-permute-done((bf16[2,2,136,128]{3,2,1,0:T(8,128)(2,1)S(1)}, bf16[2,2,136,128]{3,2,1,0:T(8,128)(2,1)S(1)}, u32[]{:S(2)}, u32[]{:S(2)}) %collective-permute-start.8) | collective-permute-done | bytes 139296 | tf_op jit(solution)/shard_map/ppermute | solution.py:346
  37.9 1.5 %collective-permute-done.7 = bf16[2,2,136,128]{3,2,1,0:T(8,128)(2,1)S(1)} collective-permute-done((bf16[2,2,136,128]{3,2,1,0:T(8,128)(2,1)S(1)}, bf16[2,2,136,128]{3,2,1,0:T(8,128)(2,1)S(1)}, u32[]{:S(2)}, u32[]{:S(2)}) %collective-permute-start.7) | collective-permute-done | bytes 139296 | tf_op jit(solution)/shard_map/ppermute | solution.py:346
  41.2 4.7 %collective-permute-start.14 = (bf16[3,64,128]{2,1,0:T(8,128)(2,1)S(1)}, bf16[3,64,128]{2,1,0:T(8,128)(2,1)S(1)}, u32[]{:S(2)}, u32[]{:S(2)}) collective-permute-start(bf16[3,64,128]{2,1,0:T(8,128)(2,1)S(1)} %get-tuple-element.67), channel_id=1, source_target_pairs={{0,240},{16,32},{32,16},{48,64},{64,48},{80,96},{96,80},{112,128},... | collective-permute-start | bytes 147464 | tf_op jit(solution)/shard_map/ppermute | solution.py:359
  46.2 3.4 %collective-permute-start.12 = (bf16[136,128]{1,0:T(8,128)(2,1)S(1)}, bf16[136,128]{1,0:T(8,128)(2,1)S(1)}, u32[]{:S(2)}, u32[]{:S(2)}) collective-permute-start(bf16[136,128]{1,0:T(8,128)(2,1)S(1)} %get-tuple-element.108), channel_id=1, source_target_pairs={{0,32},{1,33},{2,34},{3,35},{4,36},{5,37},{6,38},{7,39},{8,40},{9,... | collective-permute-start | bytes 104456 | tf_op jit(solution)/shard_map/ppermute | solution.py:378
  49.6 1.5 %collective-permute-done.11 = bf16[328,128]{1,0:T(8,128)(2,1)S(1)} collective-permute-done((bf16[328,128]{1,0:T(8,128)(2,1)S(1)}, bf16[328,128]{1,0:T(8,128)(2,1)S(1)}, u32[]{:S(2)}, u32[]{:S(2)}) %collective-permute-start.11) | collective-permute-done | bytes 84000 | tf_op jit(solution)/shard_map/ppermute | solution.py:378
  52.1 3.9 %collective-permute-start.17 = (bf16[136,128]{1,0:T(8,128)(2,1)S(1)}, bf16[136,128]{1,0:T(8,128)(2,1)S(1)}, u32[]{:S(2)}, u32[]{:S(2)}) collective-permute-start(bf16[136,128]{1,0:T(8,128)(2,1)S(1)} %fusion.11), channel_id=1, source_target_pairs={{0,193},{1,192},{2,195},{3,194},{4,197},{5,196},{6,199},{7,198},{8... | collective-permute-start | bytes 104456 | tf_op jit(solution)/shard_map/ppermute | solution.py:378
  56.6 1.9 %collective-permute-start.15 = (bf16[136,128]{1,0:T(8,128)(2,1)S(1)}, bf16[136,128]{1,0:T(8,128)(2,1)S(1)}, u32[]{:S(2)}, u32[]{:S(2)}) collective-permute-start(bf16[136,128]{1,0:T(8,128)(2,1)S(1)} %fusion.11), channel_id=1, source_target_pairs={{0,65},{1,64},{2,67},{3,66},{4,69},{5,68},{6,71},{7,70},{8,73},{9,... | collective-permute-start | bytes 104456 | tf_op jit(solution)/shard_map/ppermute | solution.py:378
  58.6 5.3 %collective-permute-done.16 = bf16[136,128]{1,0:T(8,128)(2,1)S(1)} collective-permute-done((bf16[136,128]{1,0:T(8,128)(2,1)S(1)}, bf16[136,128]{1,0:T(8,128)(2,1)S(1)}, u32[]{:S(2)}, u32[]{:S(2)}) %collective-permute-start.16) | collective-permute-done | bytes 34848 | tf_op jit(solution)/shard_map/ppermute | solution.py:378
  64.0 3.7 %collective-permute-done.18 = f32[136,128]{1,0:T(8,128)S(1)} collective-permute-done((f32[136,128]{1,0:T(8,128)S(1)}, f32[136,128]{1,0:T(8,128)S(1)}, u32[]{:S(2)}, u32[]{:S(2)}) %collective-permute-start.18) | collective-permute-done | bytes 69664 | tf_op jit(solution)/shard_map/ppermute | solution.py:346
  67.8 1.5 %collective-permute-start.21 = (bf16[136,128]{1,0:T(8,128)(2,1)S(1)}, bf16[136,128]{1,0:T(8,128)(2,1)S(1)}, u32[]{:S(2)}, u32[]{:S(2)}) collective-permute-start(bf16[136,128]{1,0:T(8,128)(2,1)S(1)} %add_convert_fusion), channel_id=1, source_target_pairs={{0,32},{1,33},{2,34},{3,35},{4,36},{5,37},{6,38},{7,39},{8,40},{9,... | collective-permute-start | bytes 104456 | tf_op jit(solution)/shard_map/ppermute | solution.py:378
  72.4 2.0 %collective-permute-done.20 = bf16[136,128]{1,0:T(8,128)(2,1)S(1)} collective-permute-done((bf16[136,128]{1,0:T(8,128)(2,1)S(1)}, bf16[136,128]{1,0:T(8,128)(2,1)S(1)}, u32[]{:S(2)}, u32[]{:S(2)}) %collective-permute-start.20) | collective-permute-done | bytes 34848 | tf_op jit(solution)/shard_map/ppermute | solution.py:378
  76.5 2.3 %collective-permute-done.23 = bf16[2,136,128]{2,1,0:T(8,128)(2,1)S(1)} collective-permute-done((bf16[2,136,128]{2,1,0:T(8,128)(2,1)S(1)}, bf16[2,136,128]{2,1,0:T(8,128)(2,1)S(1)}, u32[]{:S(2)}, u32[]{:S(2)}) %collective-permute-start.23) | collective-permute-done | bytes 69664 | tf_op jit(solution)/shard_map/ppermute | solution.py:346
  78.8 1.8 %collective-permute-done.22 = bf16[2,136,128]{2,1,0:T(8,128)(2,1)S(1)} collective-permute-done((bf16[2,136,128]{2,1,0:T(8,128)(2,1)S(1)}, bf16[2,136,128]{2,1,0:T(8,128)(2,1)S(1)}, u32[]{:S(2)}, u32[]{:S(2)}) %collective-permute-start.22) | collective-permute-done | bytes 69664 | tf_op jit(solution)/shard_map/ppermute | solution.py:346
  80.7 1.5 %collective-permute-start.25 = (bf16[2,2,136,128]{3,2,1,0:T(8,128)(2,1)S(1)}, bf16[2,2,136,128]{3,2,1,0:T(8,128)(2,1)S(1)}, u32[]{:S(2)}, u32[]{:S(2)}) collective-permute-start(bf16[2,2,136,128]{3,2,1,0:T(8,128)(2,1)S(1)} %pad_maximum_fusion.2.b0_ref), channel_id=1, source_target_pairs={{0,7},{1,6},{2,5},{3,4},{4,3},{5,2},{6,1},{7,0},{8,15},{9,14},{10,... | collective-permute-start | bytes 417800 | tf_op jit(solution)/shard_map/ppermute | solution.py:346
  82.2 4.1 %collective-permute-done.24.a1_ref = bf16[2,2,136,128]{3,2,1,0:T(8,128)(2,1)S(1)} collective-permute-done((bf16[2,2,136,128]{3,2,1,0:T(8,128)(2,1)S(1)}, bf16[2,2,136,128]{3,2,1,0:T(8,128)(2,1)S(1)}, u32[]{:S(2)}, u32[]{:S(2)}) %collective-permute-start.24) | collective-permute-done | bytes 139296 | tf_op jit(solution)/shard_map/ppermute | solution.py:346
  89.6 1.7 %unpack.1 = (f32[1728,192]{1,0:T(8,128)}, f32[1728,128]{1,0:T(8,128)}) custom-call(bf16[2,2,136,128]{3,2,1,0:T(8,128)(2,1)S(1)} %pad_maximum_fusion.1.a0_ref, bf16[2,2,136,128]{3,2,1,0:T(8,128)(2,1)S(1)} %collective-permute-done.24.a1_ref, bf16[2,2,136,128]{3,2,1,0:T(8,128)(2,1)S(1)} %pad_maximum_fusion.2.b0_ref, ...), custom_call_target="tpu_custom_call" | custom-call | flops 1000000 | bytes 5000000 | tf_op jit(solution)/shard_map/unpack/pallas_call | solution.py:121
  (67 shorter events, 16.5 us)
Async XLA Ops:
  2.1 12.3 %collective-permute-start = (bf16[3,64,128]{2,1,0:T(8,128)(2,1)S(1)}, bf16[3,64,128]{2,1,0:T(8,128)(2,1)S(1)}, u32[]{:S(2)}, u32[]{:S(2)}) collective-permute-start(bf16[3,64,128]{2,1,0:T(8,128)(2,1)S(1)} %get-tuple-element.52), channel_id=1, source_target_pairs={{0,240},{16,32},{32,16},{48,64},{64,48},{80,96},{96,80},{112,128},... | collective-permute-start | bytes 147464 | tf_op jit(solution)/shard_map/ppermute | solution.py:359
  11.2 8.8 %collective-permute-start.1 = (bf16[7,64,128]{2,1,0:T(8,128)(2,1)S(1)}, bf16[7,64,128]{2,1,0:T(8,128)(2,1)S(1)}, u32[]{:S(2)}, u32[]{:S(2)}) collective-permute-start(bf16[7,64,128]{2,1,0:T(8,128)(2,1)S(1)} %get-tuple-element.53), channel_id=1, source_target_pairs={{0,240},{16,32},{32,16},{48,64},{64,48},{80,96},{96,80},{112,128},... | collective-permute-start | bytes 344072 | tf_op jit(solution)/shard_map/ppermute | solution.py:359
  12.0 8.0 %collective-permute-start.3 = (bf16[7,64,128]{2,1,0:T(8,128)(2,1)S(1)}, bf16[7,64,128]{2,1,0:T(8,128)(2,1)S(1)}, u32[]{:S(2)}, u32[]{:S(2)}) collective-permute-start(bf16[7,64,128]{2,1,0:T(8,128)(2,1)S(1)} %get-tuple-element.55), channel_id=1, source_target_pairs={{0,16},{16,0},{32,48},{48,32},{64,80},{80,64},{96,112},{112,96},{1... | collective-permute-start | bytes 344072 | tf_op jit(solution)/shard_map/ppermute | solution.py:359
  14.5 6.2 %collective-permute-start.4 = (bf16[6,64,128]{2,1,0:T(8,128)(2,1)S(1)}, bf16[6,64,128]{2,1,0:T(8,128)(2,1)S(1)}, u32[]{:S(2)}, u32[]{:S(2)}) collective-permute-start(bf16[6,64,128]{2,1,0:T(8,128)(2,1)S(1)} %get-tuple-element.59), channel_id=1, source_target_pairs={{0,15},{1,2},{2,1},{3,4},{4,3},{5,6},{6,5},{7,8},{8,7},{9,10},{10,... | collective-permute-start | bytes 294920 | tf_op jit(solution)/shard_map/ppermute | solution.py:359
  26.6 4.1 %collective-permute-start.6 = (bf16[2368,128]{1,0:T(8,128)(2,1)S(1)}, bf16[2368,128]{1,0:T(8,128)(2,1)S(1)}, u32[]{:S(2)}, u32[]{:S(2)}) collective-permute-start(bf16[2368,128]{1,0:T(8,128)(2,1)S(1)} %get-tuple-element.62), channel_id=1, source_target_pairs={{0,1},{1,0},{2,3},{3,2},{4,5},{5,4},{6,7},{7,6},{8,9},{9,8},{10,11... | collective-permute-start | bytes 1818632 | tf_op jit(solution)/shard_map/ppermute | solution.py:346
  30.9 7.0 %collective-permute-start.8 = (bf16[2,2,136,128]{3,2,1,0:T(8,128)(2,1)S(1)}, bf16[2,2,136,128]{3,2,1,0:T(8,128)(2,1)S(1)}, u32[]{:S(2)}, u32[]{:S(2)}) collective-permute-start(bf16[2,2,136,128]{3,2,1,0:T(8,128)(2,1)S(1)} %pad_maximum_fusion), channel_id=1, source_target_pairs={{0,7},{1,6},{2,5},{3,4},{4,3},{5,2},{6,1},{7,0},{8,15},{9,14},{10,... | collective-permute-start | bytes 417800 | tf_op jit(solution)/shard_map/ppermute | solution.py:346
  33.9 5.4 %collective-permute-start.7 = (bf16[2,2,136,128]{3,2,1,0:T(8,128)(2,1)S(1)}, bf16[2,2,136,128]{3,2,1,0:T(8,128)(2,1)S(1)}, u32[]{:S(2)}, u32[]{:S(2)}) collective-permute-start(bf16[2,2,136,128]{3,2,1,0:T(8,128)(2,1)S(1)} %stack.56), channel_id=1, source_target_pairs={{0,3},{1,2},{2,1},{3,0},{4,7},{5,6},{6,5},{7,4},{8,11},{9,10},{10,... | collective-permute-start | bytes 417800 | tf_op jit(solution)/shard_map/ppermute | solution.py:346
  39.4 6.5 %collective-permute-start.10 = (bf16[2,136,128]{2,1,0:T(8,128)(2,1)S(1)}, bf16[2,136,128]{2,1,0:T(8,128)(2,1)S(1)}, u32[]{:S(2)}, u32[]{:S(2)}) collective-permute-start(bf16[2,136,128]{2,1,0:T(8,128)(2,1)S(1)} %get-tuple-element.99), channel_id=1, source_target_pairs={{0,3},{1,2},{2,1},{3,0},{4,7},{5,6},{6,5},{7,4},{8,11},{9,10},{10,... | collective-permute-start | bytes 208904 | tf_op jit(solution)/shard_map/ppermute | solution.py:346
  39.8 6.1 %collective-permute-start.9 = (bf16[2,136,128]{2,1,0:T(8,128)(2,1)S(1)}, bf16[2,136,128]{2,1,0:T(8,128)(2,1)S(1)}, u32[]{:S(2)}, u32[]{:S(2)}) collective-permute-start(bf16[2,136,128]{2,1,0:T(8,128)(2,1)S(1)} %get-tuple-element.100), channel_id=1, source_target_pairs={{0,7},{1,6},{2,5},{3,4},{4,3},{5,2},{6,1},{7,0},{8,15},{9,14},{10,... | collective-permute-start | bytes 208904 | tf_op jit(solution)/shard_map/ppermute | solution.py:346
  41.2 10.0 %collective-permute-start.14 = (bf16[3,64,128]{2,1,0:T(8,128)(2,1)S(1)}, bf16[3,64,128]{2,1,0:T(8,128)(2,1)S(1)}, u32[]{:S(2)}, u32[]{:S(2)}) collective-permute-start(bf16[3,64,128]{2,1,0:T(8,128)(2,1)S(1)} %get-tuple-element.67), channel_id=1, source_target_pairs={{0,240},{16,32},{32,16},{48,64},{64,48},{80,96},{96,80},{112,128},... | collective-permute-start | bytes 147464 | tf_op jit(solution)/shard_map/ppermute | solution.py:359
  46.0 5.1 %collective-permute-start.11 = (bf16[328,128]{1,0:T(8,128)(2,1)S(1)}, bf16[328,128]{1,0:T(8,128)(2,1)S(1)}, u32[]{:S(2)}, u32[]{:S(2)}) collective-permute-start(bf16[328,128]{1,0:T(8,128)(2,1)S(1)} %pad_maximum_fusion.3), channel_id=1, source_target_pairs={{0,17},{1,16},{2,19},{3,18},{4,21},{5,20},{6,23},{7,22},{8,25},{9,... | collective-permute-start | bytes 251912 | tf_op jit(solution)/shard_map/ppermute | solution.py:378
  46.1 5.9 %collective-permute-start.13 = (bf16[136,128]{1,0:T(8,128)(2,1)S(1)}, bf16[136,128]{1,0:T(8,128)(2,1)S(1)}, u32[]{:S(2)}, u32[]{:S(2)}) collective-permute-start(bf16[136,128]{1,0:T(8,128)(2,1)S(1)} %get-tuple-element.107), channel_id=1, source_target_pairs={{0,49},{1,48},{2,51},{3,50},{4,53},{5,52},{6,55},{7,54},{8,57},{9,... | collective-permute-start | bytes 104456 | tf_op jit(solution)/shard_map/ppermute | solution.py:378
  46.2 5.8 %collective-permute-start.12 = (bf16[136,128]{1,0:T(8,128)(2,1)S(1)}, bf16[136,128]{1,0:T(8,128)(2,1)S(1)}, u32[]{:S(2)}, u32[]{:S(2)}) collective-permute-start(bf16[136,128]{1,0:T(8,128)(2,1)S(1)} %get-tuple-element.108), channel_id=1, source_target_pairs={{0,32},{1,33},{2,34},{3,35},{4,36},{5,37},{6,38},{7,39},{8,40},{9,... | collective-permute-start | bytes 104456 | tf_op jit(solution)/shard_map/ppermute | solution.py:378
  52.1 6.5 %collective-permute-start.17 = (bf16[136,128]{1,0:T(8,128)(2,1)S(1)}, bf16[136,128]{1,0:T(8,128)(2,1)S(1)}, u32[]{:S(2)}, u32[]{:S(2)}) collective-permute-start(bf16[136,128]{1,0:T(8,128)(2,1)S(1)} %fusion.11), channel_id=1, source_target_pairs={{0,193},{1,192},{2,195},{3,194},{4,197},{5,196},{6,199},{7,198},{8... | collective-permute-start | bytes 104456 | tf_op jit(solution)/shard_map/ppermute | solution.py:378
  56.0 7.9 %collective-permute-start.16 = (bf16[136,128]{1,0:T(8,128)(2,1)S(1)}, bf16[136,128]{1,0:T(8,128)(2,1)S(1)}, u32[]{:S(2)}, u32[]{:S(2)}) collective-permute-start(bf16[136,128]{1,0:T(8,128)(2,1)S(1)} %fusion.11), channel_id=1, source_target_pairs={{0,128},{1,129},{2,130},{3,131},{4,132},{5,133},{6,134},{7,135},{8... | collective-permute-start | bytes 104456 | tf_op jit(solution)/shard_map/ppermute | solution.py:378
  56.6 7.4 %collective-permute-start.15 = (bf16[136,128]{1,0:T(8,128)(2,1)S(1)}, bf16[136,128]{1,0:T(8,128)(2,1)S(1)}, u32[]{:S(2)}, u32[]{:S(2)}) collective-permute-start(bf16[136,128]{1,0:T(8,128)(2,1)S(1)} %fusion.11), channel_id=1, source_target_pairs={{0,65},{1,64},{2,67},{3,66},{4,69},{5,68},{6,71},{7,70},{8,73},{9,... | collective-permute-start | bytes 104456 | tf_op jit(solution)/shard_map/ppermute | solution.py:378
  67.8 4.7 %collective-permute-start.21 = (bf16[136,128]{1,0:T(8,128)(2,1)S(1)}, bf16[136,128]{1,0:T(8,128)(2,1)S(1)}, u32[]{:S(2)}, u32[]{:S(2)}) collective-permute-start(bf16[136,128]{1,0:T(8,128)(2,1)S(1)} %add_convert_fusion), channel_id=1, source_target_pairs={{0,32},{1,33},{2,34},{3,35},{4,36},{5,37},{6,38},{7,39},{8,40},{9,... | collective-permute-start | bytes 104456 | tf_op jit(solution)/shard_map/ppermute | solution.py:378
  69.3 5.2 %collective-permute-start.20 = (bf16[136,128]{1,0:T(8,128)(2,1)S(1)}, bf16[136,128]{1,0:T(8,128)(2,1)S(1)}, u32[]{:S(2)}, u32[]{:S(2)}) collective-permute-start(bf16[136,128]{1,0:T(8,128)(2,1)S(1)} %add_convert_fusion), channel_id=1, source_target_pairs={{0,49},{1,48},{2,51},{3,50},{4,53},{5,52},{6,55},{7,54},{8,57},{9,... | collective-permute-start | bytes 104456 | tf_op jit(solution)/shard_map/ppermute | solution.py:378
  70.8 11.4 %collective-permute-start.26 = (bf16[64,128]{1,0:T(8,128)(2,1)S(1)}, bf16[64,128]{1,0:T(8,128)(2,1)S(1)}, u32[]{:S(2)}, u32[]{:S(2)}) collective-permute-start(bf16[64,128]{1,0:T(8,128)(2,1)S(1)} %get-tuple-element.86), channel_id=1, source_target_pairs={{0,1},{1,0},{2,3},{3,2},{4,5},{5,4},{6,7},{7,6},{8,9},{9,8},{10,11... | collective-permute-start | bytes 49160 | tf_op jit(solution)/shard_map/ppermute | solution.py:359
  71.4 10.8 %collective-permute-start.27 = (bf16[64,128]{1,0:T(8,128)(2,1)S(1)}, bf16[64,128]{1,0:T(8,128)(2,1)S(1)}, u32[]{:S(2)}, u32[]{:S(2)}) collective-permute-start(bf16[64,128]{1,0:T(8,128)(2,1)S(1)} %get-tuple-element.87), channel_id=1, source_target_pairs={{0,15},{1,2},{2,1},{3,4},{4,3},{5,6},{6,5},{7,8},{8,7},{9,10},{10,... | collective-permute-start | bytes 49160 | tf_op jit(solution)/shard_map/ppermute | solution.py:359
  74.5 4.3 %collective-permute-start.23 = (bf16[2,136,128]{2,1,0:T(8,128)(2,1)S(1)}, bf16[2,136,128]{2,1,0:T(8,128)(2,1)S(1)}, u32[]{:S(2)}, u32[]{:S(2)}) collective-permute-start(bf16[2,136,128]{2,1,0:T(8,128)(2,1)S(1)} %get-tuple-element.104), channel_id=1, source_target_pairs={{0,3},{1,2},{2,1},{3,0},{4,7},{5,6},{6,5},{7,4},{8,11},{9,10},{10,... | collective-permute-start | bytes 208904 | tf_op jit(solution)/shard_map/ppermute | solution.py:346
  75.3 5.2 %collective-permute-start.22 = (bf16[2,136,128]{2,1,0:T(8,128)(2,1)S(1)}, bf16[2,136,128]{2,1,0:T(8,128)(2,1)S(1)}, u32[]{:S(2)}, u32[]{:S(2)}) collective-permute-start(bf16[2,136,128]{2,1,0:T(8,128)(2,1)S(1)} %get-tuple-element.106), channel_id=1, source_target_pairs={{0,7},{1,6},{2,5},{3,4},{4,3},{5,2},{6,1},{7,0},{8,15},{9,14},{10,... | collective-permute-start | bytes 208904 | tf_op jit(solution)/shard_map/ppermute | solution.py:346
  80.6 5.8 %collective-permute-start.24 = (bf16[2,2,136,128]{3,2,1,0:T(8,128)(2,1)S(1)}, bf16[2,2,136,128]{3,2,1,0:T(8,128)(2,1)S(1)}, u32[]{:S(2)}, u32[]{:S(2)}) collective-permute-start(bf16[2,2,136,128]{3,2,1,0:T(8,128)(2,1)S(1)} %pad_maximum_fusion.1.a0_ref), channel_id=1, source_target_pairs={{0,3},{1,2},{2,1},{3,0},{4,7},{5,6},{6,5},{7,4},{8,11},{9,10},{10,... | collective-permute-start | bytes 417800 | tf_op jit(solution)/shard_map/ppermute | solution.py:346
  80.7 6.8 %collective-permute-start.25 = (bf16[2,2,136,128]{3,2,1,0:T(8,128)(2,1)S(1)}, bf16[2,2,136,128]{3,2,1,0:T(8,128)(2,1)S(1)}, u32[]{:S(2)}, u32[]{:S(2)}) collective-permute-start(bf16[2,2,136,128]{3,2,1,0:T(8,128)(2,1)S(1)} %pad_maximum_fusion.2.b0_ref), channel_id=1, source_target_pairs={{0,7},{1,6},{2,5},{3,4},{4,3},{5,2},{6,1},{7,0},{8,15},{9,14},{10,... | collective-permute-start | bytes 417800 | tf_op jit(solution)/shard_map/ppermute | solution.py:346
  (5 other events, 15.7 us)

commit v8 on v7

--- a/solution.py
+++ b/solution.py
@@ -465,7 +465,8 @@
     got = [swap_z(mine, flip) for flip in (1, 2, 3)]
     *got, rows, qone, qtwo = together((*got, rows, qone, qtwo))
     part = (wide(mine) + wide(got[0])) + (wide(got[1]) + wide(got[2]))
-    part = (part + swap(part, "gy", 9)).astype(BF16)
+    mine = part.astype(BF16)
+    part = (wide(mine) + wide(swap(mine, "gy", 9))).astype(BF16)
     got = together([swap_x(part, flip) for flip in (1, 3, 2)])
     part = jnp.stack([part, got[0], got[2], got[1]])
     a, b = part[:2], part[2:]

time: 91.5 us -> 91 us (level)
  waiting for transfers between devices: 34 us -> 32.7 us
where the time goes in v8:
time: 91 us; the launch traced here: 90.8 us
  starting transfers between devices  44.6 us (49%)
  waiting for transfers between devices  32.7 us (36%)
  Pallas kernels  11.9 us (13%)
  between operations  1.05 us (1%)
    ppermute x11, waiting for transfers between devices, swap(): lax.ppermute(value, axis, [(i, i ^ flip) for i in range(lax.axis_size(axi...  19.9 us
    ppermute x9, starting transfers between devices, swap_side(): lax.ppermute(value, axis, [(i, partner(i, which, count)) for i in range(c...  19.7 us
    ppermute x9, starting transfers between devices, swap_far(): return lax.ppermute(value, ('gx', 'gy'), pairs)  13 us
    ppermute x11, starting transfers between devices, swap(): lax.ppermute(value, axis, [(i, i ^ flip) for i in range(lax.axis_size(axi...  12 us
    pallas_call x7, Pallas kernels, call(): pl.pallas_call(kernel, out_shape=tuple((jax.ShapeDtypeStruct(shape, dtype...  11.9 us
    ppermute x9, waiting for transfers between devices, swap_far(): return lax.ppermute(value, ('gx', 'gy'), pairs)  10.4 us
    ppermute x9, waiting for transfers between devices, swap_side(): lax.ppermute(value, axis, [(i, partner(i, which, count)) for i in range(c...  2.5 us
  transfers between devices with their start and end apart: 29, of which 16 were waited for; matrix products, arithmetic and copies ran while one was open for 0% of the time, Pallas kernels for 3%

profile of v8, /device:TPU:1, one launch (start us, length us, event | category | flops | bytes accessed | tf_op | source)
XLA Modules:
  0.0 90.8 jit_solution(5913342614285844765)
XLA Ops:
  2.1 9.1 %collective-permute-start = (bf16[3,64,128]{2,1,0:T(8,128)(2,1)S(1)}, bf16[3,64,128]{2,1,0:T(8,128)(2,1)S(1)}, u32[]{:S(2)}, u32[]{:S(2)}) collective-permute-start(bf16[3,64,128]{2,1,0:T(8,128)(2,1)S(1)} %get-tuple-element.52), channel_id=1, source_target_pairs={{0,240},{16,32},{32,16},{48,64},{64,48},{80,96},{96,80},{112,128},... | collective-permute-start | bytes 147464 | tf_op jit(solution)/shard_map/ppermute | solution.py:359
  12.7 1.7 %lay_weights.1 = (bf16[192,1728]{1,0:T(8,128)(2,1)S(1)}, bf16[128,1728]{1,0:T(8,128)(2,1)S(1)}, bf16[576,384]{1,0:T(8,128)(2,1)S(1)}) custom-call(bf16[1728,192]{1,0:T(8,128)(2,1)} %bitcast.55, bf16[1728,128]{1,0:T(8,128)(2,1)} %bitcast.56), custom_call_target="tpu_custom_call" | custom-call | flops 1000000 | bytes 2500000 | tf_op jit(solution)/shard_map/lay_weights/pallas_call | solution.py:121
  14.5 3.6 %collective-permute-start.4 = (bf16[6,64,128]{2,1,0:T(8,128)(2,1)S(1)}, bf16[6,64,128]{2,1,0:T(8,128)(2,1)S(1)}, u32[]{:S(2)}, u32[]{:S(2)}) collective-permute-start(bf16[6,64,128]{2,1,0:T(8,128)(2,1)S(1)} %get-tuple-element.59), channel_id=1, source_target_pairs={{0,15},{1,2},{2,1},{3,4},{4,3},{5,6},{6,5},{7,8},{8,7},{9,10},{10,... | collective-permute-start | bytes 294920 | tf_op jit(solution)/shard_map/ppermute | solution.py:359
  18.3 1.7 %collective-permute-done.1.xmid_ref = bf16[7,64,128]{2,1,0:T(8,128)(2,1)S(1)} collective-permute-done((bf16[7,64,128]{2,1,0:T(8,128)(2,1)S(1)}, bf16[7,64,128]{2,1,0:T(8,128)(2,1)S(1)}, u32[]{:S(2)}, u32[]{:S(2)}) %collective-permute-start.1) | collective-permute-done | bytes 114720 | tf_op jit(solution)/shard_map/ppermute | solution.py:359
  20.8 5.8 %local_grads.1 = (bf16[2368,128]{1,0:T(8,128)(2,1)S(1)}, f32[4,4,136,128]{3,2,1,0:T(8,128)S(1)}, f32[16,64,128]{2,1,0:T(8,128)S(1)}, f32[6,64,128]{2,1,0:T(8,128)S(1)}, bf16[3,64,128]{2,1,0:T(8,128)(2,1)S(1)}) custom-call(bf16[16,64,128]{2,1,0:T(8,128)(2,1)S(1)} %get-tuple-element.49.skip_ref, bf16[16,64,128]{2,1,0:T(8,128)(2,1)S(1)} %get-tuple-element.50.cot_ref, ...), custom_call_target="tpu_custom_call" | custom-call | flops 3000000000 | bytes 8000000 | tf_op jit(solution)/shard_map/local_grads/pallas_call | solution.py:121
  26.6 2.5 %collective-permute-start.6 = (bf16[2368,128]{1,0:T(8,128)(2,1)S(1)}, bf16[2368,128]{1,0:T(8,128)(2,1)S(1)}, u32[]{:S(2)}, u32[]{:S(2)}) collective-permute-start(bf16[2368,128]{1,0:T(8,128)(2,1)S(1)} %get-tuple-element.62), channel_id=1, source_target_pairs={{0,1},{1,0},{2,3},{3,2},{4,5},{5,4},{6,7},{7,6},{8,9},{9,8},{10,11... | collective-permute-start | bytes 1818632 | tf_op jit(solution)/shard_map/ppermute | solution.py:346
  29.0 1.7 %collective-permute-done.6 = bf16[2368,128]{1,0:T(8,128)(2,1)S(1)} collective-permute-done((bf16[2368,128]{1,0:T(8,128)(2,1)S(1)}, bf16[2368,128]{1,0:T(8,128)(2,1)S(1)}, u32[]{:S(2)}, u32[]{:S(2)}) %collective-permute-start.6) | collective-permute-done | bytes 606240 | tf_op jit(solution)/shard_map/ppermute | solution.py:346
  30.9 3.0 %collective-permute-start.8 = (bf16[2,2,136,128]{3,2,1,0:T(8,128)(2,1)S(1)}, bf16[2,2,136,128]{3,2,1,0:T(8,128)(2,1)S(1)}, u32[]{:S(2)}, u32[]{:S(2)}) collective-permute-start(bf16[2,2,136,128]{3,2,1,0:T(8,128)(2,1)S(1)} %pad_maximum_fusion), channel_id=1, source_target_pairs={{0,7},{1,6},{2,5},{3,4},{4,3},{5,2},{6,1},{7,0},{8,15},{9,14},{10,... | collective-permute-start | bytes 417800 | tf_op jit(solution)/shard_map/ppermute | solution.py:346
  33.9 4.0 %collective-permute-done.8 = bf16[2,2,136,128]{3,2,1,0:T(8,128)(2,1)S(1)} collective-permute-done((bf16[2,2,136,128]{3,2,1,0:T(8,128)(2,1)S(1)}, bf16[2,2,136,128]{3,2,1,0:T(8,128)(2,1)S(1)}, u32[]{:S(2)}, u32[]{:S(2)}) %collective-permute-start.8) | collective-permute-done | bytes 139296 | tf_op jit(solution)/shard_map/ppermute | solution.py:346
  37.9 1.5 %collective-permute-done.7 = bf16[2,2,136,128]{3,2,1,0:T(8,128)(2,1)S(1)} collective-permute-done((bf16[2,2,136,128]{3,2,1,0:T(8,128)(2,1)S(1)}, bf16[2,2,136,128]{3,2,1,0:T(8,128)(2,1)S(1)}, u32[]{:S(2)}, u32[]{:S(2)}) %collective-permute-start.7) | collective-permute-done | bytes 139296 | tf_op jit(solution)/shard_map/ppermute | solution.py:346
  41.2 4.7 %collective-permute-start.14 = (bf16[3,64,128]{2,1,0:T(8,128)(2,1)S(1)}, bf16[3,64,128]{2,1,0:T(8,128)(2,1)S(1)}, u32[]{:S(2)}, u32[]{:S(2)}) collective-permute-start(bf16[3,64,128]{2,1,0:T(8,128)(2,1)S(1)} %get-tuple-element.67), channel_id=1, source_target_pairs={{0,240},{16,32},{32,16},{48,64},{64,48},{80,96},{96,80},{112,128},... | collective-permute-start | bytes 147464 | tf_op jit(solution)/shard_map/ppermute | solution.py:359
  46.2 3.4 %collective-permute-start.12 = (bf16[136,128]{1,0:T(8,128)(2,1)S(1)}, bf16[136,128]{1,0:T(8,128)(2,1)S(1)}, u32[]{:S(2)}, u32[]{:S(2)}) collective-permute-start(bf16[136,128]{1,0:T(8,128)(2,1)S(1)} %get-tuple-element.108), channel_id=1, source_target_pairs={{0,32},{1,33},{2,34},{3,35},{4,36},{5,37},{6,38},{7,39},{8,40},{9,... | collective-permute-start | bytes 104456 | tf_op jit(solution)/shard_map/ppermute | solution.py:378
  49.6 1.5 %collective-permute-done.11 = bf16[328,128]{1,0:T(8,128)(2,1)S(1)} collective-permute-done((bf16[328,128]{1,0:T(8,128)(2,1)S(1)}, bf16[328,128]{1,0:T(8,128)(2,1)S(1)}, u32[]{:S(2)}, u32[]{:S(2)}) %collective-permute-start.11) | collective-permute-done | bytes 84000 | tf_op jit(solution)/shard_map/ppermute | solution.py:378
  52.1 3.9 %collective-permute-start.17 = (bf16[136,128]{1,0:T(8,128)(2,1)S(1)}, bf16[136,128]{1,0:T(8,128)(2,1)S(1)}, u32[]{:S(2)}, u32[]{:S(2)}) collective-permute-start(bf16[136,128]{1,0:T(8,128)(2,1)S(1)} %fusion.11), channel_id=1, source_target_pairs={{0,193},{1,192},{2,195},{3,194},{4,197},{5,196},{6,199},{7,198},{8... | collective-permute-start | bytes 104456 | tf_op jit(solution)/shard_map/ppermute | solution.py:378
  56.6 1.9 %collective-permute-start.15 = (bf16[136,128]{1,0:T(8,128)(2,1)S(1)}, bf16[136,128]{1,0:T(8,128)(2,1)S(1)}, u32[]{:S(2)}, u32[]{:S(2)}) collective-permute-start(bf16[136,128]{1,0:T(8,128)(2,1)S(1)} %fusion.11), channel_id=1, source_target_pairs={{0,65},{1,64},{2,67},{3,66},{4,69},{5,68},{6,71},{7,70},{8,73},{9,... | collective-permute-start | bytes 104456 | tf_op jit(solution)/shard_map/ppermute | solution.py:378
  58.6 5.3 %collective-permute-done.16 = bf16[136,128]{1,0:T(8,128)(2,1)S(1)} collective-permute-done((bf16[136,128]{1,0:T(8,128)(2,1)S(1)}, bf16[136,128]{1,0:T(8,128)(2,1)S(1)}, u32[]{:S(2)}, u32[]{:S(2)}) %collective-permute-start.16) | collective-permute-done | bytes 34848 | tf_op jit(solution)/shard_map/ppermute | solution.py:378
  64.0 3.3 %collective-permute-done.18 = bf16[136,128]{1,0:T(8,128)(2,1)S(1)} collective-permute-done((bf16[136,128]{1,0:T(8,128)(2,1)S(1)}, bf16[136,128]{1,0:T(8,128)(2,1)S(1)}, u32[]{:S(2)}, u32[]{:S(2)}) %collective-permute-start.18) | collective-permute-done | bytes 34848 | tf_op jit(solution)/shard_map/ppermute | solution.py:346
  68.5 1.5 %collective-permute-start.20 = (bf16[136,128]{1,0:T(8,128)(2,1)S(1)}, bf16[136,128]{1,0:T(8,128)(2,1)S(1)}, u32[]{:S(2)}, u32[]{:S(2)}) collective-permute-start(bf16[136,128]{1,0:T(8,128)(2,1)S(1)} %add_convert_fusion), channel_id=1, source_target_pairs={{0,49},{1,48},{2,51},{3,50},{4,53},{5,52},{6,55},{7,54},{8,57},{9,... | collective-permute-start | bytes 104456 | tf_op jit(solution)/shard_map/ppermute | solution.py:378
  72.1 1.7 %collective-permute-done.20 = bf16[136,128]{1,0:T(8,128)(2,1)S(1)} collective-permute-done((bf16[136,128]{1,0:T(8,128)(2,1)S(1)}, bf16[136,128]{1,0:T(8,128)(2,1)S(1)}, u32[]{:S(2)}, u32[]{:S(2)}) %collective-permute-start.20) | collective-permute-done | bytes 34848 | tf_op jit(solution)/shard_map/ppermute | solution.py:378
  74.6 1.5 %collective-permute-start.22 = (bf16[2,136,128]{2,1,0:T(8,128)(2,1)S(1)}, bf16[2,136,128]{2,1,0:T(8,128)(2,1)S(1)}, u32[]{:S(2)}, u32[]{:S(2)}) collective-permute-start(bf16[2,136,128]{2,1,0:T(8,128)(2,1)S(1)} %get-tuple-element.106), channel_id=1, source_target_pairs={{0,7},{1,6},{2,5},{3,4},{4,3},{5,2},{6,1},{7,0},{8,15},{9,14},{10,... | collective-permute-start | bytes 208904 | tf_op jit(solution)/shard_map/ppermute | solution.py:346
  76.1 2.5 %collective-permute-done.23 = bf16[2,136,128]{2,1,0:T(8,128)(2,1)S(1)} collective-permute-done((bf16[2,136,128]{2,1,0:T(8,128)(2,1)S(1)}, bf16[2,136,128]{2,1,0:T(8,128)(2,1)S(1)}, u32[]{:S(2)}, u32[]{:S(2)}) %collective-permute-start.23) | collective-permute-done | bytes 69664 | tf_op jit(solution)/shard_map/ppermute | solution.py:346
  79.9 1.7 %collective-permute-start.25 = (bf16[2,2,136,128]{3,2,1,0:T(8,128)(2,1)S(1)}, bf16[2,2,136,128]{3,2,1,0:T(8,128)(2,1)S(1)}, u32[]{:S(2)}, u32[]{:S(2)}) collective-permute-start(bf16[2,2,136,128]{3,2,1,0:T(8,128)(2,1)S(1)} %pad_maximum_fusion.2.b0_ref), channel_id=1, source_target_pairs={{0,7},{1,6},{2,5},{3,4},{4,3},{5,2},{6,1},{7,0},{8,15},{9,14},{10,... | collective-permute-start | bytes 417800 | tf_op jit(solution)/shard_map/ppermute | solution.py:346
  81.7 4.0 %collective-permute-done.24.a1_ref = bf16[2,2,136,128]{3,2,1,0:T(8,128)(2,1)S(1)} collective-permute-done((bf16[2,2,136,128]{3,2,1,0:T(8,128)(2,1)S(1)}, bf16[2,2,136,128]{3,2,1,0:T(8,128)(2,1)S(1)}, u32[]{:S(2)}, u32[]{:S(2)}) %collective-permute-start.24) | collective-permute-done | bytes 139296 | tf_op jit(solution)/shard_map/ppermute | solution.py:346
  89.0 1.7 %unpack.1 = (f32[1728,192]{1,0:T(8,128)}, f32[1728,128]{1,0:T(8,128)}) custom-call(bf16[2,2,136,128]{3,2,1,0:T(8,128)(2,1)S(1)} %pad_maximum_fusion.1.a0_ref, bf16[2,2,136,128]{3,2,1,0:T(8,128)(2,1)S(1)} %collective-permute-done.24.a1_ref, bf16[2,2,136,128]{3,2,1,0:T(8,128)(2,1)S(1)} %pad_maximum_fusion.2.b0_ref, ...), custom_call_target="tpu_custom_call" | custom-call | flops 1000000 | bytes 5000000 | tf_op jit(solution)/shard_map/unpack/pallas_call | solution.py:121
  (67 shorter events, 16.7 us)
Async XLA Ops:
  2.1 12.3 %collective-permute-start = (bf16[3,64,128]{2,1,0:T(8,128)(2,1)S(1)}, bf16[3,64,128]{2,1,0:T(8,128)(2,1)S(1)}, u32[]{:S(2)}, u32[]{:S(2)}) collective-permute-start(bf16[3,64,128]{2,1,0:T(8,128)(2,1)S(1)} %get-tuple-element.52), channel_id=1, source_target_pairs={{0,240},{16,32},{32,16},{48,64},{64,48},{80,96},{96,80},{112,128},... | collective-permute-start | bytes 147464 | tf_op jit(solution)/shard_map/ppermute | solution.py:359
  11.2 8.8 %collective-permute-start.1 = (bf16[7,64,128]{2,1,0:T(8,128)(2,1)S(1)}, bf16[7,64,128]{2,1,0:T(8,128)(2,1)S(1)}, u32[]{:S(2)}, u32[]{:S(2)}) collective-permute-start(bf16[7,64,128]{2,1,0:T(8,128)(2,1)S(1)} %get-tuple-element.53), channel_id=1, source_target_pairs={{0,240},{16,32},{32,16},{48,64},{64,48},{80,96},{96,80},{112,128},... | collective-permute-start | bytes 344072 | tf_op jit(solution)/shard_map/ppermute | solution.py:359
  12.0 8.0 %collective-permute-start.3 = (bf16[7,64,128]{2,1,0:T(8,128)(2,1)S(1)}, bf16[7,64,128]{2,1,0:T(8,128)(2,1)S(1)}, u32[]{:S(2)}, u32[]{:S(2)}) collective-permute-start(bf16[7,64,128]{2,1,0:T(8,128)(2,1)S(1)} %get-tuple-element.55), channel_id=1, source_target_pairs={{0,16},{16,0},{32,48},{48,32},{64,80},{80,64},{96,112},{112,96},{1... | collective-permute-start | bytes 344072 | tf_op jit(solution)/shard_map/ppermute | solution.py:359
  14.5 6.2 %collective-permute-start.4 = (bf16[6,64,128]{2,1,0:T(8,128)(2,1)S(1)}, bf16[6,64,128]{2,1,0:T(8,128)(2,1)S(1)}, u32[]{:S(2)}, u32[]{:S(2)}) collective-permute-start(bf16[6,64,128]{2,1,0:T(8,128)(2,1)S(1)} %get-tuple-element.59), channel_id=1, source_target_pairs={{0,15},{1,2},{2,1},{3,4},{4,3},{5,6},{6,5},{7,8},{8,7},{9,10},{10,... | collective-permute-start | bytes 294920 | tf_op jit(solution)/shard_map/ppermute | solution.py:359
  26.6 4.1 %collective-permute-start.6 = (bf16[2368,128]{1,0:T(8,128)(2,1)S(1)}, bf16[2368,128]{1,0:T(8,128)(2,1)S(1)}, u32[]{:S(2)}, u32[]{:S(2)}) collective-permute-start(bf16[2368,128]{1,0:T(8,128)(2,1)S(1)} %get-tuple-element.62), channel_id=1, source_target_pairs={{0,1},{1,0},{2,3},{3,2},{4,5},{5,4},{6,7},{7,6},{8,9},{9,8},{10,11... | collective-permute-start | bytes 1818632 | tf_op jit(solution)/shard_map/ppermute | solution.py:346
  30.9 7.0 %collective-permute-start.8 = (bf16[2,2,136,128]{3,2,1,0:T(8,128)(2,1)S(1)}, bf16[2,2,136,128]{3,2,1,0:T(8,128)(2,1)S(1)}, u32[]{:S(2)}, u32[]{:S(2)}) collective-permute-start(bf16[2,2,136,128]{3,2,1,0:T(8,128)(2,1)S(1)} %pad_maximum_fusion), channel_id=1, source_target_pairs={{0,7},{1,6},{2,5},{3,4},{4,3},{5,2},{6,1},{7,0},{8,15},{9,14},{10,... | collective-permute-start | bytes 417800 | tf_op jit(solution)/shard_map/ppermute | solution.py:346
  33.9 5.4 %collective-permute-start.7 = (bf16[2,2,136,128]{3,2,1,0:T(8,128)(2,1)S(1)}, bf16[2,2,136,128]{3,2,1,0:T(8,128)(2,1)S(1)}, u32[]{:S(2)}, u32[]{:S(2)}) collective-permute-start(bf16[2,2,136,128]{3,2,1,0:T(8,128)(2,1)S(1)} %stack.56), channel_id=1, source_target_pairs={{0,3},{1,2},{2,1},{3,0},{4,7},{5,6},{6,5},{7,4},{8,11},{9,10},{10,... | collective-permute-start | bytes 417800 | tf_op jit(solution)/shard_map/ppermute | solution.py:346
  39.4 6.5 %collective-permute-start.10 = (bf16[2,136,128]{2,1,0:T(8,128)(2,1)S(1)}, bf16[2,136,128]{2,1,0:T(8,128)(2,1)S(1)}, u32[]{:S(2)}, u32[]{:S(2)}) collective-permute-start(bf16[2,136,128]{2,1,0:T(8,128)(2,1)S(1)} %get-tuple-element.99), channel_id=1, source_target_pairs={{0,3},{1,2},{2,1},{3,0},{4,7},{5,6},{6,5},{7,4},{8,11},{9,10},{10,... | collective-permute-start | bytes 208904 | tf_op jit(solution)/shard_map/ppermute | solution.py:346
  39.8 6.1 %collective-permute-start.9 = (bf16[2,136,128]{2,1,0:T(8,128)(2,1)S(1)}, bf16[2,136,128]{2,1,0:T(8,128)(2,1)S(1)}, u32[]{:S(2)}, u32[]{:S(2)}) collective-permute-start(bf16[2,136,128]{2,1,0:T(8,128)(2,1)S(1)} %get-tuple-element.100), channel_id=1, source_target_pairs={{0,7},{1,6},{2,5},{3,4},{4,3},{5,2},{6,1},{7,0},{8,15},{9,14},{10,... | collective-permute-start | bytes 208904 | tf_op jit(solution)/shard_map/ppermute | solution.py:346
  41.2 10.0 %collective-permute-start.14 = (bf16[3,64,128]{2,1,0:T(8,128)(2,1)S(1)}, bf16[3,64,128]{2,1,0:T(8,128)(2,1)S(1)}, u32[]{:S(2)}, u32[]{:S(2)}) collective-permute-start(bf16[3,64,128]{2,1,0:T(8,128)(2,1)S(1)} %get-tuple-element.67), channel_id=1, source_target_pairs={{0,240},{16,32},{32,16},{48,64},{64,48},{80,96},{96,80},{112,128},... | collective-permute-start | bytes 147464 | tf_op jit(solution)/shard_map/ppermute | solution.py:359
  46.0 5.1 %collective-permute-start.11 = (bf16[328,128]{1,0:T(8,128)(2,1)S(1)}, bf16[328,128]{1,0:T(8,128)(2,1)S(1)}, u32[]{:S(2)}, u32[]{:S(2)}) collective-permute-start(bf16[328,128]{1,0:T(8,128)(2,1)S(1)} %pad_maximum_fusion.3), channel_id=1, source_target_pairs={{0,17},{1,16},{2,19},{3,18},{4,21},{5,20},{6,23},{7,22},{8,25},{9,... | collective-permute-start | bytes 251912 | tf_op jit(solution)/shard_map/ppermute | solution.py:378
  46.1 5.9 %collective-permute-start.13 = (bf16[136,128]{1,0:T(8,128)(2,1)S(1)}, bf16[136,128]{1,0:T(8,128)(2,1)S(1)}, u32[]{:S(2)}, u32[]{:S(2)}) collective-permute-start(bf16[136,128]{1,0:T(8,128)(2,1)S(1)} %get-tuple-element.107), channel_id=1, source_target_pairs={{0,49},{1,48},{2,51},{3,50},{4,53},{5,52},{6,55},{7,54},{8,57},{9,... | collective-permute-start | bytes 104456 | tf_op jit(solution)/shard_map/ppermute | solution.py:378
  46.2 5.8 %collective-permute-start.12 = (bf16[136,128]{1,0:T(8,128)(2,1)S(1)}, bf16[136,128]{1,0:T(8,128)(2,1)S(1)}, u32[]{:S(2)}, u32[]{:S(2)}) collective-permute-start(bf16[136,128]{1,0:T(8,128)(2,1)S(1)} %get-tuple-element.108), channel_id=1, source_target_pairs={{0,32},{1,33},{2,34},{3,35},{4,36},{5,37},{6,38},{7,39},{8,40},{9,... | collective-permute-start | bytes 104456 | tf_op jit(solution)/shard_map/ppermute | solution.py:378
  52.1 6.5 %collective-permute-start.17 = (bf16[136,128]{1,0:T(8,128)(2,1)S(1)}, bf16[136,128]{1,0:T(8,128)(2,1)S(1)}, u32[]{:S(2)}, u32[]{:S(2)}) collective-permute-start(bf16[136,128]{1,0:T(8,128)(2,1)S(1)} %fusion.11), channel_id=1, source_target_pairs={{0,193},{1,192},{2,195},{3,194},{4,197},{5,196},{6,199},{7,198},{8... | collective-permute-start | bytes 104456 | tf_op jit(solution)/shard_map/ppermute | solution.py:378
  56.0 7.9 %collective-permute-start.16 = (bf16[136,128]{1,0:T(8,128)(2,1)S(1)}, bf16[136,128]{1,0:T(8,128)(2,1)S(1)}, u32[]{:S(2)}, u32[]{:S(2)}) collective-permute-start(bf16[136,128]{1,0:T(8,128)(2,1)S(1)} %fusion.11), channel_id=1, source_target_pairs={{0,128},{1,129},{2,130},{3,131},{4,132},{5,133},{6,134},{7,135},{8... | collective-permute-start | bytes 104456 | tf_op jit(solution)/shard_map/ppermute | solution.py:378
  56.6 7.4 %collective-permute-start.15 = (bf16[136,128]{1,0:T(8,128)(2,1)S(1)}, bf16[136,128]{1,0:T(8,128)(2,1)S(1)}, u32[]{:S(2)}, u32[]{:S(2)}) collective-permute-start(bf16[136,128]{1,0:T(8,128)(2,1)S(1)} %fusion.11), channel_id=1, source_target_pairs={{0,65},{1,64},{2,67},{3,66},{4,69},{5,68},{6,71},{7,70},{8,73},{9,... | collective-permute-start | bytes 104456 | tf_op jit(solution)/shard_map/ppermute | solution.py:378
  67.4 4.7 %collective-permute-start.21 = (bf16[136,128]{1,0:T(8,128)(2,1)S(1)}, bf16[136,128]{1,0:T(8,128)(2,1)S(1)}, u32[]{:S(2)}, u32[]{:S(2)}) collective-permute-start(bf16[136,128]{1,0:T(8,128)(2,1)S(1)} %add_convert_fusion), channel_id=1, source_target_pairs={{0,32},{1,33},{2,34},{3,35},{4,36},{5,37},{6,38},{7,39},{8,40},{9,... | collective-permute-start | bytes 104456 | tf_op jit(solution)/shard_map/ppermute | solution.py:378
  68.5 5.2 %collective-permute-start.20 = (bf16[136,128]{1,0:T(8,128)(2,1)S(1)}, bf16[136,128]{1,0:T(8,128)(2,1)S(1)}, u32[]{:S(2)}, u32[]{:S(2)}) collective-permute-start(bf16[136,128]{1,0:T(8,128)(2,1)S(1)} %add_convert_fusion), channel_id=1, source_target_pairs={{0,49},{1,48},{2,51},{3,50},{4,53},{5,52},{6,55},{7,54},{8,57},{9,... | collective-permute-start | bytes 104456 | tf_op jit(solution)/shard_map/ppermute | solution.py:378
  70.4 11.2 %collective-permute-start.26 = (bf16[64,128]{1,0:T(8,128)(2,1)S(1)}, bf16[64,128]{1,0:T(8,128)(2,1)S(1)}, u32[]{:S(2)}, u32[]{:S(2)}) collective-permute-start(bf16[64,128]{1,0:T(8,128)(2,1)S(1)} %get-tuple-element.86), channel_id=1, source_target_pairs={{0,1},{1,0},{2,3},{3,2},{4,5},{5,4},{6,7},{7,6},{8,9},{9,8},{10,11... | collective-permute-start | bytes 49160 | tf_op jit(solution)/shard_map/ppermute | solution.py:359
  71.1 10.6 %collective-permute-start.27 = (bf16[64,128]{1,0:T(8,128)(2,1)S(1)}, bf16[64,128]{1,0:T(8,128)(2,1)S(1)}, u32[]{:S(2)}, u32[]{:S(2)}) collective-permute-start(bf16[64,128]{1,0:T(8,128)(2,1)S(1)} %get-tuple-element.87), channel_id=1, source_target_pairs={{0,15},{1,2},{2,1},{3,4},{4,3},{5,6},{6,5},{7,8},{8,7},{9,10},{10,... | collective-permute-start | bytes 49160 | tf_op jit(solution)/shard_map/ppermute | solution.py:359
  73.8 4.8 %collective-permute-start.23 = (bf16[2,136,128]{2,1,0:T(8,128)(2,1)S(1)}, bf16[2,136,128]{2,1,0:T(8,128)(2,1)S(1)}, u32[]{:S(2)}, u32[]{:S(2)}) collective-permute-start(bf16[2,136,128]{2,1,0:T(8,128)(2,1)S(1)} %get-tuple-element.104), channel_id=1, source_target_pairs={{0,3},{1,2},{2,1},{3,0},{4,7},{5,6},{6,5},{7,4},{8,11},{9,10},{10,... | collective-permute-start | bytes 208904 | tf_op jit(solution)/shard_map/ppermute | solution.py:346
  74.6 5.2 %collective-permute-start.22 = (bf16[2,136,128]{2,1,0:T(8,128)(2,1)S(1)}, bf16[2,136,128]{2,1,0:T(8,128)(2,1)S(1)}, u32[]{:S(2)}, u32[]{:S(2)}) collective-permute-start(bf16[2,136,128]{2,1,0:T(8,128)(2,1)S(1)} %get-tuple-element.106), channel_id=1, source_target_pairs={{0,7},{1,6},{2,5},{3,4},{4,3},{5,2},{6,1},{7,0},{8,15},{9,14},{10,... | collective-permute-start | bytes 208904 | tf_op jit(solution)/shard_map/ppermute | solution.py:346
  79.8 5.8 %collective-permute-start.24 = (bf16[2,2,136,128]{3,2,1,0:T(8,128)(2,1)S(1)}, bf16[2,2,136,128]{3,2,1,0:T(8,128)(2,1)S(1)}, u32[]{:S(2)}, u32[]{:S(2)}) collective-permute-start(bf16[2,2,136,128]{3,2,1,0:T(8,128)(2,1)S(1)} %pad_maximum_fusion.1.a0_ref), channel_id=1, source_target_pairs={{0,3},{1,2},{2,1},{3,0},{4,7},{5,6},{6,5},{7,4},{8,11},{9,10},{10,... | collective-permute-start | bytes 417800 | tf_op jit(solution)/shard_map/ppermute | solution.py:346
  79.9 6.9 %collective-permute-start.25 = (bf16[2,2,136,128]{3,2,1,0:T(8,128)(2,1)S(1)}, bf16[2,2,136,128]{3,2,1,0:T(8,128)(2,1)S(1)}, u32[]{:S(2)}, u32[]{:S(2)}) collective-permute-start(bf16[2,2,136,128]{3,2,1,0:T(8,128)(2,1)S(1)} %pad_maximum_fusion.2.b0_ref), channel_id=1, source_target_pairs={{0,7},{1,6},{2,5},{3,4},{4,3},{5,2},{6,1},{7,0},{8,15},{9,14},{10,... | collective-permute-start | bytes 417800 | tf_op jit(solution)/shard_map/ppermute | solution.py:346
  (5 other events, 15.0 us)

commit v9 on v7

--- a/solution.py
+++ b/solution.py
@@ -317,7 +317,7 @@
     out_ref[...] = cells_ref[...].reshape(SKIP, SIZE_X, SIZE_Y, LANES).astype(BF16)
 
 
-def unpack_kernel(a0_ref, a1_ref, b0_ref, b1_ref, other_ref, dec_hbm, coarse_hbm, full_ref, dec_ref, sent):
+def unpack_kernel(a0_ref, a1_ref, b0_ref, b1_ref, near_ref, far_ref, dec_hbm, coarse_hbm, full_ref, dec_ref, sent):
     place = places()
     half, y, x = half_of(place), (place[1] >> 1) & 3, place[0] & 3
     for side, (refs, order) in enumerate((((a0_ref, a1_ref), ORDER_A), ((b0_ref, b1_ref), ORDER_B))):
@@ -327,7 +327,7 @@
                 row = pl.multiple_of((at + 16 * half) * ROWS, ROWS)
                 full_ref[pl.ds(row, ROWS), :] = refs[index // 2][index % 2, xr].astype(F32)
                 row = pl.multiple_of((at + 16 * (1 - half)) * ROWS, ROWS)
-                full_ref[pl.ds(row, ROWS), :] = other_ref[4 * side + index, xr].astype(F32)
+                full_ref[pl.ds(row, ROWS), :] = (near_ref, far_ref)[index // 2][2 * side + index % 2, xr].astype(F32)
     middle, part = LANES // 2, DEC // 2
     copies = [pltpu.make_async_copy(full_ref.at[pl.ds(DEC + part, DEC)], coarse_hbm, sent.at[0])]
     copies[0].start()
@@ -469,10 +469,13 @@
     got = together([swap_x(part, flip) for flip in (1, 3, 2)])
     part = jnp.stack([part, got[0], got[2], got[1]])
     a, b = part[:2], part[2:]
-    a_got, b_got = together((swap_y(a, A_SECOND), swap_y(b, B_SECOND)))
+    a_got, b_got, qone, qtwo = together(
+        (swap_y(a, A_SECOND), swap_y(b, B_SECOND), swap_side(qone, "gy", 0), swap_side(qtwo, "gy", 1))
+    )
     a_near, b_near = jnp.stack([a, a_got]), jnp.stack([b, b_got])
-    a_far, b_far, qone, qtwo = together((swap_y(a_near, A_FIRST), swap_y(b_near, B_FIRST), swap_side(qone, "gy", 0), swap_side(qtwo, "gy", 1)))
-    other = swap(jnp.concatenate([a_near, a_far, b_near, b_far]), "gy", 1)
+    a_far, b_far = together((swap_y(a_near, A_FIRST), swap_y(b_near, B_FIRST)))
+    near = swap(jnp.concatenate([a_near, b_near]), "gy", 1)
+    far = swap(jnp.concatenate([a_far, b_far]), "gy", 1)
     (skip_grad,) = call(
         skip_kernel, "skip_gradient", (((SKIP, SIZE_X, SIZE_Y, LANES), BF16),), (((SKIP * BLOCKS, LANES), F32),),
         8, (1_000_000, 1_000_000), rows, qone, qtwo, jskip,
@@ -480,7 +483,7 @@
     dec, coarse = call(
         unpack_kernel, "unpack", (((DEC, JOINED), F32), ((DEC, COARSE), F32)),
         (((CHUNKS * ROWS, LANES), F32), ((DEC, JOINED), F32), pltpu.SemaphoreType.DMA((3,))),
-        16, (1_000_000, 5_000_000), a_near, a_far, b_near, b_far, other, gives=pltpu.HBM,
+        16, (1_000_000, 5_000_000), a_near, a_far, b_near, b_far, near, far, gives=pltpu.HBM,
     )
     return (
         skip_grad,

time: 91.5 us -> 92.1 us (level)
  starting transfers between devices: 43.9 us -> 48.3 us
  waiting for transfers between devices: 34 us -> 30.2 us
    ppermute x11 -> x12, waiting for transfers between devices: 20.8 us -> 13.7 us  [swap(): lax.ppermute(value, axis, [(i, i ^ flip) for i in range(lax.axis_size(axi...]
    ppermute x11 -> x12, starting transfers between devices: 11.3 us -> 15.2 us  [swap(): lax.ppermute(value, axis, [(i, i ^ flip) for i in range(lax.axis_size(axi...]
    ppermute x9, waiting for transfers between devices: 2.5 us -> 5.17 us  [swap_side(): lax.ppermute(value, axis, [(i, partner(i, which, count)) for i in range(c...]
  transfers between devices with their start and end apart: 29 -> 30, of which waited for: 16 -> 16; matrix products, arithmetic and copies ran while one was open for 0% -> 0% of each run, Pallas kernels for 3% -> 3%
where the time goes in v9:
time: 92.1 us; the launch traced here: 91.9 us
  starting transfers between devices  48.3 us (52%)
  waiting for transfers between devices  30.2 us (33%)
  Pallas kernels  11.9 us (13%)
  between operations  1 us (1%)
    ppermute x9, starting transfers between devices, swap_side(): lax.ppermute(value, axis, [(i, partner(i, which, count)) for i in range(c...  20.1 us
    ppermute x12, starting transfers between devices, swap(): lax.ppermute(value, axis, [(i, i ^ flip) for i in range(lax.axis_size(axi...  15.2 us
    ppermute x12, waiting for transfers between devices, swap(): lax.ppermute(value, axis, [(i, i ^ flip) for i in range(lax.axis_size(axi...  13.7 us
    ppermute x9, starting transfers between devices, swap_far(): return lax.ppermute(value, ('gx', 'gy'), pairs)  13 us
    pallas_call x7, Pallas kernels, call(): pl.pallas_call(kernel, out_shape=tuple((jax.ShapeDtypeStruct(shape, dtype...  11.9 us
    ppermute x9, waiting for transfers between devices, swap_far(): return lax.ppermute(value, ('gx', 'gy'), pairs)  11.4 us
    ppermute x9, waiting for transfers between devices, swap_side(): lax.ppermute(value, axis, [(i, partner(i, which, count)) for i in range(c...  5.17 us
  transfers between devices with their start and end apart: 30, of which 16 were waited for; matrix products, arithmetic and copies ran while one was open for 0% of the time, Pallas kernels for 3%

profile of v9, /device:TPU:1, one launch (start us, length us, event | category | flops | bytes accessed | tf_op | source)
XLA Modules:
  0.0 91.9 jit_solution(9728584790514701940)
XLA Ops:
  2.1 9.1 %collective-permute-start = (bf16[3,64,128]{2,1,0:T(8,128)(2,1)S(1)}, bf16[3,64,128]{2,1,0:T(8,128)(2,1)S(1)}, u32[]{:S(2)}, u32[]{:S(2)}) collective-permute-start(bf16[3,64,128]{2,1,0:T(8,128)(2,1)S(1)} %get-tuple-element.52), channel_id=1, source_target_pairs={{0,240},{16,32},{32,16},{48,64},{64,48},{80,96},{96,80},{112,128},... | collective-permute-start | bytes 147464 | tf_op jit(solution)/shard_map/ppermute | solution.py:359
  12.7 1.7 %lay_weights.1 = (bf16[192,1728]{1,0:T(8,128)(2,1)S(1)}, bf16[128,1728]{1,0:T(8,128)(2,1)S(1)}, bf16[576,384]{1,0:T(8,128)(2,1)S(1)}) custom-call(bf16[1728,192]{1,0:T(8,128)(2,1)} %bitcast.51, bf16[1728,128]{1,0:T(8,128)(2,1)} %bitcast.52), custom_call_target="tpu_custom_call" | custom-call | flops 1000000 | bytes 2500000 | tf_op jit(solution)/shard_map/lay_weights/pallas_call | solution.py:121
  14.5 3.6 %collective-permute-start.4 = (bf16[6,64,128]{2,1,0:T(8,128)(2,1)S(1)}, bf16[6,64,128]{2,1,0:T(8,128)(2,1)S(1)}, u32[]{:S(2)}, u32[]{:S(2)}) collective-permute-start(bf16[6,64,128]{2,1,0:T(8,128)(2,1)S(1)} %get-tuple-element.59), channel_id=1, source_target_pairs={{0,15},{1,2},{2,1},{3,4},{4,3},{5,6},{6,5},{7,8},{8,7},{9,10},{10,... | collective-permute-start | bytes 294920 | tf_op jit(solution)/shard_map/ppermute | solution.py:359
  18.3 1.7 %collective-permute-done.1.xmid_ref = bf16[7,64,128]{2,1,0:T(8,128)(2,1)S(1)} collective-permute-done((bf16[7,64,128]{2,1,0:T(8,128)(2,1)S(1)}, bf16[7,64,128]{2,1,0:T(8,128)(2,1)S(1)}, u32[]{:S(2)}, u32[]{:S(2)}) %collective-permute-start.1) | collective-permute-done | bytes 114720 | tf_op jit(solution)/shard_map/ppermute | solution.py:359
  20.8 5.8 %local_grads.1 = (bf16[2368,128]{1,0:T(8,128)(2,1)S(1)}, f32[4,4,136,128]{3,2,1,0:T(8,128)S(1)}, f32[16,64,128]{2,1,0:T(8,128)S(1)}, f32[6,64,128]{2,1,0:T(8,128)S(1)}, bf16[3,64,128]{2,1,0:T(8,128)(2,1)S(1)}) custom-call(bf16[16,64,128]{2,1,0:T(8,128)(2,1)S(1)} %get-tuple-element.49.skip_ref, bf16[16,64,128]{2,1,0:T(8,128)(2,1)S(1)} %get-tuple-element.50.cot_ref, ...), custom_call_target="tpu_custom_call" | custom-call | flops 3000000000 | bytes 8000000 | tf_op jit(solution)/shard_map/local_grads/pallas_call | solution.py:121
  26.6 2.5 %collective-permute-start.6 = (bf16[2368,128]{1,0:T(8,128)(2,1)S(1)}, bf16[2368,128]{1,0:T(8,128)(2,1)S(1)}, u32[]{:S(2)}, u32[]{:S(2)}) collective-permute-start(bf16[2368,128]{1,0:T(8,128)(2,1)S(1)} %get-tuple-element.62), channel_id=1, source_target_pairs={{0,1},{1,0},{2,3},{3,2},{4,5},{5,4},{6,7},{7,6},{8,9},{9,8},{10,11... | collective-permute-start | bytes 1818632 | tf_op jit(solution)/shard_map/ppermute | solution.py:346
  29.0 1.7 %collective-permute-done.6 = bf16[2368,128]{1,0:T(8,128)(2,1)S(1)} collective-permute-done((bf16[2368,128]{1,0:T(8,128)(2,1)S(1)}, bf16[2368,128]{1,0:T(8,128)(2,1)S(1)}, u32[]{:S(2)}, u32[]{:S(2)}) %collective-permute-start.6) | collective-permute-done | bytes 606240 | tf_op jit(solution)/shard_map/ppermute | solution.py:346
  30.9 3.0 %collective-permute-start.8 = (bf16[2,2,136,128]{3,2,1,0:T(8,128)(2,1)S(1)}, bf16[2,2,136,128]{3,2,1,0:T(8,128)(2,1)S(1)}, u32[]{:S(2)}, u32[]{:S(2)}) collective-permute-start(bf16[2,2,136,128]{3,2,1,0:T(8,128)(2,1)S(1)} %pad_maximum_fusion.2), channel_id=1, source_target_pairs={{0,7},{1,6},{2,5},{3,4},{4,3},{5,2},{6,1},{7,0},{8,15},{9,14},{10,... | collective-permute-start | bytes 417800 | tf_op jit(solution)/shard_map/ppermute | solution.py:346
  33.9 4.0 %collective-permute-done.8 = bf16[2,2,136,128]{3,2,1,0:T(8,128)(2,1)S(1)} collective-permute-done((bf16[2,2,136,128]{3,2,1,0:T(8,128)(2,1)S(1)}, bf16[2,2,136,128]{3,2,1,0:T(8,128)(2,1)S(1)}, u32[]{:S(2)}, u32[]{:S(2)}) %collective-permute-start.8) | collective-permute-done | bytes 139296 | tf_op jit(solution)/shard_map/ppermute | solution.py:346
  41.2 4.7 %collective-permute-start.14 = (bf16[3,64,128]{2,1,0:T(8,128)(2,1)S(1)}, bf16[3,64,128]{2,1,0:T(8,128)(2,1)S(1)}, u32[]{:S(2)}, u32[]{:S(2)}) collective-permute-start(bf16[3,64,128]{2,1,0:T(8,128)(2,1)S(1)} %get-tuple-element.67), channel_id=1, source_target_pairs={{0,240},{16,32},{32,16},{48,64},{64,48},{80,96},{96,80},{112,128},... | collective-permute-start | bytes 147464 | tf_op jit(solution)/shard_map/ppermute | solution.py:359
  46.2 3.4 %collective-permute-start.12 = (bf16[136,128]{1,0:T(8,128)(2,1)S(1)}, bf16[136,128]{1,0:T(8,128)(2,1)S(1)}, u32[]{:S(2)}, u32[]{:S(2)}) collective-permute-start(bf16[136,128]{1,0:T(8,128)(2,1)S(1)} %get-tuple-element.108), channel_id=1, source_target_pairs={{0,32},{1,33},{2,34},{3,35},{4,36},{5,37},{6,38},{7,39},{8,40},{9,... | collective-permute-start | bytes 104456 | tf_op jit(solution)/shard_map/ppermute | solution.py:378
  49.6 1.5 %collective-permute-done.11 = bf16[328,128]{1,0:T(8,128)(2,1)S(1)} collective-permute-done((bf16[328,128]{1,0:T(8,128)(2,1)S(1)}, bf16[328,128]{1,0:T(8,128)(2,1)S(1)}, u32[]{:S(2)}, u32[]{:S(2)}) %collective-permute-start.11) | collective-permute-done | bytes 84000 | tf_op jit(solution)/shard_map/ppermute | solution.py:378
  52.1 3.9 %collective-permute-start.17 = (bf16[136,128]{1,0:T(8,128)(2,1)S(1)}, bf16[136,128]{1,0:T(8,128)(2,1)S(1)}, u32[]{:S(2)}, u32[]{:S(2)}) collective-permute-start(bf16[136,128]{1,0:T(8,128)(2,1)S(1)} %fusion.11), channel_id=1, source_target_pairs={{0,193},{1,192},{2,195},{3,194},{4,197},{5,196},{6,199},{7,198},{8... | collective-permute-start | bytes 104456 | tf_op jit(solution)/shard_map/ppermute | solution.py:378
  56.6 1.9 %collective-permute-start.15 = (bf16[136,128]{1,0:T(8,128)(2,1)S(1)}, bf16[136,128]{1,0:T(8,128)(2,1)S(1)}, u32[]{:S(2)}, u32[]{:S(2)}) collective-permute-start(bf16[136,128]{1,0:T(8,128)(2,1)S(1)} %fusion.11), channel_id=1, source_target_pairs={{0,65},{1,64},{2,67},{3,66},{4,69},{5,68},{6,71},{7,70},{8,73},{9,... | collective-permute-start | bytes 104456 | tf_op jit(solution)/shard_map/ppermute | solution.py:378
  58.6 5.3 %collective-permute-done.16 = bf16[136,128]{1,0:T(8,128)(2,1)S(1)} collective-permute-done((bf16[136,128]{1,0:T(8,128)(2,1)S(1)}, bf16[136,128]{1,0:T(8,128)(2,1)S(1)}, u32[]{:S(2)}, u32[]{:S(2)}) %collective-permute-start.16) | collective-permute-done | bytes 34848 | tf_op jit(solution)/shard_map/ppermute | solution.py:378
  64.0 3.7 %collective-permute-done.18 = f32[136,128]{1,0:T(8,128)S(1)} collective-permute-done((f32[136,128]{1,0:T(8,128)S(1)}, f32[136,128]{1,0:T(8,128)S(1)}, u32[]{:S(2)}, u32[]{:S(2)}) %collective-permute-start.18) | collective-permute-done | bytes 69664 | tf_op jit(solution)/shard_map/ppermute | solution.py:346
  67.8 1.5 %collective-permute-start.21 = (bf16[136,128]{1,0:T(8,128)(2,1)S(1)}, bf16[136,128]{1,0:T(8,128)(2,1)S(1)}, u32[]{:S(2)}, u32[]{:S(2)}) collective-permute-start(bf16[136,128]{1,0:T(8,128)(2,1)S(1)} %add_convert_fusion), channel_id=1, source_target_pairs={{0,32},{1,33},{2,34},{3,35},{4,36},{5,37},{6,38},{7,39},{8,40},{9,... | collective-permute-start | bytes 104456 | tf_op jit(solution)/shard_map/ppermute | solution.py:378
  70.8 1.6 %collective-permute-done.21 = bf16[136,128]{1,0:T(8,128)(2,1)S(1)} collective-permute-done((bf16[136,128]{1,0:T(8,128)(2,1)S(1)}, bf16[136,128]{1,0:T(8,128)(2,1)S(1)}, u32[]{:S(2)}, u32[]{:S(2)}) %collective-permute-start.21) | collective-permute-done | bytes 34848 | tf_op jit(solution)/shard_map/ppermute | solution.py:378
  72.4 2.0 %collective-permute-done.20 = bf16[136,128]{1,0:T(8,128)(2,1)S(1)} collective-permute-done((bf16[136,128]{1,0:T(8,128)(2,1)S(1)}, bf16[136,128]{1,0:T(8,128)(2,1)S(1)}, u32[]{:S(2)}, u32[]{:S(2)}) %collective-permute-start.20) | collective-permute-done | bytes 34848 | tf_op jit(solution)/shard_map/ppermute | solution.py:378
  77.8 2.4 %collective-permute-done.25.ytwo_ref = bf16[64,128]{1,0:T(8,128)(2,1)S(1)} collective-permute-done((bf16[64,128]{1,0:T(8,128)(2,1)S(1)}, bf16[64,128]{1,0:T(8,128)(2,1)S(1)}, u32[]{:S(2)}, u32[]{:S(2)}) %collective-permute-start.25) | collective-permute-done | bytes 16416 | tf_op jit(solution)/shard_map/ppermute | solution.py:359
  81.9 2.5 %collective-permute-start.28 = (bf16[4,2,136,128]{3,2,1,0:T(8,128)(2,1)S(1)}, bf16[4,2,136,128]{3,2,1,0:T(8,128)(2,1)S(1)}, u32[]{:S(2)}, u32[]{:S(2)}) collective-permute-start(bf16[4,2,136,128]{3,2,1,0:T(8,128)(2,1)S(1)} %pad_maximum_fusion), channel_id=1, source_target_pairs={{0,1},{1,0},{2,3},{3,2},{4,5},{5,4},{6,7},{7,6},{8,9},{9,8},{10,11... | collective-permute-start | bytes 835592 | tf_op jit(solution)/shard_map/ppermute | solution.py:346
  84.5 2.4 %collective-permute-done.27.b1_ref = bf16[2,2,136,128]{3,2,1,0:T(8,128)(2,1)S(1)} collective-permute-done((bf16[2,2,136,128]{3,2,1,0:T(8,128)(2,1)S(1)}, bf16[2,2,136,128]{3,2,1,0:T(8,128)(2,1)S(1)}, u32[]{:S(2)}, u32[]{:S(2)}) %collective-permute-start.27) | collective-permute-done | bytes 139296 | tf_op jit(solution)/shard_map/ppermute | solution.py:346
  86.9 2.0 %collective-permute-start.29 = (bf16[4,2,136,128]{3,2,1,0:T(8,128)(2,1)S(1)}, bf16[4,2,136,128]{3,2,1,0:T(8,128)(2,1)S(1)}, u32[]{:S(2)}, u32[]{:S(2)}) collective-permute-start(bf16[4,2,136,128]{3,2,1,0:T(8,128)(2,1)S(1)} %pad_maximum_fusion.1), channel_id=1, source_target_pairs={{0,1},{1,0},{2,3},{3,2},{4,5},{5,4},{6,7},{7,6},{8,9},{9,8},{10,11... | collective-permute-start | bytes 835592 | tf_op jit(solution)/shard_map/ppermute | solution.py:346
  90.1 1.7 %unpack.1 = (f32[1728,192]{1,0:T(8,128)}, f32[1728,128]{1,0:T(8,128)}) custom-call(bf16[2,2,136,128]{3,2,1,0:T(8,128)(2,1)S(1)} %pad_maximum_fusion.3.a0_ref, bf16[2,2,136,128]{3,2,1,0:T(8,128)(2,1)S(1)} %collective-permute-done.26.a1_ref, bf16[2,2,136,128]{3,2,1,0:T(8,128)(2,1)S(1)} %pad_maximum_fusion.4.b0_ref, ...), custom_call_target="tpu_custom_call" | custom-call | flops 1000000 | bytes 5000000 | tf_op jit(solution)/shard_map/unpack/pallas_call | solution.py:121
  (64 shorter events, 17.3 us)
Async XLA Ops:
  2.1 12.3 %collective-permute-start = (bf16[3,64,128]{2,1,0:T(8,128)(2,1)S(1)}, bf16[3,64,128]{2,1,0:T(8,128)(2,1)S(1)}, u32[]{:S(2)}, u32[]{:S(2)}) collective-permute-start(bf16[3,64,128]{2,1,0:T(8,128)(2,1)S(1)} %get-tuple-element.52), channel_id=1, source_target_pairs={{0,240},{16,32},{32,16},{48,64},{64,48},{80,96},{96,80},{112,128},... | collective-permute-start | bytes 147464 | tf_op jit(solution)/shard_map/ppermute | solution.py:359
  11.2 8.8 %collective-permute-start.1 = (bf16[7,64,128]{2,1,0:T(8,128)(2,1)S(1)}, bf16[7,64,128]{2,1,0:T(8,128)(2,1)S(1)}, u32[]{:S(2)}, u32[]{:S(2)}) collective-permute-start(bf16[7,64,128]{2,1,0:T(8,128)(2,1)S(1)} %get-tuple-element.53), channel_id=1, source_target_pairs={{0,240},{16,32},{32,16},{48,64},{64,48},{80,96},{96,80},{112,128},... | collective-permute-start | bytes 344072 | tf_op jit(solution)/shard_map/ppermute | solution.py:359
  12.0 8.0 %collective-permute-start.3 = (bf16[7,64,128]{2,1,0:T(8,128)(2,1)S(1)}, bf16[7,64,128]{2,1,0:T(8,128)(2,1)S(1)}, u32[]{:S(2)}, u32[]{:S(2)}) collective-permute-start(bf16[7,64,128]{2,1,0:T(8,128)(2,1)S(1)} %get-tuple-element.55), channel_id=1, source_target_pairs={{0,16},{16,0},{32,48},{48,32},{64,80},{80,64},{96,112},{112,96},{1... | collective-permute-start | bytes 344072 | tf_op jit(solution)/shard_map/ppermute | solution.py:359
  14.5 6.2 %collective-permute-start.4 = (bf16[6,64,128]{2,1,0:T(8,128)(2,1)S(1)}, bf16[6,64,128]{2,1,0:T(8,128)(2,1)S(1)}, u32[]{:S(2)}, u32[]{:S(2)}) collective-permute-start(bf16[6,64,128]{2,1,0:T(8,128)(2,1)S(1)} %get-tuple-element.59), channel_id=1, source_target_pairs={{0,15},{1,2},{2,1},{3,4},{4,3},{5,6},{6,5},{7,8},{8,7},{9,10},{10,... | collective-permute-start | bytes 294920 | tf_op jit(solution)/shard_map/ppermute | solution.py:359
  26.6 4.1 %collective-permute-start.6 = (bf16[2368,128]{1,0:T(8,128)(2,1)S(1)}, bf16[2368,128]{1,0:T(8,128)(2,1)S(1)}, u32[]{:S(2)}, u32[]{:S(2)}) collective-permute-start(bf16[2368,128]{1,0:T(8,128)(2,1)S(1)} %get-tuple-element.62), channel_id=1, source_target_pairs={{0,1},{1,0},{2,3},{3,2},{4,5},{5,4},{6,7},{7,6},{8,9},{9,8},{10,11... | collective-permute-start | bytes 1818632 | tf_op jit(solution)/shard_map/ppermute | solution.py:346
  30.9 7.0 %collective-permute-start.8 = (bf16[2,2,136,128]{3,2,1,0:T(8,128)(2,1)S(1)}, bf16[2,2,136,128]{3,2,1,0:T(8,128)(2,1)S(1)}, u32[]{:S(2)}, u32[]{:S(2)}) collective-permute-start(bf16[2,2,136,128]{3,2,1,0:T(8,128)(2,1)S(1)} %pad_maximum_fusion.2), channel_id=1, source_target_pairs={{0,7},{1,6},{2,5},{3,4},{4,3},{5,2},{6,1},{7,0},{8,15},{9,14},{10,... | collective-permute-start | bytes 417800 | tf_op jit(solution)/shard_map/ppermute | solution.py:346
  33.9 5.4 %collective-permute-start.7 = (bf16[2,2,136,128]{3,2,1,0:T(8,128)(2,1)S(1)}, bf16[2,2,136,128]{3,2,1,0:T(8,128)(2,1)S(1)}, u32[]{:S(2)}, u32[]{:S(2)}) collective-permute-start(bf16[2,2,136,128]{3,2,1,0:T(8,128)(2,1)S(1)} %stack.56), channel_id=1, source_target_pairs={{0,3},{1,2},{2,1},{3,0},{4,7},{5,6},{6,5},{7,4},{8,11},{9,10},{10,... | collective-permute-start | bytes 417800 | tf_op jit(solution)/shard_map/ppermute | solution.py:346
  39.4 6.5 %collective-permute-start.10 = (bf16[2,136,128]{2,1,0:T(8,128)(2,1)S(1)}, bf16[2,136,128]{2,1,0:T(8,128)(2,1)S(1)}, u32[]{:S(2)}, u32[]{:S(2)}) collective-permute-start(bf16[2,136,128]{2,1,0:T(8,128)(2,1)S(1)} %get-tuple-element.99), channel_id=1, source_target_pairs={{0,3},{1,2},{2,1},{3,0},{4,7},{5,6},{6,5},{7,4},{8,11},{9,10},{10,... | collective-permute-start | bytes 208904 | tf_op jit(solution)/shard_map/ppermute | solution.py:346
  39.8 6.1 %collective-permute-start.9 = (bf16[2,136,128]{2,1,0:T(8,128)(2,1)S(1)}, bf16[2,136,128]{2,1,0:T(8,128)(2,1)S(1)}, u32[]{:S(2)}, u32[]{:S(2)}) collective-permute-start(bf16[2,136,128]{2,1,0:T(8,128)(2,1)S(1)} %get-tuple-element.100), channel_id=1, source_target_pairs={{0,7},{1,6},{2,5},{3,4},{4,3},{5,2},{6,1},{7,0},{8,15},{9,14},{10,... | collective-permute-start | bytes 208904 | tf_op jit(solution)/shard_map/ppermute | solution.py:346
  41.2 10.0 %collective-permute-start.14 = (bf16[3,64,128]{2,1,0:T(8,128)(2,1)S(1)}, bf16[3,64,128]{2,1,0:T(8,128)(2,1)S(1)}, u32[]{:S(2)}, u32[]{:S(2)}) collective-permute-start(bf16[3,64,128]{2,1,0:T(8,128)(2,1)S(1)} %get-tuple-element.67), channel_id=1, source_target_pairs={{0,240},{16,32},{32,16},{48,64},{64,48},{80,96},{96,80},{112,128},... | collective-permute-start | bytes 147464 | tf_op jit(solution)/shard_map/ppermute | solution.py:359
  46.0 5.1 %collective-permute-start.11 = (bf16[328,128]{1,0:T(8,128)(2,1)S(1)}, bf16[328,128]{1,0:T(8,128)(2,1)S(1)}, u32[]{:S(2)}, u32[]{:S(2)}) collective-permute-start(bf16[328,128]{1,0:T(8,128)(2,1)S(1)} %pad_maximum_fusion.5), channel_id=1, source_target_pairs={{0,17},{1,16},{2,19},{3,18},{4,21},{5,20},{6,23},{7,22},{8,25},{9,... | collective-permute-start | bytes 251912 | tf_op jit(solution)/shard_map/ppermute | solution.py:378
  46.1 5.9 %collective-permute-start.13 = (bf16[136,128]{1,0:T(8,128)(2,1)S(1)}, bf16[136,128]{1,0:T(8,128)(2,1)S(1)}, u32[]{:S(2)}, u32[]{:S(2)}) collective-permute-start(bf16[136,128]{1,0:T(8,128)(2,1)S(1)} %get-tuple-element.107), channel_id=1, source_target_pairs={{0,49},{1,48},{2,51},{3,50},{4,53},{5,52},{6,55},{7,54},{8,57},{9,... | collective-permute-start | bytes 104456 | tf_op jit(solution)/shard_map/ppermute | solution.py:378
  46.2 5.8 %collective-permute-start.12 = (bf16[136,128]{1,0:T(8,128)(2,1)S(1)}, bf16[136,128]{1,0:T(8,128)(2,1)S(1)}, u32[]{:S(2)}, u32[]{:S(2)}) collective-permute-start(bf16[136,128]{1,0:T(8,128)(2,1)S(1)} %get-tuple-element.108), channel_id=1, source_target_pairs={{0,32},{1,33},{2,34},{3,35},{4,36},{5,37},{6,38},{7,39},{8,40},{9,... | collective-permute-start | bytes 104456 | tf_op jit(solution)/shard_map/ppermute | solution.py:378
  52.1 6.5 %collective-permute-start.17 = (bf16[136,128]{1,0:T(8,128)(2,1)S(1)}, bf16[136,128]{1,0:T(8,128)(2,1)S(1)}, u32[]{:S(2)}, u32[]{:S(2)}) collective-permute-start(bf16[136,128]{1,0:T(8,128)(2,1)S(1)} %fusion.11), channel_id=1, source_target_pairs={{0,193},{1,192},{2,195},{3,194},{4,197},{5,196},{6,199},{7,198},{8... | collective-permute-start | bytes 104456 | tf_op jit(solution)/shard_map/ppermute | solution.py:378
  56.0 7.9 %collective-permute-start.16 = (bf16[136,128]{1,0:T(8,128)(2,1)S(1)}, bf16[136,128]{1,0:T(8,128)(2,1)S(1)}, u32[]{:S(2)}, u32[]{:S(2)}) collective-permute-start(bf16[136,128]{1,0:T(8,128)(2,1)S(1)} %fusion.11), channel_id=1, source_target_pairs={{0,128},{1,129},{2,130},{3,131},{4,132},{5,133},{6,134},{7,135},{8... | collective-permute-start | bytes 104456 | tf_op jit(solution)/shard_map/ppermute | solution.py:378
  56.6 7.4 %collective-permute-start.15 = (bf16[136,128]{1,0:T(8,128)(2,1)S(1)}, bf16[136,128]{1,0:T(8,128)(2,1)S(1)}, u32[]{:S(2)}, u32[]{:S(2)}) collective-permute-start(bf16[136,128]{1,0:T(8,128)(2,1)S(1)} %fusion.11), channel_id=1, source_target_pairs={{0,65},{1,64},{2,67},{3,66},{4,69},{5,68},{6,71},{7,70},{8,73},{9,... | collective-permute-start | bytes 104456 | tf_op jit(solution)/shard_map/ppermute | solution.py:378
  67.8 4.7 %collective-permute-start.21 = (bf16[136,128]{1,0:T(8,128)(2,1)S(1)}, bf16[136,128]{1,0:T(8,128)(2,1)S(1)}, u32[]{:S(2)}, u32[]{:S(2)}) collective-permute-start(bf16[136,128]{1,0:T(8,128)(2,1)S(1)} %add_convert_fusion), channel_id=1, source_target_pairs={{0,32},{1,33},{2,34},{3,35},{4,36},{5,37},{6,38},{7,39},{8,40},{9,... | collective-permute-start | bytes 104456 | tf_op jit(solution)/shard_map/ppermute | solution.py:378
  69.3 5.2 %collective-permute-start.20 = (bf16[136,128]{1,0:T(8,128)(2,1)S(1)}, bf16[136,128]{1,0:T(8,128)(2,1)S(1)}, u32[]{:S(2)}, u32[]{:S(2)}) collective-permute-start(bf16[136,128]{1,0:T(8,128)(2,1)S(1)} %add_convert_fusion), channel_id=1, source_target_pairs={{0,49},{1,48},{2,51},{3,50},{4,53},{5,52},{6,55},{7,54},{8,57},{9,... | collective-permute-start | bytes 104456 | tf_op jit(solution)/shard_map/ppermute | solution.py:378
  70.4 4.1 %collective-permute-start.19 = (bf16[136,128]{1,0:T(8,128)(2,1)S(1)}, bf16[136,128]{1,0:T(8,128)(2,1)S(1)}, u32[]{:S(2)}, u32[]{:S(2)}) collective-permute-start(bf16[136,128]{1,0:T(8,128)(2,1)S(1)} %add_convert_fusion), channel_id=1, source_target_pairs={{0,17},{1,16},{2,19},{3,18},{4,21},{5,20},{6,23},{7,22},{8,25},{9,... | collective-permute-start | bytes 104456 | tf_op jit(solution)/shard_map/ppermute | solution.py:378
  74.5 5.7 %collective-permute-start.23 = (bf16[2,136,128]{2,1,0:T(8,128)(2,1)S(1)}, bf16[2,136,128]{2,1,0:T(8,128)(2,1)S(1)}, u32[]{:S(2)}, u32[]{:S(2)}) collective-permute-start(bf16[2,136,128]{2,1,0:T(8,128)(2,1)S(1)} %get-tuple-element.104), channel_id=1, source_target_pairs={{0,3},{1,2},{2,1},{3,0},{4,7},{5,6},{6,5},{7,4},{8,11},{9,10},{10,... | collective-permute-start | bytes 208904 | tf_op jit(solution)/shard_map/ppermute | solution.py:346
  75.3 5.1 %collective-permute-start.22 = (bf16[2,136,128]{2,1,0:T(8,128)(2,1)S(1)}, bf16[2,136,128]{2,1,0:T(8,128)(2,1)S(1)}, u32[]{:S(2)}, u32[]{:S(2)}) collective-permute-start(bf16[2,136,128]{2,1,0:T(8,128)(2,1)S(1)} %get-tuple-element.109), channel_id=1, source_target_pairs={{0,7},{1,6},{2,5},{3,4},{4,3},{5,2},{6,1},{7,0},{8,15},{9,14},{10,... | collective-permute-start | bytes 208904 | tf_op jit(solution)/shard_map/ppermute | solution.py:346
  80.5 6.4 %collective-permute-start.27 = (bf16[2,2,136,128]{3,2,1,0:T(8,128)(2,1)S(1)}, bf16[2,2,136,128]{3,2,1,0:T(8,128)(2,1)S(1)}, u32[]{:S(2)}, u32[]{:S(2)}) collective-permute-start(bf16[2,2,136,128]{3,2,1,0:T(8,128)(2,1)S(1)} %pad_maximum_fusion.4.b0_ref), channel_id=1, source_target_pairs={{0,7},{1,6},{2,5},{3,4},{4,3},{5,2},{6,1},{7,0},{8,15},{9,14},{10,... | collective-permute-start | bytes 417800 | tf_op jit(solution)/shard_map/ppermute | solution.py:346
  81.7 5.2 %collective-permute-start.26 = (bf16[2,2,136,128]{3,2,1,0:T(8,128)(2,1)S(1)}, bf16[2,2,136,128]{3,2,1,0:T(8,128)(2,1)S(1)}, u32[]{:S(2)}, u32[]{:S(2)}) collective-permute-start(bf16[2,2,136,128]{3,2,1,0:T(8,128)(2,1)S(1)} %pad_maximum_fusion.3.a0_ref), channel_id=1, source_target_pairs={{0,3},{1,2},{2,1},{3,0},{4,7},{5,6},{6,5},{7,4},{8,11},{9,10},{10,... | collective-permute-start | bytes 417800 | tf_op jit(solution)/shard_map/ppermute | solution.py:346
  81.9 8.0 %collective-permute-start.28 = (bf16[4,2,136,128]{3,2,1,0:T(8,128)(2,1)S(1)}, bf16[4,2,136,128]{3,2,1,0:T(8,128)(2,1)S(1)}, u32[]{:S(2)}, u32[]{:S(2)}) collective-permute-start(bf16[4,2,136,128]{3,2,1,0:T(8,128)(2,1)S(1)} %pad_maximum_fusion), channel_id=1, source_target_pairs={{0,1},{1,0},{2,3},{3,2},{4,5},{5,4},{6,7},{7,6},{8,9},{9,8},{10,11... | collective-permute-start | bytes 835592 | tf_op jit(solution)/shard_map/ppermute | solution.py:346
  (6 other events, 17.4 us)
